TPU v7x, 32 devices: a whole 2x2x4 slice. The times are simulated.
32 devices in a mesh: dom: 1, ep: 16 (over z, y, x), grp: 2 (over core).
Axes of the slice: x: 2, y: 2, z: 4, core: 2. Of those that a mesh axis runs over, the one named last changes fastest.
Arguments:
- hidden: bfloat16 [512, 7168], P(('dom', 'ep', 'grp')), may hold values from -6 to 6
- gain: float32 [7168], replicated, may hold values from 0.1 to 1.9
- router_w: bfloat16 [7168, 8], replicated, may hold values from -0.0625 to 0.0625
- routes: int32 [512, 4], P(('dom', 'ep', 'grp')), may hold values from 0 to 7, all different within a row; in each aligned block of 16 rows (0 to 15, 16 to 31, ...) at most 16 rows name the same one
- w_gate: bfloat16 [16, 2, 7168, 256], P('ep', 'grp'), may hold values from -0.0625 to 0.0625
- w_up: bfloat16 [16, 2, 7168, 256], P('ep', 'grp'), may hold values from -0.0625 to 0.0625
- w_down: bfloat16 [16, 2, 256, 7168], P('ep', 'grp'), may hold values from -0.1875 to 0.1875
Outputs:
- mixed: bfloat16 [512, 7168], P(('dom', 'ep', 'grp'))
Inputs may be any that keep to these rules, and one draw needn't show every extreme that they name: `routes`: each token names 4 different experts; among the tokens of one device no expert is named by more than 16 tokens, a bound that some block reaches.
All inputs are finite; a program needn't handle non-finite values.
Results may differ from a plain program's by a relative error of at most 0.0072.
Values may be sent and summed in bfloat16 or wider, within the bound.
No kernel may reach another device: no remote copies, remote signals or barrier semaphores. Data moves between devices by JAX's collectives and lax.ppermute only.
A program may use at most 64 MiB of HBM per device.

v0:
```python
import jax
import jax.numpy as jnp
from jax import lax
from jax.sharding import PartitionSpec as P

SPLIT = 4
TOP = 4


EPSILON = 1e-06
ROUTE_SCALE = 2.5


def normalize(hidden, gain):
    values = hidden.astype(jnp.float32)
    square_mean = jnp.mean(values * values, axis=1, keepdims=True)
    return (values * lax.rsqrt(square_mean + EPSILON) * gain[None, :]).astype(jnp.bfloat16)


def affinity_weights(normed, router_w, routes, expert_count):
    logits = jnp.dot(normed, router_w, preferred_element_type=jnp.float32)
    scores = jax.nn.sigmoid(logits)
    one_hot = (
        routes[:, :, None] == jnp.arange(expert_count, dtype=jnp.int32)[None, None, :]
    ).astype(jnp.float32)
    chosen = jnp.sum(one_hot * scores[:, None, :], axis=2)
    return ROUTE_SCALE * chosen / jnp.sum(chosen, axis=1, keepdims=True)


def slot_table(expert_ids, valid, expert_count, slot_cap):
    flat_ids = expert_ids.reshape(-1)
    flat_valid = valid.reshape(-1)
    one_hot = (
        (flat_ids[:, None] == jnp.arange(expert_count, dtype=jnp.int32)[None, :])
        & flat_valid[:, None]
    ).astype(jnp.int32)
    before = jnp.cumsum(one_hot, axis=0) - one_hot
    position = jnp.sum(before * one_hot, axis=1)
    target = jnp.where(flat_valid, flat_ids * slot_cap + position, -1)
    table = (
        target[None, :] == jnp.arange(expert_count * slot_cap, dtype=jnp.int32)[:, None]
    ).astype(jnp.float32)
    return table.reshape(expert_count * slot_cap, expert_ids.shape[0], expert_ids.shape[1])


def gather_slots(table, normed):
    selector = jnp.sum(table, axis=2).astype(jnp.bfloat16)
    return jnp.dot(selector, normed, preferred_element_type=jnp.float32).astype(jnp.bfloat16)


def combine_rows(table, weights, summed):
    mixing = jnp.sum(table * weights[None, :, :], axis=2).T
    return jnp.dot(
        mixing, summed, preferred_element_type=jnp.float32, precision=lax.Precision.HIGHEST
    )


def expert_rows(received, gate_w, up_w, down_w):
    shape_in = received.shape
    flat_rows = received.reshape(-1, shape_in[-1])
    gate_part = jnp.dot(flat_rows, gate_w, preferred_element_type=jnp.float32)
    up_part = jnp.dot(flat_rows, up_w, preferred_element_type=jnp.float32)
    activated = (jax.nn.silu(gate_part) * up_part).astype(jnp.bfloat16)
    output = jnp.dot(activated, down_w, preferred_element_type=jnp.float32).astype(jnp.bfloat16)
    return output.reshape(shape_in[:-1] + (down_w.shape[1],))


def local(hidden, gain, router_w, routes, w_gate, w_up, w_down):
    ep_count = lax.axis_size("ep")
    grp_count = lax.axis_size("grp")
    local_experts = ep_count // SPLIT
    expert_count = local_experts * grp_count
    tok_rows = hidden.shape[0]
    width = hidden.shape[1]
    slot_cap = max(2, min(tok_rows, 2 * tok_rows * TOP // expert_count))
    gate_w = w_gate[0, 0]
    up_w = w_up[0, 0]
    down_w = w_down[0, 0]
    normed = normalize(hidden, gain)
    weights = affinity_weights(normed, router_w, routes, expert_count)
    valid = jnp.ones(routes.shape, jnp.bool_)
    table = slot_table(routes, valid, expert_count, slot_cap)
    buffers = gather_slots(table, normed)
    buffers = buffers.reshape(grp_count, local_experts, slot_cap, width).transpose(1, 0, 2, 3)
    buffers = jnp.broadcast_to(buffers[:, None], (local_experts, SPLIT, grp_count, slot_cap, width))
    buffers = buffers.reshape(ep_count * grp_count, slot_cap, width)
    partial_value = expert_rows(
        lax.all_to_all(buffers, ("ep", "grp"), split_axis=0, concat_axis=0, tiled=True),
        gate_w,
        up_w,
        down_w,
    )
    returned = lax.all_to_all(partial_value, ("ep", "grp"), split_axis=0, concat_axis=0, tiled=True)
    summed = (
        returned.reshape(local_experts, SPLIT, grp_count, slot_cap, width)
        .astype(jnp.float32)
        .sum(axis=1)
    )
    summed = summed.transpose(1, 0, 2, 3).reshape(expert_count * slot_cap, width)
    mixed = combine_rows(table, weights, summed)
    return mixed.astype(jnp.bfloat16)


def solution(mesh):
    in_specs = (
        P(("dom", "ep", "grp"), None),
        P(),
        P(),
        P(("dom", "ep", "grp"), None),
        P("ep", "grp", None, None),
        P("ep", "grp", None, None),
        P("ep", "grp", None, None),
    )
    out_specs = P(("dom", "ep", "grp"), None)
    return jax.shard_map(local, mesh=mesh, in_specs=in_specs, out_specs=out_specs, check_vma=False)
```

profile of v0, /device:TPU:0, one launch (start us, length us, event | category | flops | bytes accessed | tf_op | source)
XLA Modules:
  0.0 366.4 jit_solution(10210975816192610915)
XLA Ops:
  0.0 1.1 fusion.16
  1.2 0.8 copy.29
  1.9 1.2 fusion.13
  3.1 0.7 select_reduce_fusion.2
  3.8 0.1 eq.42
  3.9 0.1 fusion.22
  4.0 0.1 reduce_window_sum.11
  4.1 0.2 select_reduce_fusion.1
  4.3 0.1 reduce_sum.66
  4.4 0.1 copy.30
  4.5 0.7 multiply_add_fusion
  5.2 0.1 convert_reduce_fusion.1
  5.3 1.6 convolution_convert_fusion.1
  6.9 0.2 copy.31
  7.1 0.9 broadcast_in_dim.3
  8.0 0.0 copy-start.2
  8.0 168.2 %all_to_all.10 = bf16[32,16,7168]{2,1,0:T(8,128)(2,1)S(1)} all-to-all(bf16[32,16,7168]{2,1,0:T(8,128)(2,1)S(1)} %bitcast.34), channel_id=1, replica_groups=mesh['dom'=1,'ep'=16,'grp'=2] {'ep','grp'}, dimensions={0} | all-to-all | bytes 14680064 | tf_op jit(solution)/shard_map/all_to_all | solution.py:88
  176.1 3.0 copy-done.1
  179.1 2.1 fusion.3
  181.2 16.0 %convolution_convert_fusion = bf16[512,7168]{1,0:T(8,128)(2,1)} fusion(bf16[1,1,256,7168]{3,2,1,0:T(8,128)(2,1)} %param.13, bf16[512,7168]{1,0:T(8,128)(2,1)} %bitcast.32, bf16[1,1,7168,256]{3,2,1,0:T(8,128)(2,1)} %param.12, f32[512,256]{1,0:T(8,128)S(1)} %fusion.3), kind=kOutput, calls=%fused_computation.1 | convolution fusion | flops 3762552832 | bytes 22544384 | tf_op jit(solution)/shard_map/dot_general | solution.py:64
  197.2 164.9 %all_to_all.11 = bf16[32,16,7168]{2,1,0:T(8,128)(2,1)S(1)} all-to-all(bf16[32,16,7168]{2,1,0:T(8,128)(2,1)} %bitcast.33), channel_id=1, replica_groups=mesh['dom'=1,'ep'=16,'grp'=2] {'ep','grp'}, dimensions={0} | all-to-all | bytes 14680064 | tf_op jit(solution)/shard_map/all_to_all | solution.py:93
  362.1 1.5 convert_reduce_fusion
  363.6 0.3 copy.32
  363.9 2.5 convolution_convert_fusion.2
  (6 shorter events, 0.0 us)
Async XLA Ops:
  0.0 1.9 copy-start
  8.0 171.2 %copy-start.2 = (bf16[1,1,7168,256]{3,2,1,0:T(8,128)(2,1)S(1)}, bf16[1,1,7168,256]{3,2,1,0:T(8,128)(2,1)}, u32[]{:S(2)}) copy-start(bf16[1,1,7168,256]{3,2,1,0:T(8,128)(2,1)} %param.11) | copy-start | bytes 11010052
  176.1 3.0 copy-start.1
where the time goes:
time: 367 us; the launch traced here: 366 us
  blocking collectives  333 us (91%)
  matrix products  23.4 us (6%)
  local copies, waits for them, and re-layouts  5.34 us (1%)
  other arithmetic  4.48 us (1%)
    all_to_all x1, blocking collectives, local(): lax.all_to_all(buffers, ('ep', 'grp'), split_axis=0, concat_axis=0, tiled...  168 us
    all_to_all x1, blocking collectives, local(): lax.all_to_all(partial_value, ('ep', 'grp'), split_axis=0, concat_axis=0,...  165 us
    dot_general x1, matrix products, expert_rows(): jnp.dot(activated, down_w, preferred_element_type=jnp.float32)  16 us

commit v1 on v0

v1 whole, which is shorter than its diff:
```python
import jax
import jax.numpy as jnp
from jax import lax
from jax.sharding import PartitionSpec as P

SPLIT = 4
TOP = 4

EPSILON = 1e-06
ROUTE_SCALE = 2.5


def normalize(hidden, gain):
    values = hidden.astype(jnp.float32)
    square_mean = jnp.mean(values * values, axis=1, keepdims=True)
    return (values * lax.rsqrt(square_mean + EPSILON) * gain[None, :]).astype(jnp.bfloat16)


def expert_coeffs(normed, router_w, routes, expert_count):
    logits = jnp.dot(normed, router_w, preferred_element_type=jnp.float32)
    scores = jax.nn.sigmoid(logits)
    named = (routes[:, :, None] == jnp.arange(expert_count, dtype=jnp.int32)[None, None, :]).any(axis=1)
    chosen = jnp.where(named, scores, 0.0)
    return ROUTE_SCALE * chosen / jnp.sum(chosen, axis=1, keepdims=True)


def local(hidden, gain, router_w, routes, w_gate, w_up, w_down):
    ep_count = lax.axis_size("ep")
    grp_count = lax.axis_size("grp")
    local_experts = ep_count // SPLIT
    expert_count = local_experts * grp_count
    normed = normalize(hidden, gain)
    coeffs = expert_coeffs(normed, router_w, routes, expert_count)
    all_coeffs = lax.all_gather(coeffs, ("ep", "grp"), axis=0, tiled=True)
    tokens = lax.all_gather(normed, ("ep", "grp"), axis=0, tiled=True)
    owner = lax.axis_index("grp") * local_experts + lax.axis_index("ep") // SPLIT
    column = lax.dynamic_slice_in_dim(all_coeffs, owner, 1, axis=1)
    gate_part = jnp.dot(tokens, w_gate[0, 0], preferred_element_type=jnp.float32)
    up_part = jnp.dot(tokens, w_up[0, 0], preferred_element_type=jnp.float32)
    activated = (jax.nn.silu(gate_part) * up_part).astype(jnp.bfloat16)
    partial_value = jnp.dot(activated, w_down[0, 0], preferred_element_type=jnp.float32)
    weighted = (partial_value * column).astype(jnp.bfloat16)
    return lax.psum_scatter(weighted, ("ep", "grp"), scatter_dimension=0, tiled=True)


def solution(mesh):
    in_specs = (
        P(("dom", "ep", "grp"), None),
        P(),
        P(),
        P(("dom", "ep", "grp"), None),
        P("ep", "grp", None, None),
        P("ep", "grp", None, None),
        P("ep", "grp", None, None),
    )
    out_specs = P(("dom", "ep", "grp"), None)
    return jax.shard_map(local, mesh=mesh, in_specs=in_specs, out_specs=out_specs, check_vma=False)
```

time: 367 us -> 262 us (0.71)
  blocking collectives: 333 us -> 43.9 us
  waiting for transfers between devices: 0 us -> 177 us
  between operations: 0.08 us -> 13.5 us
  local copies, waits for them, and re-layouts: 5.34 us -> 0.15 us
    all_to_all x2 -> x0, blocking collectives: 333 us -> none  [the longest x1 168 us: local(): lax.all_to_all(buffers, ('ep', 'grp'), split_axis=0, concat_axis=0, tiled...]
    reduce_scatter x0 -> x1, waiting for transfers between devices: none -> 146 us  [local(): lax.psum_scatter(weighted, ('ep', 'grp'), scatter_dimension=0, tiled=True)]
    all_gather x0 -> x1, blocking collectives: none -> 43.9 us  [local(): all_coeffs = lax.all_gather(coeffs, ('ep', 'grp'), axis=0, tiled=True)]
    all_gather x0 -> x1, waiting for transfers between devices: none -> 31.2 us  [local(): tokens = lax.all_gather(normed, ('ep', 'grp'), axis=0, tiled=True)]
    dot_general x5 -> x3, matrix products: 23.4 us -> 23.3 us  [the longest x1 16 us: local(): jnp.dot(activated, w_down[0, 0], preferred_element_type=jnp.float32)]
  transfers between devices with their start and end apart: 0 -> 2, of which waited for: 0 -> 2; matrix products, arithmetic and copies ran while one was open for 0% -> 1% of each run, Pallas kernels for 0% -> 0%
where the time goes in v1:
time: 262 us; the launch traced here: 261 us
  waiting for transfers between devices  177 us (68%)
  blocking collectives  43.9 us (17%)
  matrix products  23.3 us (9%)
  between operations  13.5 us (5%)
  other arithmetic  3.61 us (1%)
    reduce_scatter x1, waiting for transfers between devices, local(): lax.psum_scatter(weighted, ('ep', 'grp'), scatter_dimension=0, tiled=True)  146 us
    all_gather x1, blocking collectives, local(): all_coeffs = lax.all_gather(coeffs, ('ep', 'grp'), axis=0, tiled=True)  43.9 us
    all_gather x1, waiting for transfers between devices, local(): tokens = lax.all_gather(normed, ('ep', 'grp'), axis=0, tiled=True)  31.2 us
    dot_general x1, matrix products, local(): jnp.dot(activated, w_down[0, 0], preferred_element_type=jnp.float32)  16 us
    dot_general x1, matrix products, local(): jnp.dot(tokens, w_gate[0, 0], preferred_element_type=jnp.float32)  6.18 us
  transfers between devices with their start and end apart: 2, of which 2 were waited for; matrix products, arithmetic and copies ran while one was open for 1% of the time, Pallas kernels for 0%

profile of v1, /device:TPU:0, one launch (start us, length us, event | category | flops | bytes accessed | tf_op | source)
XLA Modules:
  0.0 261.4 jit_solution(8840083850985341005)
XLA Ops:
  6.5 0.0 copy-start
  6.5 0.0 all-gather.3.cloned.1.call-start
  6.5 1.1 fusion.15
  7.7 1.8 fusion.17
  9.4 0.0 all-gather.3.cloned.1.call-update
  9.5 0.0 reduce-scatter.2.cloned.1.call-start
  9.5 0.7 fusion.21
  10.2 0.0 copy-done
  10.2 1.1 fusion.23
  11.4 43.9 %all-gather = f32[32,16,8]{1,2,0:T(8,128)S(1)} all-gather(f32[1,16,8]{1,2,0:T(8,128)S(1)} %divide_bitcast_fusion), channel_id=1, replica_groups=mesh['dom'=1,'ep'=16,'grp'=2] {'ep','grp'}, dimensions={0}, use_global_device_ids=true | all-gather | bytes 16896 | tf_op jit(solution)/shard_map/all_gather | solution.py:34
  55.3 0.1 reshape.12
  55.4 31.2 %all-gather.3.cloned.1.call-done = bf16[512,7168]{1,0:T(8,128)(2,1)} async-done(((bf16[16,7168]{1,0:T(8,128)(2,1)}), bf16[512,7168]{1,0:T(8,128)(2,1)}) %all-gather.3.cloned.1.call-update) | async-done | bytes 7340048 | tf_op jit(solution)/shard_map/all_gather | solution.py:35
  86.7 6.2 %fusion.3 = f32[512,256]{1,0:T(8,128)S(1)} fusion(bf16[512,7168]{1,0:T(8,128)(2,1)} %all-gather.3.cloned.1.call-done, bf16[1,1,7168,256]{3,2,1,0:T(8,128)(2,1)} %param.11), kind=kOutput, calls=%fused_computation.4 | convolution fusion | flops 1879048192 | bytes 11534336 | tf_op jit(solution)/shard_map/dot_general | solution.py:38
  92.9 16.0 %multiply_convert_fusion = bf16[512,7168]{1,0:T(8,128)(2,1)} fusion(f32[512]{0:T(512)S(1)} %bitcast.24, bf16[1,1,256,7168]{3,2,1,0:T(8,128)(2,1)} %param.13, bf16[512,7168]{1,0:T(8,128)(2,1)} %all-gather.3.cloned.1.call-done, bf16[1,1,7168,256]{3,2,1,0:T(8,128)(2,1)} %param.12, f32[512,256]{1,0:T(8,128)S(1)} %fusion.3), kind=kOutput, calls=%fused_computation | convolution fusion | flops 3766222848 | bytes 22546432 | tf_op jit(solution)/shard_map/dot_general | solution.py:41
  108.9 0.0 reduce-scatter.2.cloned.1.call-update
  108.9 145.6 %reduce-scatter.2.cloned.1.call-done = bf16[16,7168]{1,0:T(8,128)(2,1)} async-done(((bf16[512,7168]{1,0:T(8,128)(2,1)}), bf16[16,7168]{1,0:T(8,128)(2,1)}) %reduce-scatter.2.cloned.1.call-update) | async-done | bytes 229392 | tf_op jit(solution)/shard_map/reduce_scatter | solution.py:43
  (4 shorter events, 0.1 us)
Async XLA Ops:
  6.5 3.7 %copy-start = (bf16[7168,8]{0,1:T(8,128)(2,1)S(1)}, bf16[7168,8]{0,1:T(8,128)(2,1)}, u32[]{:S(2)}) copy-start(bf16[7168,8]{0,1:T(8,128)(2,1)} %param.9) | copy-start | bytes 344068
  6.5 80.2 %all-gather.3.cloned.1.call-start = ((), (), s32[]{:S(2)}) async-start(), calls=%async_computation.1 | async-start | bytes 7569408 | tf_op jit(solution)/shard_map/all_gather | solution.py:35
  9.5 245.1 %reduce-scatter.2.cloned.1.call-start = ((), (), s32[]{:S(2)}) async-start(), calls=%async_computation.2 | async-start | bytes 7569408 | tf_op jit(solution)/shard_map/reduce_scatter | solution.py:43
Sparse Core Ops, SparseCore 0:
  10.2 76.4 all-gather.2
  109.0 145.4 reduce-scatter.1

commit v2 on v1

v2 whole, which is shorter than its diff:
```python
import functools

import jax
import jax.numpy as jnp
from jax import lax
from jax.experimental import pallas as pl
from jax.experimental.pallas import tpu as pltpu
from jax.sharding import PartitionSpec as P

SPLIT = 4
LANES = 128

EPSILON = 1e-06
ROUTE_SCALE = 2.5
VMEM_LIMIT = 56 * 1024 * 1024

TREE_16 = (
    (4, 4), (1, 1), (2, 2), (8, 8),
    (5, 1), (6, 2), (12, 4), (9, 1), (10, 2),
    (3, 1), (7, 2), (13, 4), (11, 1), (15, 2), (14, 4),
)


def gather_tree(ep_count):
    if ep_count == 16:
        return TREE_16
    return tuple((r, 1 << (r.bit_length() - 1)) for r in range(1, ep_count))


def across(value, bit, ep_count):
    return lax.ppermute(value, "ep", [(i, i ^ bit) for i in range(ep_count)])


def prepare_kernel(hidden_ref, gain_ref, routes_ref, out_ref):
    values = hidden_ref[...].astype(jnp.float32)
    width = values.shape[1]
    square_mean = jnp.mean(values * values, axis=1, keepdims=True)
    normed = values * lax.rsqrt(square_mean + EPSILON) * gain_ref[...]
    out_ref[:, :width] = normed.astype(jnp.bfloat16)
    routes = routes_ref[...]
    lanes = lax.broadcasted_iota(jnp.int32, (values.shape[0], LANES), 1)
    named = jnp.zeros((values.shape[0], LANES), jnp.float32)
    for k in range(routes.shape[1]):
        named = jnp.where(lanes == routes[:, k : k + 1], 1.0, named)
    out_ref[:, width:] = named.astype(jnp.bfloat16)


def prepare(hidden, gain, routes):
    rows, width = hidden.shape
    return pl.pallas_call(
        prepare_kernel,
        out_shape=jax.ShapeDtypeStruct((rows, width + LANES), jnp.bfloat16),
        compiler_params=pltpu.CompilerParams(vmem_limit_bytes=VMEM_LIMIT),
        cost_estimate=pl.CostEstimate(flops=6 * rows * width, bytes_accessed=4 * rows * width, transcendentals=rows),
        name="prepare",
    )(hidden, gain[None, :], routes)


def experts_kernel(blocks, k_steps, k_tile, ids_ref, *refs):
    token_refs = refs[:blocks]
    router_ref, gate0_ref, gate1_ref, up0_ref, up1_ref, down0_ref, down1_ref = refs[blocks : blocks + 7]
    out_refs = refs[blocks + 7 : 2 * blocks + 7]
    gates_ref, logits_ref, act_ref, coeff_ref = refs[2 * blocks + 7 :]
    step = pl.program_id(0)
    rows = token_refs[0].shape[0]
    hidden_units = gate0_ref.shape[1]
    width = k_steps * k_tile

    @pl.when(step < k_steps)
    def _():
        columns = pl.ds(pl.multiple_of(step * k_tile, LANES), k_tile)
        tokens = jnp.concatenate([ref[:, columns] for ref in token_refs], axis=0)
        parts = [
            jnp.dot(tokens, ref[...], preferred_element_type=jnp.float32)
            for ref in (gate0_ref, gate1_ref, up0_ref, up1_ref)
        ]
        logits = lax.dot_general(
            tokens, router_ref[...], (((1,), (1,)), ((), ())), preferred_element_type=jnp.float32
        )

        @pl.when(step == 0)
        def _():
            for i, part in enumerate(parts):
                gates_ref[:, i * hidden_units : (i + 1) * hidden_units] = part
            logits_ref[...] = logits

        @pl.when(step > 0)
        def _():
            for i, part in enumerate(parts):
                gates_ref[:, i * hidden_units : (i + 1) * hidden_units] += part
            logits_ref[...] += logits

    @pl.when(step == k_steps - 1)
    def _():
        gate_part = gates_ref[:, : 2 * hidden_units]
        up_part = gates_ref[:, 2 * hidden_units :]
        act_ref[...] = (jax.nn.silu(gate_part) * up_part).astype(jnp.bfloat16)
        named = jnp.concatenate([ref[:, width : width + LANES] for ref in token_refs], axis=0)
        experts = logits_ref.shape[1]
        scores = jax.nn.sigmoid(logits_ref[...])
        chosen = named[:, :experts].astype(jnp.float32) * scores
        weights = ROUTE_SCALE * chosen / jnp.sum(chosen, axis=1, keepdims=True)
        lanes = lax.broadcasted_iota(jnp.int32, weights.shape, 1)
        for i in range(2):
            column = jnp.sum(jnp.where(lanes == ids_ref[i], weights, 0.0), axis=1, keepdims=True)
            coeff_ref[:, i * LANES : (i + 1) * LANES] = jnp.broadcast_to(column, (column.shape[0], LANES))

    @pl.when(step >= k_steps)
    def _():
        total = coeff_ref[:, 0:1] * jnp.dot(
            act_ref[:, :hidden_units], down0_ref[...], preferred_element_type=jnp.float32
        ) + coeff_ref[:, LANES : LANES + 1] * jnp.dot(
            act_ref[:, hidden_units:], down1_ref[...], preferred_element_type=jnp.float32
        )
        for i, ref in enumerate(out_refs):
            ref[...] = total[i * rows : (i + 1) * rows].astype(jnp.bfloat16)


def experts(ids, token_blocks, router_t, gates, ups, downs):
    blocks = len(token_blocks)
    rows = token_blocks[0].shape[0]
    width, hidden_units = gates[0].shape
    k_tile = n_tile = 1024
    k_steps, n_steps = width // k_tile, width // n_tile
    all_rows = blocks * rows

    def at_k(step, ids_ref):
        return jnp.minimum(step, k_steps - 1)

    def at_n(step, ids_ref):
        return jnp.maximum(step - k_steps, 0)

    whole = pl.BlockSpec(token_blocks[0].shape, lambda step, ids_ref: (0, 0))
    in_specs = [whole] * blocks
    in_specs += [pl.BlockSpec((router_t.shape[0], k_tile), lambda step, ids_ref: (0, at_k(step, ids_ref)))]
    in_specs += [pl.BlockSpec((k_tile, hidden_units), lambda step, ids_ref: (at_k(step, ids_ref), 0))] * 4
    in_specs += [pl.BlockSpec((hidden_units, n_tile), lambda step, ids_ref: (0, at_n(step, ids_ref)))] * 2
    out_specs = [pl.BlockSpec((rows, n_tile), lambda step, ids_ref: (0, at_n(step, ids_ref)))] * blocks
    return pl.pallas_call(
        functools.partial(experts_kernel, blocks, k_steps, k_tile),
        grid_spec=pltpu.PrefetchScalarGridSpec(
            num_scalar_prefetch=1,
            grid=(k_steps + n_steps,),
            in_specs=in_specs,
            out_specs=out_specs,
            scratch_shapes=[
                pltpu.VMEM((all_rows, 4 * hidden_units), jnp.float32),
                pltpu.VMEM((all_rows, router_t.shape[0]), jnp.float32),
                pltpu.VMEM((all_rows, 2 * hidden_units), jnp.bfloat16),
                pltpu.VMEM((all_rows, 2 * LANES), jnp.float32),
            ],
        ),
        out_shape=[jax.ShapeDtypeStruct((rows, width), jnp.bfloat16)] * blocks,
        compiler_params=pltpu.CompilerParams(vmem_limit_bytes=VMEM_LIMIT),
        cost_estimate=pl.CostEstimate(
            flops=12 * all_rows * width * hidden_units,
            bytes_accessed=12 * width * hidden_units + 4 * all_rows * width,
            transcendentals=2 * all_rows * hidden_units,
        ),
        name="experts",
    )(ids, *token_blocks, router_t, *gates, *ups, *downs)


def local(hidden, gain, router_w, routes, w_gate, w_up, w_down):
    ep_count = lax.axis_size("ep")
    local_experts = ep_count // SPLIT
    expert_count = local_experts * lax.axis_size("grp")
    tree = gather_tree(ep_count)
    swap = [(0, 1), (1, 0)]
    own_weights = (w_gate[0, 0], w_up[0, 0], w_down[0, 0])
    other_weights = [lax.ppermute(w, "grp", swap) for w in own_weights]
    gates, ups, downs = zip(own_weights, other_weights)

    held = {0: prepare(hidden, gain, routes)}
    for r, bit in tree:
        held[r] = across(held[r ^ bit], bit, ep_count)

    place, core = lax.axis_index("ep") // SPLIT, lax.axis_index("grp")
    ids = jnp.stack([core * local_experts + place, (1 - core) * local_experts + place]).astype(jnp.int32)
    router_t = jnp.pad(router_w.T, ((0, -expert_count % 16), (0, 0)))
    parts = experts(ids, [held[r] for r in range(ep_count)], router_t, gates, ups, downs)

    arrived = {r: [] for r in range(ep_count)}

    def summed(r):
        total = parts[r].astype(jnp.float32)
        for value in arrived[r]:
            total = total + value.astype(jnp.float32)
        return total.astype(jnp.bfloat16)

    for r, bit in reversed(tree):
        arrived[r ^ bit].append(across(summed(r), bit, ep_count))
    return summed(0)


def solution(mesh):
    in_specs = (
        P(("dom", "ep", "grp"), None),
        P(),
        P(),
        P(("dom", "ep", "grp"), None),
        P("ep", "grp", None, None),
        P("ep", "grp", None, None),
        P("ep", "grp", None, None),
    )
    out_specs = P(("dom", "ep", "grp"), None)
    return jax.shard_map(local, mesh=mesh, in_specs=in_specs, out_specs=out_specs, check_vma=False)
```

time: 262 us -> 136 us (0.52)
  waiting for transfers between devices: 177 us -> 63.9 us
  blocking collectives: 43.9 us -> 0 us
  starting transfers between devices: 0.04 us -> 39.3 us
  matrix products: 23.3 us -> 0 us
  Pallas kernels: 0 us -> 22.2 us
  between operations: 13.5 us -> 0.26 us
  local copies, waits for them, and re-layouts: 0.15 us -> 3.56 us
  other arithmetic: 3.61 us -> 6.7 us
    reduce_scatter x1 -> x0, waiting for transfers between devices: 146 us -> none  [local(): lax.psum_scatter(weighted, ('ep', 'grp'), scatter_dimension=0, tiled=True)]
    ppermute x0 -> x33, waiting for transfers between devices: none -> 63.9 us  [the longest x30 63.9 us: across(): return lax.ppermute(value, 'ep', [(i, i ^ bit) for i in range(ep_count)])]
    all_gather x1 -> x0, blocking collectives: 43.9 us -> none  [local(): all_coeffs = lax.all_gather(coeffs, ('ep', 'grp'), axis=0, tiled=True)]
    ppermute x0 -> x33, starting transfers between devices: none -> 39.3 us  [the longest x30 38.3 us: across(): return lax.ppermute(value, 'ep', [(i, i ^ bit) for i in range(ep_count)])]
    all_gather x1 -> x0, waiting for transfers between devices: 31.2 us -> none  [local(): tokens = lax.all_gather(normed, ('ep', 'grp'), axis=0, tiled=True)]
    dot_general x3 -> x0, matrix products: 23.3 us -> none  [the longest x1 16 us: local(): jnp.dot(activated, w_down[0, 0], preferred_element_type=jnp.float32)]
    pallas_call x0 -> x2, Pallas kernels: none -> 22.2 us  [the longest x1 20.3 us: experts(): pl.pallas_call(functools.partial(experts_kernel, blocks, k_steps, k_tile)...]
    convert_element_type x1 -> x8, other arithmetic: 1.76 us -> 6.04 us  [summed(): return total.astype(jnp.bfloat16)]
  transfers between devices with their start and end apart: 2 -> 33, of which waited for: 2 -> 18; matrix products, arithmetic and copies ran while one was open for 1% -> 6% of each run, Pallas kernels for 0% -> 1%
where the time goes in v2:
time: 136 us
  waiting for transfers between devices  63.9 us (47%)
  starting transfers between devices  39.3 us (29%)
  Pallas kernels  22.2 us (16%)
  other arithmetic  6.7 us (5%)
  local copies, waits for them, and re-layouts  3.56 us (3%)
    ppermute x30, waiting for transfers between devices, across(): return lax.ppermute(value, 'ep', [(i, i ^ bit) for i in range(ep_count)])  63.9 us
    ppermute x30, starting transfers between devices, across(): return lax.ppermute(value, 'ep', [(i, i ^ bit) for i in range(ep_count)])  38.3 us
    pallas_call x1, Pallas kernels, experts(): pl.pallas_call(functools.partial(experts_kernel, blocks, k_steps, k_tile)...  20.3 us
    convert_element_type x8, other arithmetic, summed(): return total.astype(jnp.bfloat16)  6.04 us
  transfers between devices with their start and end apart: 33, of which 18 were waited for; matrix products, arithmetic and copies ran while one was open for 6% of the time, Pallas kernels for 1%

profile of v2, /device:TPU:0, one launch (start us, length us, event | category | flops | bytes accessed | tf_op | source)
XLA Modules:
  0.0 135.9 jit_solution(6174744321544316841)
XLA Ops:
  2.3 1.9 %prepare.1.refs_0_ = bf16[16,7296]{1,0:T(8,128)(2,1)} custom-call(bf16[16,7168]{1,0:T(8,128)(2,1)} %hidden_ref.1, f32[1,7168]{1,0:T(1,128)} %bitcast.14, s32[16,4]{1,0:T(8,128)} %copy.8.routes_ref), custom_call_target="tpu_custom_call" | custom-call | flops 688128 | bytes 458752 | tf_op jit(solution)/shard_map/prepare/pallas_call | solution.py:50
  4.2 3.6 %collective-permute-start.7 = (bf16[16,7296]{1,0:T(8,128)(2,1)}, bf16[16,7296]{1,0:T(8,128)(2,1)S(1)}, u32[]{:S(2)}, u32[]{:S(2)}) collective-permute-start(bf16[16,7296]{1,0:T(8,128)(2,1)} %prepare.1.refs_0_), channel_id=1, source_target_pairs={{0,16},{2,18},{4,20},{6,22},{8,24},{10,26},{12,28},{14,30},{16,0},... | collective-permute-start | bytes 700424 | tf_op jit(solution)/shard_map/ppermute | solution.py:31
  7.8 1.6 %collective-permute-start.3 = (bf16[16,7296]{1,0:T(8,128)(2,1)}, bf16[16,7296]{1,0:T(8,128)(2,1)S(1)}, u32[]{:S(2)}, u32[]{:S(2)}) collective-permute-start(bf16[16,7296]{1,0:T(8,128)(2,1)} %prepare.1.refs_0_), channel_id=1, source_target_pairs={{0,8},{2,10},{4,12},{6,14},{8,0},{10,2},{12,4},{14,6},{16,24},{18,... | collective-permute-start | bytes 700424 | tf_op jit(solution)/shard_map/ppermute | solution.py:31
  9.3 10.1 %collective-permute-done.7.refs_8_ = bf16[16,7296]{1,0:T(8,128)(2,1)S(1)} collective-permute-done((bf16[16,7296]{1,0:T(8,128)(2,1)}, bf16[16,7296]{1,0:T(8,128)(2,1)S(1)}, u32[]{:S(2)}, u32[]{:S(2)}) %collective-permute-start.7) | collective-permute-done | bytes 233504 | tf_op jit(solution)/shard_map/ppermute | solution.py:31
  19.5 1.6 %collective-permute-start.1 = (bf16[16,7296]{1,0:T(8,128)(2,1)}, bf16[16,7296]{1,0:T(8,128)(2,1)S(1)}, u32[]{:S(2)}, u32[]{:S(2)}) collective-permute-start(bf16[16,7296]{1,0:T(8,128)(2,1)} %prepare.1.refs_0_), channel_id=1, source_target_pairs={{0,4},{2,6},{4,0},{6,2},{8,12},{10,14},{12,8},{14,10},{16,20},{18,... | collective-permute-start | bytes 700424 | tf_op jit(solution)/shard_map/ppermute | solution.py:31
  22.5 4.6 %collective-permute-done.1.refs_2_ = bf16[16,7296]{1,0:T(8,128)(2,1)S(1)} collective-permute-done((bf16[16,7296]{1,0:T(8,128)(2,1)}, bf16[16,7296]{1,0:T(8,128)(2,1)S(1)}, u32[]{:S(2)}, u32[]{:S(2)}) %collective-permute-start.1) | collective-permute-done | bytes 233504 | tf_op jit(solution)/shard_map/ppermute | solution.py:31
  29.6 4.1 %collective-permute-done.11.refs_12_ = bf16[16,7296]{1,0:T(8,128)(2,1)S(1)} collective-permute-done((bf16[16,7296]{1,0:T(8,128)(2,1)S(1)}, bf16[16,7296]{1,0:T(8,128)(2,1)S(1)}, u32[]{:S(2)}, u32[]{:S(2)}) %collective-permute-start.11) | collective-permute-done | bytes 233504 | tf_op jit(solution)/shard_map/ppermute | solution.py:31
  34.8 1.5 %collective-permute-start.5 = (bf16[16,7296]{1,0:T(8,128)(2,1)S(1)}, bf16[16,7296]{1,0:T(8,128)(2,1)S(1)}, u32[]{:S(2)}, u32[]{:S(2)}) collective-permute-start(bf16[16,7296]{1,0:T(8,128)(2,1)S(1)} %collective-permute-done.3.refs_4_), channel_id=1, source_target_pairs={{0,4},{2,6},{4,0},{6,2},{8,12},{10,14},{12,8},{14,10},{16,20},{18,... | collective-permute-start | bytes 700424 | tf_op jit(solution)/shard_map/ppermute | solution.py:31
  36.4 3.8 %collective-permute-done.8.refs_9_ = bf16[16,7296]{1,0:T(8,128)(2,1)S(1)} collective-permute-done((bf16[16,7296]{1,0:T(8,128)(2,1)S(1)}, bf16[16,7296]{1,0:T(8,128)(2,1)S(1)}, u32[]{:S(2)}, u32[]{:S(2)}) %collective-permute-start.8) | collective-permute-done | bytes 233504 | tf_op jit(solution)/shard_map/ppermute | solution.py:31
  42.2 5.1 %collective-permute-done.4.refs_5_ = bf16[16,7296]{1,0:T(8,128)(2,1)S(1)} collective-permute-done((bf16[16,7296]{1,0:T(8,128)(2,1)S(1)}, bf16[16,7296]{1,0:T(8,128)(2,1)S(1)}, u32[]{:S(2)}, u32[]{:S(2)}) %collective-permute-start.4) | collective-permute-done | bytes 233504 | tf_op jit(solution)/shard_map/ppermute | solution.py:31
  48.5 2.6 %collective-permute-done.2.refs_3_ = bf16[16,7296]{1,0:T(8,128)(2,1)S(1)} collective-permute-done((bf16[16,7296]{1,0:T(8,128)(2,1)S(1)}, bf16[16,7296]{1,0:T(8,128)(2,1)S(1)}, u32[]{:S(2)}, u32[]{:S(2)}) %collective-permute-start.2) | collective-permute-done | bytes 233504 | tf_op jit(solution)/shard_map/ppermute | solution.py:31
  52.4 2.5 %collective-permute-done.13.refs_14_ = bf16[16,7296]{1,0:T(8,128)(2,1)S(1)} collective-permute-done((bf16[16,7296]{1,0:T(8,128)(2,1)S(1)}, bf16[16,7296]{1,0:T(8,128)(2,1)S(1)}, u32[]{:S(2)}, u32[]{:S(2)}) %collective-permute-start.13) | collective-permute-done | bytes 233504 | tf_op jit(solution)/shard_map/ppermute | solution.py:31
  58.5 2.5 %collective-permute-done.12.refs_13_ = bf16[16,7296]{1,0:T(8,128)(2,1)S(1)} collective-permute-done((bf16[16,7296]{1,0:T(8,128)(2,1)S(1)}, bf16[16,7296]{1,0:T(8,128)(2,1)S(1)}, u32[]{:S(2)}, u32[]{:S(2)}) %collective-permute-start.12) | collective-permute-done | bytes 233504 | tf_op jit(solution)/shard_map/ppermute | solution.py:31
  62.1 1.6 %pad.4.refs_16_ = bf16[16,7168]{1,0:T(8,128)(2,1)} pad(bf16[8,7168]{1,0:T(8,128)(2,1)} %bitcast.13, bf16[]{:T(256)} %constant.28.clone.1), padding=0_8x0_0 | pad | bytes 344066 | tf_op jit(solution)/shard_map/jit(_pad)/pad | solution.py:180
  64.4 2.7 %collective-permute-done.14.refs_15_ = bf16[16,7296]{1,0:T(8,128)(2,1)S(1)} collective-permute-done((bf16[16,7296]{1,0:T(8,128)(2,1)S(1)}, bf16[16,7296]{1,0:T(8,128)(2,1)S(1)}, u32[]{:S(2)}, u32[]{:S(2)}) %collective-permute-start.14) | collective-permute-done | bytes 233504 | tf_op jit(solution)/shard_map/ppermute | solution.py:31
  67.8 20.3 %experts.1 = (bf16[16,7168]{1,0:T(8,128)(2,1)}, bf16[16,7168]{1,0:T(8,128)(2,1)}, bf16[16,7168]{1,0:T(8,128)(2,1)}, bf16[16,7168]{1,0:T(8,128)(2,1)}, bf16[16,71...) custom-call(s32[2]{0:T(128)} %pad_add_fusion.ids_ref, ...), custom_call_target="tpu_custom_call" | custom-call | flops 5637144576 | bytes 29360128 | tf_op jit(solution)/shard_map/experts/pallas_call | solution.py:139
  99.6 1.5 %collective-permute-start.30 = (bf16[16,7168]{1,0:T(8,128)(2,1)}, bf16[16,7168]{1,0:T(8,128)(2,1)S(1)}, u32[]{:S(2)}, u32[]{:S(2)}) collective-permute-start(bf16[16,7168]{1,0:T(8,128)(2,1)} %get-tuple-element.36), channel_id=1, source_target_pairs={{0,4},{2,6},{4,0},{6,2},{8,12},{10,14},{12,8},{14,10},{16,20},{18,... | collective-permute-start | bytes 688136 | tf_op jit(solution)/shard_map/ppermute | solution.py:31
  103.7 2.1 %collective-permute-done.30 = bf16[16,7168]{1,0:T(8,128)(2,1)S(1)} collective-permute-done((bf16[16,7168]{1,0:T(8,128)(2,1)}, bf16[16,7168]{1,0:T(8,128)(2,1)S(1)}, u32[]{:S(2)}, u32[]{:S(2)}) %collective-permute-start.30) | collective-permute-done | bytes 229408 | tf_op jit(solution)/shard_map/ppermute | solution.py:31
  107.3 5.8 %collective-permute-done.22 = bf16[16,7168]{1,0:T(8,128)(2,1)S(1)} collective-permute-done((bf16[16,7168]{1,0:T(8,128)(2,1)S(1)}, bf16[16,7168]{1,0:T(8,128)(2,1)S(1)}, u32[]{:S(2)}, u32[]{:S(2)}) %collective-permute-start.22) | collective-permute-done | bytes 229408 | tf_op jit(solution)/shard_map/ppermute | solution.py:31
  114.8 1.6 %collective-permute-start.27 = (bf16[16,7168]{1,0:T(8,128)(2,1)S(1)}, bf16[16,7168]{1,0:T(8,128)(2,1)S(1)}, u32[]{:S(2)}, u32[]{:S(2)}) collective-permute-start(bf16[16,7168]{1,0:T(8,128)(2,1)S(1)} %add_convert_fusion.3), channel_id=1, source_target_pairs={{0,4},{2,6},{4,0},{6,2},{8,12},{10,14},{12,8},{14,10},{16,20},{18,... | collective-permute-start | bytes 688136 | tf_op jit(solution)/shard_map/ppermute | solution.py:31
  116.4 2.7 %collective-permute-done.31 = bf16[16,7168]{1,0:T(8,128)(2,1)S(1)} collective-permute-done((bf16[16,7168]{1,0:T(8,128)(2,1)S(1)}, bf16[16,7168]{1,0:T(8,128)(2,1)S(1)}, u32[]{:S(2)}, u32[]{:S(2)}) %collective-permute-start.31) | collective-permute-done | bytes 229408 | tf_op jit(solution)/shard_map/ppermute | solution.py:31
  120.0 5.1 %collective-permute-done.23 = bf16[16,7168]{1,0:T(8,128)(2,1)S(1)} collective-permute-done((bf16[16,7168]{1,0:T(8,128)(2,1)S(1)}, bf16[16,7168]{1,0:T(8,128)(2,1)S(1)}, u32[]{:S(2)}, u32[]{:S(2)}) %collective-permute-start.23) | collective-permute-done | bytes 229408 | tf_op jit(solution)/shard_map/ppermute | solution.py:31
  125.2 3.3 %collective-permute-start.25 = (bf16[16,7168]{1,0:T(8,128)(2,1)S(1)}, bf16[16,7168]{1,0:T(8,128)(2,1)S(1)}, u32[]{:S(2)}, u32[]{:S(2)}) collective-permute-start(bf16[16,7168]{1,0:T(8,128)(2,1)S(1)} %add_convert_fusion.4), channel_id=1, source_target_pairs={{0,16},{2,18},{4,20},{6,22},{8,24},{10,26},{12,28},{14,30},{16,0},... | collective-permute-start | bytes 688136 | tf_op jit(solution)/shard_map/ppermute | solution.py:31
  128.6 6.4 %collective-permute-done.25 = bf16[16,7168]{1,0:T(8,128)(2,1)S(1)} collective-permute-done((bf16[16,7168]{1,0:T(8,128)(2,1)S(1)}, bf16[16,7168]{1,0:T(8,128)(2,1)S(1)}, u32[]{:S(2)}, u32[]{:S(2)}) %collective-permute-start.25) | collective-permute-done | bytes 229408 | tf_op jit(solution)/shard_map/ppermute | solution.py:31
  (91 shorter events, 37.0 us)
Async XLA Ops:
  0.0 67.1 %collective-permute-start.15 = (bf16[7168,256]{1,0:T(8,128)(2,1)}, bf16[7168,256]{1,0:T(8,128)(2,1)}, u32[]{:S(2)}, u32[]{:S(2)}) collective-permute-start(bf16[7168,256]{1,0:T(8,128)(2,1)} %bitcast.7), channel_id=1, source_target_pairs={{0,1},{1,0},{2,3},{3,2},{4,5},{5,4},{6,7},{7,6},{8,9},{9,8},{10,11... | collective-permute-start | bytes 11010056 | tf_op jit(solution)/shard_map/ppermute | solution.py:171
  0.5 66.6 %collective-permute-start.16 = (bf16[7168,256]{1,0:T(8,128)(2,1)}, bf16[7168,256]{1,0:T(8,128)(2,1)}, u32[]{:S(2)}, u32[]{:S(2)}) collective-permute-start(bf16[7168,256]{1,0:T(8,128)(2,1)} %bitcast.9), channel_id=1, source_target_pairs={{0,1},{1,0},{2,3},{3,2},{4,5},{5,4},{6,7},{7,6},{8,9},{9,8},{10,11... | collective-permute-start | bytes 11010056 | tf_op jit(solution)/shard_map/ppermute | solution.py:171
  0.5 66.6 %collective-permute-start.17 = (bf16[256,7168]{1,0:T(8,128)(2,1)}, bf16[256,7168]{1,0:T(8,128)(2,1)}, u32[]{:S(2)}, u32[]{:S(2)}) collective-permute-start(bf16[256,7168]{1,0:T(8,128)(2,1)} %bitcast.11), channel_id=1, source_target_pairs={{0,1},{1,0},{2,3},{3,2},{4,5},{5,4},{6,7},{7,6},{8,9},{9,8},{10,11... | collective-permute-start | bytes 11010056 | tf_op jit(solution)/shard_map/ppermute | solution.py:171
  4.2 15.3 %collective-permute-start.7 = (bf16[16,7296]{1,0:T(8,128)(2,1)}, bf16[16,7296]{1,0:T(8,128)(2,1)S(1)}, u32[]{:S(2)}, u32[]{:S(2)}) collective-permute-start(bf16[16,7296]{1,0:T(8,128)(2,1)} %prepare.1.refs_0_), channel_id=1, source_target_pairs={{0,16},{2,18},{4,20},{6,22},{8,24},{10,26},{12,28},{14,30},{16,0},... | collective-permute-start | bytes 700424 | tf_op jit(solution)/shard_map/ppermute | solution.py:31
  7.8 13.3 %collective-permute-start.3 = (bf16[16,7296]{1,0:T(8,128)(2,1)}, bf16[16,7296]{1,0:T(8,128)(2,1)S(1)}, u32[]{:S(2)}, u32[]{:S(2)}) collective-permute-start(bf16[16,7296]{1,0:T(8,128)(2,1)} %prepare.1.refs_0_), channel_id=1, source_target_pairs={{0,8},{2,10},{4,12},{6,14},{8,0},{10,2},{12,4},{14,6},{16,24},{18,... | collective-permute-start | bytes 700424 | tf_op jit(solution)/shard_map/ppermute | solution.py:31
  19.5 7.7 %collective-permute-start.1 = (bf16[16,7296]{1,0:T(8,128)(2,1)}, bf16[16,7296]{1,0:T(8,128)(2,1)S(1)}, u32[]{:S(2)}, u32[]{:S(2)}) collective-permute-start(bf16[16,7296]{1,0:T(8,128)(2,1)} %prepare.1.refs_0_), channel_id=1, source_target_pairs={{0,4},{2,6},{4,0},{6,2},{8,12},{10,14},{12,8},{14,10},{16,20},{18,... | collective-permute-start | bytes 700424 | tf_op jit(solution)/shard_map/ppermute | solution.py:31
  21.0 7.2 %collective-permute-start = (bf16[16,7296]{1,0:T(8,128)(2,1)}, bf16[16,7296]{1,0:T(8,128)(2,1)S(1)}, u32[]{:S(2)}, u32[]{:S(2)}) collective-permute-start(bf16[16,7296]{1,0:T(8,128)(2,1)} %prepare.1.refs_0_), channel_id=1, source_target_pairs={{0,2},{2,0},{4,6},{6,4},{8,10},{10,8},{12,14},{14,12},{16,18},{18,... | collective-permute-start | bytes 700424 | tf_op jit(solution)/shard_map/ppermute | solution.py:31
  27.1 6.6 %collective-permute-start.11 = (bf16[16,7296]{1,0:T(8,128)(2,1)S(1)}, bf16[16,7296]{1,0:T(8,128)(2,1)S(1)}, u32[]{:S(2)}, u32[]{:S(2)}) collective-permute-start(bf16[16,7296]{1,0:T(8,128)(2,1)S(1)} %collective-permute-done.7.refs_8_), channel_id=1, source_target_pairs={{0,8},{2,10},{4,12},{6,14},{8,0},{10,2},{12,4},{14,6},{16,24},{18,... | collective-permute-start | bytes 700424 | tf_op jit(solution)/shard_map/ppermute | solution.py:31
  28.2 6.6 %collective-permute-start.9 = (bf16[16,7296]{1,0:T(8,128)(2,1)S(1)}, bf16[16,7296]{1,0:T(8,128)(2,1)S(1)}, u32[]{:S(2)}, u32[]{:S(2)}) collective-permute-start(bf16[16,7296]{1,0:T(8,128)(2,1)S(1)} %collective-permute-done.7.refs_8_), channel_id=1, source_target_pairs={{0,4},{2,6},{4,0},{6,2},{8,12},{10,14},{12,8},{14,10},{16,20},{18,... | collective-permute-start | bytes 700424 | tf_op jit(solution)/shard_map/ppermute | solution.py:31
  34.8 6.7 %collective-permute-start.5 = (bf16[16,7296]{1,0:T(8,128)(2,1)S(1)}, bf16[16,7296]{1,0:T(8,128)(2,1)S(1)}, u32[]{:S(2)}, u32[]{:S(2)}) collective-permute-start(bf16[16,7296]{1,0:T(8,128)(2,1)S(1)} %collective-permute-done.3.refs_4_), channel_id=1, source_target_pairs={{0,4},{2,6},{4,0},{6,2},{8,12},{10,14},{12,8},{14,10},{16,20},{18,... | collective-permute-start | bytes 700424 | tf_op jit(solution)/shard_map/ppermute | solution.py:31
  40.2 7.1 %collective-permute-start.4 = (bf16[16,7296]{1,0:T(8,128)(2,1)S(1)}, bf16[16,7296]{1,0:T(8,128)(2,1)S(1)}, u32[]{:S(2)}, u32[]{:S(2)}) collective-permute-start(bf16[16,7296]{1,0:T(8,128)(2,1)S(1)} %collective-permute-done.3.refs_4_), channel_id=1, source_target_pairs={{0,2},{2,0},{4,6},{6,4},{8,10},{10,8},{12,14},{14,12},{16,18},{18,... | collective-permute-start | bytes 700424 | tf_op jit(solution)/shard_map/ppermute | solution.py:31
  41.6 9.5 %collective-permute-start.2 = (bf16[16,7296]{1,0:T(8,128)(2,1)S(1)}, bf16[16,7296]{1,0:T(8,128)(2,1)S(1)}, u32[]{:S(2)}, u32[]{:S(2)}) collective-permute-start(bf16[16,7296]{1,0:T(8,128)(2,1)S(1)} %collective-permute-done.1.refs_2_), channel_id=1, source_target_pairs={{0,2},{2,0},{4,6},{6,4},{8,10},{10,8},{12,14},{14,12},{16,18},{18,... | collective-permute-start | bytes 700424 | tf_op jit(solution)/shard_map/ppermute | solution.py:31
  47.3 7.6 %collective-permute-start.13 = (bf16[16,7296]{1,0:T(8,128)(2,1)S(1)}, bf16[16,7296]{1,0:T(8,128)(2,1)S(1)}, u32[]{:S(2)}, u32[]{:S(2)}) collective-permute-start(bf16[16,7296]{1,0:T(8,128)(2,1)S(1)} %collective-permute-done.9.refs_10_), channel_id=1, source_target_pairs={{0,8},{2,10},{4,12},{6,14},{8,0},{10,2},{12,4},{14,6},{16,24},{18,... | collective-permute-start | bytes 700424 | tf_op jit(solution)/shard_map/ppermute | solution.py:31
  57.1 7.3 %collective-permute-start.6 = (bf16[16,7296]{1,0:T(8,128)(2,1)S(1)}, bf16[16,7296]{1,0:T(8,128)(2,1)S(1)}, u32[]{:S(2)}, u32[]{:S(2)}) collective-permute-start(bf16[16,7296]{1,0:T(8,128)(2,1)S(1)} %collective-permute-done.4.refs_5_), channel_id=1, source_target_pairs={{0,4},{2,6},{4,0},{6,2},{8,12},{10,14},{12,8},{14,10},{16,20},{18,... | collective-permute-start | bytes 700424 | tf_op jit(solution)/shard_map/ppermute | solution.py:31
  90.8 8.8 %collective-permute-start.21 = (bf16[16,7168]{1,0:T(8,128)(2,1)}, bf16[16,7168]{1,0:T(8,128)(2,1)S(1)}, u32[]{:S(2)}, u32[]{:S(2)}) collective-permute-start(bf16[16,7168]{1,0:T(8,128)(2,1)} %get-tuple-element.28), channel_id=1, source_target_pairs={{0,4},{2,6},{4,0},{6,2},{8,12},{10,14},{12,8},{14,10},{16,20},{18,... | collective-permute-start | bytes 688136 | tf_op jit(solution)/shard_map/ppermute | solution.py:31
  92.3 27.6 %collective-permute-start.24 = (bf16[16,7168]{1,0:T(8,128)(2,1)}, bf16[16,7168]{1,0:T(8,128)(2,1)S(1)}, u32[]{:S(2)}, u32[]{:S(2)}) collective-permute-start(bf16[16,7168]{1,0:T(8,128)(2,1)} %get-tuple-element.29), channel_id=1, source_target_pairs={{0,8},{2,10},{4,12},{6,14},{8,0},{10,2},{12,4},{14,6},{16,24},{18,... | collective-permute-start | bytes 688136 | tf_op jit(solution)/shard_map/ppermute | solution.py:31
  92.8 9.3 %collective-permute-start.26 = (bf16[16,7168]{1,0:T(8,128)(2,1)}, bf16[16,7168]{1,0:T(8,128)(2,1)S(1)}, u32[]{:S(2)}, u32[]{:S(2)}) collective-permute-start(bf16[16,7168]{1,0:T(8,128)(2,1)} %get-tuple-element.31), channel_id=1, source_target_pairs={{0,2},{2,0},{4,6},{6,4},{8,10},{10,8},{12,14},{14,12},{16,18},{18,... | collective-permute-start | bytes 688136 | tf_op jit(solution)/shard_map/ppermute | solution.py:31
  94.4 34.2 %collective-permute-start.28 = (bf16[16,7168]{1,0:T(8,128)(2,1)}, bf16[16,7168]{1,0:T(8,128)(2,1)S(1)}, u32[]{:S(2)}, u32[]{:S(2)}) collective-permute-start(bf16[16,7168]{1,0:T(8,128)(2,1)} %get-tuple-element.32), channel_id=1, source_target_pairs={{0,2},{2,0},{4,6},{6,4},{8,10},{10,8},{12,14},{14,12},{16,18},{18,... | collective-permute-start | bytes 688136 | tf_op jit(solution)/shard_map/ppermute | solution.py:31
  95.6 19.3 %collective-permute-start.29 = (bf16[16,7168]{1,0:T(8,128)(2,1)}, bf16[16,7168]{1,0:T(8,128)(2,1)S(1)}, u32[]{:S(2)}, u32[]{:S(2)}) collective-permute-start(bf16[16,7168]{1,0:T(8,128)(2,1)} %get-tuple-element.34), channel_id=1, source_target_pairs={{0,4},{2,6},{4,0},{6,2},{8,12},{10,14},{12,8},{14,10},{16,20},{18,... | collective-permute-start | bytes 688136 | tf_op jit(solution)/shard_map/ppermute | solution.py:31
  102.1 17.9 %collective-permute-start.20 = (bf16[16,7168]{1,0:T(8,128)(2,1)S(1)}, bf16[16,7168]{1,0:T(8,128)(2,1)S(1)}, u32[]{:S(2)}, u32[]{:S(2)}) collective-permute-start(bf16[16,7168]{1,0:T(8,128)(2,1)S(1)} %add_convert_fusion.7), channel_id=1, source_target_pairs={{0,4},{2,6},{4,0},{6,2},{8,12},{10,14},{12,8},{14,10},{16,20},{18,... | collective-permute-start | bytes 688136 | tf_op jit(solution)/shard_map/ppermute | solution.py:31
  105.8 7.3 %collective-permute-start.22 = (bf16[16,7168]{1,0:T(8,128)(2,1)S(1)}, bf16[16,7168]{1,0:T(8,128)(2,1)S(1)}, u32[]{:S(2)}, u32[]{:S(2)}) collective-permute-start(bf16[16,7168]{1,0:T(8,128)(2,1)S(1)} %add_convert_fusion.6), channel_id=1, source_target_pairs={{0,8},{2,10},{4,12},{6,14},{8,0},{10,2},{12,4},{14,6},{16,24},{18,... | collective-permute-start | bytes 688136 | tf_op jit(solution)/shard_map/ppermute | solution.py:31
  114.8 13.8 %collective-permute-start.27 = (bf16[16,7168]{1,0:T(8,128)(2,1)S(1)}, bf16[16,7168]{1,0:T(8,128)(2,1)S(1)}, u32[]{:S(2)}, u32[]{:S(2)}) collective-permute-start(bf16[16,7168]{1,0:T(8,128)(2,1)S(1)} %add_convert_fusion.3), channel_id=1, source_target_pairs={{0,4},{2,6},{4,0},{6,2},{8,12},{10,14},{12,8},{14,10},{16,20},{18,... | collective-permute-start | bytes 688136 | tf_op jit(solution)/shard_map/ppermute | solution.py:31
  120.0 8.6 %collective-permute-start.32 = (bf16[16,7168]{1,0:T(8,128)(2,1)S(1)}, bf16[16,7168]{1,0:T(8,128)(2,1)S(1)}, u32[]{:S(2)}, u32[]{:S(2)}) collective-permute-start(bf16[16,7168]{1,0:T(8,128)(2,1)S(1)} %add_convert_fusion.1), channel_id=1, source_target_pairs={{0,8},{2,10},{4,12},{6,14},{8,0},{10,2},{12,4},{14,6},{16,24},{18,... | collective-permute-start | bytes 688136 | tf_op jit(solution)/shard_map/ppermute | solution.py:31
  125.2 9.8 %collective-permute-start.25 = (bf16[16,7168]{1,0:T(8,128)(2,1)S(1)}, bf16[16,7168]{1,0:T(8,128)(2,1)S(1)}, u32[]{:S(2)}, u32[]{:S(2)}) collective-permute-start(bf16[16,7168]{1,0:T(8,128)(2,1)S(1)} %add_convert_fusion.4), channel_id=1, source_target_pairs={{0,16},{2,18},{4,20},{6,22},{8,24},{10,26},{12,28},{14,30},{16,0},... | collective-permute-start | bytes 688136 | tf_op jit(solution)/shard_map/ppermute | solution.py:31
  (27 other events, 530.1 us)

commit v3 on v2

--- a/solution.py
+++ b/solution.py
@@ -12,13 +12,15 @@
 
 EPSILON = 1e-06
 ROUTE_SCALE = 2.5
-VMEM_LIMIT = 56 * 1024 * 1024
+PREPARE_VMEM = 4 * 1024 * 1024
+EXPERTS_VMEM = 50 * 1024 * 1024
 
 TREE_16 = (
-    (4, 4), (1, 1), (2, 2), (8, 8),
-    (5, 1), (6, 2), (12, 4), (9, 1), (10, 2),
-    (3, 1), (7, 2), (13, 4), (11, 1), (15, 2), (14, 4),
+    (8, 8), (2, 2), (4, 4), (1, 1), (3, 2),
+    (12, 4), (9, 1), (10, 2), (6, 4), (13, 1),
+    (14, 2), (11, 8), (7, 4), (5, 1), (15, 2),
 )
+OPEN = 5
 
 
 def gather_tree(ep_count):
@@ -50,7 +52,7 @@
     return pl.pallas_call(
         prepare_kernel,
         out_shape=jax.ShapeDtypeStruct((rows, width + LANES), jnp.bfloat16),
-        compiler_params=pltpu.CompilerParams(vmem_limit_bytes=VMEM_LIMIT),
+        compiler_params=pltpu.CompilerParams(vmem_limit_bytes=PREPARE_VMEM),
         cost_estimate=pl.CostEstimate(flops=6 * rows * width, bytes_accessed=4 * rows * width, transcendentals=rows),
         name="prepare",
     )(hidden, gain[None, :], routes)
@@ -58,12 +60,12 @@
 
 def experts_kernel(blocks, k_steps, k_tile, ids_ref, *refs):
     token_refs = refs[:blocks]
-    router_ref, gate0_ref, gate1_ref, up0_ref, up1_ref, down0_ref, down1_ref = refs[blocks : blocks + 7]
-    out_refs = refs[blocks + 7 : 2 * blocks + 7]
-    gates_ref, logits_ref, act_ref, coeff_ref = refs[2 * blocks + 7 :]
+    router_ref, gate_ref, up_ref, down_ref = refs[blocks : blocks + 4]
+    out_refs = refs[blocks + 4 : 2 * blocks + 4]
+    gates_ref, logits_ref, act_ref, coeff_ref = refs[2 * blocks + 4 :]
     step = pl.program_id(0)
     rows = token_refs[0].shape[0]
-    hidden_units = gate0_ref.shape[1]
+    hidden_units = gate_ref.shape[2]
     width = k_steps * k_tile
 
     @pl.when(step < k_steps)
@@ -71,8 +73,9 @@
         columns = pl.ds(pl.multiple_of(step * k_tile, LANES), k_tile)
         tokens = jnp.concatenate([ref[:, columns] for ref in token_refs], axis=0)
         parts = [
-            jnp.dot(tokens, ref[...], preferred_element_type=jnp.float32)
-            for ref in (gate0_ref, gate1_ref, up0_ref, up1_ref)
+            jnp.dot(tokens, ref[i], preferred_element_type=jnp.float32)
+            for ref in (gate_ref, up_ref)
+            for i in range(2)
         ]
         logits = lax.dot_general(
             tokens, router_ref[...], (((1,), (1,)), ((), ())), preferred_element_type=jnp.float32
@@ -108,9 +111,9 @@
     @pl.when(step >= k_steps)
     def _():
         total = coeff_ref[:, 0:1] * jnp.dot(
-            act_ref[:, :hidden_units], down0_ref[...], preferred_element_type=jnp.float32
+            act_ref[:, :hidden_units], down_ref[0], preferred_element_type=jnp.float32
         ) + coeff_ref[:, LANES : LANES + 1] * jnp.dot(
-            act_ref[:, hidden_units:], down1_ref[...], preferred_element_type=jnp.float32
+            act_ref[:, hidden_units:], down_ref[1], preferred_element_type=jnp.float32
         )
         for i, ref in enumerate(out_refs):
             ref[...] = total[i * rows : (i + 1) * rows].astype(jnp.bfloat16)
@@ -119,8 +122,8 @@
 def experts(ids, token_blocks, router_t, gates, ups, downs):
     blocks = len(token_blocks)
     rows = token_blocks[0].shape[0]
-    width, hidden_units = gates[0].shape
-    k_tile = n_tile = 1024
+    _, width, hidden_units = gates.shape
+    k_tile = n_tile = width // 4
     k_steps, n_steps = width // k_tile, width // n_tile
     all_rows = blocks * rows
 
@@ -133,8 +136,8 @@
     whole = pl.BlockSpec(token_blocks[0].shape, lambda step, ids_ref: (0, 0))
     in_specs = [whole] * blocks
     in_specs += [pl.BlockSpec((router_t.shape[0], k_tile), lambda step, ids_ref: (0, at_k(step, ids_ref)))]
-    in_specs += [pl.BlockSpec((k_tile, hidden_units), lambda step, ids_ref: (at_k(step, ids_ref), 0))] * 4
-    in_specs += [pl.BlockSpec((hidden_units, n_tile), lambda step, ids_ref: (0, at_n(step, ids_ref)))] * 2
+    in_specs += [pl.BlockSpec((2, k_tile, hidden_units), lambda step, ids_ref: (0, at_k(step, ids_ref), 0))] * 2
+    in_specs += [pl.BlockSpec((2, hidden_units, n_tile), lambda step, ids_ref: (0, 0, at_n(step, ids_ref)))]
     out_specs = [pl.BlockSpec((rows, n_tile), lambda step, ids_ref: (0, at_n(step, ids_ref)))] * blocks
     return pl.pallas_call(
         functools.partial(experts_kernel, blocks, k_steps, k_tile),
@@ -151,14 +154,14 @@
             ],
         ),
         out_shape=[jax.ShapeDtypeStruct((rows, width), jnp.bfloat16)] * blocks,
-        compiler_params=pltpu.CompilerParams(vmem_limit_bytes=VMEM_LIMIT),
+        compiler_params=pltpu.CompilerParams(vmem_limit_bytes=EXPERTS_VMEM),
         cost_estimate=pl.CostEstimate(
             flops=12 * all_rows * width * hidden_units,
             bytes_accessed=12 * width * hidden_units + 4 * all_rows * width,
             transcendentals=2 * all_rows * hidden_units,
         ),
         name="experts",
-    )(ids, *token_blocks, router_t, *gates, *ups, *downs)
+    )(ids, *token_blocks, router_t, gates, ups, downs)
 
 
 def local(hidden, gain, router_w, routes, w_gate, w_up, w_down):
@@ -166,17 +169,16 @@
     local_experts = ep_count // SPLIT
     expert_count = local_experts * lax.axis_size("grp")
     tree = gather_tree(ep_count)
-    swap = [(0, 1), (1, 0)]
-    own_weights = (w_gate[0, 0], w_up[0, 0], w_down[0, 0])
-    other_weights = [lax.ppermute(w, "grp", swap) for w in own_weights]
-    gates, ups, downs = zip(own_weights, other_weights)
+    gates, ups, downs = (lax.all_gather(w[0, 0], "grp") for w in (w_gate, w_up, w_down))
 
     held = {0: prepare(hidden, gain, routes)}
-    for r, bit in tree:
-        held[r] = across(held[r ^ bit], bit, ep_count)
-
-    place, core = lax.axis_index("ep") // SPLIT, lax.axis_index("grp")
-    ids = jnp.stack([core * local_experts + place, (1 - core) * local_experts + place]).astype(jnp.int32)
+    for k, (r, bit) in enumerate(tree):
+        block = held[r ^ bit]
+        if k >= OPEN:
+            block, _ = lax.optimization_barrier((block, held[tree[k - OPEN][0]]))
+        held[r] = across(block, bit, ep_count)
+
+    ids = (jnp.arange(2) * local_experts + lax.axis_index("ep") // SPLIT).astype(jnp.int32)
     router_t = jnp.pad(router_w.T, ((0, -expert_count % 16), (0, 0)))
     parts = experts(ids, [held[r] for r in range(ep_count)], router_t, gates, ups, downs)
 

time: 136 us -> 147 us (1.081)
  between operations: 0.26 us -> 13.4 us
  waiting for transfers between devices: 63.9 us -> 69.7 us
  Pallas kernels: 22.2 us -> 16.5 us
  other arithmetic: 6.7 us -> 1.37 us
  starting transfers between devices: 39.3 us -> 44.6 us
  local copies, waits for them, and re-layouts: 3.56 us -> 1.12 us
    all_gather x0 -> x3, waiting for transfers between devices: none -> 22.8 us  [local(): lax.all_gather(w[0, 0], 'grp')]
    ppermute x30, waiting for transfers between devices: 63.9 us -> 44.9 us  [across(): return lax.ppermute(value, 'ep', [(i, i ^ bit) for i in range(ep_count)])]
    ppermute x30, starting transfers between devices: 38.3 us -> 44.5 us  [across(): return lax.ppermute(value, 'ep', [(i, i ^ bit) for i in range(ep_count)])]
    convert_element_type x8, other arithmetic: 6.04 us -> 1.37 us  [summed(): return total.astype(jnp.bfloat16)]
    pallas_call x1, Pallas kernels: 20.3 us -> 16.3 us  [experts(): pl.pallas_call(functools.partial(experts_kernel, blocks, k_steps, k_tile)...]
    unnamed x0 -> x3, waiting for transfers between devices: none -> 2.09 us
    unnamed x37 -> x35, local copies, waits for them, and re-layouts: 1.96 us -> 0.15 us
    pallas_call x1, Pallas kernels: 1.86 us -> 0.22 us  [prepare(): pl.pallas_call(prepare_kernel, out_shape=jax.ShapeDtypeStruct((rows, widt...]
  transfers between devices with their start and end apart: 33 -> 33, of which waited for: 18 -> 14; matrix products, arithmetic and copies ran while one was open for 6% -> 1% of each run, Pallas kernels for 1% -> 0%
where the time goes in v3:
time: 147 us
  waiting for transfers between devices  69.7 us (47%)
  starting transfers between devices  44.6 us (30%)
  Pallas kernels  16.5 us (11%)
  between operations  13.4 us (9%)
    ppermute x30, waiting for transfers between devices, across(): return lax.ppermute(value, 'ep', [(i, i ^ bit) for i in range(ep_count)])  44.9 us
    ppermute x30, starting transfers between devices, across(): return lax.ppermute(value, 'ep', [(i, i ^ bit) for i in range(ep_count)])  44.5 us
    all_gather x3, waiting for transfers between devices, local(): lax.all_gather(w[0, 0], 'grp')  22.8 us
    pallas_call x1, Pallas kernels, experts(): pl.pallas_call(functools.partial(experts_kernel, blocks, k_steps, k_tile)...  16.3 us
  transfers between devices with their start and end apart: 33, of which 14 were waited for; matrix products, arithmetic and copies ran while one was open for 1% of the time, Pallas kernels for 0%

profile of v3, /device:TPU:0, one launch (start us, length us, event | category | flops | bytes accessed | tf_op | source)
XLA Modules:
  0.0 146.7 jit_solution(13786742609974306620)
XLA Ops:
  9.1 4.1 %collective-permute-start.6 = (bf16[16,7296]{1,0:T(8,128)(2,1)S(1)}, bf16[16,7296]{1,0:T(8,128)(2,1)S(1)}, u32[]{:S(2)}, u32[]{:S(2)}) collective-permute-start(bf16[16,7296]{1,0:T(8,128)(2,1)S(1)} %prepare.1.refs_0_), channel_id=1, source_target_pairs={{0,16},{2,18},{4,20},{6,22},{8,24},{10,26},{12,28},{14,30},{16,0},... | collective-permute-start | bytes 700424 | tf_op jit(solution)/shard_map/ppermute | solution.py:33
  14.7 1.5 %collective-permute-start.1 = (bf16[16,7296]{1,0:T(8,128)(2,1)S(1)}, bf16[16,7296]{1,0:T(8,128)(2,1)S(1)}, u32[]{:S(2)}, u32[]{:S(2)}) collective-permute-start(bf16[16,7296]{1,0:T(8,128)(2,1)S(1)} %prepare.1.refs_0_), channel_id=1, source_target_pairs={{0,4},{2,6},{4,0},{6,2},{8,12},{10,14},{12,8},{14,10},{16,20},{18,... | collective-permute-start | bytes 700424 | tf_op jit(solution)/shard_map/ppermute | solution.py:33
  16.2 1.6 %collective-permute-start.3 = (bf16[16,7296]{1,0:T(8,128)(2,1)S(1)}, bf16[16,7296]{1,0:T(8,128)(2,1)S(1)}, u32[]{:S(2)}, u32[]{:S(2)}) collective-permute-start(bf16[16,7296]{1,0:T(8,128)(2,1)S(1)} %prepare.1.refs_0_), channel_id=1, source_target_pairs={{0,8},{2,10},{4,12},{6,14},{8,0},{10,2},{12,4},{14,6},{16,24},{18,... | collective-permute-start | bytes 700424 | tf_op jit(solution)/shard_map/ppermute | solution.py:33
  17.8 6.2 %collective-permute-done.6.refs_8_ = bf16[16,7296]{1,0:T(8,128)(2,1)S(1)} collective-permute-done((bf16[16,7296]{1,0:T(8,128)(2,1)S(1)}, bf16[16,7296]{1,0:T(8,128)(2,1)S(1)}, u32[]{:S(2)}, u32[]{:S(2)}) %collective-permute-start.6) | collective-permute-done | bytes 233504 | tf_op jit(solution)/shard_map/ppermute | solution.py:33
  24.6 1.5 %collective-permute-start.2 = (bf16[16,7296]{1,0:T(8,128)(2,1)S(1)}, bf16[16,7296]{1,0:T(8,128)(2,1)S(1)}, u32[]{:S(2)}, u32[]{:S(2)}) collective-permute-start(bf16[16,7296]{1,0:T(8,128)(2,1)S(1)} %collective-permute-done.refs_1_), channel_id=1, source_target_pairs={{0,4},{2,6},{4,0},{6,2},{8,12},{10,14},{12,8},{14,10},{16,20},{18,... | collective-permute-start | bytes 700424 | tf_op jit(solution)/shard_map/ppermute | solution.py:33
  27.6 1.5 %collective-permute-start.9 = (bf16[16,7296]{1,0:T(8,128)(2,1)S(1)}, bf16[16,7296]{1,0:T(8,128)(2,1)S(1)}, u32[]{:S(2)}, u32[]{:S(2)}) collective-permute-start(bf16[16,7296]{1,0:T(8,128)(2,1)S(1)} %collective-permute-done.6.refs_8_), channel_id=1, source_target_pairs={{0,2},{2,0},{4,6},{6,4},{8,10},{10,8},{12,14},{14,12},{16,18},{18,... | collective-permute-start | bytes 700424 | tf_op jit(solution)/shard_map/ppermute | solution.py:33
  29.6 3.0 %collective-permute-done.11.refs_12_ = bf16[16,7296]{1,0:T(8,128)(2,1)S(1)} collective-permute-done((bf16[16,7296]{1,0:T(8,128)(2,1)S(1)}, bf16[16,7296]{1,0:T(8,128)(2,1)S(1)}, u32[]{:S(2)}, u32[]{:S(2)}) %collective-permute-start.11) | collective-permute-done | bytes 233504 | tf_op jit(solution)/shard_map/ppermute | solution.py:33
  38.9 3.3 %collective-permute-start.10 = (bf16[16,7296]{1,0:T(8,128)(2,1)S(1)}, bf16[16,7296]{1,0:T(8,128)(2,1)}, u32[]{:S(2)}, u32[]{:S(2)}) collective-permute-start(bf16[16,7296]{1,0:T(8,128)(2,1)S(1)} %collective-permute-done.2.refs_3_), channel_id=1, source_target_pairs={{0,16},{2,18},{4,20},{6,22},{8,24},{10,26},{12,28},{14,30},{16,0},... | collective-permute-start | bytes 700424 | tf_op jit(solution)/shard_map/ppermute | solution.py:33
  44.7 3.7 %collective-permute-done.8.refs_7_ = bf16[16,7296]{1,0:T(8,128)(2,1)S(1)} collective-permute-done((bf16[16,7296]{1,0:T(8,128)(2,1)S(1)}, bf16[16,7296]{1,0:T(8,128)(2,1)S(1)}, u32[]{:S(2)}, u32[]{:S(2)}) %collective-permute-start.8) | collective-permute-done | bytes 233504 | tf_op jit(solution)/shard_map/ppermute | solution.py:33
  49.3 1.7 %all-gather.9.cloned.1.call-done = bf16[2,1,7168,256]{3,2,1,0:T(8,128)(2,1)} async-done(((bf16[1,1,7168,256]{3,2,1,0:T(8,128)(2,1)}), bf16[2,1,7168,256]{3,2,1,0:T(8,128)(2,1)}) %all-gather.9.cloned.1.call-update) | async-done | bytes 7340048 | tf_op jit(solution)/shard_map/all_gather | solution.py:172
  51.0 21.1 %all-gather.11.cloned.1.call-done = bf16[2,1,256,7168]{3,2,1,0:T(8,128)(2,1)} async-done(((bf16[1,1,256,7168]{3,2,1,0:T(8,128)(2,1)}), bf16[2,1,256,7168]{3,2,1,0:T(8,128)(2,1)}) %all-gather.11.cloned.1.call-update) | async-done | bytes 7340048 | tf_op jit(solution)/shard_map/all_gather | solution.py:172
  72.2 16.3 %experts.1 = (bf16[16,7168]{1,0:T(8,128)(2,1)S(1)}, bf16[16,7168]{1,0:T(8,128)(2,1)S(1)}, bf16[16,7168]{1,0:T(8,128)(2,1)S(1)}, bf16[16,7168]{1,0:T(8,128)(2,1)S...) custom-call(s32[2]{0:T(128)S(1)} %multiply_add_fusion.ids_ref, ...), custom_call_target="tpu_custom_call" | custom-call | flops 5637144576 | bytes 29360128 | tf_op jit(solution)/shard_map/experts/pallas_call | solution.py:142
  88.5 1.8 %collective-permute-start.15 = (bf16[16,7168]{1,0:T(8,128)(2,1)S(1)}, bf16[16,7168]{1,0:T(8,128)(2,1)S(1)}, u32[]{:S(2)}, u32[]{:S(2)}) collective-permute-start(bf16[16,7168]{1,0:T(8,128)(2,1)S(1)} %get-tuple-element.44), channel_id=1, source_target_pairs={{0,8},{2,10},{4,12},{6,14},{8,0},{10,2},{12,4},{14,6},{16,24},{18,... | collective-permute-start | bytes 688136 | tf_op jit(solution)/shard_map/ppermute | solution.py:33
  90.3 2.4 %collective-permute-start.16 = (bf16[16,7168]{1,0:T(8,128)(2,1)S(1)}, bf16[16,7168]{1,0:T(8,128)(2,1)S(1)}, u32[]{:S(2)}, u32[]{:S(2)}) collective-permute-start(bf16[16,7168]{1,0:T(8,128)(2,1)S(1)} %get-tuple-element.45), channel_id=1, source_target_pairs={{0,16},{2,18},{4,20},{6,22},{8,24},{10,26},{12,28},{14,30},{16,0},... | collective-permute-start | bytes 688136 | tf_op jit(solution)/shard_map/ppermute | solution.py:33
  96.2 5.5 %collective-permute-done.15 = bf16[16,7168]{1,0:T(8,128)(2,1)S(1)} collective-permute-done((bf16[16,7168]{1,0:T(8,128)(2,1)S(1)}, bf16[16,7168]{1,0:T(8,128)(2,1)S(1)}, u32[]{:S(2)}, u32[]{:S(2)}) %collective-permute-start.15) | collective-permute-done | bytes 229408 | tf_op jit(solution)/shard_map/ppermute | solution.py:33
  101.7 1.7 %collective-permute-start.24 = (bf16[16,7168]{1,0:T(8,128)(2,1)S(1)}, bf16[16,7168]{1,0:T(8,128)(2,1)S(1)}, u32[]{:S(2)}, u32[]{:S(2)}) collective-permute-start(bf16[16,7168]{1,0:T(8,128)(2,1)S(1)} %get-tuple-element.52), channel_id=1, source_target_pairs={{0,2},{2,0},{4,6},{6,4},{8,10},{10,8},{12,14},{14,12},{16,18},{18,... | collective-permute-start | bytes 688136 | tf_op jit(solution)/shard_map/ppermute | solution.py:33
  105.7 8.8 %collective-permute-done.26 = bf16[16,7168]{1,0:T(8,128)(2,1)S(1)} collective-permute-done((bf16[16,7168]{1,0:T(8,128)(2,1)S(1)}, bf16[16,7168]{1,0:T(8,128)(2,1)S(1)}, u32[]{:S(2)}, u32[]{:S(2)}) %collective-permute-start.26) | collective-permute-done | bytes 229408 | tf_op jit(solution)/shard_map/ppermute | solution.py:33
  117.2 2.0 %collective-permute-start.20 = (bf16[16,7168]{1,0:T(8,128)(2,1)S(1)}, bf16[16,7168]{1,0:T(8,128)(2,1)S(1)}, u32[]{:S(2)}, u32[]{:S(2)}) collective-permute-start(bf16[16,7168]{1,0:T(8,128)(2,1)S(1)} %add_convert_fusion.5), channel_id=1, source_target_pairs={{0,8},{2,10},{4,12},{6,14},{8,0},{10,2},{12,4},{14,6},{16,24},{18,... | collective-permute-start | bytes 688136 | tf_op jit(solution)/shard_map/ppermute | solution.py:33
  119.1 2.9 %collective-permute-done.27 = bf16[16,7168]{1,0:T(8,128)(2,1)S(1)} collective-permute-done((bf16[16,7168]{1,0:T(8,128)(2,1)S(1)}, bf16[16,7168]{1,0:T(8,128)(2,1)S(1)}, u32[]{:S(2)}, u32[]{:S(2)}) %collective-permute-start.27) | collective-permute-done | bytes 229408 | tf_op jit(solution)/shard_map/ppermute | solution.py:33
  122.7 1.5 %collective-permute-start.28 = (bf16[16,7168]{1,0:T(8,128)(2,1)S(1)}, bf16[16,7168]{1,0:T(8,128)(2,1)S(1)}, u32[]{:S(2)}, u32[]{:S(2)}) collective-permute-start(bf16[16,7168]{1,0:T(8,128)(2,1)S(1)} %add_convert_fusion.2), channel_id=1, source_target_pairs={{0,8},{2,10},{4,12},{6,14},{8,0},{10,2},{12,4},{14,6},{16,24},{18,... | collective-permute-start | bytes 688136 | tf_op jit(solution)/shard_map/ppermute | solution.py:33
  124.3 1.5 %collective-permute-start.18 = (bf16[16,7168]{1,0:T(8,128)(2,1)S(1)}, bf16[16,7168]{1,0:T(8,128)(2,1)S(1)}, u32[]{:S(2)}, u32[]{:S(2)}) collective-permute-start(bf16[16,7168]{1,0:T(8,128)(2,1)S(1)} %add_convert_fusion.6), channel_id=1, source_target_pairs={{0,2},{2,0},{4,6},{6,4},{8,10},{10,8},{12,14},{14,12},{16,18},{18,... | collective-permute-start | bytes 688136 | tf_op jit(solution)/shard_map/ppermute | solution.py:33
  125.9 2.9 %collective-permute-done.28 = bf16[16,7168]{1,0:T(8,128)(2,1)S(1)} collective-permute-done((bf16[16,7168]{1,0:T(8,128)(2,1)S(1)}, bf16[16,7168]{1,0:T(8,128)(2,1)S(1)}, u32[]{:S(2)}, u32[]{:S(2)}) %collective-permute-start.28) | collective-permute-done | bytes 229408 | tf_op jit(solution)/shard_map/ppermute | solution.py:33
  128.9 1.5 %collective-permute-start.29 = (bf16[16,7168]{1,0:T(8,128)(2,1)S(1)}, bf16[16,7168]{1,0:T(8,128)(2,1)S(1)}, u32[]{:S(2)}, u32[]{:S(2)}) collective-permute-start(bf16[16,7168]{1,0:T(8,128)(2,1)S(1)} %add_convert_fusion.1), channel_id=1, source_target_pairs={{0,16},{2,18},{4,20},{6,22},{8,24},{10,26},{12,28},{14,30},{16,0},... | collective-permute-start | bytes 688136 | tf_op jit(solution)/shard_map/ppermute | solution.py:33
  130.5 8.9 %collective-permute-done.29 = bf16[16,7168]{1,0:T(8,128)(2,1)S(1)} collective-permute-done((bf16[16,7168]{1,0:T(8,128)(2,1)S(1)}, bf16[16,7168]{1,0:T(8,128)(2,1)S(1)}, u32[]{:S(2)}, u32[]{:S(2)}) %collective-permute-start.29) | collective-permute-done | bytes 229408 | tf_op jit(solution)/shard_map/ppermute | solution.py:33
  (92 shorter events, 26.2 us)
Async XLA Ops:
  6.5 42.7 %all-gather.7.cloned.1.call-start = ((), (), s32[]{:S(2)}) async-start(), calls=%async_computation | async-start | bytes 11010048 | tf_op jit(solution)/shard_map/all_gather | solution.py:172
  7.3 43.7 %all-gather.9.cloned.1.call-start = ((), (), s32[]{:S(2)}) async-start(), calls=%async_computation.1 | async-start | bytes 11010048 | tf_op jit(solution)/shard_map/all_gather | solution.py:172
  8.0 64.0 %all-gather.11.cloned.1.call-start = ((), (), s32[]{:S(2)}) async-start(), calls=%async_computation.2 | async-start | bytes 11010048 | tf_op jit(solution)/shard_map/all_gather | solution.py:172
  9.1 14.9 %collective-permute-start.6 = (bf16[16,7296]{1,0:T(8,128)(2,1)S(1)}, bf16[16,7296]{1,0:T(8,128)(2,1)S(1)}, u32[]{:S(2)}, u32[]{:S(2)}) collective-permute-start(bf16[16,7296]{1,0:T(8,128)(2,1)S(1)} %prepare.1.refs_0_), channel_id=1, source_target_pairs={{0,16},{2,18},{4,20},{6,22},{8,24},{10,26},{12,28},{14,30},{16,0},... | collective-permute-start | bytes 700424 | tf_op jit(solution)/shard_map/ppermute | solution.py:33
  13.2 11.5 %collective-permute-start = (bf16[16,7296]{1,0:T(8,128)(2,1)S(1)}, bf16[16,7296]{1,0:T(8,128)(2,1)S(1)}, u32[]{:S(2)}, u32[]{:S(2)}) collective-permute-start(bf16[16,7296]{1,0:T(8,128)(2,1)S(1)} %prepare.1.refs_0_), channel_id=1, source_target_pairs={{0,2},{2,0},{4,6},{6,4},{8,10},{10,8},{12,14},{14,12},{16,18},{18,... | collective-permute-start | bytes 700424 | tf_op jit(solution)/shard_map/ppermute | solution.py:33
  14.7 11.5 %collective-permute-start.1 = (bf16[16,7296]{1,0:T(8,128)(2,1)S(1)}, bf16[16,7296]{1,0:T(8,128)(2,1)S(1)}, u32[]{:S(2)}, u32[]{:S(2)}) collective-permute-start(bf16[16,7296]{1,0:T(8,128)(2,1)S(1)} %prepare.1.refs_0_), channel_id=1, source_target_pairs={{0,4},{2,6},{4,0},{6,2},{8,12},{10,14},{12,8},{14,10},{16,20},{18,... | collective-permute-start | bytes 700424 | tf_op jit(solution)/shard_map/ppermute | solution.py:33
  16.2 12.9 %collective-permute-start.3 = (bf16[16,7296]{1,0:T(8,128)(2,1)S(1)}, bf16[16,7296]{1,0:T(8,128)(2,1)S(1)}, u32[]{:S(2)}, u32[]{:S(2)}) collective-permute-start(bf16[16,7296]{1,0:T(8,128)(2,1)S(1)} %prepare.1.refs_0_), channel_id=1, source_target_pairs={{0,8},{2,10},{4,12},{6,14},{8,0},{10,2},{12,4},{14,6},{16,24},{18,... | collective-permute-start | bytes 700424 | tf_op jit(solution)/shard_map/ppermute | solution.py:33
  26.2 10.5 %collective-permute-start.4 = (bf16[16,7296]{1,0:T(8,128)(2,1)S(1)}, bf16[16,7296]{1,0:T(8,128)(2,1)S(1)}, u32[]{:S(2)}, u32[]{:S(2)}) collective-permute-start(bf16[16,7296]{1,0:T(8,128)(2,1)S(1)} %collective-permute-done.1.refs_2_), channel_id=1, source_target_pairs={{0,8},{2,10},{4,12},{6,14},{8,0},{10,2},{12,4},{14,6},{16,24},{18,... | collective-permute-start | bytes 700424 | tf_op jit(solution)/shard_map/ppermute | solution.py:33
  27.6 9.6 %collective-permute-start.9 = (bf16[16,7296]{1,0:T(8,128)(2,1)S(1)}, bf16[16,7296]{1,0:T(8,128)(2,1)S(1)}, u32[]{:S(2)}, u32[]{:S(2)}) collective-permute-start(bf16[16,7296]{1,0:T(8,128)(2,1)S(1)} %collective-permute-done.6.refs_8_), channel_id=1, source_target_pairs={{0,2},{2,0},{4,6},{6,4},{8,10},{10,8},{12,14},{14,12},{16,18},{18,... | collective-permute-start | bytes 700424 | tf_op jit(solution)/shard_map/ppermute | solution.py:33
  29.1 9.2 %collective-permute-start.7 = (bf16[16,7296]{1,0:T(8,128)(2,1)S(1)}, bf16[16,7296]{1,0:T(8,128)(2,1)S(1)}, u32[]{:S(2)}, u32[]{:S(2)}) collective-permute-start(bf16[16,7296]{1,0:T(8,128)(2,1)S(1)} %collective-permute-done.6.refs_8_), channel_id=1, source_target_pairs={{0,4},{2,6},{4,0},{6,2},{8,12},{10,14},{12,8},{14,10},{16,20},{18,... | collective-permute-start | bytes 700424 | tf_op jit(solution)/shard_map/ppermute | solution.py:33
  33.2 9.0 %collective-permute-start.12 = (bf16[16,7296]{1,0:T(8,128)(2,1)S(1)}, bf16[16,7296]{1,0:T(8,128)(2,1)S(1)}, u32[]{:S(2)}, u32[]{:S(2)}) collective-permute-start(bf16[16,7296]{1,0:T(8,128)(2,1)S(1)} %collective-permute-done.11.refs_12_), channel_id=1, source_target_pairs={{0,2},{2,0},{4,6},{6,4},{8,10},{10,8},{12,14},{14,12},{16,18},{18,... | collective-permute-start | bytes 700424 | tf_op jit(solution)/shard_map/ppermute | solution.py:33
  34.7 9.9 %collective-permute-start.13 = (bf16[16,7296]{1,0:T(8,128)(2,1)S(1)}, bf16[16,7296]{1,0:T(8,128)(2,1)S(1)}, u32[]{:S(2)}, u32[]{:S(2)}) collective-permute-start(bf16[16,7296]{1,0:T(8,128)(2,1)S(1)} %collective-permute-done.11.refs_12_), channel_id=1, source_target_pairs={{0,4},{2,6},{4,0},{6,2},{8,12},{10,14},{12,8},{14,10},{16,20},{18,... | collective-permute-start | bytes 700424 | tf_op jit(solution)/shard_map/ppermute | solution.py:33
  38.3 10.2 %collective-permute-start.8 = (bf16[16,7296]{1,0:T(8,128)(2,1)S(1)}, bf16[16,7296]{1,0:T(8,128)(2,1)S(1)}, u32[]{:S(2)}, u32[]{:S(2)}) collective-permute-start(bf16[16,7296]{1,0:T(8,128)(2,1)S(1)} %collective-permute-done.2.refs_3_), channel_id=1, source_target_pairs={{0,8},{2,10},{4,12},{6,14},{8,0},{10,2},{12,4},{14,6},{16,24},{18,... | collective-permute-start | bytes 700424 | tf_op jit(solution)/shard_map/ppermute | solution.py:33
  38.9 10.4 %collective-permute-start.10 = (bf16[16,7296]{1,0:T(8,128)(2,1)S(1)}, bf16[16,7296]{1,0:T(8,128)(2,1)}, u32[]{:S(2)}, u32[]{:S(2)}) collective-permute-start(bf16[16,7296]{1,0:T(8,128)(2,1)S(1)} %collective-permute-done.2.refs_3_), channel_id=1, source_target_pairs={{0,16},{2,18},{4,20},{6,22},{8,24},{10,26},{12,28},{14,30},{16,0},... | collective-permute-start | bytes 700424 | tf_op jit(solution)/shard_map/ppermute | solution.py:33
  88.5 13.2 %collective-permute-start.15 = (bf16[16,7168]{1,0:T(8,128)(2,1)S(1)}, bf16[16,7168]{1,0:T(8,128)(2,1)S(1)}, u32[]{:S(2)}, u32[]{:S(2)}) collective-permute-start(bf16[16,7168]{1,0:T(8,128)(2,1)S(1)} %get-tuple-element.44), channel_id=1, source_target_pairs={{0,8},{2,10},{4,12},{6,14},{8,0},{10,2},{12,4},{14,6},{16,24},{18,... | collective-permute-start | bytes 688136 | tf_op jit(solution)/shard_map/ppermute | solution.py:33
  90.3 13.1 %collective-permute-start.16 = (bf16[16,7168]{1,0:T(8,128)(2,1)S(1)}, bf16[16,7168]{1,0:T(8,128)(2,1)S(1)}, u32[]{:S(2)}, u32[]{:S(2)}) collective-permute-start(bf16[16,7168]{1,0:T(8,128)(2,1)S(1)} %get-tuple-element.45), channel_id=1, source_target_pairs={{0,16},{2,18},{4,20},{6,22},{8,24},{10,26},{12,28},{14,30},{16,0},... | collective-permute-start | bytes 688136 | tf_op jit(solution)/shard_map/ppermute | solution.py:33
  92.7 12.3 %collective-permute-start.19 = (bf16[16,7168]{1,0:T(8,128)(2,1)S(1)}, bf16[16,7168]{1,0:T(8,128)(2,1)S(1)}, u32[]{:S(2)}, u32[]{:S(2)}) collective-permute-start(bf16[16,7168]{1,0:T(8,128)(2,1)S(1)} %get-tuple-element.47), channel_id=1, source_target_pairs={{0,2},{2,0},{4,6},{6,4},{8,10},{10,8},{12,14},{14,12},{16,18},{18,... | collective-permute-start | bytes 688136 | tf_op jit(solution)/shard_map/ppermute | solution.py:33
  94.2 21.8 %collective-permute-start.21 = (bf16[16,7168]{1,0:T(8,128)(2,1)S(1)}, bf16[16,7168]{1,0:T(8,128)(2,1)S(1)}, u32[]{:S(2)}, u32[]{:S(2)}) collective-permute-start(bf16[16,7168]{1,0:T(8,128)(2,1)S(1)} %get-tuple-element.49), channel_id=1, source_target_pairs={{0,8},{2,10},{4,12},{6,14},{8,0},{10,2},{12,4},{14,6},{16,24},{18,... | collective-permute-start | bytes 688136 | tf_op jit(solution)/shard_map/ppermute | solution.py:33
  94.7 29.6 %collective-permute-start.23 = (bf16[16,7168]{1,0:T(8,128)(2,1)S(1)}, bf16[16,7168]{1,0:T(8,128)(2,1)S(1)}, u32[]{:S(2)}, u32[]{:S(2)}) collective-permute-start(bf16[16,7168]{1,0:T(8,128)(2,1)S(1)} %get-tuple-element.51), channel_id=1, source_target_pairs={{0,4},{2,6},{4,0},{6,2},{8,12},{10,14},{12,8},{14,10},{16,20},{18,... | collective-permute-start | bytes 688136 | tf_op jit(solution)/shard_map/ppermute | solution.py:33
  101.7 24.2 %collective-permute-start.24 = (bf16[16,7168]{1,0:T(8,128)(2,1)S(1)}, bf16[16,7168]{1,0:T(8,128)(2,1)S(1)}, u32[]{:S(2)}, u32[]{:S(2)}) collective-permute-start(bf16[16,7168]{1,0:T(8,128)(2,1)S(1)} %get-tuple-element.52), channel_id=1, source_target_pairs={{0,2},{2,0},{4,6},{6,4},{8,10},{10,8},{12,14},{14,12},{16,18},{18,... | collective-permute-start | bytes 688136 | tf_op jit(solution)/shard_map/ppermute | solution.py:33
  103.4 13.7 %collective-permute-start.25 = (bf16[16,7168]{1,0:T(8,128)(2,1)S(1)}, bf16[16,7168]{1,0:T(8,128)(2,1)S(1)}, u32[]{:S(2)}, u32[]{:S(2)}) collective-permute-start(bf16[16,7168]{1,0:T(8,128)(2,1)S(1)} %get-tuple-element.54), channel_id=1, source_target_pairs={{0,4},{2,6},{4,0},{6,2},{8,12},{10,14},{12,8},{14,10},{16,20},{18,... | collective-permute-start | bytes 688136 | tf_op jit(solution)/shard_map/ppermute | solution.py:33
  105.0 9.4 %collective-permute-start.26 = (bf16[16,7168]{1,0:T(8,128)(2,1)S(1)}, bf16[16,7168]{1,0:T(8,128)(2,1)S(1)}, u32[]{:S(2)}, u32[]{:S(2)}) collective-permute-start(bf16[16,7168]{1,0:T(8,128)(2,1)S(1)} %get-tuple-element.56), channel_id=1, source_target_pairs={{0,4},{2,6},{4,0},{6,2},{8,12},{10,14},{12,8},{14,10},{16,20},{18,... | collective-permute-start | bytes 688136 | tf_op jit(solution)/shard_map/ppermute | solution.py:33
  117.2 13.3 %collective-permute-start.20 = (bf16[16,7168]{1,0:T(8,128)(2,1)S(1)}, bf16[16,7168]{1,0:T(8,128)(2,1)S(1)}, u32[]{:S(2)}, u32[]{:S(2)}) collective-permute-start(bf16[16,7168]{1,0:T(8,128)(2,1)S(1)} %add_convert_fusion.5), channel_id=1, source_target_pairs={{0,8},{2,10},{4,12},{6,14},{8,0},{10,2},{12,4},{14,6},{16,24},{18,... | collective-permute-start | bytes 688136 | tf_op jit(solution)/shard_map/ppermute | solution.py:33
  128.9 10.4 %collective-permute-start.29 = (bf16[16,7168]{1,0:T(8,128)(2,1)S(1)}, bf16[16,7168]{1,0:T(8,128)(2,1)S(1)}, u32[]{:S(2)}, u32[]{:S(2)}) collective-permute-start(bf16[16,7168]{1,0:T(8,128)(2,1)S(1)} %add_convert_fusion.1), channel_id=1, source_target_pairs={{0,16},{2,18},{4,20},{6,22},{8,24},{10,26},{12,28},{14,30},{16,0},... | collective-permute-start | bytes 688136 | tf_op jit(solution)/shard_map/ppermute | solution.py:33
  (26 other events, 612.5 us)
Sparse Core Ops, SparseCore 0:
  8.9 20.9 all-gather.6
  31.5 19.4 all-gather.8
  52.5 19.4 all-gather.10

commit v4 on v2

--- a/solution.py
+++ b/solution.py
@@ -12,23 +12,29 @@
 
 EPSILON = 1e-06
 ROUTE_SCALE = 2.5
-VMEM_LIMIT = 56 * 1024 * 1024
-
-TREE_16 = (
-    (4, 4), (1, 1), (2, 2), (8, 8),
-    (5, 1), (6, 2), (12, 4), (9, 1), (10, 2),
-    (3, 1), (7, 2), (13, 4), (11, 1), (15, 2), (14, 4),
-)
-
-
-def gather_tree(ep_count):
-    if ep_count == 16:
-        return TREE_16
-    return tuple((r, 1 << (r.bit_length() - 1)) for r in range(1, ep_count))
-
-
-def across(value, bit, ep_count):
-    return lax.ppermute(value, "ep", [(i, i ^ bit) for i in range(ep_count)])
+PREPARE_VMEM = 4 * 1024 * 1024
+EXPERTS_VMEM = 44 * 1024 * 1024
+
+PLAN_16 = ((0, 4, 8), (0, 1, 2), (1, 1, 2), (1, 2, 1), (2, 2, 0), (3, 8, 1), (3, 2, 4), (6, 1, 4))
+
+
+def plan_for(ep_count, grp_count):
+    if ep_count == 16 and grp_count == 2:
+        return PLAN_16, True
+    plan = []
+    for r in range(1, ep_count):
+        bit = 1 << (r.bit_length() - 1)
+        plan.append((r ^ bit, bit, bit))
+    return tuple(plan), False
+
+
+def across(value, bits, ep_count):
+    pairs = [(i * 2 + c, (i ^ bit) * 2 + c) for c, bit in enumerate(bits) if bit for i in range(ep_count)]
+    return lax.ppermute(value, ("ep", "grp"), pairs)
+
+
+def between_cores(value):
+    return lax.ppermute(value, "grp", [(0, 1), (1, 0)])
 
 
 def prepare_kernel(hidden_ref, gain_ref, routes_ref, out_ref):
@@ -50,7 +56,7 @@
     return pl.pallas_call(
         prepare_kernel,
         out_shape=jax.ShapeDtypeStruct((rows, width + LANES), jnp.bfloat16),
-        compiler_params=pltpu.CompilerParams(vmem_limit_bytes=VMEM_LIMIT),
+        compiler_params=pltpu.CompilerParams(vmem_limit_bytes=PREPARE_VMEM),
         cost_estimate=pl.CostEstimate(flops=6 * rows * width, bytes_accessed=4 * rows * width, transcendentals=rows),
         name="prepare",
     )(hidden, gain[None, :], routes)
@@ -120,7 +126,7 @@
     blocks = len(token_blocks)
     rows = token_blocks[0].shape[0]
     width, hidden_units = gates[0].shape
-    k_tile = n_tile = 1024
+    k_tile = n_tile = width // 4
     k_steps, n_steps = width // k_tile, width // n_tile
     all_rows = blocks * rows
 
@@ -151,7 +157,7 @@
             ],
         ),
         out_shape=[jax.ShapeDtypeStruct((rows, width), jnp.bfloat16)] * blocks,
-        compiler_params=pltpu.CompilerParams(vmem_limit_bytes=VMEM_LIMIT),
+        compiler_params=pltpu.CompilerParams(vmem_limit_bytes=EXPERTS_VMEM),
         cost_estimate=pl.CostEstimate(
             flops=12 * all_rows * width * hidden_units,
             bytes_accessed=12 * width * hidden_units + 4 * all_rows * width,
@@ -162,35 +168,45 @@
 
 
 def local(hidden, gain, router_w, routes, w_gate, w_up, w_down):
-    ep_count = lax.axis_size("ep")
+    ep_count, grp_count = lax.axis_size("ep"), lax.axis_size("grp")
     local_experts = ep_count // SPLIT
-    expert_count = local_experts * lax.axis_size("grp")
-    tree = gather_tree(ep_count)
-    swap = [(0, 1), (1, 0)]
-    own_weights = (w_gate[0, 0], w_up[0, 0], w_down[0, 0])
-    other_weights = [lax.ppermute(w, "grp", swap) for w in own_weights]
-    gates, ups, downs = zip(own_weights, other_weights)
-
-    held = {0: prepare(hidden, gain, routes)}
-    for r, bit in tree:
-        held[r] = across(held[r ^ bit], bit, ep_count)
-
+    expert_count = local_experts * grp_count
     place, core = lax.axis_index("ep") // SPLIT, lax.axis_index("grp")
+    plan, paired = plan_for(ep_count, grp_count)
+    rows = hidden.shape[0]
+    gates, ups, downs = ((w[0, 0], between_cores(w[0, 0])) for w in (w_gate, w_up, w_down))
+
+    own = prepare(hidden, gain, routes)
+    if paired:
+        own = jnp.concatenate([own, between_cores(own)], axis=0)
+    held = [own]
+    for parent, *bits in plan:
+        held.append(across(held[parent], bits, ep_count))
+    first = 0
+    if paired:
+        first = 1
+        spare = [0 in bits for _, *bits in plan].index(True) + 1
+        held[spare] = jnp.where(core == 1, own, held[spare])
+
     ids = jnp.stack([core * local_experts + place, (1 - core) * local_experts + place]).astype(jnp.int32)
     router_t = jnp.pad(router_w.T, ((0, -expert_count % 16), (0, 0)))
-    parts = experts(ids, [held[r] for r in range(ep_count)], router_t, gates, ups, downs)
-
-    arrived = {r: [] for r in range(ep_count)}
-
-    def summed(r):
-        total = parts[r].astype(jnp.float32)
-        for value in arrived[r]:
-            total = total + value.astype(jnp.float32)
-        return total.astype(jnp.bfloat16)
-
-    for r, bit in reversed(tree):
-        arrived[r ^ bit].append(across(summed(r), bit, ep_count))
-    return summed(0)
+    parts = experts(ids, held[first:], router_t, gates, ups, downs)
+
+    terms = [[] for _ in range(first)] + [[part] for part in parts]
+    if paired:
+        terms[0].append(jnp.where(core == 1, parts[spare - 1], jnp.zeros_like(parts[spare - 1])))
+
+    def summed(slot):
+        return sum(term.astype(jnp.float32) for term in terms[slot])
+
+    for slot in range(len(plan), 0, -1):
+        parent, *bits = plan[slot - 1]
+        terms[parent].append(across(summed(slot).astype(jnp.bfloat16), bits, ep_count))
+    total = summed(0)
+    if paired:
+        arrived = between_cores(total[rows:].astype(jnp.bfloat16))
+        total = total[:rows] + arrived.astype(jnp.float32)
+    return total.astype(jnp.bfloat16)
 
 
 def solution(mesh):

time: 136 us -> 120 us (0.88)
  starting transfers between devices: 39.3 us -> 27.2 us
  waiting for transfers between devices: 63.9 us -> 71.8 us
  Pallas kernels: 22.2 us -> 15 us
  other arithmetic: 6.7 us -> 1.7 us
    ppermute x33 -> x21, starting transfers between devices: 39.3 us -> 27.2 us  [the longest x16 26 us: across(): return lax.ppermute(value, ('ep', 'grp'), pairs)]
    ppermute x33 -> x21, waiting for transfers between devices: 63.9 us -> 71.8 us  [the longest x16 69.8 us: across(): return lax.ppermute(value, ('ep', 'grp'), pairs)]
    pallas_call x1, Pallas kernels: 20.3 us -> 14.8 us  [experts(): pl.pallas_call(functools.partial(experts_kernel, blocks, k_steps, k_tile)...]
    convert_element_type x8 -> x5, other arithmetic: 6.04 us -> 1.3 us  [the longest x1 0.74 us: local(): return total.astype(jnp.bfloat16)]
    pallas_call x1, Pallas kernels: 1.86 us -> 0.22 us  [prepare(): pl.pallas_call(prepare_kernel, out_shape=jax.ShapeDtypeStruct((rows, widt...]
  transfers between devices with their start and end apart: 33 -> 21, of which waited for: 18 -> 13; matrix products, arithmetic and copies ran while one was open for 6% -> 1% of each run, Pallas kernels for 1% -> 0%
where the time goes in v4:
time: 120 us; the launch traced here: 119 us
  waiting for transfers between devices  71.8 us (60%)
  starting transfers between devices  27.2 us (23%)
  Pallas kernels  15 us (12%)
  local copies, waits for them, and re-layouts  3.38 us (3%)
  other arithmetic  1.7 us (1%)
    ppermute x16, waiting for transfers between devices, across(): return lax.ppermute(value, ('ep', 'grp'), pairs)  69.8 us
    ppermute x16, starting transfers between devices, across(): return lax.ppermute(value, ('ep', 'grp'), pairs)  26 us
    pallas_call x1, Pallas kernels, experts(): pl.pallas_call(functools.partial(experts_kernel, blocks, k_steps, k_tile)...  14.8 us
    unnamed x5, local copies, waits for them, and re-layouts  2.44 us
  transfers between devices with their start and end apart: 21, of which 13 were waited for; matrix products, arithmetic and copies ran while one was open for 1% of the time, Pallas kernels for 0%

profile of v4, /device:TPU:0, one launch (start us, length us, event | category | flops | bytes accessed | tf_op | source)
XLA Modules:
  0.0 119.2 jit_solution(413905574018440570)
XLA Ops:
  0.8 0.9 copy-done
  4.3 2.9 %collective-permute-start.2 = (bf16[32,7296]{1,0:T(8,128)(2,1)S(1)}, bf16[32,7296]{1,0:T(8,128)(2,1)S(1)}, u32[]{:S(2)}, u32[]{:S(2)}) collective-permute-start(bf16[32,7296]{1,0:T(8,128)(2,1)S(1)} %pad_maximum_fusion), channel_id=1, source_target_pairs={{0,2},{2,0},{4,6},{6,4},{8,10},{10,8},{12,14},{14,12},{16,18},{18,... | collective-permute-start | bytes 1400840 | tf_op jit(solution)/shard_map/ppermute | solution.py:33
  7.3 1.6 %collective-permute-start.1 = (bf16[32,7296]{1,0:T(8,128)(2,1)S(1)}, bf16[32,7296]{1,0:T(8,128)(2,1)S(1)}, u32[]{:S(2)}, u32[]{:S(2)}) collective-permute-start(bf16[32,7296]{1,0:T(8,128)(2,1)S(1)} %pad_maximum_fusion), channel_id=1, source_target_pairs={{0,8},{2,10},{4,12},{6,14},{8,0},{10,2},{12,4},{14,6},{16,24},{18,... | collective-permute-start | bytes 1400840 | tf_op jit(solution)/shard_map/ppermute | solution.py:33
  8.8 5.0 %collective-permute-done.2.refs_1_ = bf16[32,7296]{1,0:T(8,128)(2,1)S(1)} collective-permute-done((bf16[32,7296]{1,0:T(8,128)(2,1)S(1)}, bf16[32,7296]{1,0:T(8,128)(2,1)S(1)}, u32[]{:S(2)}, u32[]{:S(2)}) %collective-permute-start.2) | collective-permute-done | bytes 466976 | tf_op jit(solution)/shard_map/ppermute | solution.py:33
  13.8 3.9 %collective-permute-start.5 = (bf16[32,7296]{1,0:T(8,128)(2,1)S(1)}, bf16[32,7296]{1,0:T(8,128)(2,1)S(1)}, u32[]{:S(2)}, u32[]{:S(2)}) collective-permute-start(bf16[32,7296]{1,0:T(8,128)(2,1)S(1)} %collective-permute-done.2.refs_1_), channel_id=1, source_target_pairs={{0,4},{2,6},{4,0},{6,2},{8,12},{10,14},{12,8},{14,10},{16,20},{18,... | collective-permute-start | bytes 1400840 | tf_op jit(solution)/shard_map/ppermute | solution.py:33
  17.8 2.8 %collective-permute-done.1.refs_0_ = bf16[32,7296]{1,0:T(8,128)(2,1)S(1)} collective-permute-done((bf16[32,7296]{1,0:T(8,128)(2,1)S(1)}, bf16[32,7296]{1,0:T(8,128)(2,1)S(1)}, u32[]{:S(2)}, u32[]{:S(2)}) %collective-permute-start.1) | collective-permute-done | bytes 466976 | tf_op jit(solution)/shard_map/ppermute | solution.py:33
  20.5 5.9 %collective-permute-done.5 = bf16[32,7296]{1,0:T(8,128)(2,1)S(1)} collective-permute-done((bf16[32,7296]{1,0:T(8,128)(2,1)S(1)}, bf16[32,7296]{1,0:T(8,128)(2,1)S(1)}, u32[]{:S(2)}, u32[]{:S(2)}) %collective-permute-start.5) | collective-permute-done | bytes 466976 | tf_op jit(solution)/shard_map/ppermute | solution.py:33
  26.5 2.5 %collective-permute-start.4 = (bf16[32,7296]{1,0:T(8,128)(2,1)S(1)}, bf16[32,7296]{1,0:T(8,128)(2,1)S(1)}, u32[]{:S(2)}, u32[]{:S(2)}) collective-permute-start(bf16[32,7296]{1,0:T(8,128)(2,1)S(1)} %collective-permute-done.1.refs_0_), channel_id=1, source_target_pairs={{0,4},{2,6},{4,0},{6,2},{8,12},{10,14},{12,8},{14,10},{16,20},{18,... | collective-permute-start | bytes 1400840 | tf_op jit(solution)/shard_map/ppermute | solution.py:33
  29.0 5.1 %collective-permute-done.3.refs_2_ = bf16[32,7296]{1,0:T(8,128)(2,1)S(1)} collective-permute-done((bf16[32,7296]{1,0:T(8,128)(2,1)S(1)}, bf16[32,7296]{1,0:T(8,128)(2,1)S(1)}, u32[]{:S(2)}, u32[]{:S(2)}) %collective-permute-start.3) | collective-permute-done | bytes 466976 | tf_op jit(solution)/shard_map/ppermute | solution.py:33
  34.1 1.8 %collective-permute-start.6 = (bf16[32,7296]{1,0:T(8,128)(2,1)S(1)}, bf16[32,7296]{1,0:T(8,128)(2,1)S(1)}, u32[]{:S(2)}, u32[]{:S(2)}) collective-permute-start(bf16[32,7296]{1,0:T(8,128)(2,1)S(1)} %collective-permute-done.3.refs_2_), channel_id=1, source_target_pairs={{0,16},{2,18},{4,20},{6,22},{8,24},{10,26},{12,28},{14,30},{16,0},... | collective-permute-start | bytes 1400840 | tf_op jit(solution)/shard_map/ppermute | solution.py:33
  36.9 1.7 %collective-permute-start.7 = (bf16[32,7296]{1,0:T(8,128)(2,1)S(1)}, bf16[32,7296]{1,0:T(8,128)(2,1)S(1)}, u32[]{:S(2)}, u32[]{:S(2)}) collective-permute-start(bf16[32,7296]{1,0:T(8,128)(2,1)S(1)} %collective-permute-done.3.refs_2_), channel_id=1, source_target_pairs={{0,4},{2,6},{4,0},{6,2},{8,12},{10,14},{12,8},{14,10},{16,20},{18,... | collective-permute-start | bytes 1400840 | tf_op jit(solution)/shard_map/ppermute | solution.py:33
  38.5 9.3 %collective-permute-done.6.refs_5_ = bf16[32,7296]{1,0:T(8,128)(2,1)S(1)} collective-permute-done((bf16[32,7296]{1,0:T(8,128)(2,1)S(1)}, bf16[32,7296]{1,0:T(8,128)(2,1)S(1)}, u32[]{:S(2)}, u32[]{:S(2)}) %collective-permute-start.6) | collective-permute-done | bytes 466976 | tf_op jit(solution)/shard_map/ppermute | solution.py:33
  48.6 7.8 %collective-permute-done.8.refs_7_ = bf16[32,7296]{1,0:T(8,128)(2,1)S(1)} collective-permute-done((bf16[32,7296]{1,0:T(8,128)(2,1)S(1)}, bf16[32,7296]{1,0:T(8,128)(2,1)S(1)}, u32[]{:S(2)}, u32[]{:S(2)}) %collective-permute-start.8) | collective-permute-done | bytes 466976 | tf_op jit(solution)/shard_map/ppermute | solution.py:33
  56.4 14.8 %experts.1 = (bf16[32,7168]{1,0:T(8,128)(2,1)S(1)}, bf16[32,7168]{1,0:T(8,128)(2,1)S(1)}, bf16[32,7168]{1,0:T(8,128)(2,1)S(1)}, bf16[32,7168]{1,0:T(8,128)(2,1)S...) custom-call(s32[2]{0:T(128)S(1)} %pad_add_fusion.ids_ref, ...), custom_call_target="tpu_custom_call" | custom-call | flops 5637144576 | bytes 29360128 | tf_op jit(solution)/shard_map/experts/pallas_call | solution.py:145
  72.3 12.0 %collective-permute-done.16 = bf16[32,7168]{1,0:T(8,128)(2,1)S(1)} collective-permute-done((bf16[32,7168]{1,0:T(8,128)(2,1)S(1)}, bf16[32,7168]{1,0:T(8,128)(2,1)S(1)}, u32[]{:S(2)}, u32[]{:S(2)}) %collective-permute-start.16) | collective-permute-done | bytes 458784 | tf_op jit(solution)/shard_map/ppermute | solution.py:33
  84.5 2.4 %collective-permute-start.17 = (bf16[32,7168]{1,0:T(8,128)(2,1)S(1)}, bf16[32,7168]{1,0:T(8,128)(2,1)S(1)}, u32[]{:S(2)}, u32[]{:S(2)}) collective-permute-start(bf16[32,7168]{1,0:T(8,128)(2,1)S(1)} %add_convert_fusion.2), channel_id=1, source_target_pairs={{0,16},{2,18},{4,20},{6,22},{8,24},{10,26},{12,28},{14,30},{16,0},... | collective-permute-start | bytes 1376264 | tf_op jit(solution)/shard_map/ppermute | solution.py:33
  86.9 1.6 %collective-permute-start.14 = (bf16[32,7168]{1,0:T(8,128)(2,1)S(1)}, bf16[32,7168]{1,0:T(8,128)(2,1)S(1)}, u32[]{:S(2)}, u32[]{:S(2)}) collective-permute-start(bf16[32,7168]{1,0:T(8,128)(2,1)S(1)} %get-tuple-element.16), channel_id=1, source_target_pairs={{0,4},{2,6},{4,0},{6,2},{8,12},{10,14},{12,8},{14,10},{16,20},{18,... | collective-permute-start | bytes 1376264 | tf_op jit(solution)/shard_map/ppermute | solution.py:33
  88.5 2.3 %collective-permute-start.12 = (bf16[32,7168]{1,0:T(8,128)(2,1)S(1)}, bf16[32,7168]{1,0:T(8,128)(2,1)S(1)}, u32[]{:S(2)}, u32[]{:S(2)}) collective-permute-start(bf16[32,7168]{1,0:T(8,128)(2,1)S(1)} %get-tuple-element.13), channel_id=1, source_target_pairs={{0,4},{2,6},{4,0},{6,2},{8,12},{10,14},{12,8},{14,10},{16,20},{18,... | collective-permute-start | bytes 1376264 | tf_op jit(solution)/shard_map/ppermute | solution.py:33
  90.8 8.0 %collective-permute-done.17 = bf16[32,7168]{1,0:T(8,128)(2,1)S(1)} collective-permute-done((bf16[32,7168]{1,0:T(8,128)(2,1)S(1)}, bf16[32,7168]{1,0:T(8,128)(2,1)S(1)}, u32[]{:S(2)}, u32[]{:S(2)}) %collective-permute-start.17) | collective-permute-done | bytes 458784 | tf_op jit(solution)/shard_map/ppermute | solution.py:33
  99.5 7.4 %collective-permute-done.12 = bf16[32,7168]{1,0:T(8,128)(2,1)S(1)} collective-permute-done((bf16[32,7168]{1,0:T(8,128)(2,1)S(1)}, bf16[32,7168]{1,0:T(8,128)(2,1)S(1)}, u32[]{:S(2)}, u32[]{:S(2)}) %collective-permute-start.12) | collective-permute-done | bytes 458784 | tf_op jit(solution)/shard_map/ppermute | solution.py:33
  107.9 2.3 %collective-permute-start.19 = (bf16[32,7168]{1,0:T(8,128)(2,1)S(1)}, bf16[32,7168]{1,0:T(8,128)(2,1)S(1)}, u32[]{:S(2)}, u32[]{:S(2)}) collective-permute-start(bf16[32,7168]{1,0:T(8,128)(2,1)S(1)} %add_convert_fusion), channel_id=1, source_target_pairs={{0,8},{2,10},{4,12},{6,14},{8,0},{10,2},{12,4},{14,6},{16,24},{18,... | collective-permute-start | bytes 1376264 | tf_op jit(solution)/shard_map/ppermute | solution.py:33
  110.2 5.4 %collective-permute-done.13 = bf16[32,7168]{1,0:T(8,128)(2,1)S(1)} collective-permute-done((bf16[32,7168]{1,0:T(8,128)(2,1)S(1)}, bf16[32,7168]{1,0:T(8,128)(2,1)S(1)}, u32[]{:S(2)}, u32[]{:S(2)}) %collective-permute-start.13) | collective-permute-done | bytes 458784 | tf_op jit(solution)/shard_map/ppermute | solution.py:33
  115.6 1.1 collective-permute-done.19
  117.0 1.5 %collective-permute-done.20 = bf16[16,7168]{1,0:T(8,128)(2,1)S(1)} collective-permute-done((bf16[16,7168]{1,0:T(8,128)(2,1)S(1)}, bf16[16,7168]{1,0:T(8,128)(2,1)S(1)}, u32[]{:S(2)}, u32[]{:S(2)}) %collective-permute-start.20) | collective-permute-done | bytes 229408 | tf_op jit(solution)/shard_map/ppermute | solution.py:37
  (36 shorter events, 9.1 us)
Async XLA Ops:
  0.8 0.9 copy-start
  1.7 0.7 copy-start.1
  2.7 1.6 %collective-permute-start = (bf16[16,7296]{1,0:T(8,128)(2,1)S(1)}, bf16[16,7296]{1,0:T(8,128)(2,1)S(1)}, u32[]{:S(2)}, u32[]{:S(2)}) collective-permute-start(bf16[16,7296]{1,0:T(8,128)(2,1)S(1)} %prepare.1), channel_id=1, source_target_pairs={{0,1},{1,0},{2,3},{3,2},{4,5},{5,4},{6,7},{7,6},{8,9},{9,8},{10,11... | collective-permute-start | bytes 700424 | tf_op jit(solution)/shard_map/ppermute | solution.py:37
  3.2 53.2 %collective-permute-start.9 = (bf16[7168,256]{1,0:T(8,128)(2,1)}, bf16[7168,256]{1,0:T(8,128)(2,1)}, u32[]{:S(2)}, u32[]{:S(2)}) collective-permute-start(bf16[7168,256]{1,0:T(8,128)(2,1)} %bitcast.8), channel_id=1, source_target_pairs={{0,1},{1,0},{2,3},{3,2},{4,5},{5,4},{6,7},{7,6},{8,9},{9,8},{10,11... | collective-permute-start | bytes 11010056 | tf_op jit(solution)/shard_map/ppermute | solution.py:37
  3.3 53.1 %collective-permute-start.10 = (bf16[7168,256]{1,0:T(8,128)(2,1)}, bf16[7168,256]{1,0:T(8,128)(2,1)}, u32[]{:S(2)}, u32[]{:S(2)}) collective-permute-start(bf16[7168,256]{1,0:T(8,128)(2,1)} %bitcast.10), channel_id=1, source_target_pairs={{0,1},{1,0},{2,3},{3,2},{4,5},{5,4},{6,7},{7,6},{8,9},{9,8},{10,11... | collective-permute-start | bytes 11010056 | tf_op jit(solution)/shard_map/ppermute | solution.py:37
  3.7 52.7 %collective-permute-start.11 = (bf16[256,7168]{1,0:T(8,128)(2,1)}, bf16[256,7168]{1,0:T(8,128)(2,1)}, u32[]{:S(2)}, u32[]{:S(2)}) collective-permute-start(bf16[256,7168]{1,0:T(8,128)(2,1)} %bitcast.12), channel_id=1, source_target_pairs={{0,1},{1,0},{2,3},{3,2},{4,5},{5,4},{6,7},{7,6},{8,9},{9,8},{10,11... | collective-permute-start | bytes 11010056 | tf_op jit(solution)/shard_map/ppermute | solution.py:37
  4.3 9.5 %collective-permute-start.2 = (bf16[32,7296]{1,0:T(8,128)(2,1)S(1)}, bf16[32,7296]{1,0:T(8,128)(2,1)S(1)}, u32[]{:S(2)}, u32[]{:S(2)}) collective-permute-start(bf16[32,7296]{1,0:T(8,128)(2,1)S(1)} %pad_maximum_fusion), channel_id=1, source_target_pairs={{0,2},{2,0},{4,6},{6,4},{8,10},{10,8},{12,14},{14,12},{16,18},{18,... | collective-permute-start | bytes 1400840 | tf_op jit(solution)/shard_map/ppermute | solution.py:33
  7.3 13.3 %collective-permute-start.1 = (bf16[32,7296]{1,0:T(8,128)(2,1)S(1)}, bf16[32,7296]{1,0:T(8,128)(2,1)S(1)}, u32[]{:S(2)}, u32[]{:S(2)}) collective-permute-start(bf16[32,7296]{1,0:T(8,128)(2,1)S(1)} %pad_maximum_fusion), channel_id=1, source_target_pairs={{0,8},{2,10},{4,12},{6,14},{8,0},{10,2},{12,4},{14,6},{16,24},{18,... | collective-permute-start | bytes 1400840 | tf_op jit(solution)/shard_map/ppermute | solution.py:33
  13.8 12.7 %collective-permute-start.5 = (bf16[32,7296]{1,0:T(8,128)(2,1)S(1)}, bf16[32,7296]{1,0:T(8,128)(2,1)S(1)}, u32[]{:S(2)}, u32[]{:S(2)}) collective-permute-start(bf16[32,7296]{1,0:T(8,128)(2,1)S(1)} %collective-permute-done.2.refs_1_), channel_id=1, source_target_pairs={{0,4},{2,6},{4,0},{6,2},{8,12},{10,14},{12,8},{14,10},{16,20},{18,... | collective-permute-start | bytes 1400840 | tf_op jit(solution)/shard_map/ppermute | solution.py:33
  20.5 13.5 %collective-permute-start.3 = (bf16[32,7296]{1,0:T(8,128)(2,1)S(1)}, bf16[32,7296]{1,0:T(8,128)(2,1)S(1)}, u32[]{:S(2)}, u32[]{:S(2)}) collective-permute-start(bf16[32,7296]{1,0:T(8,128)(2,1)S(1)} %collective-permute-done.1.refs_0_), channel_id=1, source_target_pairs={{0,2},{2,0},{4,6},{6,4},{8,10},{10,8},{12,14},{14,12},{16,18},{18,... | collective-permute-start | bytes 1400840 | tf_op jit(solution)/shard_map/ppermute | solution.py:33
  26.5 10.4 %collective-permute-start.4 = (bf16[32,7296]{1,0:T(8,128)(2,1)S(1)}, bf16[32,7296]{1,0:T(8,128)(2,1)S(1)}, u32[]{:S(2)}, u32[]{:S(2)}) collective-permute-start(bf16[32,7296]{1,0:T(8,128)(2,1)S(1)} %collective-permute-done.1.refs_0_), channel_id=1, source_target_pairs={{0,4},{2,6},{4,0},{6,2},{8,12},{10,14},{12,8},{14,10},{16,20},{18,... | collective-permute-start | bytes 1400840 | tf_op jit(solution)/shard_map/ppermute | solution.py:33
  34.1 13.8 %collective-permute-start.6 = (bf16[32,7296]{1,0:T(8,128)(2,1)S(1)}, bf16[32,7296]{1,0:T(8,128)(2,1)S(1)}, u32[]{:S(2)}, u32[]{:S(2)}) collective-permute-start(bf16[32,7296]{1,0:T(8,128)(2,1)S(1)} %collective-permute-done.3.refs_2_), channel_id=1, source_target_pairs={{0,16},{2,18},{4,20},{6,22},{8,24},{10,26},{12,28},{14,30},{16,0},... | collective-permute-start | bytes 1400840 | tf_op jit(solution)/shard_map/ppermute | solution.py:33
  36.9 11.7 %collective-permute-start.7 = (bf16[32,7296]{1,0:T(8,128)(2,1)S(1)}, bf16[32,7296]{1,0:T(8,128)(2,1)S(1)}, u32[]{:S(2)}, u32[]{:S(2)}) collective-permute-start(bf16[32,7296]{1,0:T(8,128)(2,1)S(1)} %collective-permute-done.3.refs_2_), channel_id=1, source_target_pairs={{0,4},{2,6},{4,0},{6,2},{8,12},{10,14},{12,8},{14,10},{16,20},{18,... | collective-permute-start | bytes 1400840 | tf_op jit(solution)/shard_map/ppermute | solution.py:33
  47.8 8.6 %collective-permute-start.8 = (bf16[32,7296]{1,0:T(8,128)(2,1)S(1)}, bf16[32,7296]{1,0:T(8,128)(2,1)S(1)}, u32[]{:S(2)}, u32[]{:S(2)}) collective-permute-start(bf16[32,7296]{1,0:T(8,128)(2,1)S(1)} %collective-permute-done.6.refs_5_), channel_id=1, source_target_pairs={{0,2},{2,0},{4,6},{6,4},{8,10},{10,8},{12,14},{14,12},{16,18},{18,... | collective-permute-start | bytes 1400840 | tf_op jit(solution)/shard_map/ppermute | solution.py:33
  71.2 13.1 %collective-permute-start.16 = (bf16[32,7168]{1,0:T(8,128)(2,1)S(1)}, bf16[32,7168]{1,0:T(8,128)(2,1)S(1)}, u32[]{:S(2)}, u32[]{:S(2)}) collective-permute-start(bf16[32,7168]{1,0:T(8,128)(2,1)S(1)} %get-tuple-element.20), channel_id=1, source_target_pairs={{0,2},{2,0},{4,6},{6,4},{8,10},{10,8},{12,14},{14,12},{16,18},{18,... | collective-permute-start | bytes 1376264 | tf_op jit(solution)/shard_map/ppermute | solution.py:33
  71.9 18.9 %collective-permute-start.15 = (bf16[32,7168]{1,0:T(8,128)(2,1)S(1)}, bf16[32,7168]{1,0:T(8,128)(2,1)S(1)}, u32[]{:S(2)}, u32[]{:S(2)}) collective-permute-start(bf16[32,7168]{1,0:T(8,128)(2,1)S(1)} %get-tuple-element.18), channel_id=1, source_target_pairs={{0,4},{2,6},{4,0},{6,2},{8,12},{10,14},{12,8},{14,10},{16,20},{18,... | collective-permute-start | bytes 1376264 | tf_op jit(solution)/shard_map/ppermute | solution.py:33
  84.5 14.4 %collective-permute-start.17 = (bf16[32,7168]{1,0:T(8,128)(2,1)S(1)}, bf16[32,7168]{1,0:T(8,128)(2,1)S(1)}, u32[]{:S(2)}, u32[]{:S(2)}) collective-permute-start(bf16[32,7168]{1,0:T(8,128)(2,1)S(1)} %add_convert_fusion.2), channel_id=1, source_target_pairs={{0,16},{2,18},{4,20},{6,22},{8,24},{10,26},{12,28},{14,30},{16,0},... | collective-permute-start | bytes 1376264 | tf_op jit(solution)/shard_map/ppermute | solution.py:33
  86.9 20.9 %collective-permute-start.14 = (bf16[32,7168]{1,0:T(8,128)(2,1)S(1)}, bf16[32,7168]{1,0:T(8,128)(2,1)S(1)}, u32[]{:S(2)}, u32[]{:S(2)}) collective-permute-start(bf16[32,7168]{1,0:T(8,128)(2,1)S(1)} %get-tuple-element.16), channel_id=1, source_target_pairs={{0,4},{2,6},{4,0},{6,2},{8,12},{10,14},{12,8},{14,10},{16,20},{18,... | collective-permute-start | bytes 1376264 | tf_op jit(solution)/shard_map/ppermute | solution.py:33
  88.5 18.5 %collective-permute-start.12 = (bf16[32,7168]{1,0:T(8,128)(2,1)S(1)}, bf16[32,7168]{1,0:T(8,128)(2,1)S(1)}, u32[]{:S(2)}, u32[]{:S(2)}) collective-permute-start(bf16[32,7168]{1,0:T(8,128)(2,1)S(1)} %get-tuple-element.13), channel_id=1, source_target_pairs={{0,4},{2,6},{4,0},{6,2},{8,12},{10,14},{12,8},{14,10},{16,20},{18,... | collective-permute-start | bytes 1376264 | tf_op jit(solution)/shard_map/ppermute | solution.py:33
  99.0 8.8 %collective-permute-start.18 = (bf16[32,7168]{1,0:T(8,128)(2,1)S(1)}, bf16[32,7168]{1,0:T(8,128)(2,1)S(1)}, u32[]{:S(2)}, u32[]{:S(2)}) collective-permute-start(bf16[32,7168]{1,0:T(8,128)(2,1)S(1)} %add_convert_fusion.1), channel_id=1, source_target_pairs={{0,2},{2,0},{4,6},{6,4},{8,10},{10,8},{12,14},{14,12},{16,18},{18,... | collective-permute-start | bytes 1376264 | tf_op jit(solution)/shard_map/ppermute | solution.py:33
  107.1 8.5 %collective-permute-start.13 = (bf16[32,7168]{1,0:T(8,128)(2,1)S(1)}, bf16[32,7168]{1,0:T(8,128)(2,1)S(1)}, u32[]{:S(2)}, u32[]{:S(2)}) collective-permute-start(bf16[32,7168]{1,0:T(8,128)(2,1)S(1)} %add_convert_fusion.3), channel_id=1, source_target_pairs={{0,2},{2,0},{4,6},{6,4},{8,10},{10,8},{12,14},{14,12},{16,18},{18,... | collective-permute-start | bytes 1376264 | tf_op jit(solution)/shard_map/ppermute | solution.py:33
  107.9 8.7 %collective-permute-start.19 = (bf16[32,7168]{1,0:T(8,128)(2,1)S(1)}, bf16[32,7168]{1,0:T(8,128)(2,1)S(1)}, u32[]{:S(2)}, u32[]{:S(2)}) collective-permute-start(bf16[32,7168]{1,0:T(8,128)(2,1)S(1)} %add_convert_fusion), channel_id=1, source_target_pairs={{0,8},{2,10},{4,12},{6,14},{8,0},{10,2},{12,4},{14,6},{16,24},{18,... | collective-permute-start | bytes 1376264 | tf_op jit(solution)/shard_map/ppermute | solution.py:33
  116.9 1.6 %collective-permute-start.20 = (bf16[16,7168]{1,0:T(8,128)(2,1)S(1)}, bf16[16,7168]{1,0:T(8,128)(2,1)S(1)}, u32[]{:S(2)}, u32[]{:S(2)}) collective-permute-start(bf16[16,7168]{1,0:T(8,128)(2,1)S(1)} %slice.15), channel_id=1, source_target_pairs={{0,1},{1,0},{2,3},{3,2},{4,5},{5,4},{6,7},{7,6},{8,9},{9,8},{10,11... | collective-permute-start | bytes 688136 | tf_op jit(solution)/shard_map/ppermute | solution.py:37

commit v5 on v4

--- a/solution.py
+++ b/solution.py
@@ -15,22 +15,31 @@
 PREPARE_VMEM = 4 * 1024 * 1024
 EXPERTS_VMEM = 44 * 1024 * 1024
 
-PLAN_16 = ((0, 4, 8), (0, 1, 2), (1, 1, 2), (1, 2, 1), (2, 2, 0), (3, 8, 1), (3, 2, 4), (6, 1, 4))
+PLAN_16 = ((0, 4, 8), (0, 2, 1), (1, 2, 1), (1, 8, 2), (3, 1, 4), (1, 1, 0), (4, 2, 1), (5, 4, 2))
+RETURN_16 = (6, 8, 7, 5, 4, 3, 1, 2)
+OPEN_16 = (2, 2, 2, 2, 2, 3, 4, 4)
+WEIGHTS_END_16 = {6: 0, 7: 1}
+OPEN_RETURN = 4
 
 
 def plan_for(ep_count, grp_count):
     if ep_count == 16 and grp_count == 2:
-        return PLAN_16, True
+        return PLAN_16, RETURN_16, OPEN_16, WEIGHTS_END_16, True
     plan = []
     for r in range(1, ep_count):
         bit = 1 << (r.bit_length() - 1)
         plan.append((r ^ bit, bit, bit))
-    return tuple(plan), False
+    slots = len(plan)
+    return tuple(plan), tuple(range(slots, 0, -1)), (OPEN_RETURN,) * slots, {}, False
 
 
 def across(value, bits, ep_count):
     pairs = [(i * 2 + c, (i ^ bit) * 2 + c) for c, bit in enumerate(bits) if bit for i in range(ep_count)]
     return lax.ppermute(value, ("ep", "grp"), pairs)
+
+
+def after(value, earlier):
+    return lax.optimization_barrier((value, *earlier))[0] if earlier else value
 
 
 def between_cores(value):
@@ -43,12 +52,19 @@
     square_mean = jnp.mean(values * values, axis=1, keepdims=True)
     normed = values * lax.rsqrt(square_mean + EPSILON) * gain_ref[...]
     out_ref[:, :width] = normed.astype(jnp.bfloat16)
+    rows = values.shape[0]
     routes = routes_ref[...]
-    lanes = lax.broadcasted_iota(jnp.int32, (values.shape[0], LANES), 1)
-    named = jnp.zeros((values.shape[0], LANES), jnp.float32)
-    for k in range(routes.shape[1]):
-        named = jnp.where(lanes == routes[:, k : k + 1], 1.0, named)
-    out_ref[:, width:] = named.astype(jnp.bfloat16)
+    experts_down = lax.broadcasted_iota(jnp.int32, (LANES, rows), 0)
+    named = jnp.zeros((LANES, rows), jnp.float32)
+    for k in range(routes.shape[0]):
+        named = jnp.where(experts_down == routes[k : k + 1, :], 1.0, named)
+    same = lax.broadcasted_iota(jnp.int32, (rows, rows), 0) == lax.broadcasted_iota(jnp.int32, (rows, rows), 1)
+    out_ref[:, width:] = lax.dot_general(
+        same.astype(jnp.bfloat16),
+        named.astype(jnp.bfloat16),
+        (((1,), (1,)), ((), ())),
+        preferred_element_type=jnp.float32,
+    ).astype(jnp.bfloat16)
 
 
 def prepare(hidden, gain, routes):
@@ -59,7 +75,7 @@
         compiler_params=pltpu.CompilerParams(vmem_limit_bytes=PREPARE_VMEM),
         cost_estimate=pl.CostEstimate(flops=6 * rows * width, bytes_accessed=4 * rows * width, transcendentals=rows),
         name="prepare",
-    )(hidden, gain[None, :], routes)
+    )(hidden, gain[None, :], routes.T)
 
 
 def experts_kernel(blocks, k_steps, k_tile, ids_ref, *refs):
@@ -172,16 +188,19 @@
     local_experts = ep_count // SPLIT
     expert_count = local_experts * grp_count
     place, core = lax.axis_index("ep") // SPLIT, lax.axis_index("grp")
-    plan, paired = plan_for(ep_count, grp_count)
+    plan, return_order, most_open, weights_end, paired = plan_for(ep_count, grp_count)
     rows = hidden.shape[0]
-    gates, ups, downs = ((w[0, 0], between_cores(w[0, 0])) for w in (w_gate, w_up, w_down))
+    weights = [(w[0, 0], between_cores(w[0, 0])) for w in (w_gate, w_up, w_down)]
 
     own = prepare(hidden, gain, routes)
     if paired:
         own = jnp.concatenate([own, between_cores(own)], axis=0)
     held = [own]
-    for parent, *bits in plan:
-        held.append(across(held[parent], bits, ep_count))
+    for slot, (parent, *bits) in enumerate(plan, 1):
+        ended = held[1 : slot + 1 - most_open[slot - 1]]
+        if slot in weights_end:
+            ended.append(weights[weights_end[slot]][1])
+        held.append(across(after(held[parent], ended), bits, ep_count))
     first = 0
     if paired:
         first = 1
@@ -190,7 +209,7 @@
 
     ids = jnp.stack([core * local_experts + place, (1 - core) * local_experts + place]).astype(jnp.int32)
     router_t = jnp.pad(router_w.T, ((0, -expert_count % 16), (0, 0)))
-    parts = experts(ids, held[first:], router_t, gates, ups, downs)
+    parts = experts(ids, held[first:], router_t, *weights)
 
     terms = [[] for _ in range(first)] + [[part] for part in parts]
     if paired:
@@ -199,9 +218,12 @@
     def summed(slot):
         return sum(term.astype(jnp.float32) for term in terms[slot])
 
-    for slot in range(len(plan), 0, -1):
+    returned = []
+    for slot in return_order:
         parent, *bits = plan[slot - 1]
-        terms[parent].append(across(summed(slot).astype(jnp.bfloat16), bits, ep_count))
+        value = after(summed(slot).astype(jnp.bfloat16), returned[: max(0, len(returned) + 1 - OPEN_RETURN)])
+        returned.append(across(value, bits, ep_count))
+        terms[parent].append(returned[-1])
     total = summed(0)
     if paired:
         arrived = between_cores(total[rows:].astype(jnp.bfloat16))

time: 120 us -> 114 us (0.950)
  waiting for transfers between devices: 71.8 us -> 63.8 us
  starting transfers between devices: 27.2 us -> 29.2 us
    ppermute x16, waiting for transfers between devices: 69.8 us -> 58.9 us  [across(): return lax.ppermute(value, ('ep', 'grp'), pairs)]
    ppermute x5, waiting for transfers between devices: 2.01 us -> 4.92 us  [between_cores(): return lax.ppermute(value, 'grp', [(0, 1), (1, 0)])]
    ppermute x16, starting transfers between devices: 26 us -> 28 us  [across(): return lax.ppermute(value, ('ep', 'grp'), pairs)]
    unnamed x5 -> x6, local copies, waits for them, and re-layouts: 2.44 us -> 2.37 us
  transfers between devices with their start and end apart: 21 -> 21, of which waited for: 13 -> 15; matrix products, arithmetic and copies ran while one was open for 1% -> 2% of each run, Pallas kernels for 0% -> 0%
where the time goes in v5:
time: 114 us; the launch traced here: 113 us
  waiting for transfers between devices  63.8 us (56%)
  starting transfers between devices  29.2 us (26%)
  Pallas kernels  15 us (13%)
  local copies, waits for them, and re-layouts  3.31 us (3%)
  other arithmetic  1.73 us (2%)
    ppermute x16, waiting for transfers between devices, across(): return lax.ppermute(value, ('ep', 'grp'), pairs)  58.9 us
    ppermute x16, starting transfers between devices, across(): return lax.ppermute(value, ('ep', 'grp'), pairs)  28 us
    pallas_call x1, Pallas kernels, experts(): pl.pallas_call(functools.partial(experts_kernel, blocks, k_steps, k_tile)...  14.8 us
    ppermute x5, waiting for transfers between devices, between_cores(): return lax.ppermute(value, 'grp', [(0, 1), (1, 0)])  4.92 us
    unnamed x6, local copies, waits for them, and re-layouts  2.37 us
  transfers between devices with their start and end apart: 21, of which 15 were waited for; matrix products, arithmetic and copies ran while one was open for 2% of the time, Pallas kernels for 0%

profile of v5, /device:TPU:0, one launch (start us, length us, event | category | flops | bytes accessed | tf_op | source)
XLA Modules:
  0.0 113.2 jit_solution(607398719294051588)
XLA Ops:
  3.7 3.4 %collective-permute-done = bf16[16,7296]{1,0:T(8,128)(2,1)S(1)} collective-permute-done((bf16[16,7296]{1,0:T(8,128)(2,1)S(1)}, bf16[16,7296]{1,0:T(8,128)(2,1)S(1)}, u32[]{:S(2)}, u32[]{:S(2)}) %collective-permute-start) | collective-permute-done | bytes 233504 | tf_op jit(solution)/shard_map/ppermute | solution.py:46
  7.2 3.0 %collective-permute-start.1 = (bf16[32,7296]{1,0:T(8,128)(2,1)S(1)}, bf16[32,7296]{1,0:T(8,128)(2,1)S(1)}, u32[]{:S(2)}, u32[]{:S(2)}) collective-permute-start(bf16[32,7296]{1,0:T(8,128)(2,1)S(1)} %pad_maximum_fusion), channel_id=1, source_target_pairs={{0,8},{2,10},{4,12},{6,14},{8,0},{10,2},{12,4},{14,6},{16,24},{18,... | collective-permute-start | bytes 1400840 | tf_op jit(solution)/shard_map/ppermute | solution.py:38
  10.2 1.5 %collective-permute-start.2 = (bf16[32,7296]{1,0:T(8,128)(2,1)S(1)}, bf16[32,7296]{1,0:T(8,128)(2,1)S(1)}, u32[]{:S(2)}, u32[]{:S(2)}) collective-permute-start(bf16[32,7296]{1,0:T(8,128)(2,1)S(1)} %pad_maximum_fusion), channel_id=1, source_target_pairs={{0,4},{2,6},{4,0},{6,2},{8,12},{10,14},{12,8},{14,10},{16,20},{18,... | collective-permute-start | bytes 1400840 | tf_op jit(solution)/shard_map/ppermute | solution.py:38
  11.7 9.6 %collective-permute-done.1.refs_0_ = bf16[32,7296]{1,0:T(8,128)(2,1)S(1)} collective-permute-done((bf16[32,7296]{1,0:T(8,128)(2,1)S(1)}, bf16[32,7296]{1,0:T(8,128)(2,1)S(1)}, u32[]{:S(2)}, u32[]{:S(2)}) %collective-permute-start.1) | collective-permute-done | bytes 466976 | tf_op jit(solution)/shard_map/ppermute | solution.py:38
  21.3 2.3 %collective-permute-start.3 = (bf16[32,7296]{1,0:T(8,128)(2,1)S(1)}, bf16[32,7296]{1,0:T(8,128)(2,1)S(1)}, u32[]{:S(2)}, u32[]{:S(2)}) collective-permute-start(bf16[32,7296]{1,0:T(8,128)(2,1)S(1)} %collective-permute-done.1.refs_0_), channel_id=1, source_target_pairs={{0,4},{2,6},{4,0},{6,2},{8,12},{10,14},{12,8},{14,10},{16,20},{18,... | collective-permute-start | bytes 1400840 | tf_op jit(solution)/shard_map/ppermute | solution.py:38
  23.7 1.7 %collective-permute-start.4 = (bf16[32,7296]{1,0:T(8,128)(2,1)S(1)}, bf16[32,7296]{1,0:T(8,128)(2,1)S(1)}, u32[]{:S(2)}, u32[]{:S(2)}) collective-permute-start(bf16[32,7296]{1,0:T(8,128)(2,1)S(1)} %collective-permute-done.1.refs_0_), channel_id=1, source_target_pairs={{0,16},{2,18},{4,20},{6,22},{8,24},{10,26},{12,28},{14,30},{16,0},... | collective-permute-start | bytes 1400840 | tf_op jit(solution)/shard_map/ppermute | solution.py:38
  25.4 9.2 %collective-permute-done.3.refs_2_ = bf16[32,7296]{1,0:T(8,128)(2,1)S(1)} collective-permute-done((bf16[32,7296]{1,0:T(8,128)(2,1)S(1)}, bf16[32,7296]{1,0:T(8,128)(2,1)S(1)}, u32[]{:S(2)}, u32[]{:S(2)}) %collective-permute-start.3) | collective-permute-done | bytes 466976 | tf_op jit(solution)/shard_map/ppermute | solution.py:38
  34.5 1.8 %collective-permute-start.5 = (bf16[32,7296]{1,0:T(8,128)(2,1)S(1)}, bf16[32,7296]{1,0:T(8,128)(2,1)S(1)}, u32[]{:S(2)}, u32[]{:S(2)}) collective-permute-start(bf16[32,7296]{1,0:T(8,128)(2,1)S(1)} %collective-permute-done.3.refs_2_), channel_id=1, source_target_pairs={{0,2},{2,0},{4,6},{6,4},{8,10},{10,8},{12,14},{14,12},{16,18},{18,... | collective-permute-start | bytes 1400840 | tf_op jit(solution)/shard_map/ppermute | solution.py:38
  36.3 2.1 %collective-permute-start.7 = (bf16[32,7296]{1,0:T(8,128)(2,1)S(1)}, bf16[32,7296]{1,0:T(8,128)(2,1)S(1)}, u32[]{:S(2)}, u32[]{:S(2)}) collective-permute-start(bf16[32,7296]{1,0:T(8,128)(2,1)S(1)} %collective-permute-done.1.refs_0_), channel_id=1, source_target_pairs={{0,2},{2,0},{4,6},{6,4},{8,10},{10,8},{12,14},{14,12},{16,18},{18,... | collective-permute-start | bytes 1400840 | tf_op jit(solution)/shard_map/ppermute | solution.py:38
  39.5 3.6 %collective-permute-done.5.refs_4_ = bf16[32,7296]{1,0:T(8,128)(2,1)S(1)} collective-permute-done((bf16[32,7296]{1,0:T(8,128)(2,1)S(1)}, bf16[32,7296]{1,0:T(8,128)(2,1)S(1)}, u32[]{:S(2)}, u32[]{:S(2)}) %collective-permute-start.5) | collective-permute-done | bytes 466976 | tf_op jit(solution)/shard_map/ppermute | solution.py:38
  43.1 2.8 %collective-permute-start.10 = (bf16[32,7296]{1,0:T(8,128)(2,1)S(1)}, bf16[32,7296]{1,0:T(8,128)(2,1)S(1)}, u32[]{:S(2)}, u32[]{:S(2)}) collective-permute-start(bf16[32,7296]{1,0:T(8,128)(2,1)S(1)} %collective-permute-done.5.refs_4_), channel_id=1, source_target_pairs={{0,8},{2,10},{4,12},{6,14},{8,0},{10,2},{12,4},{14,6},{16,24},{18,... | collective-permute-start | bytes 1400840 | tf_op jit(solution)/shard_map/ppermute | solution.py:38
  45.9 2.4 %collective-permute-start.9 = (bf16[32,7296]{1,0:T(8,128)(2,1)S(1)}, bf16[32,7296]{1,0:T(8,128)(2,1)S(1)}, u32[]{:S(2)}, u32[]{:S(2)}) collective-permute-start(bf16[32,7296]{1,0:T(8,128)(2,1)S(1)} %collective-permute-done.4.refs_3_), channel_id=1, source_target_pairs={{0,4},{2,6},{4,0},{6,2},{8,12},{10,14},{12,8},{14,10},{16,20},{18,... | collective-permute-start | bytes 1400840 | tf_op jit(solution)/shard_map/ppermute | solution.py:38
  48.3 2.8 %collective-permute-done.7 = bf16[32,7296]{1,0:T(8,128)(2,1)S(1)} collective-permute-done((bf16[32,7296]{1,0:T(8,128)(2,1)S(1)}, bf16[32,7296]{1,0:T(8,128)(2,1)S(1)}, u32[]{:S(2)}, u32[]{:S(2)}) %collective-permute-start.7) | collective-permute-done | bytes 466976 | tf_op jit(solution)/shard_map/ppermute | solution.py:38
  52.5 2.4 %collective-permute-done.9.refs_6_ = bf16[32,7296]{1,0:T(8,128)(2,1)S(1)} collective-permute-done((bf16[32,7296]{1,0:T(8,128)(2,1)S(1)}, bf16[32,7296]{1,0:T(8,128)(2,1)S(1)}, u32[]{:S(2)}, u32[]{:S(2)}) %collective-permute-start.9) | collective-permute-done | bytes 466976 | tf_op jit(solution)/shard_map/ppermute | solution.py:38
  54.9 14.8 %experts.1 = (bf16[32,7168]{1,0:T(8,128)(2,1)S(1)}, bf16[32,7168]{1,0:T(8,128)(2,1)S(1)}, bf16[32,7168]{1,0:T(8,128)(2,1)S(1)}, bf16[32,7168]{1,0:T(8,128)(2,1)S...) custom-call(s32[2]{0:T(128)S(1)} %pad_add_fusion.ids_ref, ...), custom_call_target="tpu_custom_call" | custom-call | flops 5637144576 | bytes 29360128 | tf_op jit(solution)/shard_map/experts/pallas_call | solution.py:161
  70.3 1.5 %collective-permute-start.13 = (bf16[32,7168]{1,0:T(8,128)(2,1)S(1)}, bf16[32,7168]{1,0:T(8,128)(2,1)S(1)}, u32[]{:S(2)}, u32[]{:S(2)}) collective-permute-start(bf16[32,7168]{1,0:T(8,128)(2,1)S(1)} %get-tuple-element.32), channel_id=1, source_target_pairs={{0,4},{2,6},{4,0},{6,2},{8,12},{10,14},{12,8},{14,10},{16,20},{18,... | collective-permute-start | bytes 1376264 | tf_op jit(solution)/shard_map/ppermute | solution.py:38
  71.8 2.4 %collective-permute-start.12 = (bf16[32,7168]{1,0:T(8,128)(2,1)S(1)}, bf16[32,7168]{1,0:T(8,128)(2,1)S(1)}, u32[]{:S(2)}, u32[]{:S(2)}) collective-permute-start(bf16[32,7168]{1,0:T(8,128)(2,1)S(1)} %get-tuple-element.29), channel_id=1, source_target_pairs={{0,2},{2,0},{4,6},{6,4},{8,10},{10,8},{12,14},{14,12},{16,18},{18,... | collective-permute-start | bytes 1376264 | tf_op jit(solution)/shard_map/ppermute | solution.py:38
  74.3 3.9 %collective-permute-done.15 = bf16[32,7168]{1,0:T(8,128)(2,1)S(1)} collective-permute-done((bf16[32,7168]{1,0:T(8,128)(2,1)S(1)}, bf16[32,7168]{1,0:T(8,128)(2,1)S(1)}, u32[]{:S(2)}, u32[]{:S(2)}) %collective-permute-start.15) | collective-permute-done | bytes 458784 | tf_op jit(solution)/shard_map/ppermute | solution.py:38
  79.1 2.1 %collective-permute-done.13 = bf16[32,7168]{1,0:T(8,128)(2,1)S(1)} collective-permute-done((bf16[32,7168]{1,0:T(8,128)(2,1)S(1)}, bf16[32,7168]{1,0:T(8,128)(2,1)S(1)}, u32[]{:S(2)}, u32[]{:S(2)}) %collective-permute-start.13) | collective-permute-done | bytes 458784 | tf_op jit(solution)/shard_map/ppermute | solution.py:38
  82.7 2.0 %collective-permute-start.14 = (bf16[32,7168]{1,0:T(8,128)(2,1)S(1)}, bf16[32,7168]{1,0:T(8,128)(2,1)S(1)}, u32[]{:S(2)}, u32[]{:S(2)}) collective-permute-start(bf16[32,7168]{1,0:T(8,128)(2,1)S(1)} %add_convert_fusion.3), channel_id=1, source_target_pairs={{0,16},{2,18},{4,20},{6,22},{8,24},{10,26},{12,28},{14,30},{16,0},... | collective-permute-start | bytes 1376264 | tf_op jit(solution)/shard_map/ppermute | solution.py:38
  84.7 2.9 %collective-permute-done.16 = bf16[32,7168]{1,0:T(8,128)(2,1)S(1)} collective-permute-done((bf16[32,7168]{1,0:T(8,128)(2,1)S(1)}, bf16[32,7168]{1,0:T(8,128)(2,1)S(1)}, u32[]{:S(2)}, u32[]{:S(2)}) %collective-permute-start.16) | collective-permute-done | bytes 458784 | tf_op jit(solution)/shard_map/ppermute | solution.py:38
  89.8 7.2 %collective-permute-done.14 = bf16[32,7168]{1,0:T(8,128)(2,1)S(1)} collective-permute-done((bf16[32,7168]{1,0:T(8,128)(2,1)S(1)}, bf16[32,7168]{1,0:T(8,128)(2,1)S(1)}, u32[]{:S(2)}, u32[]{:S(2)}) %collective-permute-start.14) | collective-permute-done | bytes 458784 | tf_op jit(solution)/shard_map/ppermute | solution.py:38
  98.0 3.2 %collective-permute-done.19 = bf16[32,7168]{1,0:T(8,128)(2,1)S(1)} collective-permute-done((bf16[32,7168]{1,0:T(8,128)(2,1)S(1)}, bf16[32,7168]{1,0:T(8,128)(2,1)S(1)}, u32[]{:S(2)}, u32[]{:S(2)}) %collective-permute-start.19) | collective-permute-done | bytes 458784 | tf_op jit(solution)/shard_map/ppermute | solution.py:38
  101.2 9.4 %collective-permute-done.18 = bf16[32,7168]{1,0:T(8,128)(2,1)S(1)} collective-permute-done((bf16[32,7168]{1,0:T(8,128)(2,1)S(1)}, bf16[32,7168]{1,0:T(8,128)(2,1)S(1)}, u32[]{:S(2)}, u32[]{:S(2)}) %collective-permute-start.18) | collective-permute-done | bytes 458784 | tf_op jit(solution)/shard_map/ppermute | solution.py:38
  (37 shorter events, 14.9 us)
Async XLA Ops:
  0.0 36.3 %collective-permute-start.6 = (bf16[7168,256]{1,0:T(8,128)(2,1)}, bf16[7168,256]{1,0:T(8,128)(2,1)}, u32[]{:S(2)}, u32[]{:S(2)}) collective-permute-start(bf16[7168,256]{1,0:T(8,128)(2,1)} %bitcast.10), channel_id=1, source_target_pairs={{0,1},{1,0},{2,3},{3,2},{4,5},{5,4},{6,7},{7,6},{8,9},{9,8},{10,11... | collective-permute-start | bytes 11010056 | tf_op jit(solution)/shard_map/ppermute | solution.py:46
  0.5 45.5 %collective-permute-start.8 = (bf16[7168,256]{1,0:T(8,128)(2,1)}, bf16[7168,256]{1,0:T(8,128)(2,1)}, u32[]{:S(2)}, u32[]{:S(2)}) collective-permute-start(bf16[7168,256]{1,0:T(8,128)(2,1)} %bitcast.12), channel_id=1, source_target_pairs={{0,1},{1,0},{2,3},{3,2},{4,5},{5,4},{6,7},{7,6},{8,9},{9,8},{10,11... | collective-permute-start | bytes 11010056 | tf_op jit(solution)/shard_map/ppermute | solution.py:46
  0.5 0.9 copy-start
  1.5 0.7 copy-start.1
  2.2 0.7 copy-start.2
  3.1 4.0 %collective-permute-start = (bf16[16,7296]{1,0:T(8,128)(2,1)S(1)}, bf16[16,7296]{1,0:T(8,128)(2,1)S(1)}, u32[]{:S(2)}, u32[]{:S(2)}) collective-permute-start(bf16[16,7296]{1,0:T(8,128)(2,1)S(1)} %prepare.1), channel_id=1, source_target_pairs={{0,1},{1,0},{2,3},{3,2},{4,5},{5,4},{6,7},{7,6},{8,9},{9,8},{10,11... | collective-permute-start | bytes 700424 | tf_op jit(solution)/shard_map/ppermute | solution.py:46
  3.6 48.8 %collective-permute-start.11 = (bf16[256,7168]{1,0:T(8,128)(2,1)}, bf16[256,7168]{1,0:T(8,128)(2,1)}, u32[]{:S(2)}, u32[]{:S(2)}) collective-permute-start(bf16[256,7168]{1,0:T(8,128)(2,1)} %bitcast.14), channel_id=1, source_target_pairs={{0,1},{1,0},{2,3},{3,2},{4,5},{5,4},{6,7},{7,6},{8,9},{9,8},{10,11... | collective-permute-start | bytes 11010056 | tf_op jit(solution)/shard_map/ppermute | solution.py:46
  7.2 14.1 %collective-permute-start.1 = (bf16[32,7296]{1,0:T(8,128)(2,1)S(1)}, bf16[32,7296]{1,0:T(8,128)(2,1)S(1)}, u32[]{:S(2)}, u32[]{:S(2)}) collective-permute-start(bf16[32,7296]{1,0:T(8,128)(2,1)S(1)} %pad_maximum_fusion), channel_id=1, source_target_pairs={{0,8},{2,10},{4,12},{6,14},{8,0},{10,2},{12,4},{14,6},{16,24},{18,... | collective-permute-start | bytes 1400840 | tf_op jit(solution)/shard_map/ppermute | solution.py:38
  10.2 13.5 %collective-permute-start.2 = (bf16[32,7296]{1,0:T(8,128)(2,1)S(1)}, bf16[32,7296]{1,0:T(8,128)(2,1)S(1)}, u32[]{:S(2)}, u32[]{:S(2)}) collective-permute-start(bf16[32,7296]{1,0:T(8,128)(2,1)S(1)} %pad_maximum_fusion), channel_id=1, source_target_pairs={{0,4},{2,6},{4,0},{6,2},{8,12},{10,14},{12,8},{14,10},{16,20},{18,... | collective-permute-start | bytes 1400840 | tf_op jit(solution)/shard_map/ppermute | solution.py:38
  21.3 13.2 %collective-permute-start.3 = (bf16[32,7296]{1,0:T(8,128)(2,1)S(1)}, bf16[32,7296]{1,0:T(8,128)(2,1)S(1)}, u32[]{:S(2)}, u32[]{:S(2)}) collective-permute-start(bf16[32,7296]{1,0:T(8,128)(2,1)S(1)} %collective-permute-done.1.refs_0_), channel_id=1, source_target_pairs={{0,4},{2,6},{4,0},{6,2},{8,12},{10,14},{12,8},{14,10},{16,20},{18,... | collective-permute-start | bytes 1400840 | tf_op jit(solution)/shard_map/ppermute | solution.py:38
  23.7 15.8 %collective-permute-start.4 = (bf16[32,7296]{1,0:T(8,128)(2,1)S(1)}, bf16[32,7296]{1,0:T(8,128)(2,1)S(1)}, u32[]{:S(2)}, u32[]{:S(2)}) collective-permute-start(bf16[32,7296]{1,0:T(8,128)(2,1)S(1)} %collective-permute-done.1.refs_0_), channel_id=1, source_target_pairs={{0,16},{2,18},{4,20},{6,22},{8,24},{10,26},{12,28},{14,30},{16,0},... | collective-permute-start | bytes 1400840 | tf_op jit(solution)/shard_map/ppermute | solution.py:38
  34.5 8.6 %collective-permute-start.5 = (bf16[32,7296]{1,0:T(8,128)(2,1)S(1)}, bf16[32,7296]{1,0:T(8,128)(2,1)S(1)}, u32[]{:S(2)}, u32[]{:S(2)}) collective-permute-start(bf16[32,7296]{1,0:T(8,128)(2,1)S(1)} %collective-permute-done.3.refs_2_), channel_id=1, source_target_pairs={{0,2},{2,0},{4,6},{6,4},{8,10},{10,8},{12,14},{14,12},{16,18},{18,... | collective-permute-start | bytes 1400840 | tf_op jit(solution)/shard_map/ppermute | solution.py:38
  36.3 14.7 %collective-permute-start.7 = (bf16[32,7296]{1,0:T(8,128)(2,1)S(1)}, bf16[32,7296]{1,0:T(8,128)(2,1)S(1)}, u32[]{:S(2)}, u32[]{:S(2)}) collective-permute-start(bf16[32,7296]{1,0:T(8,128)(2,1)S(1)} %collective-permute-done.1.refs_0_), channel_id=1, source_target_pairs={{0,2},{2,0},{4,6},{6,4},{8,10},{10,8},{12,14},{14,12},{16,18},{18,... | collective-permute-start | bytes 1400840 | tf_op jit(solution)/shard_map/ppermute | solution.py:38
  43.1 9.4 %collective-permute-start.10 = (bf16[32,7296]{1,0:T(8,128)(2,1)S(1)}, bf16[32,7296]{1,0:T(8,128)(2,1)S(1)}, u32[]{:S(2)}, u32[]{:S(2)}) collective-permute-start(bf16[32,7296]{1,0:T(8,128)(2,1)S(1)} %collective-permute-done.5.refs_4_), channel_id=1, source_target_pairs={{0,8},{2,10},{4,12},{6,14},{8,0},{10,2},{12,4},{14,6},{16,24},{18,... | collective-permute-start | bytes 1400840 | tf_op jit(solution)/shard_map/ppermute | solution.py:38
  45.9 8.9 %collective-permute-start.9 = (bf16[32,7296]{1,0:T(8,128)(2,1)S(1)}, bf16[32,7296]{1,0:T(8,128)(2,1)S(1)}, u32[]{:S(2)}, u32[]{:S(2)}) collective-permute-start(bf16[32,7296]{1,0:T(8,128)(2,1)S(1)} %collective-permute-done.4.refs_3_), channel_id=1, source_target_pairs={{0,4},{2,6},{4,0},{6,2},{8,12},{10,14},{12,8},{14,10},{16,20},{18,... | collective-permute-start | bytes 1400840 | tf_op jit(solution)/shard_map/ppermute | solution.py:38
  69.6 8.5 %collective-permute-start.15 = (bf16[32,7168]{1,0:T(8,128)(2,1)S(1)}, bf16[32,7168]{1,0:T(8,128)(2,1)S(1)}, u32[]{:S(2)}, u32[]{:S(2)}) collective-permute-start(bf16[32,7168]{1,0:T(8,128)(2,1)S(1)} %get-tuple-element.36), channel_id=1, source_target_pairs={{0,8},{2,10},{4,12},{6,14},{8,0},{10,2},{12,4},{14,6},{16,24},{18,... | collective-permute-start | bytes 1376264 | tf_op jit(solution)/shard_map/ppermute | solution.py:38
  70.3 10.9 %collective-permute-start.13 = (bf16[32,7168]{1,0:T(8,128)(2,1)S(1)}, bf16[32,7168]{1,0:T(8,128)(2,1)S(1)}, u32[]{:S(2)}, u32[]{:S(2)}) collective-permute-start(bf16[32,7168]{1,0:T(8,128)(2,1)S(1)} %get-tuple-element.32), channel_id=1, source_target_pairs={{0,4},{2,6},{4,0},{6,2},{8,12},{10,14},{12,8},{14,10},{16,20},{18,... | collective-permute-start | bytes 1376264 | tf_op jit(solution)/shard_map/ppermute | solution.py:38
  71.8 10.9 %collective-permute-start.12 = (bf16[32,7168]{1,0:T(8,128)(2,1)S(1)}, bf16[32,7168]{1,0:T(8,128)(2,1)S(1)}, u32[]{:S(2)}, u32[]{:S(2)}) collective-permute-start(bf16[32,7168]{1,0:T(8,128)(2,1)S(1)} %get-tuple-element.29), channel_id=1, source_target_pairs={{0,2},{2,0},{4,6},{6,4},{8,10},{10,8},{12,14},{14,12},{16,18},{18,... | collective-permute-start | bytes 1376264 | tf_op jit(solution)/shard_map/ppermute | solution.py:38
  78.3 9.3 %collective-permute-start.16 = (bf16[32,7168]{1,0:T(8,128)(2,1)S(1)}, bf16[32,7168]{1,0:T(8,128)(2,1)S(1)}, u32[]{:S(2)}, u32[]{:S(2)}) collective-permute-start(bf16[32,7168]{1,0:T(8,128)(2,1)S(1)} %add_convert_fusion.2), channel_id=1, source_target_pairs={{0,2},{2,0},{4,6},{6,4},{8,10},{10,8},{12,14},{14,12},{16,18},{18,... | collective-permute-start | bytes 1376264 | tf_op jit(solution)/shard_map/ppermute | solution.py:38
  82.7 14.3 %collective-permute-start.14 = (bf16[32,7168]{1,0:T(8,128)(2,1)S(1)}, bf16[32,7168]{1,0:T(8,128)(2,1)S(1)}, u32[]{:S(2)}, u32[]{:S(2)}) collective-permute-start(bf16[32,7168]{1,0:T(8,128)(2,1)S(1)} %add_convert_fusion.3), channel_id=1, source_target_pairs={{0,16},{2,18},{4,20},{6,22},{8,24},{10,26},{12,28},{14,30},{16,0},... | collective-permute-start | bytes 1376264 | tf_op jit(solution)/shard_map/ppermute | solution.py:38
  87.8 9.3 %collective-permute-start.17 = (bf16[32,7168]{1,0:T(8,128)(2,1)S(1)}, bf16[32,7168]{1,0:T(8,128)(2,1)S(1)}, u32[]{:S(2)}, u32[]{:S(2)}) collective-permute-start(bf16[32,7168]{1,0:T(8,128)(2,1)S(1)} %add_convert_fusion.1), channel_id=1, source_target_pairs={{0,4},{2,6},{4,0},{6,2},{8,12},{10,14},{12,8},{14,10},{16,20},{18,... | collective-permute-start | bytes 1376264 | tf_op jit(solution)/shard_map/ppermute | solution.py:38
  89.1 12.1 %collective-permute-start.19 = (bf16[32,7168]{1,0:T(8,128)(2,1)S(1)}, bf16[32,7168]{1,0:T(8,128)(2,1)S(1)}, u32[]{:S(2)}, u32[]{:S(2)}) collective-permute-start(bf16[32,7168]{1,0:T(8,128)(2,1)S(1)} %get-tuple-element.40), channel_id=1, source_target_pairs={{0,4},{2,6},{4,0},{6,2},{8,12},{10,14},{12,8},{14,10},{16,20},{18,... | collective-permute-start | bytes 1376264 | tf_op jit(solution)/shard_map/ppermute | solution.py:38
  97.2 13.4 %collective-permute-start.18 = (bf16[32,7168]{1,0:T(8,128)(2,1)S(1)}, bf16[32,7168]{1,0:T(8,128)(2,1)S(1)}, u32[]{:S(2)}, u32[]{:S(2)}) collective-permute-start(bf16[32,7168]{1,0:T(8,128)(2,1)S(1)} %add_convert_fusion), channel_id=1, source_target_pairs={{0,8},{2,10},{4,12},{6,14},{8,0},{10,2},{12,4},{14,6},{16,24},{18,... | collective-permute-start | bytes 1376264 | tf_op jit(solution)/shard_map/ppermute | solution.py:38
  110.9 1.6 %collective-permute-start.20 = (bf16[16,7168]{1,0:T(8,128)(2,1)S(1)}, bf16[16,7168]{1,0:T(8,128)(2,1)S(1)}, u32[]{:S(2)}, u32[]{:S(2)}) collective-permute-start(bf16[16,7168]{1,0:T(8,128)(2,1)S(1)} %slice.15), channel_id=1, source_target_pairs={{0,1},{1,0},{2,3},{3,2},{4,5},{5,4},{6,7},{7,6},{8,9},{9,8},{10,11... | collective-permute-start | bytes 688136 | tf_op jit(solution)/shard_map/ppermute | solution.py:46

commit v6 on v5

v6 whole, which is shorter than its diff:
```python
import functools

import jax
import jax.numpy as jnp
from jax import lax
from jax.experimental import pallas as pl
from jax.experimental.pallas import tpu as pltpu
from jax.sharding import PartitionSpec as P

SPLIT = 4
LANES = 128

EPSILON = 1e-06
ROUTE_SCALE = 2.5
PREPARE_VMEM = 60 * 1024 * 1024
EXPERTS_VMEM = 44 * 1024 * 1024

PLAN_16 = ((0, 8, 2), (0, 4, 1), (1, 2, 1), (1, 1, 4), (4, 2, 8), (4, 4, 1), (5, 4, 2), (2, 1, 0))
RETURN_16 = (7, 8, 6, 5, 2, 4, 3, 1)
OPEN_16 = (2, 2, 2, 2, 2, 3, 4, 4)
WEIGHTS_END_16 = {6: 0, 7: 1}
OPEN_RETURN = 4


def plan_for(ep_count, grp_count):
    if ep_count == 16 and grp_count == 2:
        return PLAN_16, RETURN_16, OPEN_16, WEIGHTS_END_16, True
    plan = []
    for r in range(1, ep_count):
        bit = 1 << (r.bit_length() - 1)
        plan.append((r ^ bit, bit, bit))
    slots = len(plan)
    return tuple(plan), tuple(range(slots, 0, -1)), (OPEN_RETURN,) * slots, {}, False


def across(value, bits, ep_count):
    pairs = [(i * 2 + c, (i ^ bit) * 2 + c) for c, bit in enumerate(bits) if bit for i in range(ep_count)]
    return lax.ppermute(value, ("ep", "grp"), pairs)


def after(value, earlier):
    return lax.optimization_barrier((value, *earlier))[0] if earlier else value


def between_cores(value):
    return lax.ppermute(value, "grp", [(0, 1), (1, 0)])


def prepare_kernel(hidden_hbm, gain_hbm, routes_hbm, out_ref, hidden_ref, gain_ref, routes_ref, sems):
    copies = [
        pltpu.make_async_copy(source, target, sems.at[i])
        for i, (source, target) in enumerate(
            ((hidden_hbm, hidden_ref), (gain_hbm, gain_ref), (routes_hbm, routes_ref))
        )
    ]
    for copy in copies:
        copy.start()
    for copy in copies:
        copy.wait()
    values = hidden_ref[...].astype(jnp.float32)
    width = values.shape[1]
    square_mean = jnp.mean(values * values, axis=1, keepdims=True)
    normed = values * lax.rsqrt(square_mean + EPSILON) * gain_ref[...]
    out_ref[:, :width] = normed.astype(jnp.bfloat16)
    rows = values.shape[0]
    routes = routes_ref[...]
    experts_down = lax.broadcasted_iota(jnp.int32, (LANES, rows), 0)
    named = jnp.zeros((LANES, rows), jnp.float32)
    for k in range(routes.shape[0]):
        named = jnp.where(experts_down == routes[k : k + 1, :], 1.0, named)
    same = lax.broadcasted_iota(jnp.int32, (rows, rows), 0) == lax.broadcasted_iota(jnp.int32, (rows, rows), 1)
    out_ref[:, width:] = lax.dot_general(
        same.astype(jnp.bfloat16),
        named.astype(jnp.bfloat16),
        (((1,), (1,)), ((), ())),
        preferred_element_type=jnp.float32,
    ).astype(jnp.bfloat16)


def prepare(hidden, gain, routes):
    rows, width = hidden.shape
    return pl.pallas_call(
        prepare_kernel,
        out_shape=jax.ShapeDtypeStruct((rows, width + LANES), jnp.bfloat16),
        in_specs=[pl.BlockSpec(memory_space=pltpu.HBM)] * 3,
        scratch_shapes=[
            pltpu.VMEM(hidden.shape, jnp.bfloat16),
            pltpu.VMEM((1, width), jnp.float32),
            pltpu.VMEM(routes.shape[::-1], jnp.int32),
            pltpu.SemaphoreType.DMA((3,)),
        ],
        compiler_params=pltpu.CompilerParams(vmem_limit_bytes=PREPARE_VMEM),
        cost_estimate=pl.CostEstimate(flops=6 * rows * width, bytes_accessed=4 * rows * width, transcendentals=rows),
        name="prepare",
    )(hidden, gain[None, :], routes.T)


def experts_kernel(blocks, n_tile, ids_ref, router_ref, *refs):
    token_hbm, weight_hbm, out_hbm = refs[:blocks], refs[blocks : blocks + 6], refs[blocks + 6 : 2 * blocks + 6]
    tokens_ref, *weight_refs, out_ref, token_sems, weight_sems, out_sems = refs[2 * blocks + 6 :]
    rows = token_hbm[0].shape[0]
    width = weight_hbm[0].shape[0]
    hidden_units = weight_hbm[0].shape[1]

    token_copies = [
        pltpu.make_async_copy(ref, tokens_ref.at[pl.ds(i * rows, rows)], token_sems.at[i])
        for i, ref in enumerate(token_hbm)
    ]
    weight_copies = [
        pltpu.make_async_copy(source, target, weight_sems.at[i])
        for i, (source, target) in enumerate(zip(weight_hbm, weight_refs))
    ]
    for copy in token_copies + weight_copies:
        copy.start()
    for copy in token_copies:
        copy.wait()

    experts = router_ref.shape[0]
    logits = lax.dot_general(
        tokens_ref[:, :width], router_ref[...], (((1,), (1,)), ((), ())), preferred_element_type=jnp.float32
    )
    named = tokens_ref[:, width:][:, :experts].astype(jnp.float32)
    chosen = named * jax.nn.sigmoid(logits)
    weights = ROUTE_SCALE * chosen / jnp.sum(chosen, axis=1, keepdims=True)
    lanes = lax.broadcasted_iota(jnp.int32, weights.shape, 1)

    def product(i):
        weight_copies[i].wait()
        return jnp.dot(tokens_ref[:, :width], weight_refs[i][...], preferred_element_type=jnp.float32)

    acts, columns = [], []
    for i in range(2):
        gate_part = product(2 * i)
        up_part = product(2 * i + 1)
        acts.append((jax.nn.silu(gate_part) * up_part).astype(jnp.bfloat16))
        columns.append(jnp.sum(jnp.where(lanes == ids_ref[i], weights, 0.0), axis=1, keepdims=True))

    for i in (4, 5):
        weight_copies[i].wait()
    out_copies = []
    for j in range(width // n_tile):
        span = pl.ds(j * n_tile, n_tile)
        total = columns[0] * jnp.dot(
            acts[0], weight_refs[4][:, span], preferred_element_type=jnp.float32
        ) + columns[1] * jnp.dot(acts[1], weight_refs[5][:, span], preferred_element_type=jnp.float32)
        out_ref[:, span] = total.astype(jnp.bfloat16)
        for i, ref in enumerate(out_hbm):
            copy = pltpu.make_async_copy(
                out_ref.at[pl.ds(i * rows, rows), span], ref.at[:, span], out_sems.at[j, i]
            )
            copy.start()
            out_copies.append(copy)
    for copy in out_copies:
        copy.wait()


def experts(ids, token_blocks, router_t, gates, ups, downs):
    blocks = len(token_blocks)
    rows = token_blocks[0].shape[0]
    width, hidden_units = gates[0].shape
    n_tile = 1024
    all_rows = blocks * rows
    weights = (gates[0], ups[0], gates[1], ups[1], downs[0], downs[1])
    return pl.pallas_call(
        functools.partial(experts_kernel, blocks, n_tile),
        in_specs=[pl.BlockSpec(memory_space=pltpu.SMEM), pl.BlockSpec(memory_space=pltpu.VMEM)]
        + [pl.BlockSpec(memory_space=pl.ANY)] * blocks
        + [pl.BlockSpec(memory_space=pl.ANY)] * 6,
        out_specs=[pl.BlockSpec(memory_space=pl.ANY)] * blocks,
        out_shape=[jax.ShapeDtypeStruct((rows, width), jnp.bfloat16)] * blocks,
        scratch_shapes=[pltpu.VMEM((all_rows, width + LANES), jnp.bfloat16)]
        + [pltpu.VMEM(w.shape, jnp.bfloat16) for w in weights]
        + [
            pltpu.VMEM((all_rows, width), jnp.bfloat16),
            pltpu.SemaphoreType.DMA((blocks,)),
            pltpu.SemaphoreType.DMA((6,)),
            pltpu.SemaphoreType.DMA((width // n_tile, blocks)),
        ],
        compiler_params=pltpu.CompilerParams(vmem_limit_bytes=EXPERTS_VMEM),
        cost_estimate=pl.CostEstimate(
            flops=12 * all_rows * width * hidden_units,
            bytes_accessed=12 * width * hidden_units + 4 * all_rows * width,
            transcendentals=2 * all_rows * hidden_units,
        ),
        name="experts",
    )(ids, router_t, *token_blocks, *weights)


def local(hidden, gain, router_w, routes, w_gate, w_up, w_down):
    ep_count, grp_count = lax.axis_size("ep"), lax.axis_size("grp")
    local_experts = ep_count // SPLIT
    expert_count = local_experts * grp_count
    place, core = lax.axis_index("ep") // SPLIT, lax.axis_index("grp")
    plan, return_order, most_open, weights_end, paired = plan_for(ep_count, grp_count)
    rows = hidden.shape[0]
    own = prepare(hidden, gain, routes)
    if paired:
        own = jnp.concatenate([own, between_cores(own)], axis=0)
    weights = [(w[0, 0], between_cores(after(w[0, 0], [own]))) for w in (w_gate, w_up, w_down)]
    held = [own]
    for slot, (parent, *bits) in enumerate(plan, 1):
        ended = held[1 : slot + 1 - most_open[slot - 1]]
        if slot in weights_end:
            ended.append(weights[weights_end[slot]][1])
        held.append(across(after(held[parent], ended), bits, ep_count))
    first = 0
    if paired:
        first = 1
        spare = [0 in bits for _, *bits in plan].index(True) + 1
        held[spare] = jnp.where(core == 1, own, held[spare])

    ids = jnp.stack([core * local_experts + place, (1 - core) * local_experts + place]).astype(jnp.int32)
    router_t = jnp.pad(router_w.T, ((0, -expert_count % 16), (0, 0)))
    parts = experts(ids, held[first:], router_t, *weights)

    terms = [[] for _ in range(first)] + [[part] for part in parts]
    if paired:
        terms[0].append(jnp.where(core == 1, parts[spare - 1], jnp.zeros_like(parts[spare - 1])))

    def summed(slot):
        return sum(term.astype(jnp.float32) for term in terms[slot])

    returned = []
    for slot in return_order:
        parent, *bits = plan[slot - 1]
        value = after(summed(slot).astype(jnp.bfloat16), returned[: max(0, len(returned) + 1 - OPEN_RETURN)])
        returned.append(across(value, bits, ep_count))
        terms[parent].append(returned[-1])
    total = summed(0)
    if paired:
        arrived = between_cores(total[rows:].astype(jnp.bfloat16))
        total = total[:rows] + arrived.astype(jnp.float32)
    return total.astype(jnp.bfloat16)


def solution(mesh):
    in_specs = (
        P(("dom", "ep", "grp"), None),
        P(),
        P(),
        P(("dom", "ep", "grp"), None),
        P("ep", "grp", None, None),
        P("ep", "grp", None, None),
        P("ep", "grp", None, None),
    )
    out_specs = P(("dom", "ep", "grp"), None)
    return jax.shard_map(local, mesh=mesh, in_specs=in_specs, out_specs=out_specs, check_vma=False)
```

time: 114 us -> 121 us (1.061)
  starting transfers between devices: 29.2 us -> 40.2 us
  waiting for transfers between devices: 63.8 us -> 54.5 us
  Pallas kernels: 15 us -> 21.2 us
  local copies, waits for them, and re-layouts: 3.31 us -> 0.94 us
  other arithmetic: 1.73 us -> 3.57 us
    ppermute x16, starting transfers between devices: 28 us -> 38.7 us  [across(): return lax.ppermute(value, ('ep', 'grp'), pairs)]
    ppermute x16, waiting for transfers between devices: 58.9 us -> 51.7 us  [across(): return lax.ppermute(value, ('ep', 'grp'), pairs)]
    pallas_call x1, Pallas kernels: 14.8 us -> 19.3 us  [experts(): pl.pallas_call(functools.partial(experts_kernel, blocks, n_tile), in_spec...]
    unnamed x6 -> x0, local copies, waits for them, and re-layouts: 2.37 us -> none
    ppermute x5, waiting for transfers between devices: 4.92 us -> 2.81 us  [between_cores(): return lax.ppermute(value, 'grp', [(0, 1), (1, 0)])]
    pallas_call x1, Pallas kernels: 0.24 us -> 1.88 us  [prepare(): pl.pallas_call(prepare_kernel, out_shape=jax.ShapeDtypeStruct((rows, widt...]
  transfers between devices with their start and end apart: 21 -> 21, of which waited for: 15 -> 14; matrix products, arithmetic and copies ran while one was open for 2% -> 2% of each run, Pallas kernels for 0% -> 0%
where the time goes in v6:
time: 121 us
  waiting for transfers between devices  54.5 us (45%)
  starting transfers between devices  40.2 us (33%)
  Pallas kernels  21.2 us (18%)
  other arithmetic  3.57 us (3%)
    ppermute x16, waiting for transfers between devices, across(): return lax.ppermute(value, ('ep', 'grp'), pairs)  51.7 us
    ppermute x16, starting transfers between devices, across(): return lax.ppermute(value, ('ep', 'grp'), pairs)  38.7 us
    pallas_call x1, Pallas kernels, experts(): pl.pallas_call(functools.partial(experts_kernel, blocks, n_tile), in_spec...  19.3 us
    ppermute x5, waiting for transfers between devices, between_cores(): return lax.ppermute(value, 'grp', [(0, 1), (1, 0)])  2.81 us
  transfers between devices with their start and end apart: 21, of which 14 were waited for; matrix products, arithmetic and copies ran while one was open for 2% of the time, Pallas kernels for 0%

profile of v6, /device:TPU:0, one launch (start us, length us, event | category | flops | bytes accessed | tf_op | source)
XLA Modules:
  0.0 120.6 jit_solution(14647707218382877781)
XLA Ops:
  0.0 1.9 %prepare.1 = bf16[16,7296]{1,0:T(8,128)(2,1)} custom-call(bf16[16,7168]{1,0:T(8,128)(2,1)} %hidden_hbm.1, f32[1,7168]{1,0:T(1,128)} %bitcast.15, s32[4,16]{1,0:T(4,128)} %bitcast.16), custom_call_target="tpu_custom_call" | custom-call | flops 688128 | bytes 458752 | tf_op jit(solution)/shard_map/prepare/pallas_call | solution.py:82
  5.7 2.7 %collective-permute-start.2 = (bf16[32,7296]{1,0:T(8,128)(2,1)S(1)}, bf16[32,7296]{1,0:T(8,128)(2,1)S(1)}, u32[]{:S(2)}, u32[]{:S(2)}) collective-permute-start(bf16[32,7296]{1,0:T(8,128)(2,1)S(1)} %pad_maximum_fusion), channel_id=1, source_target_pairs={{0,8},{2,10},{4,12},{6,14},{8,0},{10,2},{12,4},{14,6},{16,24},{18,... | collective-permute-start | bytes 1400840 | tf_op jit(solution)/shard_map/ppermute | solution.py:38
  8.4 2.6 %collective-permute-start.1 = (bf16[32,7296]{1,0:T(8,128)(2,1)S(1)}, bf16[32,7296]{1,0:T(8,128)(2,1)S(1)}, u32[]{:S(2)}, u32[]{:S(2)}) collective-permute-start(bf16[32,7296]{1,0:T(8,128)(2,1)S(1)} %pad_maximum_fusion), channel_id=1, source_target_pairs={{0,16},{2,18},{4,20},{6,22},{8,24},{10,26},{12,28},{14,30},{16,0},... | collective-permute-start | bytes 1400840 | tf_op jit(solution)/shard_map/ppermute | solution.py:38
  11.0 9.2 %collective-permute-done.2.refs_1_ = bf16[32,7296]{1,0:T(8,128)(2,1)S(1)} collective-permute-done((bf16[32,7296]{1,0:T(8,128)(2,1)S(1)}, bf16[32,7296]{1,0:T(8,128)(2,1)S(1)}, u32[]{:S(2)}, u32[]{:S(2)}) %collective-permute-start.2) | collective-permute-done | bytes 466976 | tf_op jit(solution)/shard_map/ppermute | solution.py:38
  20.2 1.7 %collective-permute-done.1.refs_0_ = bf16[32,7296]{1,0:T(8,128)(2,1)S(1)} collective-permute-done((bf16[32,7296]{1,0:T(8,128)(2,1)S(1)}, bf16[32,7296]{1,0:T(8,128)(2,1)S(1)}, u32[]{:S(2)}, u32[]{:S(2)}) %collective-permute-start.1) | collective-permute-done | bytes 466976 | tf_op jit(solution)/shard_map/ppermute | solution.py:38
  21.9 1.5 %collective-permute-start.3 = (bf16[32,7296]{1,0:T(8,128)(2,1)S(1)}, bf16[32,7296]{1,0:T(8,128)(2,1)S(1)}, u32[]{:S(2)}, u32[]{:S(2)}) collective-permute-start(bf16[32,7296]{1,0:T(8,128)(2,1)S(1)} %collective-permute-done.1.refs_0_), channel_id=1, source_target_pairs={{0,4},{2,6},{4,0},{6,2},{8,12},{10,14},{12,8},{14,10},{16,20},{18,... | collective-permute-start | bytes 1400840 | tf_op jit(solution)/shard_map/ppermute | solution.py:38
  24.9 5.6 %collective-permute-done.3.refs_2_ = bf16[32,7296]{1,0:T(8,128)(2,1)S(1)} collective-permute-done((bf16[32,7296]{1,0:T(8,128)(2,1)S(1)}, bf16[32,7296]{1,0:T(8,128)(2,1)S(1)}, u32[]{:S(2)}, u32[]{:S(2)}) %collective-permute-start.3) | collective-permute-done | bytes 466976 | tf_op jit(solution)/shard_map/ppermute | solution.py:38
  30.5 1.5 %collective-permute-done.4.refs_3_ = bf16[32,7296]{1,0:T(8,128)(2,1)S(1)} collective-permute-done((bf16[32,7296]{1,0:T(8,128)(2,1)S(1)}, bf16[32,7296]{1,0:T(8,128)(2,1)S(1)}, u32[]{:S(2)}, u32[]{:S(2)}) %collective-permute-start.4) | collective-permute-done | bytes 466976 | tf_op jit(solution)/shard_map/ppermute | solution.py:38
  32.5 3.4 %collective-permute-start.10 = (bf16[32,7296]{1,0:T(8,128)(2,1)S(1)}, bf16[32,7296]{1,0:T(8,128)(2,1)S(1)}, u32[]{:S(2)}, u32[]{:S(2)}) collective-permute-start(bf16[32,7296]{1,0:T(8,128)(2,1)S(1)} %collective-permute-done.2.refs_1_), channel_id=1, source_target_pairs={{0,2},{2,0},{4,6},{6,4},{8,10},{10,8},{12,14},{14,12},{16,18},{18,... | collective-permute-start | bytes 1400840 | tf_op jit(solution)/shard_map/ppermute | solution.py:38
  36.9 2.7 %collective-permute-start.7 = (bf16[32,7296]{1,0:T(8,128)(2,1)S(1)}, bf16[32,7296]{1,0:T(8,128)(2,1)S(1)}, u32[]{:S(2)}, u32[]{:S(2)}) collective-permute-start(bf16[32,7296]{1,0:T(8,128)(2,1)S(1)} %collective-permute-done.4.refs_3_), channel_id=1, source_target_pairs={{0,8},{2,10},{4,12},{6,14},{8,0},{10,2},{12,4},{14,6},{16,24},{18,... | collective-permute-start | bytes 1400840 | tf_op jit(solution)/shard_map/ppermute | solution.py:38
  40.6 4.4 %collective-permute-start.9 = (bf16[32,7296]{1,0:T(8,128)(2,1)S(1)}, bf16[32,7296]{1,0:T(8,128)(2,1)S(1)}, u32[]{:S(2)}, u32[]{:S(2)}) collective-permute-start(bf16[32,7296]{1,0:T(8,128)(2,1)S(1)} %collective-permute-done.5.refs_4_), channel_id=1, source_target_pairs={{0,8},{2,10},{4,12},{6,14},{8,0},{10,2},{12,4},{14,6},{16,24},{18,... | collective-permute-start | bytes 1400840 | tf_op jit(solution)/shard_map/ppermute | solution.py:38
  46.2 5.3 %collective-permute-done.9.refs_6_ = bf16[32,7296]{1,0:T(8,128)(2,1)S(1)} collective-permute-done((bf16[32,7296]{1,0:T(8,128)(2,1)S(1)}, bf16[32,7296]{1,0:T(8,128)(2,1)S(1)}, u32[]{:S(2)}, u32[]{:S(2)}) %collective-permute-start.9) | collective-permute-done | bytes 466976 | tf_op jit(solution)/shard_map/ppermute | solution.py:38
  51.5 19.3 %experts.1 = (bf16[32,7168]{1,0:T(8,128)(2,1)S(1)}, bf16[32,7168]{1,0:T(8,128)(2,1)S(1)}, bf16[32,7168]{1,0:T(8,128)(2,1)S(1)}, bf16[32,7168]{1,0:T(8,128)(2,1)S...) custom-call(s32[2]{0:T(128)S(1)} %pad_add_fusion.ids_ref, ...), custom_call_target="tpu_custom_call" | custom-call | flops 5637144576 | bytes 29360128 | tf_op jit(solution)/shard_map/experts/pallas_call | solution.py:164
  70.8 2.1 %collective-permute-start.13 = (bf16[32,7168]{1,0:T(8,128)(2,1)S(1)}, bf16[32,7168]{1,0:T(8,128)(2,1)S(1)}, u32[]{:S(2)}, u32[]{:S(2)}) collective-permute-start(bf16[32,7168]{1,0:T(8,128)(2,1)S(1)} %get-tuple-element.37), channel_id=1, source_target_pairs={{0,8},{2,10},{4,12},{6,14},{8,0},{10,2},{12,4},{14,6},{16,24},{18,... | collective-permute-start | bytes 1376264 | tf_op jit(solution)/shard_map/ppermute | solution.py:38
  73.0 3.8 %collective-permute-start.12 = (bf16[32,7168]{1,0:T(8,128)(2,1)S(1)}, bf16[32,7168]{1,0:T(8,128)(2,1)S(1)}, u32[]{:S(2)}, u32[]{:S(2)}) collective-permute-start(bf16[32,7168]{1,0:T(8,128)(2,1)S(1)} %get-tuple-element.35), channel_id=1, source_target_pairs={{0,2},{2,0},{4,6},{6,4},{8,10},{10,8},{12,14},{14,12},{16,18},{18,... | collective-permute-start | bytes 1376264 | tf_op jit(solution)/shard_map/ppermute | solution.py:38
  76.8 4.7 %collective-permute-done.13 = bf16[32,7168]{1,0:T(8,128)(2,1)S(1)} collective-permute-done((bf16[32,7168]{1,0:T(8,128)(2,1)S(1)}, bf16[32,7168]{1,0:T(8,128)(2,1)S(1)}, u32[]{:S(2)}, u32[]{:S(2)}) %collective-permute-start.13) | collective-permute-done | bytes 458784 | tf_op jit(solution)/shard_map/ppermute | solution.py:38
  81.6 3.0 %collective-permute-start.16 = (bf16[32,7168]{1,0:T(8,128)(2,1)S(1)}, bf16[32,7168]{1,0:T(8,128)(2,1)S(1)}, u32[]{:S(2)}, u32[]{:S(2)}) collective-permute-start(bf16[32,7168]{1,0:T(8,128)(2,1)S(1)} %add_convert_fusion.2), channel_id=1, source_target_pairs={{0,4},{2,6},{4,0},{6,2},{8,12},{10,14},{12,8},{14,10},{16,20},{18,... | collective-permute-start | bytes 1376264 | tf_op jit(solution)/shard_map/ppermute | solution.py:38
  84.7 4.6 %collective-permute-done.15 = bf16[32,7168]{1,0:T(8,128)(2,1)S(1)} collective-permute-done((bf16[32,7168]{1,0:T(8,128)(2,1)S(1)}, bf16[32,7168]{1,0:T(8,128)(2,1)S(1)}, u32[]{:S(2)}, u32[]{:S(2)}) %collective-permute-start.15) | collective-permute-done | bytes 458784 | tf_op jit(solution)/shard_map/ppermute | solution.py:38
  89.2 2.2 %collective-permute-start.18 = (bf16[32,7168]{1,0:T(8,128)(2,1)S(1)}, bf16[32,7168]{1,0:T(8,128)(2,1)S(1)}, u32[]{:S(2)}, u32[]{:S(2)}) collective-permute-start(bf16[32,7168]{1,0:T(8,128)(2,1)S(1)} %get-tuple-element.45), channel_id=1, source_target_pairs={{0,4},{2,6},{4,0},{6,2},{8,12},{10,14},{12,8},{14,10},{16,20},{18,... | collective-permute-start | bytes 1376264 | tf_op jit(solution)/shard_map/ppermute | solution.py:38
  91.8 2.5 %collective-permute-start.14 = (bf16[32,7168]{1,0:T(8,128)(2,1)S(1)}, bf16[32,7168]{1,0:T(8,128)(2,1)S(1)}, u32[]{:S(2)}, u32[]{:S(2)}) collective-permute-start(bf16[32,7168]{1,0:T(8,128)(2,1)S(1)} %add_convert_fusion.3), channel_id=1, source_target_pairs={{0,8},{2,10},{4,12},{6,14},{8,0},{10,2},{12,4},{14,6},{16,24},{18,... | collective-permute-start | bytes 1376264 | tf_op jit(solution)/shard_map/ppermute | solution.py:38
  94.3 4.1 %collective-permute-done.18 = bf16[32,7168]{1,0:T(8,128)(2,1)S(1)} collective-permute-done((bf16[32,7168]{1,0:T(8,128)(2,1)S(1)}, bf16[32,7168]{1,0:T(8,128)(2,1)S(1)}, u32[]{:S(2)}, u32[]{:S(2)}) %collective-permute-start.18) | collective-permute-done | bytes 458784 | tf_op jit(solution)/shard_map/ppermute | solution.py:38
  98.4 2.5 %collective-permute-done.17 = bf16[32,7168]{1,0:T(8,128)(2,1)S(1)} collective-permute-done((bf16[32,7168]{1,0:T(8,128)(2,1)S(1)}, bf16[32,7168]{1,0:T(8,128)(2,1)S(1)}, u32[]{:S(2)}, u32[]{:S(2)}) %collective-permute-start.17) | collective-permute-done | bytes 458784 | tf_op jit(solution)/shard_map/ppermute | solution.py:38
  101.1 5.6 %collective-permute-start.19 = (bf16[32,7168]{1,0:T(8,128)(2,1)S(1)}, bf16[32,7168]{1,0:T(8,128)(2,1)S(1)}, u32[]{:S(2)}, u32[]{:S(2)}) collective-permute-start(bf16[32,7168]{1,0:T(8,128)(2,1)S(1)} %add_convert_fusion), channel_id=1, source_target_pairs={{0,16},{2,18},{4,20},{6,22},{8,24},{10,26},{12,28},{14,30},{16,0},... | collective-permute-start | bytes 1376264 | tf_op jit(solution)/shard_map/ppermute | solution.py:38
  106.7 11.4 %collective-permute-done.19 = bf16[32,7168]{1,0:T(8,128)(2,1)S(1)} collective-permute-done((bf16[32,7168]{1,0:T(8,128)(2,1)S(1)}, bf16[32,7168]{1,0:T(8,128)(2,1)S(1)}, u32[]{:S(2)}, u32[]{:S(2)}) %collective-permute-start.19) | collective-permute-done | bytes 458784 | tf_op jit(solution)/shard_map/ppermute | solution.py:38
  (31 shorter events, 12.1 us)
Async XLA Ops:
  1.9 1.9 %collective-permute-start = (bf16[16,7296]{1,0:T(8,128)(2,1)}, bf16[16,7296]{1,0:T(8,128)(2,1)S(1)}, u32[]{:S(2)}, u32[]{:S(2)}) collective-permute-start(bf16[16,7296]{1,0:T(8,128)(2,1)} %prepare.1), channel_id=1, source_target_pairs={{0,1},{1,0},{2,3},{3,2},{4,5},{5,4},{6,7},{7,6},{8,9},{9,8},{10,11... | collective-permute-start | bytes 700424 | tf_op jit(solution)/shard_map/ppermute | solution.py:46
  4.7 32.2 %collective-permute-start.6 = (bf16[7168,256]{1,0:T(8,128)(2,1)}, bf16[7168,256]{1,0:T(8,128)(2,1)}, u32[]{:S(2)}, u32[]{:S(2)}) collective-permute-start(bf16[7168,256]{1,0:T(8,128)(2,1)} %bitcast.8), channel_id=1, source_target_pairs={{0,1},{1,0},{2,3},{3,2},{4,5},{5,4},{6,7},{7,6},{8,9},{9,8},{10,11... | collective-permute-start | bytes 11010056 | tf_op jit(solution)/shard_map/ppermute | solution.py:46
  5.2 35.4 %collective-permute-start.8 = (bf16[7168,256]{1,0:T(8,128)(2,1)}, bf16[7168,256]{1,0:T(8,128)(2,1)}, u32[]{:S(2)}, u32[]{:S(2)}) collective-permute-start(bf16[7168,256]{1,0:T(8,128)(2,1)} %bitcast.10), channel_id=1, source_target_pairs={{0,1},{1,0},{2,3},{3,2},{4,5},{5,4},{6,7},{7,6},{8,9},{9,8},{10,11... | collective-permute-start | bytes 11010056 | tf_op jit(solution)/shard_map/ppermute | solution.py:46
  5.3 40.7 %collective-permute-start.11 = (bf16[256,7168]{1,0:T(8,128)(2,1)}, bf16[256,7168]{1,0:T(8,128)(2,1)}, u32[]{:S(2)}, u32[]{:S(2)}) collective-permute-start(bf16[256,7168]{1,0:T(8,128)(2,1)} %bitcast.12), channel_id=1, source_target_pairs={{0,1},{1,0},{2,3},{3,2},{4,5},{5,4},{6,7},{7,6},{8,9},{9,8},{10,11... | collective-permute-start | bytes 11010056 | tf_op jit(solution)/shard_map/ppermute | solution.py:46
  5.7 14.5 %collective-permute-start.2 = (bf16[32,7296]{1,0:T(8,128)(2,1)S(1)}, bf16[32,7296]{1,0:T(8,128)(2,1)S(1)}, u32[]{:S(2)}, u32[]{:S(2)}) collective-permute-start(bf16[32,7296]{1,0:T(8,128)(2,1)S(1)} %pad_maximum_fusion), channel_id=1, source_target_pairs={{0,8},{2,10},{4,12},{6,14},{8,0},{10,2},{12,4},{14,6},{16,24},{18,... | collective-permute-start | bytes 1400840 | tf_op jit(solution)/shard_map/ppermute | solution.py:38
  8.4 13.6 %collective-permute-start.1 = (bf16[32,7296]{1,0:T(8,128)(2,1)S(1)}, bf16[32,7296]{1,0:T(8,128)(2,1)S(1)}, u32[]{:S(2)}, u32[]{:S(2)}) collective-permute-start(bf16[32,7296]{1,0:T(8,128)(2,1)S(1)} %pad_maximum_fusion), channel_id=1, source_target_pairs={{0,16},{2,18},{4,20},{6,22},{8,24},{10,26},{12,28},{14,30},{16,0},... | collective-permute-start | bytes 1400840 | tf_op jit(solution)/shard_map/ppermute | solution.py:38
  21.9 8.6 %collective-permute-start.3 = (bf16[32,7296]{1,0:T(8,128)(2,1)S(1)}, bf16[32,7296]{1,0:T(8,128)(2,1)S(1)}, u32[]{:S(2)}, u32[]{:S(2)}) collective-permute-start(bf16[32,7296]{1,0:T(8,128)(2,1)S(1)} %collective-permute-done.1.refs_0_), channel_id=1, source_target_pairs={{0,4},{2,6},{4,0},{6,2},{8,12},{10,14},{12,8},{14,10},{16,20},{18,... | collective-permute-start | bytes 1400840 | tf_op jit(solution)/shard_map/ppermute | solution.py:38
  23.5 8.6 %collective-permute-start.4 = (bf16[32,7296]{1,0:T(8,128)(2,1)S(1)}, bf16[32,7296]{1,0:T(8,128)(2,1)S(1)}, u32[]{:S(2)}, u32[]{:S(2)}) collective-permute-start(bf16[32,7296]{1,0:T(8,128)(2,1)S(1)} %collective-permute-done.1.refs_0_), channel_id=1, source_target_pairs={{0,2},{2,0},{4,6},{6,4},{8,10},{10,8},{12,14},{14,12},{16,18},{18,... | collective-permute-start | bytes 1400840 | tf_op jit(solution)/shard_map/ppermute | solution.py:38
  32.0 8.6 %collective-permute-start.5 = (bf16[32,7296]{1,0:T(8,128)(2,1)S(1)}, bf16[32,7296]{1,0:T(8,128)(2,1)S(1)}, u32[]{:S(2)}, u32[]{:S(2)}) collective-permute-start(bf16[32,7296]{1,0:T(8,128)(2,1)S(1)} %collective-permute-done.4.refs_3_), channel_id=1, source_target_pairs={{0,4},{2,6},{4,0},{6,2},{8,12},{10,14},{12,8},{14,10},{16,20},{18,... | collective-permute-start | bytes 1400840 | tf_op jit(solution)/shard_map/ppermute | solution.py:38
  32.5 12.4 %collective-permute-start.10 = (bf16[32,7296]{1,0:T(8,128)(2,1)S(1)}, bf16[32,7296]{1,0:T(8,128)(2,1)S(1)}, u32[]{:S(2)}, u32[]{:S(2)}) collective-permute-start(bf16[32,7296]{1,0:T(8,128)(2,1)S(1)} %collective-permute-done.2.refs_1_), channel_id=1, source_target_pairs={{0,2},{2,0},{4,6},{6,4},{8,10},{10,8},{12,14},{14,12},{16,18},{18,... | collective-permute-start | bytes 1400840 | tf_op jit(solution)/shard_map/ppermute | solution.py:38
  36.9 9.3 %collective-permute-start.7 = (bf16[32,7296]{1,0:T(8,128)(2,1)S(1)}, bf16[32,7296]{1,0:T(8,128)(2,1)S(1)}, u32[]{:S(2)}, u32[]{:S(2)}) collective-permute-start(bf16[32,7296]{1,0:T(8,128)(2,1)S(1)} %collective-permute-done.4.refs_3_), channel_id=1, source_target_pairs={{0,8},{2,10},{4,12},{6,14},{8,0},{10,2},{12,4},{14,6},{16,24},{18,... | collective-permute-start | bytes 1400840 | tf_op jit(solution)/shard_map/ppermute | solution.py:38
  40.6 10.9 %collective-permute-start.9 = (bf16[32,7296]{1,0:T(8,128)(2,1)S(1)}, bf16[32,7296]{1,0:T(8,128)(2,1)S(1)}, u32[]{:S(2)}, u32[]{:S(2)}) collective-permute-start(bf16[32,7296]{1,0:T(8,128)(2,1)S(1)} %collective-permute-done.5.refs_4_), channel_id=1, source_target_pairs={{0,8},{2,10},{4,12},{6,14},{8,0},{10,2},{12,4},{14,6},{16,24},{18,... | collective-permute-start | bytes 1400840 | tf_op jit(solution)/shard_map/ppermute | solution.py:38
  70.8 10.7 %collective-permute-start.13 = (bf16[32,7168]{1,0:T(8,128)(2,1)S(1)}, bf16[32,7168]{1,0:T(8,128)(2,1)S(1)}, u32[]{:S(2)}, u32[]{:S(2)}) collective-permute-start(bf16[32,7168]{1,0:T(8,128)(2,1)S(1)} %get-tuple-element.37), channel_id=1, source_target_pairs={{0,8},{2,10},{4,12},{6,14},{8,0},{10,2},{12,4},{14,6},{16,24},{18,... | collective-permute-start | bytes 1376264 | tf_op jit(solution)/shard_map/ppermute | solution.py:38
  72.9 16.3 %collective-permute-start.15 = (bf16[32,7168]{1,0:T(8,128)(2,1)S(1)}, bf16[32,7168]{1,0:T(8,128)(2,1)S(1)}, u32[]{:S(2)}, u32[]{:S(2)}) collective-permute-start(bf16[32,7168]{1,0:T(8,128)(2,1)S(1)} %get-tuple-element.41), channel_id=1, source_target_pairs={{0,8},{2,10},{4,12},{6,14},{8,0},{10,2},{12,4},{14,6},{16,24},{18,... | collective-permute-start | bytes 1376264 | tf_op jit(solution)/shard_map/ppermute | solution.py:38
  73.0 16.2 %collective-permute-start.12 = (bf16[32,7168]{1,0:T(8,128)(2,1)S(1)}, bf16[32,7168]{1,0:T(8,128)(2,1)S(1)}, u32[]{:S(2)}, u32[]{:S(2)}) collective-permute-start(bf16[32,7168]{1,0:T(8,128)(2,1)S(1)} %get-tuple-element.35), channel_id=1, source_target_pairs={{0,2},{2,0},{4,6},{6,4},{8,10},{10,8},{12,14},{14,12},{16,18},{18,... | collective-permute-start | bytes 1376264 | tf_op jit(solution)/shard_map/ppermute | solution.py:38
  81.6 9.8 %collective-permute-start.16 = (bf16[32,7168]{1,0:T(8,128)(2,1)S(1)}, bf16[32,7168]{1,0:T(8,128)(2,1)S(1)}, u32[]{:S(2)}, u32[]{:S(2)}) collective-permute-start(bf16[32,7168]{1,0:T(8,128)(2,1)S(1)} %add_convert_fusion.2), channel_id=1, source_target_pairs={{0,4},{2,6},{4,0},{6,2},{8,12},{10,14},{12,8},{14,10},{16,20},{18,... | collective-permute-start | bytes 1376264 | tf_op jit(solution)/shard_map/ppermute | solution.py:38
  89.2 9.2 %collective-permute-start.18 = (bf16[32,7168]{1,0:T(8,128)(2,1)S(1)}, bf16[32,7168]{1,0:T(8,128)(2,1)S(1)}, u32[]{:S(2)}, u32[]{:S(2)}) collective-permute-start(bf16[32,7168]{1,0:T(8,128)(2,1)S(1)} %get-tuple-element.45), channel_id=1, source_target_pairs={{0,4},{2,6},{4,0},{6,2},{8,12},{10,14},{12,8},{14,10},{16,20},{18,... | collective-permute-start | bytes 1376264 | tf_op jit(solution)/shard_map/ppermute | solution.py:38
  91.6 9.4 %collective-permute-start.17 = (bf16[32,7168]{1,0:T(8,128)(2,1)S(1)}, bf16[32,7168]{1,0:T(8,128)(2,1)S(1)}, u32[]{:S(2)}, u32[]{:S(2)}) collective-permute-start(bf16[32,7168]{1,0:T(8,128)(2,1)S(1)} %add_convert_fusion.1), channel_id=1, source_target_pairs={{0,2},{2,0},{4,6},{6,4},{8,10},{10,8},{12,14},{14,12},{16,18},{18,... | collective-permute-start | bytes 1376264 | tf_op jit(solution)/shard_map/ppermute | solution.py:38
  91.8 14.9 %collective-permute-start.14 = (bf16[32,7168]{1,0:T(8,128)(2,1)S(1)}, bf16[32,7168]{1,0:T(8,128)(2,1)S(1)}, u32[]{:S(2)}, u32[]{:S(2)}) collective-permute-start(bf16[32,7168]{1,0:T(8,128)(2,1)S(1)} %add_convert_fusion.3), channel_id=1, source_target_pairs={{0,8},{2,10},{4,12},{6,14},{8,0},{10,2},{12,4},{14,6},{16,24},{18,... | collective-permute-start | bytes 1376264 | tf_op jit(solution)/shard_map/ppermute | solution.py:38
  101.1 17.0 %collective-permute-start.19 = (bf16[32,7168]{1,0:T(8,128)(2,1)S(1)}, bf16[32,7168]{1,0:T(8,128)(2,1)S(1)}, u32[]{:S(2)}, u32[]{:S(2)}) collective-permute-start(bf16[32,7168]{1,0:T(8,128)(2,1)S(1)} %add_convert_fusion), channel_id=1, source_target_pairs={{0,16},{2,18},{4,20},{6,22},{8,24},{10,26},{12,28},{14,30},{16,0},... | collective-permute-start | bytes 1376264 | tf_op jit(solution)/shard_map/ppermute | solution.py:38
  118.3 1.6 %collective-permute-start.20 = (bf16[16,7168]{1,0:T(8,128)(2,1)S(1)}, bf16[16,7168]{1,0:T(8,128)(2,1)S(1)}, u32[]{:S(2)}, u32[]{:S(2)}) collective-permute-start(bf16[16,7168]{1,0:T(8,128)(2,1)S(1)} %slice.15), channel_id=1, source_target_pairs={{0,1},{1,0},{2,3},{3,2},{4,5},{5,4},{6,7},{7,6},{8,9},{9,8},{10,11... | collective-permute-start | bytes 688136 | tf_op jit(solution)/shard_map/ppermute | solution.py:46

commit v7 on v5

--- a/solution.py
+++ b/solution.py
@@ -12,14 +12,15 @@
 
 EPSILON = 1e-06
 ROUTE_SCALE = 2.5
-PREPARE_VMEM = 4 * 1024 * 1024
+PREPARE_VMEM = 60 * 1024 * 1024
 EXPERTS_VMEM = 44 * 1024 * 1024
 
-PLAN_16 = ((0, 4, 8), (0, 2, 1), (1, 2, 1), (1, 8, 2), (3, 1, 4), (1, 1, 0), (4, 2, 1), (5, 4, 2))
-RETURN_16 = (6, 8, 7, 5, 4, 3, 1, 2)
+PLAN_16 = ((0, 8, 4), (0, 1, 2), (1, 2, 8), (1, 1, 1), (3, 4, 1), (2, 2, 4), (4, 2, 2), (5, 1, 0))
+RETURN_16 = tuple((slot, PLAN_16[slot - 1]) for slot in (8, 7, 5, 4, 3, 6, 1, 2))
 OPEN_16 = (2, 2, 2, 2, 2, 3, 4, 4)
 WEIGHTS_END_16 = {6: 0, 7: 1}
-OPEN_RETURN = 4
+OPEN_RETURN = 5
+RETURN_PARTS = 2
 
 
 def plan_for(ep_count, grp_count):
@@ -30,7 +31,8 @@
         bit = 1 << (r.bit_length() - 1)
         plan.append((r ^ bit, bit, bit))
     slots = len(plan)
-    return tuple(plan), tuple(range(slots, 0, -1)), (OPEN_RETURN,) * slots, {}, False
+    back = tuple((slot, plan[slot - 1]) for slot in range(slots, 0, -1))
+    return tuple(plan), back, (OPEN_RETURN,) * slots, {}, False
 
 
 def across(value, bits, ep_count):
@@ -46,43 +48,59 @@
     return lax.ppermute(value, "grp", [(0, 1), (1, 0)])
 
 
-def prepare_kernel(hidden_ref, gain_ref, routes_ref, out_ref):
-    values = hidden_ref[...].astype(jnp.float32)
-    width = values.shape[1]
-    square_mean = jnp.mean(values * values, axis=1, keepdims=True)
-    normed = values * lax.rsqrt(square_mean + EPSILON) * gain_ref[...]
-    out_ref[:, :width] = normed.astype(jnp.bfloat16)
-    rows = values.shape[0]
-    routes = routes_ref[...]
-    experts_down = lax.broadcasted_iota(jnp.int32, (LANES, rows), 0)
-    named = jnp.zeros((LANES, rows), jnp.float32)
-    for k in range(routes.shape[0]):
-        named = jnp.where(experts_down == routes[k : k + 1, :], 1.0, named)
-    same = lax.broadcasted_iota(jnp.int32, (rows, rows), 0) == lax.broadcasted_iota(jnp.int32, (rows, rows), 1)
-    out_ref[:, width:] = lax.dot_general(
-        same.astype(jnp.bfloat16),
-        named.astype(jnp.bfloat16),
-        (((1,), (1,)), ((), ())),
-        preferred_element_type=jnp.float32,
-    ).astype(jnp.bfloat16)
-
-
-def prepare(hidden, gain, routes):
-    rows, width = hidden.shape
+def prepare_kernel(count, *refs):
+    sources, out_ref, targets, sems = refs[: 2 * count + 1], refs[2 * count + 1], refs[2 * count + 2 : -1], refs[-1]
+    copies = [
+        pltpu.make_async_copy(source, target, sems.at[i]) for i, (source, target) in enumerate(zip(sources, targets))
+    ]
+    for copy in copies:
+        copy.start()
+    for copy in copies:
+        copy.wait()
+    gain = targets[0][...]
+    for i in range(count):
+        values = targets[1 + i][...].astype(jnp.float32)
+        routes = targets[1 + count + i][...]
+        rows, width = values.shape
+        span = pl.ds(i * rows, rows)
+        square_mean = jnp.mean(values * values, axis=1, keepdims=True)
+        normed = values * lax.rsqrt(square_mean + EPSILON) * gain
+        out_ref[span, :width] = normed.astype(jnp.bfloat16)
+        experts_down = lax.broadcasted_iota(jnp.int32, (LANES, rows), 0)
+        named = jnp.zeros((LANES, rows), jnp.float32)
+        for k in range(routes.shape[0]):
+            named = jnp.where(experts_down == routes[k : k + 1, :], 1.0, named)
+        same = lax.broadcasted_iota(jnp.int32, (rows, rows), 0) == lax.broadcasted_iota(jnp.int32, (rows, rows), 1)
+        out_ref[span, width:] = lax.dot_general(
+            same.astype(jnp.bfloat16),
+            named.astype(jnp.bfloat16),
+            (((1,), (1,)), ((), ())),
+            preferred_element_type=jnp.float32,
+        ).astype(jnp.bfloat16)
+
+
+def prepare(gain, hiddens, routes):
+    rows, width = hiddens[0].shape
+    count = len(hiddens)
+    operands = (gain[None, :], *hiddens, *routes)
     return pl.pallas_call(
-        prepare_kernel,
-        out_shape=jax.ShapeDtypeStruct((rows, width + LANES), jnp.bfloat16),
+        functools.partial(prepare_kernel, count),
+        out_shape=jax.ShapeDtypeStruct((count * rows, width + LANES), jnp.bfloat16),
+        in_specs=[pl.BlockSpec(memory_space=pl.ANY)] * len(operands),
+        scratch_shapes=[pltpu.VMEM(x.shape, x.dtype) for x in operands] + [pltpu.SemaphoreType.DMA((len(operands),))],
         compiler_params=pltpu.CompilerParams(vmem_limit_bytes=PREPARE_VMEM),
-        cost_estimate=pl.CostEstimate(flops=6 * rows * width, bytes_accessed=4 * rows * width, transcendentals=rows),
+        cost_estimate=pl.CostEstimate(
+            flops=6 * count * rows * width, bytes_accessed=4 * count * rows * width, transcendentals=count * rows
+        ),
         name="prepare",
-    )(hidden, gain[None, :], routes.T)
-
-
-def experts_kernel(blocks, k_steps, k_tile, ids_ref, *refs):
+    )(*operands)
+
+
+def experts_kernel(blocks, parts, k_steps, n_steps, k_tile, ids_ref, *refs):
     token_refs = refs[:blocks]
     router_ref, gate0_ref, gate1_ref, up0_ref, up1_ref, down0_ref, down1_ref = refs[blocks : blocks + 7]
-    out_refs = refs[blocks + 7 : 2 * blocks + 7]
-    gates_ref, logits_ref, act_ref, coeff_ref = refs[2 * blocks + 7 :]
+    out_refs = refs[blocks + 7 : (1 + parts) * blocks + 7]
+    gates_ref, logits_ref, act_ref, coeff_ref = refs[(1 + parts) * blocks + 7 :]
     step = pl.program_id(0)
     rows = token_refs[0].shape[0]
     hidden_units = gate0_ref.shape[1]
@@ -134,11 +152,16 @@
         ) + coeff_ref[:, LANES : LANES + 1] * jnp.dot(
             act_ref[:, hidden_units:], down1_ref[...], preferred_element_type=jnp.float32
         )
-        for i, ref in enumerate(out_refs):
-            ref[...] = total[i * rows : (i + 1) * rows].astype(jnp.bfloat16)
-
-
-def experts(ids, token_blocks, router_t, gates, ups, downs):
+        part_steps = n_steps // parts
+        for part in range(parts):
+
+            @pl.when((step - k_steps) // part_steps == part)
+            def _():
+                for i, ref in enumerate(out_refs[part * blocks : (part + 1) * blocks]):
+                    ref[...] = total[i * rows : (i + 1) * rows].astype(jnp.bfloat16)
+
+
+def experts(ids, token_blocks, parts, router_t, gates, ups, downs):
     blocks = len(token_blocks)
     rows = token_blocks[0].shape[0]
     width, hidden_units = gates[0].shape
@@ -157,9 +180,16 @@
     in_specs += [pl.BlockSpec((router_t.shape[0], k_tile), lambda step, ids_ref: (0, at_k(step, ids_ref)))]
     in_specs += [pl.BlockSpec((k_tile, hidden_units), lambda step, ids_ref: (at_k(step, ids_ref), 0))] * 4
     in_specs += [pl.BlockSpec((hidden_units, n_tile), lambda step, ids_ref: (0, at_n(step, ids_ref)))] * 2
-    out_specs = [pl.BlockSpec((rows, n_tile), lambda step, ids_ref: (0, at_n(step, ids_ref)))] * blocks
+    part_steps = n_steps // parts
+
+    def at_part(part, step, ids_ref):
+        return 0, jnp.clip(step - k_steps - part * part_steps, 0, part_steps - 1)
+
+    out_specs = [
+        pl.BlockSpec((rows, n_tile), functools.partial(at_part, part)) for part in range(parts) for _ in range(blocks)
+    ]
     return pl.pallas_call(
-        functools.partial(experts_kernel, blocks, k_steps, k_tile),
+        functools.partial(experts_kernel, blocks, parts, k_steps, n_steps, k_tile),
         grid_spec=pltpu.PrefetchScalarGridSpec(
             num_scalar_prefetch=1,
             grid=(k_steps + n_steps,),
@@ -172,7 +202,7 @@
                 pltpu.VMEM((all_rows, 2 * LANES), jnp.float32),
             ],
         ),
-        out_shape=[jax.ShapeDtypeStruct((rows, width), jnp.bfloat16)] * blocks,
+        out_shape=[jax.ShapeDtypeStruct((rows, width // parts), jnp.bfloat16)] * (blocks * parts),
         compiler_params=pltpu.CompilerParams(vmem_limit_bytes=EXPERTS_VMEM),
         cost_estimate=pl.CostEstimate(
             flops=12 * all_rows * width * hidden_units,
@@ -188,13 +218,14 @@
     local_experts = ep_count // SPLIT
     expert_count = local_experts * grp_count
     place, core = lax.axis_index("ep") // SPLIT, lax.axis_index("grp")
-    plan, return_order, most_open, weights_end, paired = plan_for(ep_count, grp_count)
+    plan, return_plan, most_open, weights_end, paired = plan_for(ep_count, grp_count)
     rows = hidden.shape[0]
-    weights = [(w[0, 0], between_cores(w[0, 0])) for w in (w_gate, w_up, w_down)]
-
-    own = prepare(hidden, gain, routes)
+    hiddens, chosen = [hidden], [routes.T]
     if paired:
-        own = jnp.concatenate([own, between_cores(own)], axis=0)
+        hiddens.append(between_cores(hidden))
+        chosen.append(between_cores(routes.T))
+    own = prepare(gain, hiddens, chosen)
+    weights = [(w[0, 0], between_cores(after(w[0, 0], hiddens[1:] + chosen[1:]))) for w in (w_gate, w_up, w_down)]
     held = [own]
     for slot, (parent, *bits) in enumerate(plan, 1):
         ended = held[1 : slot + 1 - most_open[slot - 1]]
@@ -209,26 +240,31 @@
 
     ids = jnp.stack([core * local_experts + place, (1 - core) * local_experts + place]).astype(jnp.int32)
     router_t = jnp.pad(router_w.T, ((0, -expert_count % 16), (0, 0)))
-    parts = experts(ids, held[first:], router_t, *weights)
-
-    terms = [[] for _ in range(first)] + [[part] for part in parts]
+    outs = experts(ids, held[first:], RETURN_PARTS, router_t, *weights)
+    blocks = len(outs) // RETURN_PARTS
+
+    terms = {}
+    for part in range(RETURN_PARTS):
+        mine = outs[part * blocks : (part + 1) * blocks]
+        terms.update({(part, slot): [value] for slot, value in enumerate(mine, first)})
+        if paired:
+            terms[part, 0] = [jnp.where(core == 1, mine[spare - 1], jnp.zeros_like(mine[spare - 1]))]
+
+    def summed(part, slot):
+        return sum(term.astype(jnp.float32) for term in terms[part, slot])
+
+    returned = []
+    for slot, (parent, *bits) in return_plan:
+        for part in range(RETURN_PARTS):
+            value = summed(part, slot).astype(jnp.bfloat16)
+            value = after(value, returned[: max(0, len(returned) + 1 - OPEN_RETURN)])
+            returned.append(across(value, bits, ep_count))
+            terms[part, parent].append(returned[-1])
+    totals = [summed(part, 0) for part in range(RETURN_PARTS)]
     if paired:
-        terms[0].append(jnp.where(core == 1, parts[spare - 1], jnp.zeros_like(parts[spare - 1])))
-
-    def summed(slot):
-        return sum(term.astype(jnp.float32) for term in terms[slot])
-
-    returned = []
-    for slot in return_order:
-        parent, *bits = plan[slot - 1]
-        value = after(summed(slot).astype(jnp.bfloat16), returned[: max(0, len(returned) + 1 - OPEN_RETURN)])
-        returned.append(across(value, bits, ep_count))
-        terms[parent].append(returned[-1])
-    total = summed(0)
-    if paired:
-        arrived = between_cores(total[rows:].astype(jnp.bfloat16))
-        total = total[:rows] + arrived.astype(jnp.float32)
-    return total.astype(jnp.bfloat16)
+        arrived = [between_cores(total[rows:].astype(jnp.bfloat16)) for total in totals]
+        totals = [total[:rows] + value.astype(jnp.float32) for total, value in zip(totals, arrived)]
+    return jnp.concatenate([total.astype(jnp.bfloat16) for total in totals], axis=1)
 
 
 def solution(mesh):

time: 114 us -> 132 us (1.16)
  starting transfers between devices: 29.2 us -> 40.9 us
  waiting for transfers between devices: 63.8 us -> 70.1 us
  Pallas kernels: 15 us -> 17.3 us
  local copies, waits for them, and re-layouts: 3.31 us -> 1.06 us
    ppermute x16 -> x24, starting transfers between devices: 28 us -> 39.7 us  [across(): return lax.ppermute(value, ('ep', 'grp'), pairs)]
    ppermute x16 -> x24, waiting for transfers between devices: 58.9 us -> 67.5 us  [across(): return lax.ppermute(value, ('ep', 'grp'), pairs)]
    pallas_call x2, Pallas kernels: 15 us -> 17.3 us  [the longest x1 15.1 us: experts(): pl.pallas_call(functools.partial(experts_kernel, blocks, parts, k_steps,...]
    ppermute x5 -> x7, waiting for transfers between devices: 4.92 us -> 2.59 us  [between_cores(): return lax.ppermute(value, 'grp', [(0, 1), (1, 0)])]
    unnamed x6 -> x4, local copies, waits for them, and re-layouts: 2.37 us -> 0.12 us
  transfers between devices with their start and end apart: 21 -> 31, of which waited for: 15 -> 17; matrix products, arithmetic and copies ran while one was open for 2% -> 1% of each run, Pallas kernels for 0% -> 2%
where the time goes in v7:
time: 132 us; the launch traced here: 131 us
  waiting for transfers between devices  70.1 us (53%)
  starting transfers between devices  40.9 us (31%)
  Pallas kernels  17.3 us (13%)
  other arithmetic  1.74 us (1%)
    ppermute x24, waiting for transfers between devices, across(): return lax.ppermute(value, ('ep', 'grp'), pairs)  67.5 us
    ppermute x24, starting transfers between devices, across(): return lax.ppermute(value, ('ep', 'grp'), pairs)  39.7 us
    pallas_call x1, Pallas kernels, experts(): pl.pallas_call(functools.partial(experts_kernel, blocks, parts, k_steps,...  15.1 us
  transfers between devices with their start and end apart: 31, of which 17 were waited for; matrix products, arithmetic and copies ran while one was open for 1% of the time, Pallas kernels for 2%

profile of v7, /device:TPU:0, one launch (start us, length us, event | category | flops | bytes accessed | tf_op | source)
XLA Modules:
  0.0 131.3 jit_solution(6602326509757382248)
XLA Ops:
  2.5 2.2 %prepare.1 = bf16[32,7296]{1,0:T(8,128)(2,1)} custom-call(f32[1,7168]{1,0:T(1,128)} %bitcast.15, bf16[16,7168]{1,0:T(8,128)(2,1)} %refs_1_.1, bf16[16,7168]{1,0:T(8,128)(2,1)} %copy-done, s32[4,16]{1,0:T(4,128)} %bitcast.17, s32[4,16]{1,0:T(4,128)} %copy-done.1), custom_call_target="tpu_custom_call" | custom-call | flops 1376256 | bytes 917504 | tf_op jit(solution)/shard_map/prepare/pallas_call | solution.py:86
  4.7 4.0 %collective-permute-start.2 = (bf16[32,7296]{1,0:T(8,128)(2,1)}, bf16[32,7296]{1,0:T(8,128)(2,1)S(1)}, u32[]{:S(2)}, u32[]{:S(2)}) collective-permute-start(bf16[32,7296]{1,0:T(8,128)(2,1)} %prepare.1), channel_id=1, source_target_pairs={{0,16},{2,18},{4,20},{6,22},{8,24},{10,26},{12,28},{14,30},{16,0},... | collective-permute-start | bytes 1400840 | tf_op jit(solution)/shard_map/ppermute | solution.py:40
  10.2 9.1 %collective-permute-done.2.refs_0_ = bf16[32,7296]{1,0:T(8,128)(2,1)S(1)} collective-permute-done((bf16[32,7296]{1,0:T(8,128)(2,1)}, bf16[32,7296]{1,0:T(8,128)(2,1)S(1)}, u32[]{:S(2)}, u32[]{:S(2)}) %collective-permute-start.2) | collective-permute-done | bytes 466976 | tf_op jit(solution)/shard_map/ppermute | solution.py:40
  19.3 2.2 %collective-permute-start.4 = (bf16[32,7296]{1,0:T(8,128)(2,1)S(1)}, bf16[32,7296]{1,0:T(8,128)(2,1)S(1)}, u32[]{:S(2)}, u32[]{:S(2)}) collective-permute-start(bf16[32,7296]{1,0:T(8,128)(2,1)S(1)} %collective-permute-done.2.refs_0_), channel_id=1, source_target_pairs={{0,4},{2,6},{4,0},{6,2},{8,12},{10,14},{12,8},{14,10},{16,20},{18,... | collective-permute-start | bytes 1400840 | tf_op jit(solution)/shard_map/ppermute | solution.py:40
  22.9 5.0 %collective-permute-done.4.refs_2_ = bf16[32,7296]{1,0:T(8,128)(2,1)S(1)} collective-permute-done((bf16[32,7296]{1,0:T(8,128)(2,1)S(1)}, bf16[32,7296]{1,0:T(8,128)(2,1)S(1)}, u32[]{:S(2)}, u32[]{:S(2)}) %collective-permute-start.4) | collective-permute-done | bytes 466976 | tf_op jit(solution)/shard_map/ppermute | solution.py:40
  28.0 2.3 %collective-permute-start.6 = (bf16[32,7296]{1,0:T(8,128)(2,1)S(1)}, bf16[32,7296]{1,0:T(8,128)(2,1)S(1)}, u32[]{:S(2)}, u32[]{:S(2)}) collective-permute-start(bf16[32,7296]{1,0:T(8,128)(2,1)S(1)} %collective-permute-done.4.refs_2_), channel_id=1, source_target_pairs={{0,8},{2,10},{4,12},{6,14},{8,0},{10,2},{12,4},{14,6},{16,24},{18,... | collective-permute-start | bytes 1400840 | tf_op jit(solution)/shard_map/ppermute | solution.py:40
  30.3 3.2 %collective-permute-done.5.refs_3_ = bf16[32,7296]{1,0:T(8,128)(2,1)S(1)} collective-permute-done((bf16[32,7296]{1,0:T(8,128)(2,1)S(1)}, bf16[32,7296]{1,0:T(8,128)(2,1)S(1)}, u32[]{:S(2)}, u32[]{:S(2)}) %collective-permute-start.5) | collective-permute-done | bytes 466976 | tf_op jit(solution)/shard_map/ppermute | solution.py:40
  33.5 3.4 %collective-permute-done.6.refs_4_ = bf16[32,7296]{1,0:T(8,128)(2,1)S(1)} collective-permute-done((bf16[32,7296]{1,0:T(8,128)(2,1)S(1)}, bf16[32,7296]{1,0:T(8,128)(2,1)S(1)}, u32[]{:S(2)}, u32[]{:S(2)}) %collective-permute-start.6) | collective-permute-done | bytes 466976 | tf_op jit(solution)/shard_map/ppermute | solution.py:40
  36.9 3.6 %collective-permute-start.11 = (bf16[32,7296]{1,0:T(8,128)(2,1)S(1)}, bf16[32,7296]{1,0:T(8,128)(2,1)S(1)}, u32[]{:S(2)}, u32[]{:S(2)}) collective-permute-start(bf16[32,7296]{1,0:T(8,128)(2,1)S(1)} %collective-permute-done.6.refs_4_), channel_id=1, source_target_pairs={{0,2},{2,0},{4,6},{6,4},{8,10},{10,8},{12,14},{14,12},{16,18},{18,... | collective-permute-start | bytes 1400840 | tf_op jit(solution)/shard_map/ppermute | solution.py:40
  43.5 3.8 %collective-permute-done.11 = bf16[32,7296]{1,0:T(8,128)(2,1)S(1)} collective-permute-done((bf16[32,7296]{1,0:T(8,128)(2,1)S(1)}, bf16[32,7296]{1,0:T(8,128)(2,1)S(1)}, u32[]{:S(2)}, u32[]{:S(2)}) %collective-permute-start.11) | collective-permute-done | bytes 466976 | tf_op jit(solution)/shard_map/ppermute | solution.py:40
  47.4 6.1 %collective-permute-done.8.refs_5_ = bf16[32,7296]{1,0:T(8,128)(2,1)S(1)} collective-permute-done((bf16[32,7296]{1,0:T(8,128)(2,1)S(1)}, bf16[32,7296]{1,0:T(8,128)(2,1)S(1)}, u32[]{:S(2)}, u32[]{:S(2)}) %collective-permute-start.8) | collective-permute-done | bytes 466976 | tf_op jit(solution)/shard_map/ppermute | solution.py:40
  53.5 5.0 %collective-permute-done.10.refs_6_ = bf16[32,7296]{1,0:T(8,128)(2,1)S(1)} collective-permute-done((bf16[32,7296]{1,0:T(8,128)(2,1)S(1)}, bf16[32,7296]{1,0:T(8,128)(2,1)S(1)}, u32[]{:S(2)}, u32[]{:S(2)}) %collective-permute-start.10) | collective-permute-done | bytes 466976 | tf_op jit(solution)/shard_map/ppermute | solution.py:40
  58.5 15.1 %experts.1 = (bf16[32,3584]{1,0:T(8,128)(2,1)S(1)}, bf16[32,3584]{1,0:T(8,128)(2,1)S(1)}, bf16[32,3584]{1,0:T(8,128)(2,1)S(1)}, bf16[32,3584]{1,0:T(8,128)(2,1)S...) custom-call(s32[2]{0:T(128)S(1)} %pad_add_fusion.ids_ref, ...), custom_call_target="tpu_custom_call" | custom-call | flops 5637144576 | bytes 29360128 | tf_op jit(solution)/shard_map/experts/pallas_call | solution.py:191
  73.7 3.4 %collective-permute-start.14 = (bf16[32,3584]{1,0:T(8,128)(2,1)S(1)}, bf16[32,3584]{1,0:T(8,128)(2,1)S(1)}, u32[]{:S(2)}, u32[]{:S(2)}) collective-permute-start(bf16[32,3584]{1,0:T(8,128)(2,1)S(1)} %get-tuple-element.50), channel_id=1, source_target_pairs={{0,2},{2,0},{4,6},{6,4},{8,10},{10,8},{12,14},{14,12},{16,18},{18,... | collective-permute-start | bytes 688136 | tf_op jit(solution)/shard_map/ppermute | solution.py:40
  79.2 2.4 %collective-permute-start.15 = (bf16[32,3584]{1,0:T(8,128)(2,1)S(1)}, bf16[32,3584]{1,0:T(8,128)(2,1)S(1)}, u32[]{:S(2)}, u32[]{:S(2)}) collective-permute-start(bf16[32,3584]{1,0:T(8,128)(2,1)S(1)} %get-tuple-element.54), channel_id=1, source_target_pairs={{0,2},{2,0},{4,6},{6,4},{8,10},{10,8},{12,14},{14,12},{16,18},{18,... | collective-permute-start | bytes 688136 | tf_op jit(solution)/shard_map/ppermute | solution.py:40
  81.6 2.4 %collective-permute-done.14 = bf16[32,3584]{1,0:T(8,128)(2,1)S(1)} collective-permute-done((bf16[32,3584]{1,0:T(8,128)(2,1)S(1)}, bf16[32,3584]{1,0:T(8,128)(2,1)S(1)}, u32[]{:S(2)}, u32[]{:S(2)}) %collective-permute-start.14) | collective-permute-done | bytes 229408 | tf_op jit(solution)/shard_map/ppermute | solution.py:40
  84.1 1.7 %collective-permute-start.17 = (bf16[32,3584]{1,0:T(8,128)(2,1)S(1)}, bf16[32,3584]{1,0:T(8,128)(2,1)S(1)}, u32[]{:S(2)}, u32[]{:S(2)}) collective-permute-start(bf16[32,3584]{1,0:T(8,128)(2,1)S(1)} %add_convert_fusion.8), channel_id=1, source_target_pairs={{0,8},{2,10},{4,12},{6,14},{8,0},{10,2},{12,4},{14,6},{16,24},{18,... | collective-permute-start | bytes 688136 | tf_op jit(solution)/shard_map/ppermute | solution.py:40
  86.0 3.6 %collective-permute-done.15 = bf16[32,3584]{1,0:T(8,128)(2,1)S(1)} collective-permute-done((bf16[32,3584]{1,0:T(8,128)(2,1)S(1)}, bf16[32,3584]{1,0:T(8,128)(2,1)S(1)}, u32[]{:S(2)}, u32[]{:S(2)}) %collective-permute-start.15) | collective-permute-done | bytes 229408 | tf_op jit(solution)/shard_map/ppermute | solution.py:40
  95.1 7.7 %collective-permute-done.20 = bf16[32,3584]{1,0:T(8,128)(2,1)S(1)} collective-permute-done((bf16[32,3584]{1,0:T(8,128)(2,1)S(1)}, bf16[32,3584]{1,0:T(8,128)(2,1)S(1)}, u32[]{:S(2)}, u32[]{:S(2)}) %collective-permute-start.20) | collective-permute-done | bytes 229408 | tf_op jit(solution)/shard_map/ppermute | solution.py:40
  107.0 4.4 %collective-permute-done.23 = bf16[32,3584]{1,0:T(8,128)(2,1)S(1)} collective-permute-done((bf16[32,3584]{1,0:T(8,128)(2,1)S(1)}, bf16[32,3584]{1,0:T(8,128)(2,1)S(1)}, u32[]{:S(2)}, u32[]{:S(2)}) %collective-permute-start.23) | collective-permute-done | bytes 229408 | tf_op jit(solution)/shard_map/ppermute | solution.py:40
  111.4 6.2 %collective-permute-done.24 = bf16[32,3584]{1,0:T(8,128)(2,1)S(1)} collective-permute-done((bf16[32,3584]{1,0:T(8,128)(2,1)S(1)}, bf16[32,3584]{1,0:T(8,128)(2,1)S(1)}, u32[]{:S(2)}, u32[]{:S(2)}) %collective-permute-start.24) | collective-permute-done | bytes 229408 | tf_op jit(solution)/shard_map/ppermute | solution.py:40
  121.4 2.3 %collective-permute-done.25 = bf16[32,3584]{1,0:T(8,128)(2,1)S(1)} collective-permute-done((bf16[32,3584]{1,0:T(8,128)(2,1)S(1)}, bf16[32,3584]{1,0:T(8,128)(2,1)S(1)}, u32[]{:S(2)}, u32[]{:S(2)}) %collective-permute-start.25) | collective-permute-done | bytes 229408 | tf_op jit(solution)/shard_map/ppermute | solution.py:40
  123.9 2.3 %collective-permute-done.29 = bf16[32,3584]{1,0:T(8,128)(2,1)S(1)} collective-permute-done((bf16[32,3584]{1,0:T(8,128)(2,1)S(1)}, bf16[32,3584]{1,0:T(8,128)(2,1)S(1)}, u32[]{:S(2)}, u32[]{:S(2)}) %collective-permute-start.29) | collective-permute-done | bytes 229408 | tf_op jit(solution)/shard_map/ppermute | solution.py:40
  126.1 2.9 %collective-permute-done.27 = bf16[32,3584]{1,0:T(8,128)(2,1)S(1)} collective-permute-done((bf16[32,3584]{1,0:T(8,128)(2,1)S(1)}, bf16[32,3584]{1,0:T(8,128)(2,1)S(1)}, u32[]{:S(2)}, u32[]{:S(2)}) %collective-permute-start.27) | collective-permute-done | bytes 229408 | tf_op jit(solution)/shard_map/ppermute | solution.py:40
  (64 shorter events, 26.7 us)
Async XLA Ops:
  1.8 39.6 %collective-permute-start.7 = (bf16[7168,256]{1,0:T(8,128)(2,1)}, bf16[7168,256]{1,0:T(8,128)(2,1)}, u32[]{:S(2)}, u32[]{:S(2)}) collective-permute-start(bf16[7168,256]{1,0:T(8,128)(2,1)} %bitcast.8), channel_id=1, source_target_pairs={{0,1},{1,0},{2,3},{3,2},{4,5},{5,4},{6,7},{7,6},{8,9},{9,8},{10,11... | collective-permute-start | bytes 11010056 | tf_op jit(solution)/shard_map/ppermute | solution.py:48
  2.2 40.8 %collective-permute-start.9 = (bf16[7168,256]{1,0:T(8,128)(2,1)}, bf16[7168,256]{1,0:T(8,128)(2,1)}, u32[]{:S(2)}, u32[]{:S(2)}) collective-permute-start(bf16[7168,256]{1,0:T(8,128)(2,1)} %bitcast.10), channel_id=1, source_target_pairs={{0,1},{1,0},{2,3},{3,2},{4,5},{5,4},{6,7},{7,6},{8,9},{9,8},{10,11... | collective-permute-start | bytes 11010056 | tf_op jit(solution)/shard_map/ppermute | solution.py:48
  4.7 14.5 %collective-permute-start.2 = (bf16[32,7296]{1,0:T(8,128)(2,1)}, bf16[32,7296]{1,0:T(8,128)(2,1)S(1)}, u32[]{:S(2)}, u32[]{:S(2)}) collective-permute-start(bf16[32,7296]{1,0:T(8,128)(2,1)} %prepare.1), channel_id=1, source_target_pairs={{0,16},{2,18},{4,20},{6,22},{8,24},{10,26},{12,28},{14,30},{16,0},... | collective-permute-start | bytes 1400840 | tf_op jit(solution)/shard_map/ppermute | solution.py:40
  8.7 38.7 %collective-permute-start.12 = (bf16[256,7168]{1,0:T(8,128)(2,1)}, bf16[256,7168]{1,0:T(8,128)(2,1)}, u32[]{:S(2)}, u32[]{:S(2)}) collective-permute-start(bf16[256,7168]{1,0:T(8,128)(2,1)} %bitcast.12), channel_id=1, source_target_pairs={{0,1},{1,0},{2,3},{3,2},{4,5},{5,4},{6,7},{7,6},{8,9},{9,8},{10,11... | collective-permute-start | bytes 11010056 | tf_op jit(solution)/shard_map/ppermute | solution.py:48
  8.7 12.7 %collective-permute-start.3 = (bf16[32,7296]{1,0:T(8,128)(2,1)}, bf16[32,7296]{1,0:T(8,128)(2,1)S(1)}, u32[]{:S(2)}, u32[]{:S(2)}) collective-permute-start(bf16[32,7296]{1,0:T(8,128)(2,1)} %prepare.1), channel_id=1, source_target_pairs={{0,2},{2,0},{4,6},{6,4},{8,10},{10,8},{12,14},{14,12},{16,18},{18,... | collective-permute-start | bytes 1400840 | tf_op jit(solution)/shard_map/ppermute | solution.py:40
  19.3 8.7 %collective-permute-start.4 = (bf16[32,7296]{1,0:T(8,128)(2,1)S(1)}, bf16[32,7296]{1,0:T(8,128)(2,1)S(1)}, u32[]{:S(2)}, u32[]{:S(2)}) collective-permute-start(bf16[32,7296]{1,0:T(8,128)(2,1)S(1)} %collective-permute-done.2.refs_0_), channel_id=1, source_target_pairs={{0,4},{2,6},{4,0},{6,2},{8,12},{10,14},{12,8},{14,10},{16,20},{18,... | collective-permute-start | bytes 1400840 | tf_op jit(solution)/shard_map/ppermute | solution.py:40
  21.4 12.1 %collective-permute-start.5 = (bf16[32,7296]{1,0:T(8,128)(2,1)S(1)}, bf16[32,7296]{1,0:T(8,128)(2,1)S(1)}, u32[]{:S(2)}, u32[]{:S(2)}) collective-permute-start(bf16[32,7296]{1,0:T(8,128)(2,1)S(1)} %collective-permute-done.2.refs_0_), channel_id=1, source_target_pairs={{0,2},{2,0},{4,6},{6,4},{8,10},{10,8},{12,14},{14,12},{16,18},{18,... | collective-permute-start | bytes 1400840 | tf_op jit(solution)/shard_map/ppermute | solution.py:40
  28.0 8.9 %collective-permute-start.6 = (bf16[32,7296]{1,0:T(8,128)(2,1)S(1)}, bf16[32,7296]{1,0:T(8,128)(2,1)S(1)}, u32[]{:S(2)}, u32[]{:S(2)}) collective-permute-start(bf16[32,7296]{1,0:T(8,128)(2,1)S(1)} %collective-permute-done.4.refs_2_), channel_id=1, source_target_pairs={{0,8},{2,10},{4,12},{6,14},{8,0},{10,2},{12,4},{14,6},{16,24},{18,... | collective-permute-start | bytes 1400840 | tf_op jit(solution)/shard_map/ppermute | solution.py:40
  36.9 10.4 %collective-permute-start.11 = (bf16[32,7296]{1,0:T(8,128)(2,1)S(1)}, bf16[32,7296]{1,0:T(8,128)(2,1)S(1)}, u32[]{:S(2)}, u32[]{:S(2)}) collective-permute-start(bf16[32,7296]{1,0:T(8,128)(2,1)S(1)} %collective-permute-done.6.refs_4_), channel_id=1, source_target_pairs={{0,2},{2,0},{4,6},{6,4},{8,10},{10,8},{12,14},{14,12},{16,18},{18,... | collective-permute-start | bytes 1400840 | tf_op jit(solution)/shard_map/ppermute | solution.py:40
  41.5 12.1 %collective-permute-start.8 = (bf16[32,7296]{1,0:T(8,128)(2,1)S(1)}, bf16[32,7296]{1,0:T(8,128)(2,1)S(1)}, u32[]{:S(2)}, u32[]{:S(2)}) collective-permute-start(bf16[32,7296]{1,0:T(8,128)(2,1)S(1)} %collective-permute-done.3.refs_1_), channel_id=1, source_target_pairs={{0,4},{2,6},{4,0},{6,2},{8,12},{10,14},{12,8},{14,10},{16,20},{18,... | collective-permute-start | bytes 1400840 | tf_op jit(solution)/shard_map/ppermute | solution.py:40
  43.0 15.5 %collective-permute-start.10 = (bf16[32,7296]{1,0:T(8,128)(2,1)S(1)}, bf16[32,7296]{1,0:T(8,128)(2,1)S(1)}, u32[]{:S(2)}, u32[]{:S(2)}) collective-permute-start(bf16[32,7296]{1,0:T(8,128)(2,1)S(1)} %collective-permute-done.5.refs_3_), channel_id=1, source_target_pairs={{0,4},{2,6},{4,0},{6,2},{8,12},{10,14},{12,8},{14,10},{16,20},{18,... | collective-permute-start | bytes 1400840 | tf_op jit(solution)/shard_map/ppermute | solution.py:40
  73.7 10.4 %collective-permute-start.14 = (bf16[32,3584]{1,0:T(8,128)(2,1)S(1)}, bf16[32,3584]{1,0:T(8,128)(2,1)S(1)}, u32[]{:S(2)}, u32[]{:S(2)}) collective-permute-start(bf16[32,3584]{1,0:T(8,128)(2,1)S(1)} %get-tuple-element.50), channel_id=1, source_target_pairs={{0,2},{2,0},{4,6},{6,4},{8,10},{10,8},{12,14},{14,12},{16,18},{18,... | collective-permute-start | bytes 688136 | tf_op jit(solution)/shard_map/ppermute | solution.py:40
  77.1 8.8 %collective-permute-start.13 = (bf16[32,3584]{1,0:T(8,128)(2,1)S(1)}, bf16[32,3584]{1,0:T(8,128)(2,1)S(1)}, u32[]{:S(2)}, u32[]{:S(2)}) collective-permute-start(bf16[32,3584]{1,0:T(8,128)(2,1)S(1)} %get-tuple-element.53), channel_id=1, source_target_pairs={{0,4},{2,6},{4,0},{6,2},{8,12},{10,14},{12,8},{14,10},{16,20},{18,... | collective-permute-start | bytes 688136 | tf_op jit(solution)/shard_map/ppermute | solution.py:40
  79.2 10.4 %collective-permute-start.15 = (bf16[32,3584]{1,0:T(8,128)(2,1)S(1)}, bf16[32,3584]{1,0:T(8,128)(2,1)S(1)}, u32[]{:S(2)}, u32[]{:S(2)}) collective-permute-start(bf16[32,3584]{1,0:T(8,128)(2,1)S(1)} %get-tuple-element.54), channel_id=1, source_target_pairs={{0,2},{2,0},{4,6},{6,4},{8,10},{10,8},{12,14},{14,12},{16,18},{18,... | collective-permute-start | bytes 688136 | tf_op jit(solution)/shard_map/ppermute | solution.py:40
  84.1 9.3 %collective-permute-start.17 = (bf16[32,3584]{1,0:T(8,128)(2,1)S(1)}, bf16[32,3584]{1,0:T(8,128)(2,1)S(1)}, u32[]{:S(2)}, u32[]{:S(2)}) collective-permute-start(bf16[32,3584]{1,0:T(8,128)(2,1)S(1)} %add_convert_fusion.8), channel_id=1, source_target_pairs={{0,8},{2,10},{4,12},{6,14},{8,0},{10,2},{12,4},{14,6},{16,24},{18,... | collective-permute-start | bytes 688136 | tf_op jit(solution)/shard_map/ppermute | solution.py:40
  89.7 13.1 %collective-permute-start.16 = (bf16[32,3584]{1,0:T(8,128)(2,1)S(1)}, bf16[32,3584]{1,0:T(8,128)(2,1)S(1)}, u32[]{:S(2)}, u32[]{:S(2)}) collective-permute-start(bf16[32,3584]{1,0:T(8,128)(2,1)S(1)} %add_convert_fusion.9), channel_id=1, source_target_pairs={{0,2},{2,0},{4,6},{6,4},{8,10},{10,8},{12,14},{14,12},{16,18},{18,... | collective-permute-start | bytes 688136 | tf_op jit(solution)/shard_map/ppermute | solution.py:40
  90.4 16.2 %collective-permute-start.21 = (bf16[32,3584]{1,0:T(8,128)(2,1)S(1)}, bf16[32,3584]{1,0:T(8,128)(2,1)S(1)}, u32[]{:S(2)}, u32[]{:S(2)}) collective-permute-start(bf16[32,3584]{1,0:T(8,128)(2,1)S(1)} %add_convert_fusion.4), channel_id=1, source_target_pairs={{0,2},{2,0},{4,6},{6,4},{8,10},{10,8},{12,14},{14,12},{16,18},{18,... | collective-permute-start | bytes 688136 | tf_op jit(solution)/shard_map/ppermute | solution.py:40
  91.8 11.0 %collective-permute-start.20 = (bf16[32,3584]{1,0:T(8,128)(2,1)S(1)}, bf16[32,3584]{1,0:T(8,128)(2,1)S(1)}, u32[]{:S(2)}, u32[]{:S(2)}) collective-permute-start(bf16[32,3584]{1,0:T(8,128)(2,1)S(1)} %add_convert_fusion.5), channel_id=1, source_target_pairs={{0,8},{2,10},{4,12},{6,14},{8,0},{10,2},{12,4},{14,6},{16,24},{18,... | collective-permute-start | bytes 688136 | tf_op jit(solution)/shard_map/ppermute | solution.py:40
  93.5 13.0 %collective-permute-start.19 = (bf16[32,3584]{1,0:T(8,128)(2,1)S(1)}, bf16[32,3584]{1,0:T(8,128)(2,1)S(1)}, u32[]{:S(2)}, u32[]{:S(2)}) collective-permute-start(bf16[32,3584]{1,0:T(8,128)(2,1)S(1)} %add_convert_fusion.7), channel_id=1, source_target_pairs={{0,4},{2,6},{4,0},{6,2},{8,12},{10,14},{12,8},{14,10},{16,20},{18,... | collective-permute-start | bytes 688136 | tf_op jit(solution)/shard_map/ppermute | solution.py:40
  102.8 8.6 %collective-permute-start.23 = (bf16[32,3584]{1,0:T(8,128)(2,1)S(1)}, bf16[32,3584]{1,0:T(8,128)(2,1)S(1)}, u32[]{:S(2)}, u32[]{:S(2)}) collective-permute-start(bf16[32,3584]{1,0:T(8,128)(2,1)S(1)} %get-tuple-element.67), channel_id=1, source_target_pairs={{0,4},{2,6},{4,0},{6,2},{8,12},{10,14},{12,8},{14,10},{16,20},{18,... | collective-permute-start | bytes 688136 | tf_op jit(solution)/shard_map/ppermute | solution.py:40
  104.4 14.9 %collective-permute-start.28 = (bf16[32,3584]{1,0:T(8,128)(2,1)S(1)}, bf16[32,3584]{1,0:T(8,128)(2,1)S(1)}, u32[]{:S(2)}, u32[]{:S(2)}) collective-permute-start(bf16[32,3584]{1,0:T(8,128)(2,1)S(1)} %get-tuple-element.75), channel_id=1, source_target_pairs={{0,4},{2,6},{4,0},{6,2},{8,12},{10,14},{12,8},{14,10},{16,20},{18,... | collective-permute-start | bytes 688136 | tf_op jit(solution)/shard_map/ppermute | solution.py:40
  104.9 12.7 %collective-permute-start.24 = (bf16[32,3584]{1,0:T(8,128)(2,1)S(1)}, bf16[32,3584]{1,0:T(8,128)(2,1)S(1)}, u32[]{:S(2)}, u32[]{:S(2)}) collective-permute-start(bf16[32,3584]{1,0:T(8,128)(2,1)S(1)} %add_convert_fusion.2), channel_id=1, source_target_pairs={{0,4},{2,6},{4,0},{6,2},{8,12},{10,14},{12,8},{14,10},{16,20},{18,... | collective-permute-start | bytes 688136 | tf_op jit(solution)/shard_map/ppermute | solution.py:40
  106.6 14.8 %collective-permute-start.22 = (bf16[32,3584]{1,0:T(8,128)(2,1)S(1)}, bf16[32,3584]{1,0:T(8,128)(2,1)S(1)}, u32[]{:S(2)}, u32[]{:S(2)}) collective-permute-start(bf16[32,3584]{1,0:T(8,128)(2,1)S(1)} %add_convert_fusion.6), channel_id=1, source_target_pairs={{0,16},{2,18},{4,20},{6,22},{8,24},{10,26},{12,28},{14,30},{16,0},... | collective-permute-start | bytes 688136 | tf_op jit(solution)/shard_map/ppermute | solution.py:40
  119.9 9.2 %collective-permute-start.27 = (bf16[32,3584]{1,0:T(8,128)(2,1)S(1)}, bf16[32,3584]{1,0:T(8,128)(2,1)S(1)}, u32[]{:S(2)}, u32[]{:S(2)}) collective-permute-start(bf16[32,3584]{1,0:T(8,128)(2,1)S(1)} %add_convert_fusion.1), channel_id=1, source_target_pairs={{0,16},{2,18},{4,20},{6,22},{8,24},{10,26},{12,28},{14,30},{16,0},... | collective-permute-start | bytes 688136 | tf_op jit(solution)/shard_map/ppermute | solution.py:40
  (9 other events, 31.3 us)

commit v8 on v7

v8 whole, which is shorter than its diff:
```python
import functools

import jax
import jax.numpy as jnp
from jax import lax
from jax.experimental import pallas as pl
from jax.experimental.pallas import tpu as pltpu
from jax.sharding import PartitionSpec as P

SPLIT = 4
LANES = 128

EPSILON = 1e-06
ROUTE_SCALE = 2.5
PREPARE_VMEM = 60 * 1024 * 1024
EXPERTS_VMEM = 47 * 1024 * 1024

PLAN_16 = ((0, 1, 2), (0, 8, 4), (2, 4, 1), (2, 2, 2), (2, 1, 0), (3, 1, 2), (4, 1, 8), (6, 2, 4))
RETURN_16 = tuple((slot, PLAN_16[slot - 1]) for slot in (8, 7, 6, 4, 5, 3, 2, 1))
OPEN_16 = (2, 2, 2, 2, 2, 3, 4, 4)
WEIGHTS_END_16 = {6: 0, 7: 1}
OPEN_RETURN = 4
EARLY = 5


def plan_for(ep_count, grp_count):
    if ep_count == 16 and grp_count == 2:
        return PLAN_16, RETURN_16, OPEN_16, WEIGHTS_END_16, True
    plan = []
    for r in range(1, ep_count):
        bit = 1 << (r.bit_length() - 1)
        plan.append((r ^ bit, bit, bit))
    slots = len(plan)
    back = tuple((slot, plan[slot - 1]) for slot in range(slots, 0, -1))
    return tuple(plan), back, (OPEN_RETURN,) * slots, {}, False


def across(value, bits, ep_count):
    pairs = [(i * 2 + c, (i ^ bit) * 2 + c) for c, bit in enumerate(bits) if bit for i in range(ep_count)]
    return lax.ppermute(value, ("ep", "grp"), pairs)


def after(value, earlier):
    return lax.optimization_barrier((value, *earlier))[0] if earlier else value


def between_cores(value):
    return lax.ppermute(value, "grp", [(0, 1), (1, 0)])


def prepare_kernel(count, *refs):
    sources, out_ref, targets, sems = refs[: 2 * count + 1], refs[2 * count + 1], refs[2 * count + 2 : -1], refs[-1]
    copies = [
        pltpu.make_async_copy(source, target, sems.at[i]) for i, (source, target) in enumerate(zip(sources, targets))
    ]
    for copy in copies:
        copy.start()
    for copy in copies:
        copy.wait()
    gain = targets[0][...]
    for i in range(count):
        values = targets[1 + i][...].astype(jnp.float32)
        routes = targets[1 + count + i][...]
        rows, width = values.shape
        span = pl.ds(i * rows, rows)
        square_mean = jnp.mean(values * values, axis=1, keepdims=True)
        normed = values * lax.rsqrt(square_mean + EPSILON) * gain
        out_ref[span, :width] = normed.astype(jnp.bfloat16)
        experts_down = lax.broadcasted_iota(jnp.int32, (LANES, rows), 0)
        named = jnp.zeros((LANES, rows), jnp.float32)
        for k in range(routes.shape[0]):
            named = jnp.where(experts_down == routes[k : k + 1, :], 1.0, named)
        same = lax.broadcasted_iota(jnp.int32, (rows, rows), 0) == lax.broadcasted_iota(jnp.int32, (rows, rows), 1)
        out_ref[span, width:] = lax.dot_general(
            same.astype(jnp.bfloat16),
            named.astype(jnp.bfloat16),
            (((1,), (1,)), ((), ())),
            preferred_element_type=jnp.float32,
        ).astype(jnp.bfloat16)


def prepare(gain, hiddens, routes):
    rows, width = hiddens[0].shape
    count = len(hiddens)
    operands = (gain[None, :], *hiddens, *routes)
    return pl.pallas_call(
        functools.partial(prepare_kernel, count),
        out_shape=jax.ShapeDtypeStruct((count * rows, width + LANES), jnp.bfloat16),
        in_specs=[pl.BlockSpec(memory_space=pl.ANY)] * len(operands),
        scratch_shapes=[pltpu.VMEM(x.shape, x.dtype) for x in operands] + [pltpu.SemaphoreType.DMA((len(operands),))],
        compiler_params=pltpu.CompilerParams(vmem_limit_bytes=PREPARE_VMEM),
        cost_estimate=pl.CostEstimate(
            flops=6 * count * rows * width, bytes_accessed=4 * count * rows * width, transcendentals=count * rows
        ),
        name="prepare",
    )(*operands)


def add_products(step, k_tile, token_refs, router_ref, weight_refs, gates_ref, logits_ref):
    hidden_units = weight_refs[0].shape[1]
    columns = pl.ds(pl.multiple_of(step * k_tile, LANES), k_tile)
    tokens = jnp.concatenate([ref[:, columns] for ref in token_refs], axis=0)
    parts = [jnp.dot(tokens, ref[...], preferred_element_type=jnp.float32) for ref in weight_refs]
    logits = lax.dot_general(
        tokens, router_ref[...], (((1,), (1,)), ((), ())), preferred_element_type=jnp.float32
    )

    @pl.when(step == 0)
    def _():
        for i, part in enumerate(parts):
            gates_ref[:, i * hidden_units : (i + 1) * hidden_units] = part
        logits_ref[...] = logits

    @pl.when(step > 0)
    def _():
        for i, part in enumerate(parts):
            gates_ref[:, i * hidden_units : (i + 1) * hidden_units] += part
        logits_ref[...] += logits


def activate(width, ids_ref, token_refs, gates_ref, logits_ref):
    half = gates_ref.shape[1] // 2
    act = (jax.nn.silu(gates_ref[:, :half]) * gates_ref[:, half:]).astype(jnp.bfloat16)
    named = jnp.concatenate([ref[:, width : width + LANES] for ref in token_refs], axis=0)
    chosen = named[:, : logits_ref.shape[1]].astype(jnp.float32) * jax.nn.sigmoid(logits_ref[...])
    weights = ROUTE_SCALE * chosen / jnp.sum(chosen, axis=1, keepdims=True)
    lanes = lax.broadcasted_iota(jnp.int32, weights.shape, 1)
    columns = []
    for i in range(2):
        column = jnp.sum(jnp.where(lanes == ids_ref[i], weights, 0.0), axis=1, keepdims=True)
        columns.append(jnp.broadcast_to(column, (column.shape[0], LANES)))
    return act, jnp.concatenate(columns, axis=1)


def early_kernel(blocks, k_steps, k_tile, ids_ref, *refs):
    token_refs, router_ref, weight_refs = refs[:blocks], refs[blocks], refs[blocks + 1 : blocks + 5]
    act_ref, coeff_ref, gates_ref, logits_ref = refs[blocks + 5 :]
    step = pl.program_id(0)
    add_products(step, k_tile, token_refs, router_ref, weight_refs, gates_ref, logits_ref)

    @pl.when(step == k_steps - 1)
    def _():
        act_ref[...], coeff_ref[...] = activate(k_steps * k_tile, ids_ref, token_refs, gates_ref, logits_ref)


def early(ids, token_blocks, router_t, gates, ups):
    blocks = len(token_blocks)
    width, hidden_units = gates[0].shape
    rows = blocks * token_blocks[0].shape[0]
    k_steps = 4
    k_tile = width // k_steps
    return pl.pallas_call(
        functools.partial(early_kernel, blocks, k_steps, k_tile),
        grid_spec=pltpu.PrefetchScalarGridSpec(
            num_scalar_prefetch=1,
            grid=(k_steps,),
            in_specs=[pl.BlockSpec(token_blocks[0].shape, lambda step, ids_ref: (0, 0))] * blocks
            + [pl.BlockSpec((router_t.shape[0], k_tile), lambda step, ids_ref: (0, step))]
            + [pl.BlockSpec((k_tile, hidden_units), lambda step, ids_ref: (step, 0))] * 4,
            out_specs=[
                pl.BlockSpec((rows, 2 * hidden_units), lambda step, ids_ref: (0, 0)),
                pl.BlockSpec((rows, 2 * LANES), lambda step, ids_ref: (0, 0)),
            ],
            scratch_shapes=[
                pltpu.VMEM((rows, 4 * hidden_units), jnp.float32),
                pltpu.VMEM((rows, router_t.shape[0]), jnp.float32),
            ],
        ),
        out_shape=[
            jax.ShapeDtypeStruct((rows, 2 * hidden_units), jnp.bfloat16),
            jax.ShapeDtypeStruct((rows, 2 * LANES), jnp.float32),
        ],
        compiler_params=pltpu.CompilerParams(vmem_limit_bytes=EXPERTS_VMEM),
        cost_estimate=pl.CostEstimate(
            flops=8 * rows * width * hidden_units,
            bytes_accessed=8 * width * hidden_units + 2 * rows * width,
            transcendentals=2 * rows * hidden_units,
        ),
        name="early",
    )(ids, *token_blocks, router_t, *gates, *ups)


def experts_kernel(blocks, done_rows, rows, k_steps, k_tile, ids_ref, *refs):
    token_refs, router_ref = refs[:blocks], refs[blocks]
    weight_refs, down0_ref, down1_ref = refs[blocks + 1 : blocks + 5], refs[blocks + 5], refs[blocks + 6]
    refs = refs[blocks + 7 :]
    if done_rows:
        done_act_ref, done_coeff_ref, *refs = refs
    *out_refs, gates_ref, logits_ref, act_ref, coeff_ref = refs
    hidden_units = weight_refs[0].shape[1]
    step = pl.program_id(0)

    @pl.when(step < k_steps)
    def _():
        add_products(step, k_tile, token_refs, router_ref, weight_refs, gates_ref, logits_ref)

    @pl.when(step == k_steps - 1)
    def _():
        act, coeff = activate(k_steps * k_tile, ids_ref, token_refs, gates_ref, logits_ref)
        act_ref[done_rows:, :] = act
        coeff_ref[done_rows:, :] = coeff
        if done_rows:
            act_ref[:done_rows, :] = done_act_ref[...]
            coeff_ref[:done_rows, :] = done_coeff_ref[...]

    @pl.when(step >= k_steps)
    def _():
        total = coeff_ref[:, 0:1] * jnp.dot(
            act_ref[:, :hidden_units], down0_ref[...], preferred_element_type=jnp.float32
        ) + coeff_ref[:, LANES : LANES + 1] * jnp.dot(
            act_ref[:, hidden_units:], down1_ref[...], preferred_element_type=jnp.float32
        )
        for i, ref in enumerate(out_refs):
            ref[...] = total[i * rows : (i + 1) * rows].astype(jnp.bfloat16)


def experts(ids, token_blocks, done, router_t, gates, ups, downs):
    blocks = len(token_blocks)
    rows = token_blocks[0].shape[0]
    width, hidden_units = gates[0].shape
    k_steps = n_steps = 4
    k_tile, n_tile = width // k_steps, width // n_steps
    late_rows = blocks * rows
    done_rows = done[0].shape[0] if done else 0
    all_rows = done_rows + late_rows
    outs = all_rows // rows

    def at_k(step):
        return jnp.minimum(step, k_steps - 1)

    def at_n(step):
        return jnp.maximum(step - k_steps, 0)

    in_specs = [pl.BlockSpec(token_blocks[0].shape, lambda step, ids_ref: (0, 0))] * blocks
    in_specs += [pl.BlockSpec((router_t.shape[0], k_tile), lambda step, ids_ref: (0, at_k(step)))]
    in_specs += [pl.BlockSpec((k_tile, hidden_units), lambda step, ids_ref: (at_k(step), 0))] * 4
    in_specs += [pl.BlockSpec((hidden_units, n_tile), lambda step, ids_ref: (0, at_n(step)))] * 2
    in_specs += [pl.BlockSpec(x.shape, lambda step, ids_ref: (0, 0)) for x in done]
    return pl.pallas_call(
        functools.partial(experts_kernel, blocks, done_rows, rows, k_steps, k_tile),
        grid_spec=pltpu.PrefetchScalarGridSpec(
            num_scalar_prefetch=1,
            grid=(k_steps + n_steps,),
            in_specs=in_specs,
            out_specs=[pl.BlockSpec((rows, n_tile), lambda step, ids_ref: (0, at_n(step)))] * outs,
            scratch_shapes=[
                pltpu.VMEM((late_rows, 4 * hidden_units), jnp.float32),
                pltpu.VMEM((late_rows, router_t.shape[0]), jnp.float32),
                pltpu.VMEM((all_rows, 2 * hidden_units), jnp.bfloat16),
                pltpu.VMEM((all_rows, 2 * LANES), jnp.float32),
            ],
        ),
        out_shape=[jax.ShapeDtypeStruct((rows, width), jnp.bfloat16)] * outs,
        compiler_params=pltpu.CompilerParams(vmem_limit_bytes=EXPERTS_VMEM),
        cost_estimate=pl.CostEstimate(
            flops=(8 * late_rows + 4 * all_rows) * width * hidden_units,
            bytes_accessed=12 * width * hidden_units + 4 * all_rows * width,
            transcendentals=2 * late_rows * hidden_units,
        ),
        name="experts",
    )(ids, *token_blocks, router_t, *gates, *ups, *downs, *done)


def local(hidden, gain, router_w, routes, w_gate, w_up, w_down):
    ep_count, grp_count = lax.axis_size("ep"), lax.axis_size("grp")
    local_experts = ep_count // SPLIT
    expert_count = local_experts * grp_count
    place, core = lax.axis_index("ep") // SPLIT, lax.axis_index("grp")
    plan, return_plan, most_open, weights_end, paired = plan_for(ep_count, grp_count)
    rows = hidden.shape[0]
    hiddens, chosen = [hidden], [routes.T]
    if paired:
        hiddens.append(between_cores(hidden))
        chosen.append(between_cores(routes.T))
    own = prepare(gain, hiddens, chosen)
    weights = [(w[0, 0], between_cores(after(w[0, 0], hiddens[1:] + chosen[1:]))) for w in (w_gate, w_up, w_down)]
    held = [own]
    for slot, (parent, *bits) in enumerate(plan, 1):
        ended = held[1 : slot + 1 - most_open[slot - 1]]
        if slot in weights_end:
            ended.append(weights[weights_end[slot]][1])
        held.append(across(after(held[parent], ended), bits, ep_count))
    first = 0
    if paired:
        first = 1
        spare = [0 in bits for _, *bits in plan].index(True) + 1
        held[spare] = jnp.where(core == 1, own, held[spare])

    ids = jnp.stack([core * local_experts + place, (1 - core) * local_experts + place]).astype(jnp.int32)
    router_t = jnp.pad(router_w.T, ((0, -expert_count % 16), (0, 0)))
    done = early(ids, held[1 : 1 + EARLY], router_t, *weights[:2]) if paired else ()
    outs = experts(ids, held[1 + EARLY :] if paired else held, done, router_t, *weights)

    terms = {slot: [value] for slot, value in enumerate(outs, first)}
    if paired:
        terms[0] = [jnp.where(core == 1, outs[spare - 1], jnp.zeros_like(outs[spare - 1]))]

    def summed(slot):
        return sum(term.astype(jnp.float32) for term in terms[slot])

    returned = []
    for slot, (parent, *bits) in return_plan:
        value = summed(slot).astype(jnp.bfloat16)
        value = after(value, returned[: max(0, len(returned) + 1 - OPEN_RETURN)])
        returned.append(across(value, bits, ep_count))
        terms[parent].append(returned[-1])
    total = summed(0)
    if paired:
        arrived = between_cores(total[rows:].astype(jnp.bfloat16))
        total = total[:rows] + arrived.astype(jnp.float32)
    return total.astype(jnp.bfloat16)


def solution(mesh):
    in_specs = (
        P(("dom", "ep", "grp"), None),
        P(),
        P(),
        P(("dom", "ep", "grp"), None),
        P("ep", "grp", None, None),
        P("ep", "grp", None, None),
        P("ep", "grp", None, None),
    )
    out_specs = P(("dom", "ep", "grp"), None)
    return jax.shard_map(local, mesh=mesh, in_specs=in_specs, out_specs=out_specs, check_vma=False)
```

time: 132 us -> 110 us (0.83)
  waiting for transfers between devices: 70.1 us -> 53.6 us
  starting transfers between devices: 40.9 us -> 28.8 us
  Pallas kernels: 17.3 us -> 22.7 us
  local copies, waits for them, and re-layouts: 1.06 us -> 2.98 us
    ppermute x24 -> x16, waiting for transfers between devices: 67.5 us -> 50.9 us  [across(): return lax.ppermute(value, ('ep', 'grp'), pairs)]
    ppermute x24 -> x16, starting transfers between devices: 39.7 us -> 27.2 us  [across(): return lax.ppermute(value, ('ep', 'grp'), pairs)]
    pallas_call x1 -> x2, Pallas kernels: 15.1 us -> 20.5 us  [the longest x1 13 us: experts(): pl.pallas_call(functools.partial(experts_kernel, blocks, done_rows, rows,...]
    unnamed x4 -> x6, local copies, waits for them, and re-layouts: 0.12 us -> 2.04 us
    ppermute x7 -> x6, waiting for transfers between devices: 2.59 us -> 2.67 us  [between_cores(): return lax.ppermute(value, 'grp', [(0, 1), (1, 0)])]
  transfers between devices with their start and end apart: 31 -> 22, of which waited for: 17 -> 15; matrix products, arithmetic and copies ran while one was open for 1% -> 1% of each run, Pallas kernels for 2% -> 9%
where the time goes in v8:
time: 110 us
  waiting for transfers between devices  53.6 us (49%)
  starting transfers between devices  28.8 us (26%)
  Pallas kernels  22.7 us (21%)
  local copies, waits for them, and re-layouts  2.98 us (3%)
  other arithmetic  1.63 us (1%)
    ppermute x16, waiting for transfers between devices, across(): return lax.ppermute(value, ('ep', 'grp'), pairs)  50.9 us
    ppermute x16, starting transfers between devices, across(): return lax.ppermute(value, ('ep', 'grp'), pairs)  27.2 us
    pallas_call x1, Pallas kernels, experts(): pl.pallas_call(functools.partial(experts_kernel, blocks, done_rows, rows,...  13 us
    pallas_call x1, Pallas kernels, early(): pl.pallas_call(functools.partial(early_kernel, blocks, k_steps, k_tile),...  7.5 us
    ppermute x6, waiting for transfers between devices, between_cores(): return lax.ppermute(value, 'grp', [(0, 1), (1, 0)])  2.67 us
    pallas_call x1, Pallas kernels, prepare(): pl.pallas_call(functools.partial(prepare_kernel, count), out_shape=jax.Sh...  2.2 us
  transfers between devices with their start and end apart: 22, of which 15 were waited for; matrix products, arithmetic and copies ran while one was open for 1% of the time, Pallas kernels for 9%

profile of v8, /device:TPU:0, one launch (start us, length us, event | category | flops | bytes accessed | tf_op | source)
XLA Modules:
  0.0 109.9 jit_solution(14783817814451448179)
XLA Ops:
  2.7 2.2 %prepare.1 = bf16[32,7296]{1,0:T(8,128)(2,1)} custom-call(f32[1,7168]{1,0:T(1,128)} %bitcast.17, bf16[16,7168]{1,0:T(8,128)(2,1)} %refs_1_.1, bf16[16,7168]{1,0:T(8,128)(2,1)} %copy-done.1, s32[4,16]{1,0:T(4,128)} %bitcast.19, s32[4,16]{1,0:T(4,128)} %copy-done.2), custom_call_target="tpu_custom_call" | custom-call | flops 1376256 | bytes 917504 | tf_op jit(solution)/shard_map/prepare/pallas_call | solution.py:86
  4.9 2.7 %collective-permute-start.3 = (bf16[32,7296]{1,0:T(8,128)(2,1)}, bf16[32,7296]{1,0:T(8,128)(2,1)S(1)}, u32[]{:S(2)}, u32[]{:S(2)}) collective-permute-start(bf16[32,7296]{1,0:T(8,128)(2,1)} %prepare.1), channel_id=1, source_target_pairs={{0,2},{2,0},{4,6},{6,4},{8,10},{10,8},{12,14},{14,12},{16,18},{18,... | collective-permute-start | bytes 1400840 | tf_op jit(solution)/shard_map/ppermute | solution.py:40
  7.7 2.6 %collective-permute-start.2 = (bf16[32,7296]{1,0:T(8,128)(2,1)}, bf16[32,7296]{1,0:T(8,128)(2,1)S(1)}, u32[]{:S(2)}, u32[]{:S(2)}) collective-permute-start(bf16[32,7296]{1,0:T(8,128)(2,1)} %prepare.1), channel_id=1, source_target_pairs={{0,16},{2,18},{4,20},{6,22},{8,24},{10,26},{12,28},{14,30},{16,0},... | collective-permute-start | bytes 1400840 | tf_op jit(solution)/shard_map/ppermute | solution.py:40
  10.3 4.2 %collective-permute-done.3.refs_0_ = bf16[32,7296]{1,0:T(8,128)(2,1)S(1)} collective-permute-done((bf16[32,7296]{1,0:T(8,128)(2,1)}, bf16[32,7296]{1,0:T(8,128)(2,1)S(1)}, u32[]{:S(2)}, u32[]{:S(2)}) %collective-permute-start.3) | collective-permute-done | bytes 466976 | tf_op jit(solution)/shard_map/ppermute | solution.py:40
  14.4 7.0 %collective-permute-done.2.refs_1_ = bf16[32,7296]{1,0:T(8,128)(2,1)S(1)} collective-permute-done((bf16[32,7296]{1,0:T(8,128)(2,1)}, bf16[32,7296]{1,0:T(8,128)(2,1)S(1)}, u32[]{:S(2)}, u32[]{:S(2)}) %collective-permute-start.2) | collective-permute-done | bytes 466976 | tf_op jit(solution)/shard_map/ppermute | solution.py:40
  21.5 1.8 %collective-permute-start.4 = (bf16[32,7296]{1,0:T(8,128)(2,1)S(1)}, bf16[32,7296]{1,0:T(8,128)(2,1)S(1)}, u32[]{:S(2)}, u32[]{:S(2)}) collective-permute-start(bf16[32,7296]{1,0:T(8,128)(2,1)S(1)} %collective-permute-done.2.refs_1_), channel_id=1, source_target_pairs={{0,8},{2,10},{4,12},{6,14},{8,0},{10,2},{12,4},{14,6},{16,24},{18,... | collective-permute-start | bytes 1400840 | tf_op jit(solution)/shard_map/ppermute | solution.py:40
  23.2 1.5 %collective-permute-start.7 = (bf16[32,7296]{1,0:T(8,128)(2,1)S(1)}, bf16[32,7296]{1,0:T(8,128)(2,1)S(1)}, u32[]{:S(2)}, u32[]{:S(2)}) collective-permute-start(bf16[32,7296]{1,0:T(8,128)(2,1)S(1)} %collective-permute-done.2.refs_1_), channel_id=1, source_target_pairs={{0,4},{2,6},{4,0},{6,2},{8,12},{10,14},{12,8},{14,10},{16,20},{18,... | collective-permute-start | bytes 1400840 | tf_op jit(solution)/shard_map/ppermute | solution.py:40
  24.7 5.3 %collective-permute-done.4.refs_2_ = bf16[32,7296]{1,0:T(8,128)(2,1)S(1)} collective-permute-done((bf16[32,7296]{1,0:T(8,128)(2,1)S(1)}, bf16[32,7296]{1,0:T(8,128)(2,1)S(1)}, u32[]{:S(2)}, u32[]{:S(2)}) %collective-permute-start.4) | collective-permute-done | bytes 466976 | tf_op jit(solution)/shard_map/ppermute | solution.py:40
  30.8 3.1 %collective-permute-start.12 = (bf16[32,7296]{1,0:T(8,128)(2,1)S(1)}, bf16[32,7296]{1,0:T(8,128)(2,1)S(1)}, u32[]{:S(2)}, u32[]{:S(2)}) collective-permute-start(bf16[32,7296]{1,0:T(8,128)(2,1)S(1)} %collective-permute-done.2.refs_1_), channel_id=1, source_target_pairs={{0,2},{2,0},{4,6},{6,4},{8,10},{10,8},{12,14},{14,12},{16,18},{18,... | collective-permute-start | bytes 1400840 | tf_op jit(solution)/shard_map/ppermute | solution.py:40
  35.0 1.9 %collective-permute-done.7.refs_3_ = bf16[32,7296]{1,0:T(8,128)(2,1)S(1)} collective-permute-done((bf16[32,7296]{1,0:T(8,128)(2,1)S(1)}, bf16[32,7296]{1,0:T(8,128)(2,1)S(1)}, u32[]{:S(2)}, u32[]{:S(2)}) %collective-permute-start.7) | collective-permute-done | bytes 466976 | tf_op jit(solution)/shard_map/ppermute | solution.py:40
  36.9 1.7 %collective-permute-done.6.refs_0_ = bf16[32,7296]{1,0:T(8,128)(2,1)S(1)} collective-permute-done((bf16[32,7296]{1,0:T(8,128)(2,1)S(1)}, bf16[32,7296]{1,0:T(8,128)(2,1)S(1)}, u32[]{:S(2)}, u32[]{:S(2)}) %collective-permute-start.6) | collective-permute-done | bytes 466976 | tf_op jit(solution)/shard_map/ppermute | solution.py:40
  38.6 2.5 %collective-permute-start.10 = (bf16[32,7296]{1,0:T(8,128)(2,1)S(1)}, bf16[32,7296]{1,0:T(8,128)(2,1)S(1)}, u32[]{:S(2)}, u32[]{:S(2)}) collective-permute-start(bf16[32,7296]{1,0:T(8,128)(2,1)S(1)} %collective-permute-done.6.refs_0_), channel_id=1, source_target_pairs={{0,4},{2,6},{4,0},{6,2},{8,12},{10,14},{12,8},{14,10},{16,20},{18,... | collective-permute-start | bytes 1400840 | tf_op jit(solution)/shard_map/ppermute | solution.py:40
  41.1 2.5 %collective-permute-done.12 = bf16[32,7296]{1,0:T(8,128)(2,1)S(1)} collective-permute-done((bf16[32,7296]{1,0:T(8,128)(2,1)S(1)}, bf16[32,7296]{1,0:T(8,128)(2,1)S(1)}, u32[]{:S(2)}, u32[]{:S(2)}) %collective-permute-start.12) | collective-permute-done | bytes 466976 | tf_op jit(solution)/shard_map/ppermute | solution.py:40
  43.7 2.0 %copy-done = bf16[1,1,7168,256]{3,2,1,0:T(8,128)(2,1)S(1)} copy-done((bf16[1,1,7168,256]{3,2,1,0:T(8,128)(2,1)S(1)}, bf16[1,1,7168,256]{3,2,1,0:T(8,128)(2,1)}, u32[]{:S(2)}) %copy-start) | copy-done | bytes 3670040
  45.7 7.5 %early.1 = (bf16[160,512]{1,0:T(8,128)(2,1)S(1)}, f32[160,256]{1,0:T(8,128)S(1)}) custom-call(s32[2]{0:T(128)S(1)} %pad_add_fusion.ids_ref, bf16[32,7296]{1,0:T(8,128)(2,1)S(1)} %collective-permute-done.3.refs_0_, bf16[32,7296]{1,0:T(8,128)(2,1)S(1)} %collective-permute-done.2.refs_1_, bf16[32,7296]{1,0:T(8,128)(2,1)S(1)} %collective-permute-done.4.refs_2_, ...), custom_call_target="tpu_custom_call" | custom-call | flops 2348810240 | bytes 16973824 | tf_op jit(solution)/shard_map/early/pallas_call | solution.py:152
  53.3 13.0 %experts.1 = (bf16[32,7168]{1,0:T(8,128)(2,1)S(1)}, bf16[32,7168]{1,0:T(8,128)(2,1)S(1)}, bf16[32,7168]{1,0:T(8,128)(2,1)S(1)}, bf16[32,7168]{1,0:T(8,128)(2,1)S...) custom-call(s32[2]{0:T(128)S(1)} %pad_add_fusion.ids_ref, ...), custom_call_target="tpu_custom_call" | custom-call | flops 3288334336 | bytes 29360128 | tf_op jit(solution)/shard_map/experts/pallas_call | solution.py:239
  66.3 2.5 %collective-permute-start.15 = (bf16[32,7168]{1,0:T(8,128)(2,1)S(1)}, bf16[32,7168]{1,0:T(8,128)(2,1)S(1)}, u32[]{:S(2)}, u32[]{:S(2)}) collective-permute-start(bf16[32,7168]{1,0:T(8,128)(2,1)S(1)} %get-tuple-element.43), channel_id=1, source_target_pairs={{0,4},{2,6},{4,0},{6,2},{8,12},{10,14},{12,8},{14,10},{16,20},{18,... | collective-permute-start | bytes 1376264 | tf_op jit(solution)/shard_map/ppermute | solution.py:40
  68.8 6.4 %collective-permute-done.15 = bf16[32,7168]{1,0:T(8,128)(2,1)S(1)} collective-permute-done((bf16[32,7168]{1,0:T(8,128)(2,1)S(1)}, bf16[32,7168]{1,0:T(8,128)(2,1)S(1)}, u32[]{:S(2)}, u32[]{:S(2)}) %collective-permute-start.15) | collective-permute-done | bytes 458784 | tf_op jit(solution)/shard_map/ppermute | solution.py:40
  77.7 3.9 %collective-permute-start.16 = (bf16[32,7168]{1,0:T(8,128)(2,1)S(1)}, bf16[32,7168]{1,0:T(8,128)(2,1)S(1)}, u32[]{:S(2)}, u32[]{:S(2)}) collective-permute-start(bf16[32,7168]{1,0:T(8,128)(2,1)S(1)} %get-tuple-element.44), channel_id=1, source_target_pairs={{0,2},{2,0},{4,6},{6,4},{8,10},{10,8},{12,14},{14,12},{16,18},{18,... | collective-permute-start | bytes 1376264 | tf_op jit(solution)/shard_map/ppermute | solution.py:40
  81.6 2.3 %collective-permute-done.17 = bf16[32,7168]{1,0:T(8,128)(2,1)S(1)} collective-permute-done((bf16[32,7168]{1,0:T(8,128)(2,1)S(1)}, bf16[32,7168]{1,0:T(8,128)(2,1)S(1)}, u32[]{:S(2)}, u32[]{:S(2)}) %collective-permute-start.17) | collective-permute-done | bytes 458784 | tf_op jit(solution)/shard_map/ppermute | solution.py:40
  85.4 5.5 %collective-permute-done.14 = bf16[32,7168]{1,0:T(8,128)(2,1)S(1)} collective-permute-done((bf16[32,7168]{1,0:T(8,128)(2,1)S(1)}, bf16[32,7168]{1,0:T(8,128)(2,1)S(1)}, u32[]{:S(2)}, u32[]{:S(2)}) %collective-permute-start.14) | collective-permute-done | bytes 458784 | tf_op jit(solution)/shard_map/ppermute | solution.py:40
  92.8 3.5 %collective-permute-start.19 = (bf16[32,7168]{1,0:T(8,128)(2,1)S(1)}, bf16[32,7168]{1,0:T(8,128)(2,1)S(1)}, u32[]{:S(2)}, u32[]{:S(2)}) collective-permute-start(bf16[32,7168]{1,0:T(8,128)(2,1)S(1)} %add_convert_fusion), channel_id=1, source_target_pairs={{0,16},{2,18},{4,20},{6,22},{8,24},{10,26},{12,28},{14,30},{16,0},... | collective-permute-start | bytes 1376264 | tf_op jit(solution)/shard_map/ppermute | solution.py:40
  96.3 3.3 %collective-permute-done.20 = bf16[32,7168]{1,0:T(8,128)(2,1)S(1)} collective-permute-done((bf16[32,7168]{1,0:T(8,128)(2,1)S(1)}, bf16[32,7168]{1,0:T(8,128)(2,1)S(1)}, u32[]{:S(2)}, u32[]{:S(2)}) %collective-permute-start.20) | collective-permute-done | bytes 458784 | tf_op jit(solution)/shard_map/ppermute | solution.py:40
  99.6 7.7 %collective-permute-done.19 = bf16[32,7168]{1,0:T(8,128)(2,1)S(1)} collective-permute-done((bf16[32,7168]{1,0:T(8,128)(2,1)S(1)}, bf16[32,7168]{1,0:T(8,128)(2,1)S(1)}, u32[]{:S(2)}, u32[]{:S(2)}) %collective-permute-start.19) | collective-permute-done | bytes 458784 | tf_op jit(solution)/shard_map/ppermute | solution.py:40
  (39 shorter events, 12.9 us)
Async XLA Ops:
  0.0 1.8 %collective-permute-start = (bf16[16,7168]{1,0:T(8,128)(2,1)}, bf16[16,7168]{1,0:T(8,128)(2,1)S(1)}, u32[]{:S(2)}, u32[]{:S(2)}) collective-permute-start(bf16[16,7168]{1,0:T(8,128)(2,1)} %refs_1_.1), channel_id=1, source_target_pairs={{0,1},{1,0},{2,3},{3,2},{4,5},{5,4},{6,7},{7,6},{8,9},{9,8},{10,11... | collective-permute-start | bytes 688136 | tf_op jit(solution)/shard_map/ppermute | solution.py:48
  0.5 1.4 %collective-permute-start.1 = (s32[4,16]{1,0:T(4,128)}, s32[4,16]{1,0:T(4,128)S(1)}, u32[]{:S(2)}, u32[]{:S(2)}) collective-permute-start(s32[4,16]{1,0:T(4,128)} %bitcast.18), channel_id=1, source_target_pairs={{0,1},{1,0},{2,3},{3,2},{4,5},{5,4},{6,7},{7,6},{8,9},{9,8},{10,11... | collective-permute-start | bytes 776 | tf_op jit(solution)/shard_map/ppermute | solution.py:48
  1.8 0.9 copy-start.2
  1.8 28.2 %collective-permute-start.5 = (bf16[7168,256]{1,0:T(8,128)(2,1)}, bf16[7168,256]{1,0:T(8,128)(2,1)}, u32[]{:S(2)}, u32[]{:S(2)}) collective-permute-start(bf16[7168,256]{1,0:T(8,128)(2,1)} %bitcast.8), channel_id=1, source_target_pairs={{0,1},{1,0},{2,3},{3,2},{4,5},{5,4},{6,7},{7,6},{8,9},{9,8},{10,11... | collective-permute-start | bytes 11010056 | tf_op jit(solution)/shard_map/ppermute | solution.py:48
  2.2 34.6 %collective-permute-start.8 = (bf16[7168,256]{1,0:T(8,128)(2,1)}, bf16[7168,256]{1,0:T(8,128)(2,1)}, u32[]{:S(2)}, u32[]{:S(2)}) collective-permute-start(bf16[7168,256]{1,0:T(8,128)(2,1)} %bitcast.11), channel_id=1, source_target_pairs={{0,1},{1,0},{2,3},{3,2},{4,5},{5,4},{6,7},{7,6},{8,9},{9,8},{10,11... | collective-permute-start | bytes 11010056 | tf_op jit(solution)/shard_map/ppermute | solution.py:48
  2.4 50.8 %collective-permute-start.11 = (bf16[256,7168]{1,0:T(8,128)(2,1)}, bf16[256,7168]{1,0:T(8,128)(2,1)}, u32[]{:S(2)}, u32[]{:S(2)}) collective-permute-start(bf16[256,7168]{1,0:T(8,128)(2,1)} %bitcast.14), channel_id=1, source_target_pairs={{0,1},{1,0},{2,3},{3,2},{4,5},{5,4},{6,7},{7,6},{8,9},{9,8},{10,11... | collective-permute-start | bytes 11010056 | tf_op jit(solution)/shard_map/ppermute | solution.py:48
  4.9 9.5 %collective-permute-start.3 = (bf16[32,7296]{1,0:T(8,128)(2,1)}, bf16[32,7296]{1,0:T(8,128)(2,1)S(1)}, u32[]{:S(2)}, u32[]{:S(2)}) collective-permute-start(bf16[32,7296]{1,0:T(8,128)(2,1)} %prepare.1), channel_id=1, source_target_pairs={{0,2},{2,0},{4,6},{6,4},{8,10},{10,8},{12,14},{14,12},{16,18},{18,... | collective-permute-start | bytes 1400840 | tf_op jit(solution)/shard_map/ppermute | solution.py:40
  7.7 13.8 %collective-permute-start.2 = (bf16[32,7296]{1,0:T(8,128)(2,1)}, bf16[32,7296]{1,0:T(8,128)(2,1)S(1)}, u32[]{:S(2)}, u32[]{:S(2)}) collective-permute-start(bf16[32,7296]{1,0:T(8,128)(2,1)} %prepare.1), channel_id=1, source_target_pairs={{0,16},{2,18},{4,20},{6,22},{8,24},{10,26},{12,28},{14,30},{16,0},... | collective-permute-start | bytes 1400840 | tf_op jit(solution)/shard_map/ppermute | solution.py:40
  21.5 8.6 %collective-permute-start.4 = (bf16[32,7296]{1,0:T(8,128)(2,1)S(1)}, bf16[32,7296]{1,0:T(8,128)(2,1)S(1)}, u32[]{:S(2)}, u32[]{:S(2)}) collective-permute-start(bf16[32,7296]{1,0:T(8,128)(2,1)S(1)} %collective-permute-done.2.refs_1_), channel_id=1, source_target_pairs={{0,8},{2,10},{4,12},{6,14},{8,0},{10,2},{12,4},{14,6},{16,24},{18,... | collective-permute-start | bytes 1400840 | tf_op jit(solution)/shard_map/ppermute | solution.py:40
  23.2 13.6 %collective-permute-start.7 = (bf16[32,7296]{1,0:T(8,128)(2,1)S(1)}, bf16[32,7296]{1,0:T(8,128)(2,1)S(1)}, u32[]{:S(2)}, u32[]{:S(2)}) collective-permute-start(bf16[32,7296]{1,0:T(8,128)(2,1)S(1)} %collective-permute-done.2.refs_1_), channel_id=1, source_target_pairs={{0,4},{2,6},{4,0},{6,2},{8,12},{10,14},{12,8},{14,10},{16,20},{18,... | collective-permute-start | bytes 1400840 | tf_op jit(solution)/shard_map/ppermute | solution.py:40
  30.0 8.6 %collective-permute-start.6 = (bf16[32,7296]{1,0:T(8,128)(2,1)S(1)}, bf16[32,7296]{1,0:T(8,128)(2,1)S(1)}, u32[]{:S(2)}, u32[]{:S(2)}) collective-permute-start(bf16[32,7296]{1,0:T(8,128)(2,1)S(1)} %collective-permute-done.4.refs_2_), channel_id=1, source_target_pairs={{0,2},{2,0},{4,6},{6,4},{8,10},{10,8},{12,14},{14,12},{16,18},{18,... | collective-permute-start | bytes 1400840 | tf_op jit(solution)/shard_map/ppermute | solution.py:40
  30.8 12.8 %collective-permute-start.12 = (bf16[32,7296]{1,0:T(8,128)(2,1)S(1)}, bf16[32,7296]{1,0:T(8,128)(2,1)S(1)}, u32[]{:S(2)}, u32[]{:S(2)}) collective-permute-start(bf16[32,7296]{1,0:T(8,128)(2,1)S(1)} %collective-permute-done.2.refs_1_), channel_id=1, source_target_pairs={{0,2},{2,0},{4,6},{6,4},{8,10},{10,8},{12,14},{14,12},{16,18},{18,... | collective-permute-start | bytes 1400840 | tf_op jit(solution)/shard_map/ppermute | solution.py:40
  36.9 16.4 %collective-permute-start.9 = (bf16[32,7296]{1,0:T(8,128)(2,1)S(1)}, bf16[32,7296]{1,0:T(8,128)(2,1)S(1)}, u32[]{:S(2)}, u32[]{:S(2)}) collective-permute-start(bf16[32,7296]{1,0:T(8,128)(2,1)S(1)} %collective-permute-done.7.refs_3_), channel_id=1, source_target_pairs={{0,2},{2,0},{4,6},{6,4},{8,10},{10,8},{12,14},{14,12},{16,18},{18,... | collective-permute-start | bytes 1400840 | tf_op jit(solution)/shard_map/ppermute | solution.py:40
  38.6 14.7 %collective-permute-start.10 = (bf16[32,7296]{1,0:T(8,128)(2,1)S(1)}, bf16[32,7296]{1,0:T(8,128)(2,1)S(1)}, u32[]{:S(2)}, u32[]{:S(2)}) collective-permute-start(bf16[32,7296]{1,0:T(8,128)(2,1)S(1)} %collective-permute-done.6.refs_0_), channel_id=1, source_target_pairs={{0,4},{2,6},{4,0},{6,2},{8,12},{10,14},{12,8},{14,10},{16,20},{18,... | collective-permute-start | bytes 1400840 | tf_op jit(solution)/shard_map/ppermute | solution.py:40
  43.7 2.0 %copy-start = (bf16[1,1,7168,256]{3,2,1,0:T(8,128)(2,1)S(1)}, bf16[1,1,7168,256]{3,2,1,0:T(8,128)(2,1)}, u32[]{:S(2)}) copy-start(bf16[1,1,7168,256]{3,2,1,0:T(8,128)(2,1)} %param.11) | copy-start | bytes 11010052
  66.3 9.0 %collective-permute-start.15 = (bf16[32,7168]{1,0:T(8,128)(2,1)S(1)}, bf16[32,7168]{1,0:T(8,128)(2,1)S(1)}, u32[]{:S(2)}, u32[]{:S(2)}) collective-permute-start(bf16[32,7168]{1,0:T(8,128)(2,1)S(1)} %get-tuple-element.43), channel_id=1, source_target_pairs={{0,4},{2,6},{4,0},{6,2},{8,12},{10,14},{12,8},{14,10},{16,20},{18,... | collective-permute-start | bytes 1376264 | tf_op jit(solution)/shard_map/ppermute | solution.py:40
  68.8 8.5 %collective-permute-start.13 = (bf16[32,7168]{1,0:T(8,128)(2,1)S(1)}, bf16[32,7168]{1,0:T(8,128)(2,1)S(1)}, u32[]{:S(2)}, u32[]{:S(2)}) collective-permute-start(bf16[32,7168]{1,0:T(8,128)(2,1)S(1)} %get-tuple-element.42), channel_id=1, source_target_pairs={{0,2},{2,0},{4,6},{6,4},{8,10},{10,8},{12,14},{14,12},{16,18},{18,... | collective-permute-start | bytes 1376264 | tf_op jit(solution)/shard_map/ppermute | solution.py:40
  75.4 8.5 %collective-permute-start.17 = (bf16[32,7168]{1,0:T(8,128)(2,1)S(1)}, bf16[32,7168]{1,0:T(8,128)(2,1)S(1)}, u32[]{:S(2)}, u32[]{:S(2)}) collective-permute-start(bf16[32,7168]{1,0:T(8,128)(2,1)S(1)} %add_convert_fusion.2), channel_id=1, source_target_pairs={{0,2},{2,0},{4,6},{6,4},{8,10},{10,8},{12,14},{14,12},{16,18},{18,... | collective-permute-start | bytes 1376264 | tf_op jit(solution)/shard_map/ppermute | solution.py:40
  77.4 13.5 %collective-permute-start.14 = (bf16[32,7168]{1,0:T(8,128)(2,1)S(1)}, bf16[32,7168]{1,0:T(8,128)(2,1)S(1)}, u32[]{:S(2)}, u32[]{:S(2)}) collective-permute-start(bf16[32,7168]{1,0:T(8,128)(2,1)S(1)} %add_convert_fusion.3), channel_id=1, source_target_pairs={{0,4},{2,6},{4,0},{6,2},{8,12},{10,14},{12,8},{14,10},{16,20},{18,... | collective-permute-start | bytes 1376264 | tf_op jit(solution)/shard_map/ppermute | solution.py:40
  77.7 13.4 %collective-permute-start.16 = (bf16[32,7168]{1,0:T(8,128)(2,1)S(1)}, bf16[32,7168]{1,0:T(8,128)(2,1)S(1)}, u32[]{:S(2)}, u32[]{:S(2)}) collective-permute-start(bf16[32,7168]{1,0:T(8,128)(2,1)S(1)} %get-tuple-element.44), channel_id=1, source_target_pairs={{0,2},{2,0},{4,6},{6,4},{8,10},{10,8},{12,14},{14,12},{16,18},{18,... | collective-permute-start | bytes 1376264 | tf_op jit(solution)/shard_map/ppermute | solution.py:40
  84.0 8.5 %collective-permute-start.18 = (bf16[32,7168]{1,0:T(8,128)(2,1)S(1)}, bf16[32,7168]{1,0:T(8,128)(2,1)S(1)}, u32[]{:S(2)}, u32[]{:S(2)}) collective-permute-start(bf16[32,7168]{1,0:T(8,128)(2,1)S(1)} %add_convert_fusion.1), channel_id=1, source_target_pairs={{0,8},{2,10},{4,12},{6,14},{8,0},{10,2},{12,4},{14,6},{16,24},{18,... | collective-permute-start | bytes 1376264 | tf_op jit(solution)/shard_map/ppermute | solution.py:40
  90.9 8.7 %collective-permute-start.20 = (bf16[32,7168]{1,0:T(8,128)(2,1)S(1)}, bf16[32,7168]{1,0:T(8,128)(2,1)S(1)}, u32[]{:S(2)}, u32[]{:S(2)}) collective-permute-start(bf16[32,7168]{1,0:T(8,128)(2,1)S(1)} %get-tuple-element.50), channel_id=1, source_target_pairs={{0,2},{2,0},{4,6},{6,4},{8,10},{10,8},{12,14},{14,12},{16,18},{18,... | collective-permute-start | bytes 1376264 | tf_op jit(solution)/shard_map/ppermute | solution.py:40
  92.8 14.5 %collective-permute-start.19 = (bf16[32,7168]{1,0:T(8,128)(2,1)S(1)}, bf16[32,7168]{1,0:T(8,128)(2,1)S(1)}, u32[]{:S(2)}, u32[]{:S(2)}) collective-permute-start(bf16[32,7168]{1,0:T(8,128)(2,1)S(1)} %add_convert_fusion), channel_id=1, source_target_pairs={{0,16},{2,18},{4,20},{6,22},{8,24},{10,26},{12,28},{14,30},{16,0},... | collective-permute-start | bytes 1376264 | tf_op jit(solution)/shard_map/ppermute | solution.py:40
  107.6 1.6 %collective-permute-start.21 = (bf16[16,7168]{1,0:T(8,128)(2,1)S(1)}, bf16[16,7168]{1,0:T(8,128)(2,1)S(1)}, u32[]{:S(2)}, u32[]{:S(2)}) collective-permute-start(bf16[16,7168]{1,0:T(8,128)(2,1)S(1)} %slice.15), channel_id=1, source_target_pairs={{0,1},{1,0},{2,3},{3,2},{4,5},{5,4},{6,7},{7,6},{8,9},{9,8},{10,11... | collective-permute-start | bytes 688136 | tf_op jit(solution)/shard_map/ppermute | solution.py:48
  (1 other events, 0.9 us)

commit v9 on v8

--- a/solution.py
+++ b/solution.py
@@ -13,7 +13,7 @@
 EPSILON = 1e-06
 ROUTE_SCALE = 2.5
 PREPARE_VMEM = 60 * 1024 * 1024
-EXPERTS_VMEM = 47 * 1024 * 1024
+EXPERTS_VMEM = 16 * 1024 * 1024
 
 PLAN_16 = ((0, 1, 2), (0, 8, 4), (2, 4, 1), (2, 2, 2), (2, 1, 0), (3, 1, 2), (4, 1, 8), (6, 2, 4))
 RETURN_16 = tuple((slot, PLAN_16[slot - 1]) for slot in (8, 7, 6, 4, 5, 3, 2, 1))
@@ -96,80 +96,50 @@
     )(*operands)
 
 
-def add_products(step, k_tile, token_refs, router_ref, weight_refs, gates_ref, logits_ref):
-    hidden_units = weight_refs[0].shape[1]
-    columns = pl.ds(pl.multiple_of(step * k_tile, LANES), k_tile)
-    tokens = jnp.concatenate([ref[:, columns] for ref in token_refs], axis=0)
-    parts = [jnp.dot(tokens, ref[...], preferred_element_type=jnp.float32) for ref in weight_refs]
+def gate_up(ids_ref, token_refs, router_ref, weight_refs, tokens_ref):
+    rows = token_refs[0].shape[0]
+    width = weight_refs[0].shape[0]
+    for i, ref in enumerate(token_refs):
+        tokens_ref[i * rows : (i + 1) * rows, :] = ref[...]
+
+    def product(ref):
+        return jnp.dot(tokens_ref[:, :width], ref[...], preferred_element_type=jnp.float32)
+
     logits = lax.dot_general(
-        tokens, router_ref[...], (((1,), (1,)), ((), ())), preferred_element_type=jnp.float32
+        tokens_ref[:, :width], router_ref[...], (((1,), (1,)), ((), ())), preferred_element_type=jnp.float32
     )
-
-    @pl.when(step == 0)
-    def _():
-        for i, part in enumerate(parts):
-            gates_ref[:, i * hidden_units : (i + 1) * hidden_units] = part
-        logits_ref[...] = logits
-
-    @pl.when(step > 0)
-    def _():
-        for i, part in enumerate(parts):
-            gates_ref[:, i * hidden_units : (i + 1) * hidden_units] += part
-        logits_ref[...] += logits
-
-
-def activate(width, ids_ref, token_refs, gates_ref, logits_ref):
-    half = gates_ref.shape[1] // 2
-    act = (jax.nn.silu(gates_ref[:, :half]) * gates_ref[:, half:]).astype(jnp.bfloat16)
-    named = jnp.concatenate([ref[:, width : width + LANES] for ref in token_refs], axis=0)
-    chosen = named[:, : logits_ref.shape[1]].astype(jnp.float32) * jax.nn.sigmoid(logits_ref[...])
+    named = tokens_ref[:, width:][:, : logits.shape[1]].astype(jnp.float32)
+    chosen = named * jax.nn.sigmoid(logits)
     weights = ROUTE_SCALE * chosen / jnp.sum(chosen, axis=1, keepdims=True)
     lanes = lax.broadcasted_iota(jnp.int32, weights.shape, 1)
-    columns = []
+    acts, columns = [], []
     for i in range(2):
+        acts.append((jax.nn.silu(product(weight_refs[i])) * product(weight_refs[2 + i])).astype(jnp.bfloat16))
         column = jnp.sum(jnp.where(lanes == ids_ref[i], weights, 0.0), axis=1, keepdims=True)
         columns.append(jnp.broadcast_to(column, (column.shape[0], LANES)))
-    return act, jnp.concatenate(columns, axis=1)
-
-
-def early_kernel(blocks, k_steps, k_tile, ids_ref, *refs):
+    return jnp.concatenate(acts, axis=1), jnp.concatenate(columns, axis=1)
+
+
+def early_kernel(blocks, ids_ref, *refs):
     token_refs, router_ref, weight_refs = refs[:blocks], refs[blocks], refs[blocks + 1 : blocks + 5]
-    act_ref, coeff_ref, gates_ref, logits_ref = refs[blocks + 5 :]
-    step = pl.program_id(0)
-    add_products(step, k_tile, token_refs, router_ref, weight_refs, gates_ref, logits_ref)
-
-    @pl.when(step == k_steps - 1)
-    def _():
-        act_ref[...], coeff_ref[...] = activate(k_steps * k_tile, ids_ref, token_refs, gates_ref, logits_ref)
+    act_ref, coeff_ref, tokens_ref = refs[blocks + 5 :]
+    act_ref[...], coeff_ref[...] = gate_up(ids_ref, token_refs, router_ref, weight_refs, tokens_ref)
 
 
 def early(ids, token_blocks, router_t, gates, ups):
     blocks = len(token_blocks)
     width, hidden_units = gates[0].shape
     rows = blocks * token_blocks[0].shape[0]
-    k_steps = 4
-    k_tile = width // k_steps
+    in_vmem = pl.BlockSpec(memory_space=pltpu.VMEM)
     return pl.pallas_call(
-        functools.partial(early_kernel, blocks, k_steps, k_tile),
-        grid_spec=pltpu.PrefetchScalarGridSpec(
-            num_scalar_prefetch=1,
-            grid=(k_steps,),
-            in_specs=[pl.BlockSpec(token_blocks[0].shape, lambda step, ids_ref: (0, 0))] * blocks
-            + [pl.BlockSpec((router_t.shape[0], k_tile), lambda step, ids_ref: (0, step))]
-            + [pl.BlockSpec((k_tile, hidden_units), lambda step, ids_ref: (step, 0))] * 4,
-            out_specs=[
-                pl.BlockSpec((rows, 2 * hidden_units), lambda step, ids_ref: (0, 0)),
-                pl.BlockSpec((rows, 2 * LANES), lambda step, ids_ref: (0, 0)),
-            ],
-            scratch_shapes=[
-                pltpu.VMEM((rows, 4 * hidden_units), jnp.float32),
-                pltpu.VMEM((rows, router_t.shape[0]), jnp.float32),
-            ],
-        ),
+        functools.partial(early_kernel, blocks),
+        in_specs=[pl.BlockSpec(memory_space=pltpu.SMEM)] + [in_vmem] * (blocks + 5),
+        out_specs=[in_vmem] * 2,
         out_shape=[
             jax.ShapeDtypeStruct((rows, 2 * hidden_units), jnp.bfloat16),
             jax.ShapeDtypeStruct((rows, 2 * LANES), jnp.float32),
         ],
+        scratch_shapes=[pltpu.VMEM((rows, width + LANES), jnp.bfloat16)],
         compiler_params=pltpu.CompilerParams(vmem_limit_bytes=EXPERTS_VMEM),
         cost_estimate=pl.CostEstimate(
             flops=8 * rows * width * hidden_units,
@@ -180,77 +150,50 @@
     )(ids, *token_blocks, router_t, *gates, *ups)
 
 
-def experts_kernel(blocks, done_rows, rows, k_steps, k_tile, ids_ref, *refs):
+def experts_kernel(blocks, done_rows, rows, n_tile, ids_ref, *refs):
     token_refs, router_ref = refs[:blocks], refs[blocks]
     weight_refs, down0_ref, down1_ref = refs[blocks + 1 : blocks + 5], refs[blocks + 5], refs[blocks + 6]
     refs = refs[blocks + 7 :]
     if done_rows:
         done_act_ref, done_coeff_ref, *refs = refs
-    *out_refs, gates_ref, logits_ref, act_ref, coeff_ref = refs
-    hidden_units = weight_refs[0].shape[1]
-    step = pl.program_id(0)
-
-    @pl.when(step < k_steps)
-    def _():
-        add_products(step, k_tile, token_refs, router_ref, weight_refs, gates_ref, logits_ref)
-
-    @pl.when(step == k_steps - 1)
-    def _():
-        act, coeff = activate(k_steps * k_tile, ids_ref, token_refs, gates_ref, logits_ref)
-        act_ref[done_rows:, :] = act
-        coeff_ref[done_rows:, :] = coeff
-        if done_rows:
-            act_ref[:done_rows, :] = done_act_ref[...]
-            coeff_ref[:done_rows, :] = done_coeff_ref[...]
-
-    @pl.when(step >= k_steps)
-    def _():
+    *out_refs, tokens_ref, act_ref, coeff_ref = refs
+    hidden_units, width = down0_ref.shape
+    act, coeff = gate_up(ids_ref, token_refs, router_ref, weight_refs, tokens_ref)
+    act_ref[done_rows:, :] = act
+    coeff_ref[done_rows:, :] = coeff
+    if done_rows:
+        act_ref[:done_rows, :] = done_act_ref[...]
+        coeff_ref[:done_rows, :] = done_coeff_ref[...]
+    for j in range(width // n_tile):
+        span = slice(j * n_tile, (j + 1) * n_tile)
         total = coeff_ref[:, 0:1] * jnp.dot(
-            act_ref[:, :hidden_units], down0_ref[...], preferred_element_type=jnp.float32
+            act_ref[:, :hidden_units], down0_ref[:, span], preferred_element_type=jnp.float32
         ) + coeff_ref[:, LANES : LANES + 1] * jnp.dot(
-            act_ref[:, hidden_units:], down1_ref[...], preferred_element_type=jnp.float32
+            act_ref[:, hidden_units:], down1_ref[:, span], preferred_element_type=jnp.float32
         )
         for i, ref in enumerate(out_refs):
-            ref[...] = total[i * rows : (i + 1) * rows].astype(jnp.bfloat16)
+            ref[:, span] = total[i * rows : (i + 1) * rows].astype(jnp.bfloat16)
 
 
 def experts(ids, token_blocks, done, router_t, gates, ups, downs):
     blocks = len(token_blocks)
     rows = token_blocks[0].shape[0]
     width, hidden_units = gates[0].shape
-    k_steps = n_steps = 4
-    k_tile, n_tile = width // k_steps, width // n_steps
     late_rows = blocks * rows
     done_rows = done[0].shape[0] if done else 0
     all_rows = done_rows + late_rows
     outs = all_rows // rows
-
-    def at_k(step):
-        return jnp.minimum(step, k_steps - 1)
-
-    def at_n(step):
-        return jnp.maximum(step - k_steps, 0)
-
-    in_specs = [pl.BlockSpec(token_blocks[0].shape, lambda step, ids_ref: (0, 0))] * blocks
-    in_specs += [pl.BlockSpec((router_t.shape[0], k_tile), lambda step, ids_ref: (0, at_k(step)))]
-    in_specs += [pl.BlockSpec((k_tile, hidden_units), lambda step, ids_ref: (at_k(step), 0))] * 4
-    in_specs += [pl.BlockSpec((hidden_units, n_tile), lambda step, ids_ref: (0, at_n(step)))] * 2
-    in_specs += [pl.BlockSpec(x.shape, lambda step, ids_ref: (0, 0)) for x in done]
+    in_vmem = pl.BlockSpec(memory_space=pltpu.VMEM)
     return pl.pallas_call(
-        functools.partial(experts_kernel, blocks, done_rows, rows, k_steps, k_tile),
-        grid_spec=pltpu.PrefetchScalarGridSpec(
-            num_scalar_prefetch=1,
-            grid=(k_steps + n_steps,),
-            in_specs=in_specs,
-            out_specs=[pl.BlockSpec((rows, n_tile), lambda step, ids_ref: (0, at_n(step)))] * outs,
-            scratch_shapes=[
-                pltpu.VMEM((late_rows, 4 * hidden_units), jnp.float32),
-                pltpu.VMEM((late_rows, router_t.shape[0]), jnp.float32),
-                pltpu.VMEM((all_rows, 2 * hidden_units), jnp.bfloat16),
-                pltpu.VMEM((all_rows, 2 * LANES), jnp.float32),
-            ],
-        ),
+        functools.partial(experts_kernel, blocks, done_rows, rows, 1024),
+        in_specs=[pl.BlockSpec(memory_space=pltpu.SMEM)] + [in_vmem] * (blocks + 7 + len(done)),
+        out_specs=[in_vmem] * outs,
         out_shape=[jax.ShapeDtypeStruct((rows, width), jnp.bfloat16)] * outs,
+        scratch_shapes=[
+            pltpu.VMEM((late_rows, width + LANES), jnp.bfloat16),
+            pltpu.VMEM((all_rows, 2 * hidden_units), jnp.bfloat16),
+            pltpu.VMEM((all_rows, 2 * LANES), jnp.float32),
+        ],
         compiler_params=pltpu.CompilerParams(vmem_limit_bytes=EXPERTS_VMEM),
         cost_estimate=pl.CostEstimate(
             flops=(8 * late_rows + 4 * all_rows) * width * hidden_units,

time: 110 us -> 119 us (1.082)
  the two profiles are of different devices: /device:TPU:0 before, /device:TPU:7 now
where the time goes in v9:
time: 119 us
  waiting for transfers between devices  51.8 us (44%)
  starting transfers between devices  37.1 us (31%)
  Pallas kernels  16.4 us (14%)
  local copies, waits for them, and re-layouts  10.8 us (9%)
  other arithmetic  2.65 us (2%)
    ppermute x16, waiting for transfers between devices, across(): return lax.ppermute(value, ('ep', 'grp'), pairs)  49.3 us
    ppermute x16, starting transfers between devices, across(): return lax.ppermute(value, ('ep', 'grp'), pairs)  19.5 us
    ppermute x6, starting transfers between devices, between_cores(): return lax.ppermute(value, 'grp', [(0, 1), (1, 0)])  17.6 us
    unnamed x22, local copies, waits for them, and re-layouts  9.87 us
    pallas_call x1, Pallas kernels, experts(): pl.pallas_call(functools.partial(experts_kernel, blocks, done_rows, rows,...  8.43 us
    pallas_call x1, Pallas kernels, early(): pl.pallas_call(functools.partial(early_kernel, blocks), in_specs=[pl.Bloc...  5.77 us
    ppermute x6, waiting for transfers between devices, between_cores(): return lax.ppermute(value, 'grp', [(0, 1), (1, 0)])  2.49 us
  transfers between devices with their start and end apart: 22, of which 12 were waited for; matrix products, arithmetic and copies ran while one was open for 2% of the time, Pallas kernels for 7%

profile of v9, /device:TPU:7, one launch (start us, length us, event | category | flops | bytes accessed | tf_op | source)
XLA Modules:
  0.0 118.9 jit_solution(2635439807811503882)
XLA Ops:
  3.0 2.2 %prepare.1 = bf16[32,7296]{1,0:T(8,128)(2,1)} custom-call(f32[1,7168]{1,0:T(1,128)} %bitcast.17, bf16[16,7168]{1,0:T(8,128)(2,1)} %refs_1_.1, bf16[16,7168]{1,0:T(8,128)(2,1)} %copy-done.9, s32[4,16]{1,0:T(4,128)} %bitcast.19, s32[4,16]{1,0:T(4,128)} %copy-done.10), custom_call_target="tpu_custom_call" | custom-call | flops 1376256 | bytes 917504 | tf_op jit(solution)/shard_map/prepare/pallas_call | solution.py:86
  6.7 6.5 %collective-permute-done.3.refs_0_ = bf16[32,7296]{1,0:T(8,128)(2,1)S(1)} collective-permute-done((bf16[32,7296]{1,0:T(8,128)(2,1)}, bf16[32,7296]{1,0:T(8,128)(2,1)S(1)}, u32[]{:S(2)}, u32[]{:S(2)}) %collective-permute-start.3) | collective-permute-done | bytes 466976 | tf_op jit(solution)/shard_map/ppermute | solution.py:40
  14.0 3.5 %collective-permute-done.2.refs_1_ = bf16[32,7296]{1,0:T(8,128)(2,1)} collective-permute-done((bf16[32,7296]{1,0:T(8,128)(2,1)}, bf16[32,7296]{1,0:T(8,128)(2,1)}, u32[]{:S(2)}, u32[]{:S(2)}) %collective-permute-start.2) | collective-permute-done | bytes 466976 | tf_op jit(solution)/shard_map/ppermute | solution.py:40
  17.5 1.9 %collective-permute-start.7 = (bf16[32,7296]{1,0:T(8,128)(2,1)}, bf16[32,7296]{1,0:T(8,128)(2,1)}, u32[]{:S(2)}, u32[]{:S(2)}) collective-permute-start(bf16[32,7296]{1,0:T(8,128)(2,1)} %collective-permute-done.2.refs_1_), channel_id=1, source_target_pairs={{0,4},{2,6},{4,0},{6,2},{8,12},{10,14},{12,8},{14,10},{16,20},{18,... | collective-permute-start | bytes 1400840 | tf_op jit(solution)/shard_map/ppermute | solution.py:40
  19.4 6.1 %collective-permute-done.4.refs_2_ = bf16[32,7296]{1,0:T(8,128)(2,1)} collective-permute-done((bf16[32,7296]{1,0:T(8,128)(2,1)}, bf16[32,7296]{1,0:T(8,128)(2,1)}, u32[]{:S(2)}, u32[]{:S(2)}) %collective-permute-start.4) | collective-permute-done | bytes 466976 | tf_op jit(solution)/shard_map/ppermute | solution.py:40
  25.6 1.9 %copy-done.4 = bf16[7168,256]{1,0:T(8,128)(2,1)} copy-done((bf16[7168,256]{1,0:T(8,128)(2,1)}, bf16[7168,256]{1,0:T(8,128)(2,1)S(1)}, u32[]{:S(2)}) %copy-start.4) | copy-done | bytes 3670040
  27.5 1.9 %collective-permute-start.6 = (bf16[32,7296]{1,0:T(8,128)(2,1)}, bf16[32,7296]{1,0:T(8,128)(2,1)S(1)}, u32[]{:S(2)}, u32[]{:S(2)}) collective-permute-start(bf16[32,7296]{1,0:T(8,128)(2,1)} %collective-permute-done.4.refs_2_), channel_id=1, source_target_pairs={{0,2},{2,0},{4,6},{6,4},{8,10},{10,8},{12,14},{14,12},{16,18},{18,... | collective-permute-start | bytes 1400840 | tf_op jit(solution)/shard_map/ppermute | solution.py:40
  31.1 2.5 %collective-permute-start.9 = (bf16[32,7296]{1,0:T(8,128)(2,1)}, bf16[32,7296]{1,0:T(8,128)(2,1)S(1)}, u32[]{:S(2)}, u32[]{:S(2)}) collective-permute-start(bf16[32,7296]{1,0:T(8,128)(2,1)} %collective-permute-done.7.refs_3_), channel_id=1, source_target_pairs={{0,2},{2,0},{4,6},{6,4},{8,10},{10,8},{12,14},{14,12},{16,18},{18,... | collective-permute-start | bytes 1400840 | tf_op jit(solution)/shard_map/ppermute | solution.py:40
  33.6 2.4 %collective-permute-done.6.refs_0_ = bf16[32,7296]{1,0:T(8,128)(2,1)S(1)} collective-permute-done((bf16[32,7296]{1,0:T(8,128)(2,1)}, bf16[32,7296]{1,0:T(8,128)(2,1)S(1)}, u32[]{:S(2)}, u32[]{:S(2)}) %collective-permute-start.6) | collective-permute-done | bytes 466976 | tf_op jit(solution)/shard_map/ppermute | solution.py:40
  37.7 2.0 %copy-done = bf16[1,1,7168,256]{3,2,1,0:T(8,128)(2,1)S(1)} copy-done((bf16[1,1,7168,256]{3,2,1,0:T(8,128)(2,1)S(1)}, bf16[1,1,7168,256]{3,2,1,0:T(8,128)(2,1)}, u32[]{:S(2)}) %copy-start) | copy-done | bytes 3670040
  39.7 2.0 %copy-done.2 = bf16[1,1,7168,256]{3,2,1,0:T(8,128)(2,1)S(1)} copy-done((bf16[1,1,7168,256]{3,2,1,0:T(8,128)(2,1)S(1)}, bf16[1,1,7168,256]{3,2,1,0:T(8,128)(2,1)}, u32[]{:S(2)}) %copy-start.2) | copy-done | bytes 3670040
  41.8 2.0 %copy-done.5 = bf16[7168,256]{1,0:T(8,128)(2,1)S(1)} copy-done((bf16[7168,256]{1,0:T(8,128)(2,1)S(1)}, bf16[7168,256]{1,0:T(8,128)(2,1)}, u32[]{:S(2)}) %copy-start.5) | copy-done | bytes 3670040
  44.8 5.8 %early.1 = (bf16[160,512]{1,0:T(8,128)(2,1)S(1)}, f32[160,256]{1,0:T(8,128)S(1)}) custom-call(s32[2]{0:T(128)S(1)} %pad_add_fusion.ids_ref, bf16[32,7296]{1,0:T(8,128)(2,1)S(1)} %copy-done.8, bf16[32,7296]{1,0:T(8,128)(2,1)} %collective-permute-done.2.refs_1_, bf16[32,7296]{1,0:T(8,128)(2,1)} %collective-permute-done.4.refs_2_, ...), custom_call_target="tpu_custom_call" | custom-call | flops 2348810240 | bytes 16973824 | tf_op jit(solution)/shard_map/early/pallas_call | solution.py:134
  50.7 8.4 %experts.1 = (bf16[32,7168]{1,0:T(8,128)(2,1)S(1)}, bf16[32,7168]{1,0:T(8,128)(2,1)S(1)}, bf16[32,7168]{1,0:T(8,128)(2,1)S(1)}, bf16[32,7168]{1,0:T(8,128)(2,1)S...) custom-call(s32[2]{0:T(128)S(1)} %pad_add_fusion.ids_ref, ...), custom_call_target="tpu_custom_call" | custom-call | flops 3288334336 | bytes 29360128 | tf_op jit(solution)/shard_map/experts/pallas_call | solution.py:187
  60.0 2.4 %collective-permute-start.13 = (bf16[32,7168]{1,0:T(8,128)(2,1)S(1)}, bf16[32,7168]{1,0:T(8,128)(2,1)S(1)}, u32[]{:S(2)}, u32[]{:S(2)}) collective-permute-start(bf16[32,7168]{1,0:T(8,128)(2,1)S(1)} %get-tuple-element.42), channel_id=1, source_target_pairs={{0,2},{2,0},{4,6},{6,4},{8,10},{10,8},{12,14},{14,12},{16,18},{18,... | collective-permute-start | bytes 1376264 | tf_op jit(solution)/shard_map/ppermute | solution.py:40
  62.4 9.3 %collective-permute-done.15 = bf16[32,7168]{1,0:T(8,128)(2,1)S(1)} collective-permute-done((bf16[32,7168]{1,0:T(8,128)(2,1)S(1)}, bf16[32,7168]{1,0:T(8,128)(2,1)S(1)}, u32[]{:S(2)}, u32[]{:S(2)}) %collective-permute-start.15) | collective-permute-done | bytes 458784 | tf_op jit(solution)/shard_map/ppermute | solution.py:40
  74.2 5.3 %collective-permute-done.17 = bf16[32,7168]{1,0:T(8,128)(2,1)S(1)} collective-permute-done((bf16[32,7168]{1,0:T(8,128)(2,1)S(1)}, bf16[32,7168]{1,0:T(8,128)(2,1)S(1)}, u32[]{:S(2)}, u32[]{:S(2)}) %collective-permute-start.17) | collective-permute-done | bytes 458784 | tf_op jit(solution)/shard_map/ppermute | solution.py:40
  79.6 2.5 %collective-permute-start.18 = (bf16[32,7168]{1,0:T(8,128)(2,1)S(1)}, bf16[32,7168]{1,0:T(8,128)(2,1)S(1)}, u32[]{:S(2)}, u32[]{:S(2)}) collective-permute-start(bf16[32,7168]{1,0:T(8,128)(2,1)S(1)} %add_convert_fusion.1), channel_id=1, source_target_pairs={{0,8},{2,10},{4,12},{6,14},{8,0},{10,2},{12,4},{14,6},{16,24},{18,... | collective-permute-start | bytes 1376264 | tf_op jit(solution)/shard_map/ppermute | solution.py:40
  82.1 6.5 %collective-permute-done.14 = bf16[32,7168]{1,0:T(8,128)(2,1)S(1)} collective-permute-done((bf16[32,7168]{1,0:T(8,128)(2,1)S(1)}, bf16[32,7168]{1,0:T(8,128)(2,1)S(1)}, u32[]{:S(2)}, u32[]{:S(2)}) %collective-permute-start.14) | collective-permute-done | bytes 458784 | tf_op jit(solution)/shard_map/ppermute | solution.py:40
  88.6 2.2 %collective-permute-start.20 = (bf16[32,7168]{1,0:T(8,128)(2,1)S(1)}, bf16[32,7168]{1,0:T(8,128)(2,1)S(1)}, u32[]{:S(2)}, u32[]{:S(2)}) collective-permute-start(bf16[32,7168]{1,0:T(8,128)(2,1)S(1)} %get-tuple-element.50), channel_id=1, source_target_pairs={{0,2},{2,0},{4,6},{6,4},{8,10},{10,8},{12,14},{14,12},{16,18},{18,... | collective-permute-start | bytes 1376264 | tf_op jit(solution)/shard_map/ppermute | solution.py:40
  90.8 2.4 %collective-permute-done.18 = bf16[32,7168]{1,0:T(8,128)(2,1)S(1)} collective-permute-done((bf16[32,7168]{1,0:T(8,128)(2,1)S(1)}, bf16[32,7168]{1,0:T(8,128)(2,1)S(1)}, u32[]{:S(2)}, u32[]{:S(2)}) %collective-permute-start.18) | collective-permute-done | bytes 458784 | tf_op jit(solution)/shard_map/ppermute | solution.py:40
  93.5 3.5 %collective-permute-done.20 = bf16[32,7168]{1,0:T(8,128)(2,1)S(1)} collective-permute-done((bf16[32,7168]{1,0:T(8,128)(2,1)S(1)}, bf16[32,7168]{1,0:T(8,128)(2,1)S(1)}, u32[]{:S(2)}, u32[]{:S(2)}) %collective-permute-start.20) | collective-permute-done | bytes 458784 | tf_op jit(solution)/shard_map/ppermute | solution.py:40
  96.9 3.9 %collective-permute-done.19 = bf16[32,7168]{1,0:T(8,128)(2,1)S(1)} collective-permute-done((bf16[32,7168]{1,0:T(8,128)(2,1)S(1)}, bf16[32,7168]{1,0:T(8,128)(2,1)S(1)}, u32[]{:S(2)}, u32[]{:S(2)}) %collective-permute-start.19) | collective-permute-done | bytes 458784 | tf_op jit(solution)/shard_map/ppermute | solution.py:40
  101.0 16.0 %collective-permute-start.21 = (bf16[16,7168]{1,0:T(8,128)(2,1)S(1)}, bf16[16,7168]{1,0:T(8,128)(2,1)S(1)}, u32[]{:S(2)}, u32[]{:S(2)}) collective-permute-start(bf16[16,7168]{1,0:T(8,128)(2,1)S(1)} %slice.15), channel_id=1, source_target_pairs={{0,1},{1,0},{2,3},{3,2},{4,5},{5,4},{6,7},{7,6},{8,9},{9,8},{10,11... | collective-permute-start | bytes 688136 | tf_op jit(solution)/shard_map/ppermute | solution.py:48
  (55 shorter events, 15.7 us)
Async XLA Ops:
  0.0 2.0 %collective-permute-start = (bf16[16,7168]{1,0:T(8,128)(2,1)}, bf16[16,7168]{1,0:T(8,128)(2,1)S(1)}, u32[]{:S(2)}, u32[]{:S(2)}) collective-permute-start(bf16[16,7168]{1,0:T(8,128)(2,1)} %refs_1_.1), channel_id=1, source_target_pairs={{0,1},{1,0},{2,3},{3,2},{4,5},{5,4},{6,7},{7,6},{8,9},{9,8},{10,11... | collective-permute-start | bytes 688136 | tf_op jit(solution)/shard_map/ppermute | solution.py:48
  0.7 1.4 %collective-permute-start.1 = (s32[4,16]{1,0:T(4,128)}, s32[4,16]{1,0:T(4,128)S(1)}, u32[]{:S(2)}, u32[]{:S(2)}) collective-permute-start(s32[4,16]{1,0:T(4,128)} %bitcast.18), channel_id=1, source_target_pairs={{0,1},{1,0},{2,3},{3,2},{4,5},{5,4},{6,7},{7,6},{8,9},{9,8},{10,11... | collective-permute-start | bytes 776 | tf_op jit(solution)/shard_map/ppermute | solution.py:48
  2.1 23.5 %collective-permute-start.5 = (bf16[7168,256]{1,0:T(8,128)(2,1)}, bf16[7168,256]{1,0:T(8,128)(2,1)S(1)}, u32[]{:S(2)}, u32[]{:S(2)}) collective-permute-start(bf16[7168,256]{1,0:T(8,128)(2,1)} %bitcast.8), channel_id=1, source_target_pairs={{0,1},{1,0},{2,3},{3,2},{4,5},{5,4},{6,7},{7,6},{8,9},{9,8},{10,11... | collective-permute-start | bytes 11010056 | tf_op jit(solution)/shard_map/ppermute | solution.py:48
  2.4 28.7 %collective-permute-start.8 = (bf16[7168,256]{1,0:T(8,128)(2,1)}, bf16[7168,256]{1,0:T(8,128)(2,1)}, u32[]{:S(2)}, u32[]{:S(2)}) collective-permute-start(bf16[7168,256]{1,0:T(8,128)(2,1)} %bitcast.11), channel_id=1, source_target_pairs={{0,1},{1,0},{2,3},{3,2},{4,5},{5,4},{6,7},{7,6},{8,9},{9,8},{10,11... | collective-permute-start | bytes 11010056 | tf_op jit(solution)/shard_map/ppermute | solution.py:48
  2.6 48.0 %collective-permute-start.11 = (bf16[256,7168]{1,0:T(8,128)(2,1)}, bf16[256,7168]{1,0:T(8,128)(2,1)}, u32[]{:S(2)}, u32[]{:S(2)}) collective-permute-start(bf16[256,7168]{1,0:T(8,128)(2,1)} %bitcast.14), channel_id=1, source_target_pairs={{0,1},{1,0},{2,3},{3,2},{4,5},{5,4},{6,7},{7,6},{8,9},{9,8},{10,11... | collective-permute-start | bytes 11010056 | tf_op jit(solution)/shard_map/ppermute | solution.py:48
  5.2 8.1 %collective-permute-start.3 = (bf16[32,7296]{1,0:T(8,128)(2,1)}, bf16[32,7296]{1,0:T(8,128)(2,1)S(1)}, u32[]{:S(2)}, u32[]{:S(2)}) collective-permute-start(bf16[32,7296]{1,0:T(8,128)(2,1)} %prepare.1), channel_id=1, source_target_pairs={{0,2},{2,0},{4,6},{6,4},{8,10},{10,8},{12,14},{14,12},{16,18},{18,... | collective-permute-start | bytes 1400840 | tf_op jit(solution)/shard_map/ppermute | solution.py:40
  5.5 12.1 %collective-permute-start.2 = (bf16[32,7296]{1,0:T(8,128)(2,1)}, bf16[32,7296]{1,0:T(8,128)(2,1)}, u32[]{:S(2)}, u32[]{:S(2)}) collective-permute-start(bf16[32,7296]{1,0:T(8,128)(2,1)} %prepare.1), channel_id=1, source_target_pairs={{0,16},{2,18},{4,20},{6,22},{8,24},{10,26},{12,28},{14,30},{16,0},... | collective-permute-start | bytes 1400840 | tf_op jit(solution)/shard_map/ppermute | solution.py:40
  17.5 8.0 %collective-permute-start.4 = (bf16[32,7296]{1,0:T(8,128)(2,1)}, bf16[32,7296]{1,0:T(8,128)(2,1)}, u32[]{:S(2)}, u32[]{:S(2)}) collective-permute-start(bf16[32,7296]{1,0:T(8,128)(2,1)} %collective-permute-done.2.refs_1_), channel_id=1, source_target_pairs={{0,8},{2,10},{4,12},{6,14},{8,0},{10,2},{12,4},{14,6},{16,24},{18,... | collective-permute-start | bytes 1400840 | tf_op jit(solution)/shard_map/ppermute | solution.py:40
  17.5 13.6 %collective-permute-start.7 = (bf16[32,7296]{1,0:T(8,128)(2,1)}, bf16[32,7296]{1,0:T(8,128)(2,1)}, u32[]{:S(2)}, u32[]{:S(2)}) collective-permute-start(bf16[32,7296]{1,0:T(8,128)(2,1)} %collective-permute-done.2.refs_1_), channel_id=1, source_target_pairs={{0,4},{2,6},{4,0},{6,2},{8,12},{10,14},{12,8},{14,10},{16,20},{18,... | collective-permute-start | bytes 1400840 | tf_op jit(solution)/shard_map/ppermute | solution.py:40
  27.5 8.4 %collective-permute-start.6 = (bf16[32,7296]{1,0:T(8,128)(2,1)}, bf16[32,7296]{1,0:T(8,128)(2,1)S(1)}, u32[]{:S(2)}, u32[]{:S(2)}) collective-permute-start(bf16[32,7296]{1,0:T(8,128)(2,1)} %collective-permute-done.4.refs_2_), channel_id=1, source_target_pairs={{0,2},{2,0},{4,6},{6,4},{8,10},{10,8},{12,14},{14,12},{16,18},{18,... | collective-permute-start | bytes 1400840 | tf_op jit(solution)/shard_map/ppermute | solution.py:40
  29.4 7.2 %collective-permute-start.12 = (bf16[32,7296]{1,0:T(8,128)(2,1)}, bf16[32,7296]{1,0:T(8,128)(2,1)S(1)}, u32[]{:S(2)}, u32[]{:S(2)}) collective-permute-start(bf16[32,7296]{1,0:T(8,128)(2,1)} %collective-permute-done.2.refs_1_), channel_id=1, source_target_pairs={{0,2},{2,0},{4,6},{6,4},{8,10},{10,8},{12,14},{14,12},{16,18},{18,... | collective-permute-start | bytes 1400840 | tf_op jit(solution)/shard_map/ppermute | solution.py:40
  31.1 19.5 %collective-permute-start.9 = (bf16[32,7296]{1,0:T(8,128)(2,1)}, bf16[32,7296]{1,0:T(8,128)(2,1)S(1)}, u32[]{:S(2)}, u32[]{:S(2)}) collective-permute-start(bf16[32,7296]{1,0:T(8,128)(2,1)} %collective-permute-done.7.refs_3_), channel_id=1, source_target_pairs={{0,2},{2,0},{4,6},{6,4},{8,10},{10,8},{12,14},{14,12},{16,18},{18,... | collective-permute-start | bytes 1400840 | tf_op jit(solution)/shard_map/ppermute | solution.py:40
  35.9 14.7 %collective-permute-start.10 = (bf16[32,7296]{1,0:T(8,128)(2,1)S(1)}, bf16[32,7296]{1,0:T(8,128)(2,1)S(1)}, u32[]{:S(2)}, u32[]{:S(2)}) collective-permute-start(bf16[32,7296]{1,0:T(8,128)(2,1)S(1)} %collective-permute-done.6.refs_0_), channel_id=1, source_target_pairs={{0,4},{2,6},{4,0},{6,2},{8,12},{10,14},{12,8},{14,10},{16,20},{18,... | collective-permute-start | bytes 1400840 | tf_op jit(solution)/shard_map/ppermute | solution.py:40
  44.8 5.8 %copy-start.3 = (bf16[1,1,7168,256]{3,2,1,0:T(8,128)(2,1)S(1)}, bf16[1,1,7168,256]{3,2,1,0:T(8,128)(2,1)}, u32[]{:S(2)}) copy-start(bf16[1,1,7168,256]{3,2,1,0:T(8,128)(2,1)} %param.12) | copy-start | bytes 11010052
  44.8 5.8 %copy-start.6 = (bf16[1,1,256,7168]{3,2,1,0:T(8,128)(2,1)S(1)}, bf16[1,1,256,7168]{3,2,1,0:T(8,128)(2,1)}, u32[]{:S(2)}) copy-start(bf16[1,1,256,7168]{3,2,1,0:T(8,128)(2,1)} %param.13) | copy-start | bytes 11010052
  59.1 12.6 %collective-permute-start.15 = (bf16[32,7168]{1,0:T(8,128)(2,1)S(1)}, bf16[32,7168]{1,0:T(8,128)(2,1)S(1)}, u32[]{:S(2)}, u32[]{:S(2)}) collective-permute-start(bf16[32,7168]{1,0:T(8,128)(2,1)S(1)} %get-tuple-element.43), channel_id=1, source_target_pairs={{0,4},{2,6},{4,0},{6,2},{8,12},{10,14},{12,8},{14,10},{16,20},{18,... | collective-permute-start | bytes 1376264 | tf_op jit(solution)/shard_map/ppermute | solution.py:40
  60.0 13.3 %collective-permute-start.13 = (bf16[32,7168]{1,0:T(8,128)(2,1)S(1)}, bf16[32,7168]{1,0:T(8,128)(2,1)S(1)}, u32[]{:S(2)}, u32[]{:S(2)}) collective-permute-start(bf16[32,7168]{1,0:T(8,128)(2,1)S(1)} %get-tuple-element.42), channel_id=1, source_target_pairs={{0,2},{2,0},{4,6},{6,4},{8,10},{10,8},{12,14},{14,12},{16,18},{18,... | collective-permute-start | bytes 1376264 | tf_op jit(solution)/shard_map/ppermute | solution.py:40
  71.8 7.7 %collective-permute-start.17 = (bf16[32,7168]{1,0:T(8,128)(2,1)S(1)}, bf16[32,7168]{1,0:T(8,128)(2,1)S(1)}, u32[]{:S(2)}, u32[]{:S(2)}) collective-permute-start(bf16[32,7168]{1,0:T(8,128)(2,1)S(1)} %add_convert_fusion.2), channel_id=1, source_target_pairs={{0,2},{2,0},{4,6},{6,4},{8,10},{10,8},{12,14},{14,12},{16,18},{18,... | collective-permute-start | bytes 1376264 | tf_op jit(solution)/shard_map/ppermute | solution.py:40
  73.4 15.1 %collective-permute-start.14 = (bf16[32,7168]{1,0:T(8,128)(2,1)S(1)}, bf16[32,7168]{1,0:T(8,128)(2,1)S(1)}, u32[]{:S(2)}, u32[]{:S(2)}) collective-permute-start(bf16[32,7168]{1,0:T(8,128)(2,1)S(1)} %add_convert_fusion.3), channel_id=1, source_target_pairs={{0,4},{2,6},{4,0},{6,2},{8,12},{10,14},{12,8},{14,10},{16,20},{18,... | collective-permute-start | bytes 1376264 | tf_op jit(solution)/shard_map/ppermute | solution.py:40
  73.5 17.2 %collective-permute-start.16 = (bf16[32,7168]{1,0:T(8,128)(2,1)S(1)}, bf16[32,7168]{1,0:T(8,128)(2,1)S(1)}, u32[]{:S(2)}, u32[]{:S(2)}) collective-permute-start(bf16[32,7168]{1,0:T(8,128)(2,1)S(1)} %get-tuple-element.44), channel_id=1, source_target_pairs={{0,2},{2,0},{4,6},{6,4},{8,10},{10,8},{12,14},{14,12},{16,18},{18,... | collective-permute-start | bytes 1376264 | tf_op jit(solution)/shard_map/ppermute | solution.py:40
  79.6 13.5 %collective-permute-start.18 = (bf16[32,7168]{1,0:T(8,128)(2,1)S(1)}, bf16[32,7168]{1,0:T(8,128)(2,1)S(1)}, u32[]{:S(2)}, u32[]{:S(2)}) collective-permute-start(bf16[32,7168]{1,0:T(8,128)(2,1)S(1)} %add_convert_fusion.1), channel_id=1, source_target_pairs={{0,8},{2,10},{4,12},{6,14},{8,0},{10,2},{12,4},{14,6},{16,24},{18,... | collective-permute-start | bytes 1376264 | tf_op jit(solution)/shard_map/ppermute | solution.py:40
  88.6 8.4 %collective-permute-start.20 = (bf16[32,7168]{1,0:T(8,128)(2,1)S(1)}, bf16[32,7168]{1,0:T(8,128)(2,1)S(1)}, u32[]{:S(2)}, u32[]{:S(2)}) collective-permute-start(bf16[32,7168]{1,0:T(8,128)(2,1)S(1)} %get-tuple-element.50), channel_id=1, source_target_pairs={{0,2},{2,0},{4,6},{6,4},{8,10},{10,8},{12,14},{14,12},{16,18},{18,... | collective-permute-start | bytes 1376264 | tf_op jit(solution)/shard_map/ppermute | solution.py:40
  93.4 7.4 %collective-permute-start.19 = (bf16[32,7168]{1,0:T(8,128)(2,1)S(1)}, bf16[32,7168]{1,0:T(8,128)(2,1)S(1)}, u32[]{:S(2)}, u32[]{:S(2)}) collective-permute-start(bf16[32,7168]{1,0:T(8,128)(2,1)S(1)} %add_convert_fusion), channel_id=1, source_target_pairs={{0,16},{2,18},{4,20},{6,22},{8,24},{10,26},{12,28},{14,30},{16,0},... | collective-permute-start | bytes 1376264 | tf_op jit(solution)/shard_map/ppermute | solution.py:40
  101.0 17.2 %collective-permute-start.21 = (bf16[16,7168]{1,0:T(8,128)(2,1)S(1)}, bf16[16,7168]{1,0:T(8,128)(2,1)S(1)}, u32[]{:S(2)}, u32[]{:S(2)}) collective-permute-start(bf16[16,7168]{1,0:T(8,128)(2,1)S(1)} %slice.15), channel_id=1, source_target_pairs={{0,1},{1,0},{2,3},{3,2},{4,5},{5,4},{6,7},{7,6},{8,9},{9,8},{10,11... | collective-permute-start | bytes 688136 | tf_op jit(solution)/shard_map/ppermute | solution.py:48
  (9 other events, 17.5 us)

commit v10 on v9

--- a/solution.py
+++ b/solution.py
@@ -14,6 +14,7 @@
 ROUTE_SCALE = 2.5
 PREPARE_VMEM = 60 * 1024 * 1024
 EXPERTS_VMEM = 16 * 1024 * 1024
+EARLY_VMEM = 36 * 1024 * 1024
 
 PLAN_16 = ((0, 1, 2), (0, 8, 4), (2, 4, 1), (2, 2, 2), (2, 1, 0), (3, 1, 2), (4, 1, 8), (6, 2, 4))
 RETURN_16 = tuple((slot, PLAN_16[slot - 1]) for slot in (8, 7, 6, 4, 5, 3, 2, 1))
@@ -96,7 +97,7 @@
     )(*operands)
 
 
-def gate_up(ids_ref, token_refs, router_ref, weight_refs, tokens_ref):
+def gate_up(ids_ref, token_refs, router_ref, weight_refs, tokens_ref, copies=()):
     rows = token_refs[0].shape[0]
     width = weight_refs[0].shape[0]
     for i, ref in enumerate(token_refs):
@@ -112,42 +113,58 @@
     chosen = named * jax.nn.sigmoid(logits)
     weights = ROUTE_SCALE * chosen / jnp.sum(chosen, axis=1, keepdims=True)
     lanes = lax.broadcasted_iota(jnp.int32, weights.shape, 1)
-    acts, columns = [], []
+    acts, columns = [None, None], []
+    for i in (1, 0):
+        if i == 0:
+            for copy in copies:
+                copy.wait()
+        acts[i] = (jax.nn.silu(product(weight_refs[i])) * product(weight_refs[2 + i])).astype(jnp.bfloat16)
     for i in range(2):
-        acts.append((jax.nn.silu(product(weight_refs[i])) * product(weight_refs[2 + i])).astype(jnp.bfloat16))
         column = jnp.sum(jnp.where(lanes == ids_ref[i], weights, 0.0), axis=1, keepdims=True)
         columns.append(jnp.broadcast_to(column, (column.shape[0], LANES)))
     return jnp.concatenate(acts, axis=1), jnp.concatenate(columns, axis=1)
 
 
 def early_kernel(blocks, ids_ref, *refs):
-    token_refs, router_ref, weight_refs = refs[:blocks], refs[blocks], refs[blocks + 1 : blocks + 5]
-    act_ref, coeff_ref, tokens_ref = refs[blocks + 5 :]
-    act_ref[...], coeff_ref[...] = gate_up(ids_ref, token_refs, router_ref, weight_refs, tokens_ref)
-
-
-def early(ids, token_blocks, router_t, gates, ups):
+    token_refs, router_ref = refs[:blocks], refs[blocks]
+    gate1_ref, up1_ref, *own_hbm = refs[blocks + 1 : blocks + 6]
+    act_ref, coeff_ref, *own_refs, tokens_ref, sems = refs[blocks + 6 :]
+    copies = [
+        pltpu.make_async_copy(source, target, sems.at[i]) for i, (source, target) in enumerate(zip(own_hbm, own_refs))
+    ]
+    for copy in copies:
+        copy.start()
+    weight_refs = (own_refs[0], gate1_ref, own_refs[1], up1_ref)
+    act_ref[...], coeff_ref[...] = gate_up(ids_ref, token_refs, router_ref, weight_refs, tokens_ref, copies[:2])
+    copies[2].wait()
+
+
+def early(ids, token_blocks, router_t, gates, ups, downs):
     blocks = len(token_blocks)
     width, hidden_units = gates[0].shape
     rows = blocks * token_blocks[0].shape[0]
     in_vmem = pl.BlockSpec(memory_space=pltpu.VMEM)
+    own = (gates[0], ups[0], downs[0])
     return pl.pallas_call(
         functools.partial(early_kernel, blocks),
-        in_specs=[pl.BlockSpec(memory_space=pltpu.SMEM)] + [in_vmem] * (blocks + 5),
-        out_specs=[in_vmem] * 2,
+        in_specs=[pl.BlockSpec(memory_space=pltpu.SMEM)]
+        + [in_vmem] * (blocks + 3)
+        + [pl.BlockSpec(memory_space=pl.ANY)] * 3,
+        out_specs=[in_vmem] * 5,
         out_shape=[
             jax.ShapeDtypeStruct((rows, 2 * hidden_units), jnp.bfloat16),
             jax.ShapeDtypeStruct((rows, 2 * LANES), jnp.float32),
-        ],
-        scratch_shapes=[pltpu.VMEM((rows, width + LANES), jnp.bfloat16)],
-        compiler_params=pltpu.CompilerParams(vmem_limit_bytes=EXPERTS_VMEM),
+        ]
+        + [jax.ShapeDtypeStruct(w.shape, w.dtype) for w in own],
+        scratch_shapes=[pltpu.VMEM((rows, width + LANES), jnp.bfloat16), pltpu.SemaphoreType.DMA((3,))],
+        compiler_params=pltpu.CompilerParams(vmem_limit_bytes=EARLY_VMEM),
         cost_estimate=pl.CostEstimate(
             flops=8 * rows * width * hidden_units,
             bytes_accessed=8 * width * hidden_units + 2 * rows * width,
             transcendentals=2 * rows * hidden_units,
         ),
         name="early",
-    )(ids, *token_blocks, router_t, *gates, *ups)
+    )(ids, *token_blocks, router_t, gates[1], ups[1], *own)
 
 
 def experts_kernel(blocks, done_rows, rows, n_tile, ids_ref, *refs):
@@ -231,8 +248,12 @@
 
     ids = jnp.stack([core * local_experts + place, (1 - core) * local_experts + place]).astype(jnp.int32)
     router_t = jnp.pad(router_w.T, ((0, -expert_count % 16), (0, 0)))
-    done = early(ids, held[1 : 1 + EARLY], router_t, *weights[:2]) if paired else ()
-    outs = experts(ids, held[1 + EARLY :] if paired else held, done, router_t, *weights)
+    done, late = (), held
+    if paired:
+        *done, own_gate, own_up, own_down = early(ids, held[1 : 1 + EARLY], router_t, *weights)
+        weights = [(w, pair[1]) for w, pair in zip((own_gate, own_up, own_down), weights)]
+        late = held[1 + EARLY :]
+    outs = experts(ids, late, done, router_t, *weights)
 
     terms = {slot: [value] for slot, value in enumerate(outs, first)}
     if paired:

time: 119 us -> 118 us (level)
  local copies, waits for them, and re-layouts: 10.8 us -> 6.73 us
  Pallas kernels: 16.4 us -> 18.7 us
    unnamed x22 -> x14, local copies, waits for them, and re-layouts: 9.87 us -> 5.79 us
    pallas_call x1, Pallas kernels: 5.77 us -> 7.7 us  [early(): pl.pallas_call(functools.partial(early_kernel, blocks), in_specs=[pl.Bloc...]
  transfers between devices with their start and end apart: 22 -> 22, of which waited for: 12 -> 12; matrix products, arithmetic and copies ran while one was open for 2% -> 2% of each run, Pallas kernels for 7% -> 8%
where the time goes in v10:
time: 118 us; the launch traced here: 117 us
  waiting for transfers between devices  51.8 us (44%)
  starting transfers between devices  37.1 us (31%)
  Pallas kernels  18.7 us (16%)
  local copies, waits for them, and re-layouts  6.73 us (6%)
  other arithmetic  2.65 us (2%)
    ppermute x16, waiting for transfers between devices, across(): return lax.ppermute(value, ('ep', 'grp'), pairs)  49.3 us
    ppermute x16, starting transfers between devices, across(): return lax.ppermute(value, ('ep', 'grp'), pairs)  19.5 us
    ppermute x6, starting transfers between devices, between_cores(): return lax.ppermute(value, 'grp', [(0, 1), (1, 0)])  17.6 us
    pallas_call x1, Pallas kernels, experts(): pl.pallas_call(functools.partial(experts_kernel, blocks, done_rows, rows,...  8.84 us
    pallas_call x1, Pallas kernels, early(): pl.pallas_call(functools.partial(early_kernel, blocks), in_specs=[pl.Bloc...  7.7 us
    unnamed x14, local copies, waits for them, and re-layouts  5.79 us
    ppermute x6, waiting for transfers between devices, between_cores(): return lax.ppermute(value, 'grp', [(0, 1), (1, 0)])  2.49 us
  transfers between devices with their start and end apart: 22, of which 12 were waited for; matrix products, arithmetic and copies ran while one was open for 2% of the time, Pallas kernels for 8%

profile of v10, /device:TPU:7, one launch (start us, length us, event | category | flops | bytes accessed | tf_op | source)
XLA Modules:
  0.0 117.3 jit_solution(11915099196781076807)
XLA Ops:
  0.7 1.4 %collective-permute-done.1.refs_4_ = s32[4,16]{1,0:T(4,128)S(1)} collective-permute-done((s32[4,16]{1,0:T(4,128)}, s32[4,16]{1,0:T(4,128)S(1)}, u32[]{:S(2)}, u32[]{:S(2)}) %collective-permute-start.1) | collective-permute-done | bytes 288 | tf_op jit(solution)/shard_map/ppermute | solution.py:49
  3.0 2.2 %prepare.1 = bf16[32,7296]{1,0:T(8,128)(2,1)} custom-call(f32[1,7168]{1,0:T(1,128)} %bitcast.15, bf16[16,7168]{1,0:T(8,128)(2,1)} %refs_1_.1, bf16[16,7168]{1,0:T(8,128)(2,1)} %copy-done.5, s32[4,16]{1,0:T(4,128)} %bitcast.17, s32[4,16]{1,0:T(4,128)} %copy-done.6), custom_call_target="tpu_custom_call" | custom-call | flops 1376256 | bytes 917504 | tf_op jit(solution)/shard_map/prepare/pallas_call | solution.py:87
  6.8 6.5 %collective-permute-done.3.refs_0_ = bf16[32,7296]{1,0:T(8,128)(2,1)S(1)} collective-permute-done((bf16[32,7296]{1,0:T(8,128)(2,1)}, bf16[32,7296]{1,0:T(8,128)(2,1)S(1)}, u32[]{:S(2)}, u32[]{:S(2)}) %collective-permute-start.3) | collective-permute-done | bytes 466976 | tf_op jit(solution)/shard_map/ppermute | solution.py:41
  14.1 3.5 %collective-permute-done.2.refs_1_ = bf16[32,7296]{1,0:T(8,128)(2,1)} collective-permute-done((bf16[32,7296]{1,0:T(8,128)(2,1)}, bf16[32,7296]{1,0:T(8,128)(2,1)}, u32[]{:S(2)}, u32[]{:S(2)}) %collective-permute-start.2) | collective-permute-done | bytes 466976 | tf_op jit(solution)/shard_map/ppermute | solution.py:41
  17.5 1.9 %collective-permute-start.7 = (bf16[32,7296]{1,0:T(8,128)(2,1)}, bf16[32,7296]{1,0:T(8,128)(2,1)}, u32[]{:S(2)}, u32[]{:S(2)}) collective-permute-start(bf16[32,7296]{1,0:T(8,128)(2,1)} %collective-permute-done.2.refs_1_), channel_id=1, source_target_pairs={{0,4},{2,6},{4,0},{6,2},{8,12},{10,14},{12,8},{14,10},{16,20},{18,... | collective-permute-start | bytes 1400840 | tf_op jit(solution)/shard_map/ppermute | solution.py:41
  19.4 6.1 %collective-permute-done.4.refs_2_ = bf16[32,7296]{1,0:T(8,128)(2,1)} collective-permute-done((bf16[32,7296]{1,0:T(8,128)(2,1)}, bf16[32,7296]{1,0:T(8,128)(2,1)}, u32[]{:S(2)}, u32[]{:S(2)}) %collective-permute-start.4) | collective-permute-done | bytes 466976 | tf_op jit(solution)/shard_map/ppermute | solution.py:41
  25.6 1.9 %copy-done = bf16[7168,256]{1,0:T(8,128)(2,1)} copy-done((bf16[7168,256]{1,0:T(8,128)(2,1)}, bf16[7168,256]{1,0:T(8,128)(2,1)S(1)}, u32[]{:S(2)}) %copy-start) | copy-done | bytes 3670040
  27.5 1.9 %collective-permute-start.6 = (bf16[32,7296]{1,0:T(8,128)(2,1)}, bf16[32,7296]{1,0:T(8,128)(2,1)S(1)}, u32[]{:S(2)}, u32[]{:S(2)}) collective-permute-start(bf16[32,7296]{1,0:T(8,128)(2,1)} %collective-permute-done.4.refs_2_), channel_id=1, source_target_pairs={{0,2},{2,0},{4,6},{6,4},{8,10},{10,8},{12,14},{14,12},{16,18},{18,... | collective-permute-start | bytes 1400840 | tf_op jit(solution)/shard_map/ppermute | solution.py:41
  31.1 2.5 %collective-permute-start.9 = (bf16[32,7296]{1,0:T(8,128)(2,1)}, bf16[32,7296]{1,0:T(8,128)(2,1)S(1)}, u32[]{:S(2)}, u32[]{:S(2)}) collective-permute-start(bf16[32,7296]{1,0:T(8,128)(2,1)} %collective-permute-done.7.refs_3_), channel_id=1, source_target_pairs={{0,2},{2,0},{4,6},{6,4},{8,10},{10,8},{12,14},{14,12},{16,18},{18,... | collective-permute-start | bytes 1400840 | tf_op jit(solution)/shard_map/ppermute | solution.py:41
  33.6 2.4 %collective-permute-done.6.refs_0_ = bf16[32,7296]{1,0:T(8,128)(2,1)S(1)} collective-permute-done((bf16[32,7296]{1,0:T(8,128)(2,1)}, bf16[32,7296]{1,0:T(8,128)(2,1)S(1)}, u32[]{:S(2)}, u32[]{:S(2)}) %collective-permute-start.6) | collective-permute-done | bytes 466976 | tf_op jit(solution)/shard_map/ppermute | solution.py:41
  37.7 2.0 %copy-done.1 = bf16[7168,256]{1,0:T(8,128)(2,1)S(1)} copy-done((bf16[7168,256]{1,0:T(8,128)(2,1)S(1)}, bf16[7168,256]{1,0:T(8,128)(2,1)}, u32[]{:S(2)}) %copy-start.1) | copy-done | bytes 3670040
  40.8 7.7 %early.1 = (bf16[160,512]{1,0:T(8,128)(2,1)S(1)}, f32[160,256]{1,0:T(8,128)S(1)}, bf16[7168,256]{1,0:T(8,128)(2,1)S(1)}, bf16[7168,256]{1,0:T(8,128)(2,1)S(1)}, bf16[256,7168]{1,0:T(8,128)(2,1)S(1)}) custom-call(s32[2]{0:T(128)S(1)} %pad_add_fusion.ids_ref, bf16[32,7296]{1,0:T(8,128)(2,1)S(1)} %copy-done.4, bf16[32,7296]{1,0:T(8,128)(2,1)} %collective-permute-done.2.refs_1_, ...), custom_call_target="tpu_custom_call" | custom-call | flops 2348810240 | bytes 16973824 | tf_op jit(solution)/shard_map/early/pallas_call | solution.py:148
  48.5 8.8 %experts.1 = (bf16[32,7168]{1,0:T(8,128)(2,1)S(1)}, bf16[32,7168]{1,0:T(8,128)(2,1)S(1)}, bf16[32,7168]{1,0:T(8,128)(2,1)S(1)}, bf16[32,7168]{1,0:T(8,128)(2,1)S...) custom-call(s32[2]{0:T(128)S(1)} %pad_add_fusion.ids_ref, ...), custom_call_target="tpu_custom_call" | custom-call | flops 3288334336 | bytes 29360128 | tf_op jit(solution)/shard_map/experts/pallas_call | solution.py:204
  58.2 2.4 %collective-permute-start.13 = (bf16[32,7168]{1,0:T(8,128)(2,1)S(1)}, bf16[32,7168]{1,0:T(8,128)(2,1)S(1)}, u32[]{:S(2)}, u32[]{:S(2)}) collective-permute-start(bf16[32,7168]{1,0:T(8,128)(2,1)S(1)} %get-tuple-element.48), channel_id=1, source_target_pairs={{0,2},{2,0},{4,6},{6,4},{8,10},{10,8},{12,14},{14,12},{16,18},{18,... | collective-permute-start | bytes 1376264 | tf_op jit(solution)/shard_map/ppermute | solution.py:41
  60.6 9.3 %collective-permute-done.15 = bf16[32,7168]{1,0:T(8,128)(2,1)S(1)} collective-permute-done((bf16[32,7168]{1,0:T(8,128)(2,1)S(1)}, bf16[32,7168]{1,0:T(8,128)(2,1)S(1)}, u32[]{:S(2)}, u32[]{:S(2)}) %collective-permute-start.15) | collective-permute-done | bytes 458784 | tf_op jit(solution)/shard_map/ppermute | solution.py:41
  70.1 1.5 %collective-permute-start.17 = (bf16[32,7168]{1,0:T(8,128)(2,1)S(1)}, bf16[32,7168]{1,0:T(8,128)(2,1)S(1)}, u32[]{:S(2)}, u32[]{:S(2)}) collective-permute-start(bf16[32,7168]{1,0:T(8,128)(2,1)S(1)} %add_convert_fusion.2), channel_id=1, source_target_pairs={{0,2},{2,0},{4,6},{6,4},{8,10},{10,8},{12,14},{14,12},{16,18},{18,... | collective-permute-start | bytes 1376264 | tf_op jit(solution)/shard_map/ppermute | solution.py:41
  72.5 5.3 %collective-permute-done.17 = bf16[32,7168]{1,0:T(8,128)(2,1)S(1)} collective-permute-done((bf16[32,7168]{1,0:T(8,128)(2,1)S(1)}, bf16[32,7168]{1,0:T(8,128)(2,1)S(1)}, u32[]{:S(2)}, u32[]{:S(2)}) %collective-permute-start.17) | collective-permute-done | bytes 458784 | tf_op jit(solution)/shard_map/ppermute | solution.py:41
  77.9 2.5 %collective-permute-start.18 = (bf16[32,7168]{1,0:T(8,128)(2,1)S(1)}, bf16[32,7168]{1,0:T(8,128)(2,1)S(1)}, u32[]{:S(2)}, u32[]{:S(2)}) collective-permute-start(bf16[32,7168]{1,0:T(8,128)(2,1)S(1)} %add_convert_fusion.1), channel_id=1, source_target_pairs={{0,8},{2,10},{4,12},{6,14},{8,0},{10,2},{12,4},{14,6},{16,24},{18,... | collective-permute-start | bytes 1376264 | tf_op jit(solution)/shard_map/ppermute | solution.py:41
  80.4 6.5 %collective-permute-done.14 = bf16[32,7168]{1,0:T(8,128)(2,1)S(1)} collective-permute-done((bf16[32,7168]{1,0:T(8,128)(2,1)S(1)}, bf16[32,7168]{1,0:T(8,128)(2,1)S(1)}, u32[]{:S(2)}, u32[]{:S(2)}) %collective-permute-start.14) | collective-permute-done | bytes 458784 | tf_op jit(solution)/shard_map/ppermute | solution.py:41
  86.8 2.2 %collective-permute-start.20 = (bf16[32,7168]{1,0:T(8,128)(2,1)S(1)}, bf16[32,7168]{1,0:T(8,128)(2,1)S(1)}, u32[]{:S(2)}, u32[]{:S(2)}) collective-permute-start(bf16[32,7168]{1,0:T(8,128)(2,1)S(1)} %get-tuple-element.56), channel_id=1, source_target_pairs={{0,2},{2,0},{4,6},{6,4},{8,10},{10,8},{12,14},{14,12},{16,18},{18,... | collective-permute-start | bytes 1376264 | tf_op jit(solution)/shard_map/ppermute | solution.py:41
  89.0 2.5 %collective-permute-done.18 = bf16[32,7168]{1,0:T(8,128)(2,1)S(1)} collective-permute-done((bf16[32,7168]{1,0:T(8,128)(2,1)S(1)}, bf16[32,7168]{1,0:T(8,128)(2,1)S(1)}, u32[]{:S(2)}, u32[]{:S(2)}) %collective-permute-start.18) | collective-permute-done | bytes 458784 | tf_op jit(solution)/shard_map/ppermute | solution.py:41
  91.8 3.4 %collective-permute-done.20 = bf16[32,7168]{1,0:T(8,128)(2,1)S(1)} collective-permute-done((bf16[32,7168]{1,0:T(8,128)(2,1)S(1)}, bf16[32,7168]{1,0:T(8,128)(2,1)S(1)}, u32[]{:S(2)}, u32[]{:S(2)}) %collective-permute-start.20) | collective-permute-done | bytes 458784 | tf_op jit(solution)/shard_map/ppermute | solution.py:41
  95.2 3.9 %collective-permute-done.19 = bf16[32,7168]{1,0:T(8,128)(2,1)S(1)} collective-permute-done((bf16[32,7168]{1,0:T(8,128)(2,1)S(1)}, bf16[32,7168]{1,0:T(8,128)(2,1)S(1)}, u32[]{:S(2)}, u32[]{:S(2)}) %collective-permute-start.19) | collective-permute-done | bytes 458784 | tf_op jit(solution)/shard_map/ppermute | solution.py:41
  99.3 16.0 %collective-permute-start.21 = (bf16[16,7168]{1,0:T(8,128)(2,1)S(1)}, bf16[16,7168]{1,0:T(8,128)(2,1)S(1)}, u32[]{:S(2)}, u32[]{:S(2)}) collective-permute-start(bf16[16,7168]{1,0:T(8,128)(2,1)S(1)} %slice.15), channel_id=1, source_target_pairs={{0,1},{1,0},{2,3},{3,2},{4,5},{5,4},{6,7},{7,6},{8,9},{9,8},{10,11... | collective-permute-start | bytes 688136 | tf_op jit(solution)/shard_map/ppermute | solution.py:49
  (47 shorter events, 12.8 us)
Async XLA Ops:
  0.0 2.0 %collective-permute-start = (bf16[16,7168]{1,0:T(8,128)(2,1)}, bf16[16,7168]{1,0:T(8,128)(2,1)S(1)}, u32[]{:S(2)}, u32[]{:S(2)}) collective-permute-start(bf16[16,7168]{1,0:T(8,128)(2,1)} %refs_1_.1), channel_id=1, source_target_pairs={{0,1},{1,0},{2,3},{3,2},{4,5},{5,4},{6,7},{7,6},{8,9},{9,8},{10,11... | collective-permute-start | bytes 688136 | tf_op jit(solution)/shard_map/ppermute | solution.py:49
  0.7 1.4 %collective-permute-start.1 = (s32[4,16]{1,0:T(4,128)}, s32[4,16]{1,0:T(4,128)S(1)}, u32[]{:S(2)}, u32[]{:S(2)}) collective-permute-start(s32[4,16]{1,0:T(4,128)} %bitcast.16), channel_id=1, source_target_pairs={{0,1},{1,0},{2,3},{3,2},{4,5},{5,4},{6,7},{7,6},{8,9},{9,8},{10,11... | collective-permute-start | bytes 776 | tf_op jit(solution)/shard_map/ppermute | solution.py:49
  2.1 23.5 %collective-permute-start.5 = (bf16[7168,256]{1,0:T(8,128)(2,1)}, bf16[7168,256]{1,0:T(8,128)(2,1)S(1)}, u32[]{:S(2)}, u32[]{:S(2)}) collective-permute-start(bf16[7168,256]{1,0:T(8,128)(2,1)} %bitcast.8), channel_id=1, source_target_pairs={{0,1},{1,0},{2,3},{3,2},{4,5},{5,4},{6,7},{7,6},{8,9},{9,8},{10,11... | collective-permute-start | bytes 11010056 | tf_op jit(solution)/shard_map/ppermute | solution.py:49
  2.4 28.7 %collective-permute-start.8 = (bf16[7168,256]{1,0:T(8,128)(2,1)}, bf16[7168,256]{1,0:T(8,128)(2,1)}, u32[]{:S(2)}, u32[]{:S(2)}) collective-permute-start(bf16[7168,256]{1,0:T(8,128)(2,1)} %bitcast.10), channel_id=1, source_target_pairs={{0,1},{1,0},{2,3},{3,2},{4,5},{5,4},{6,7},{7,6},{8,9},{9,8},{10,11... | collective-permute-start | bytes 11010056 | tf_op jit(solution)/shard_map/ppermute | solution.py:49
  2.6 45.8 %collective-permute-start.12 = (bf16[256,7168]{1,0:T(8,128)(2,1)}, bf16[256,7168]{1,0:T(8,128)(2,1)}, u32[]{:S(2)}, u32[]{:S(2)}) collective-permute-start(bf16[256,7168]{1,0:T(8,128)(2,1)} %bitcast.12), channel_id=1, source_target_pairs={{0,1},{1,0},{2,3},{3,2},{4,5},{5,4},{6,7},{7,6},{8,9},{9,8},{10,11... | collective-permute-start | bytes 11010056 | tf_op jit(solution)/shard_map/ppermute | solution.py:49
  5.2 8.1 %collective-permute-start.3 = (bf16[32,7296]{1,0:T(8,128)(2,1)}, bf16[32,7296]{1,0:T(8,128)(2,1)S(1)}, u32[]{:S(2)}, u32[]{:S(2)}) collective-permute-start(bf16[32,7296]{1,0:T(8,128)(2,1)} %prepare.1), channel_id=1, source_target_pairs={{0,2},{2,0},{4,6},{6,4},{8,10},{10,8},{12,14},{14,12},{16,18},{18,... | collective-permute-start | bytes 1400840 | tf_op jit(solution)/shard_map/ppermute | solution.py:41
  5.5 12.1 %collective-permute-start.2 = (bf16[32,7296]{1,0:T(8,128)(2,1)}, bf16[32,7296]{1,0:T(8,128)(2,1)}, u32[]{:S(2)}, u32[]{:S(2)}) collective-permute-start(bf16[32,7296]{1,0:T(8,128)(2,1)} %prepare.1), channel_id=1, source_target_pairs={{0,16},{2,18},{4,20},{6,22},{8,24},{10,26},{12,28},{14,30},{16,0},... | collective-permute-start | bytes 1400840 | tf_op jit(solution)/shard_map/ppermute | solution.py:41
  17.5 8.0 %collective-permute-start.4 = (bf16[32,7296]{1,0:T(8,128)(2,1)}, bf16[32,7296]{1,0:T(8,128)(2,1)}, u32[]{:S(2)}, u32[]{:S(2)}) collective-permute-start(bf16[32,7296]{1,0:T(8,128)(2,1)} %collective-permute-done.2.refs_1_), channel_id=1, source_target_pairs={{0,8},{2,10},{4,12},{6,14},{8,0},{10,2},{12,4},{14,6},{16,24},{18,... | collective-permute-start | bytes 1400840 | tf_op jit(solution)/shard_map/ppermute | solution.py:41
  17.5 13.6 %collective-permute-start.7 = (bf16[32,7296]{1,0:T(8,128)(2,1)}, bf16[32,7296]{1,0:T(8,128)(2,1)}, u32[]{:S(2)}, u32[]{:S(2)}) collective-permute-start(bf16[32,7296]{1,0:T(8,128)(2,1)} %collective-permute-done.2.refs_1_), channel_id=1, source_target_pairs={{0,4},{2,6},{4,0},{6,2},{8,12},{10,14},{12,8},{14,10},{16,20},{18,... | collective-permute-start | bytes 1400840 | tf_op jit(solution)/shard_map/ppermute | solution.py:41
  27.5 8.4 %collective-permute-start.6 = (bf16[32,7296]{1,0:T(8,128)(2,1)}, bf16[32,7296]{1,0:T(8,128)(2,1)S(1)}, u32[]{:S(2)}, u32[]{:S(2)}) collective-permute-start(bf16[32,7296]{1,0:T(8,128)(2,1)} %collective-permute-done.4.refs_2_), channel_id=1, source_target_pairs={{0,2},{2,0},{4,6},{6,4},{8,10},{10,8},{12,14},{14,12},{16,18},{18,... | collective-permute-start | bytes 1400840 | tf_op jit(solution)/shard_map/ppermute | solution.py:41
  29.4 7.2 %collective-permute-start.11 = (bf16[32,7296]{1,0:T(8,128)(2,1)}, bf16[32,7296]{1,0:T(8,128)(2,1)S(1)}, u32[]{:S(2)}, u32[]{:S(2)}) collective-permute-start(bf16[32,7296]{1,0:T(8,128)(2,1)} %collective-permute-done.2.refs_1_), channel_id=1, source_target_pairs={{0,2},{2,0},{4,6},{6,4},{8,10},{10,8},{12,14},{14,12},{16,18},{18,... | collective-permute-start | bytes 1400840 | tf_op jit(solution)/shard_map/ppermute | solution.py:41
  31.1 17.4 %collective-permute-start.9 = (bf16[32,7296]{1,0:T(8,128)(2,1)}, bf16[32,7296]{1,0:T(8,128)(2,1)S(1)}, u32[]{:S(2)}, u32[]{:S(2)}) collective-permute-start(bf16[32,7296]{1,0:T(8,128)(2,1)} %collective-permute-done.7.refs_3_), channel_id=1, source_target_pairs={{0,2},{2,0},{4,6},{6,4},{8,10},{10,8},{12,14},{14,12},{16,18},{18,... | collective-permute-start | bytes 1400840 | tf_op jit(solution)/shard_map/ppermute | solution.py:41
  35.9 12.6 %collective-permute-start.10 = (bf16[32,7296]{1,0:T(8,128)(2,1)S(1)}, bf16[32,7296]{1,0:T(8,128)(2,1)S(1)}, u32[]{:S(2)}, u32[]{:S(2)}) collective-permute-start(bf16[32,7296]{1,0:T(8,128)(2,1)S(1)} %collective-permute-done.6.refs_0_), channel_id=1, source_target_pairs={{0,4},{2,6},{4,0},{6,2},{8,12},{10,14},{12,8},{14,10},{16,20},{18,... | collective-permute-start | bytes 1400840 | tf_op jit(solution)/shard_map/ppermute | solution.py:41
  37.7 2.0 %copy-start.1 = (bf16[7168,256]{1,0:T(8,128)(2,1)S(1)}, bf16[7168,256]{1,0:T(8,128)(2,1)}, u32[]{:S(2)}) copy-start(bf16[7168,256]{1,0:T(8,128)(2,1)} %copy-done) | copy-start | bytes 11010052
  40.7 7.7 %copy-start.2 = (bf16[7168,256]{1,0:T(8,128)(2,1)S(1)}, bf16[7168,256]{1,0:T(8,128)(2,1)}, u32[]{:S(2)}) copy-start(bf16[7168,256]{1,0:T(8,128)(2,1)} %copy-done) | copy-start | bytes 11010052
  57.4 12.6 %collective-permute-start.15 = (bf16[32,7168]{1,0:T(8,128)(2,1)S(1)}, bf16[32,7168]{1,0:T(8,128)(2,1)S(1)}, u32[]{:S(2)}, u32[]{:S(2)}) collective-permute-start(bf16[32,7168]{1,0:T(8,128)(2,1)S(1)} %get-tuple-element.49), channel_id=1, source_target_pairs={{0,4},{2,6},{4,0},{6,2},{8,12},{10,14},{12,8},{14,10},{16,20},{18,... | collective-permute-start | bytes 1376264 | tf_op jit(solution)/shard_map/ppermute | solution.py:41
  58.2 13.4 %collective-permute-start.13 = (bf16[32,7168]{1,0:T(8,128)(2,1)S(1)}, bf16[32,7168]{1,0:T(8,128)(2,1)S(1)}, u32[]{:S(2)}, u32[]{:S(2)}) collective-permute-start(bf16[32,7168]{1,0:T(8,128)(2,1)S(1)} %get-tuple-element.48), channel_id=1, source_target_pairs={{0,2},{2,0},{4,6},{6,4},{8,10},{10,8},{12,14},{14,12},{16,18},{18,... | collective-permute-start | bytes 1376264 | tf_op jit(solution)/shard_map/ppermute | solution.py:41
  70.1 7.7 %collective-permute-start.17 = (bf16[32,7168]{1,0:T(8,128)(2,1)S(1)}, bf16[32,7168]{1,0:T(8,128)(2,1)S(1)}, u32[]{:S(2)}, u32[]{:S(2)}) collective-permute-start(bf16[32,7168]{1,0:T(8,128)(2,1)S(1)} %add_convert_fusion.2), channel_id=1, source_target_pairs={{0,2},{2,0},{4,6},{6,4},{8,10},{10,8},{12,14},{14,12},{16,18},{18,... | collective-permute-start | bytes 1376264 | tf_op jit(solution)/shard_map/ppermute | solution.py:41
  71.7 15.1 %collective-permute-start.14 = (bf16[32,7168]{1,0:T(8,128)(2,1)S(1)}, bf16[32,7168]{1,0:T(8,128)(2,1)S(1)}, u32[]{:S(2)}, u32[]{:S(2)}) collective-permute-start(bf16[32,7168]{1,0:T(8,128)(2,1)S(1)} %add_convert_fusion.3), channel_id=1, source_target_pairs={{0,4},{2,6},{4,0},{6,2},{8,12},{10,14},{12,8},{14,10},{16,20},{18,... | collective-permute-start | bytes 1376264 | tf_op jit(solution)/shard_map/ppermute | solution.py:41
  71.8 17.2 %collective-permute-start.16 = (bf16[32,7168]{1,0:T(8,128)(2,1)S(1)}, bf16[32,7168]{1,0:T(8,128)(2,1)S(1)}, u32[]{:S(2)}, u32[]{:S(2)}) collective-permute-start(bf16[32,7168]{1,0:T(8,128)(2,1)S(1)} %get-tuple-element.50), channel_id=1, source_target_pairs={{0,2},{2,0},{4,6},{6,4},{8,10},{10,8},{12,14},{14,12},{16,18},{18,... | collective-permute-start | bytes 1376264 | tf_op jit(solution)/shard_map/ppermute | solution.py:41
  77.9 13.6 %collective-permute-start.18 = (bf16[32,7168]{1,0:T(8,128)(2,1)S(1)}, bf16[32,7168]{1,0:T(8,128)(2,1)S(1)}, u32[]{:S(2)}, u32[]{:S(2)}) collective-permute-start(bf16[32,7168]{1,0:T(8,128)(2,1)S(1)} %add_convert_fusion.1), channel_id=1, source_target_pairs={{0,8},{2,10},{4,12},{6,14},{8,0},{10,2},{12,4},{14,6},{16,24},{18,... | collective-permute-start | bytes 1376264 | tf_op jit(solution)/shard_map/ppermute | solution.py:41
  86.8 8.4 %collective-permute-start.20 = (bf16[32,7168]{1,0:T(8,128)(2,1)S(1)}, bf16[32,7168]{1,0:T(8,128)(2,1)S(1)}, u32[]{:S(2)}, u32[]{:S(2)}) collective-permute-start(bf16[32,7168]{1,0:T(8,128)(2,1)S(1)} %get-tuple-element.56), channel_id=1, source_target_pairs={{0,2},{2,0},{4,6},{6,4},{8,10},{10,8},{12,14},{14,12},{16,18},{18,... | collective-permute-start | bytes 1376264 | tf_op jit(solution)/shard_map/ppermute | solution.py:41
  91.7 7.4 %collective-permute-start.19 = (bf16[32,7168]{1,0:T(8,128)(2,1)S(1)}, bf16[32,7168]{1,0:T(8,128)(2,1)S(1)}, u32[]{:S(2)}, u32[]{:S(2)}) collective-permute-start(bf16[32,7168]{1,0:T(8,128)(2,1)S(1)} %add_convert_fusion), channel_id=1, source_target_pairs={{0,16},{2,18},{4,20},{6,22},{8,24},{10,26},{12,28},{14,30},{16,0},... | collective-permute-start | bytes 1376264 | tf_op jit(solution)/shard_map/ppermute | solution.py:41
  99.3 17.2 %collective-permute-start.21 = (bf16[16,7168]{1,0:T(8,128)(2,1)S(1)}, bf16[16,7168]{1,0:T(8,128)(2,1)S(1)}, u32[]{:S(2)}, u32[]{:S(2)}) collective-permute-start(bf16[16,7168]{1,0:T(8,128)(2,1)S(1)} %slice.15), channel_id=1, source_target_pairs={{0,1},{1,0},{2,3},{3,2},{4,5},{5,4},{6,7},{7,6},{8,9},{9,8},{10,11... | collective-permute-start | bytes 688136 | tf_op jit(solution)/shard_map/ppermute | solution.py:49
  (5 other events, 5.6 us)

commit v11 on v10

--- a/solution.py
+++ b/solution.py
@@ -14,14 +14,14 @@
 ROUTE_SCALE = 2.5
 PREPARE_VMEM = 60 * 1024 * 1024
 EXPERTS_VMEM = 16 * 1024 * 1024
-EARLY_VMEM = 36 * 1024 * 1024
+EARLY_VMEM = 32 * 1024 * 1024
 
 PLAN_16 = ((0, 1, 2), (0, 8, 4), (2, 4, 1), (2, 2, 2), (2, 1, 0), (3, 1, 2), (4, 1, 8), (6, 2, 4))
 RETURN_16 = tuple((slot, PLAN_16[slot - 1]) for slot in (8, 7, 6, 4, 5, 3, 2, 1))
 OPEN_16 = (2, 2, 2, 2, 2, 3, 4, 4)
 WEIGHTS_END_16 = {6: 0, 7: 1}
 OPEN_RETURN = 4
-EARLY = 5
+EARLY = 4
 
 
 def plan_for(ep_count, grp_count):

time: 118 us -> 117 us (level)
  transfers between devices with their start and end apart: 22 -> 22, of which waited for: 12 -> 13; matrix products, arithmetic and copies ran while one was open for 2% -> 2% of each run, Pallas kernels for 8% -> 8%
where the time goes in v11:
time: 117 us
  waiting for transfers between devices  52.1 us (45%)
  starting transfers between devices  36.9 us (32%)
  Pallas kernels  18.1 us (15%)
  local copies, waits for them, and re-layouts  6.73 us (6%)
  other arithmetic  2.64 us (2%)
    ppermute x16, waiting for transfers between devices, across(): return lax.ppermute(value, ('ep', 'grp'), pairs)  49.6 us
    ppermute x16, starting transfers between devices, across(): return lax.ppermute(value, ('ep', 'grp'), pairs)  19.1 us
    ppermute x6, starting transfers between devices, between_cores(): return lax.ppermute(value, 'grp', [(0, 1), (1, 0)])  17.8 us
    pallas_call x1, Pallas kernels, experts(): pl.pallas_call(functools.partial(experts_kernel, blocks, done_rows, rows,...  8.86 us
    pallas_call x1, Pallas kernels, early(): pl.pallas_call(functools.partial(early_kernel, blocks), in_specs=[pl.Bloc...  7.06 us
    unnamed x14, local copies, waits for them, and re-layouts  5.79 us
    ppermute x6, waiting for transfers between devices, between_cores(): return lax.ppermute(value, 'grp', [(0, 1), (1, 0)])  2.49 us
  transfers between devices with their start and end apart: 22, of which 13 were waited for; matrix products, arithmetic and copies ran while one was open for 2% of the time, Pallas kernels for 8%

profile of v11, /device:TPU:7, one launch (start us, length us, event | category | flops | bytes accessed | tf_op | source)
XLA Modules:
  0.0 116.6 jit_solution(10868313744450882950)
XLA Ops:
  0.7 1.4 %collective-permute-done.1.refs_4_ = s32[4,16]{1,0:T(4,128)S(1)} collective-permute-done((s32[4,16]{1,0:T(4,128)}, s32[4,16]{1,0:T(4,128)S(1)}, u32[]{:S(2)}, u32[]{:S(2)}) %collective-permute-start.1) | collective-permute-done | bytes 288 | tf_op jit(solution)/shard_map/ppermute | solution.py:49
  3.0 2.2 %prepare.1 = bf16[32,7296]{1,0:T(8,128)(2,1)} custom-call(f32[1,7168]{1,0:T(1,128)} %bitcast.15, bf16[16,7168]{1,0:T(8,128)(2,1)} %refs_1_.1, bf16[16,7168]{1,0:T(8,128)(2,1)} %copy-done.5, s32[4,16]{1,0:T(4,128)} %bitcast.17, s32[4,16]{1,0:T(4,128)} %copy-done.6), custom_call_target="tpu_custom_call" | custom-call | flops 1376256 | bytes 917504 | tf_op jit(solution)/shard_map/prepare/pallas_call | solution.py:87
  6.8 6.5 %collective-permute-done.3.refs_0_ = bf16[32,7296]{1,0:T(8,128)(2,1)S(1)} collective-permute-done((bf16[32,7296]{1,0:T(8,128)(2,1)}, bf16[32,7296]{1,0:T(8,128)(2,1)S(1)}, u32[]{:S(2)}, u32[]{:S(2)}) %collective-permute-start.3) | collective-permute-done | bytes 466976 | tf_op jit(solution)/shard_map/ppermute | solution.py:41
  14.1 3.5 %collective-permute-done.2.refs_1_ = bf16[32,7296]{1,0:T(8,128)(2,1)} collective-permute-done((bf16[32,7296]{1,0:T(8,128)(2,1)}, bf16[32,7296]{1,0:T(8,128)(2,1)}, u32[]{:S(2)}, u32[]{:S(2)}) %collective-permute-start.2) | collective-permute-done | bytes 466976 | tf_op jit(solution)/shard_map/ppermute | solution.py:41
  17.5 1.9 %collective-permute-start.8 = (bf16[32,7296]{1,0:T(8,128)(2,1)}, bf16[32,7296]{1,0:T(8,128)(2,1)}, u32[]{:S(2)}, u32[]{:S(2)}) collective-permute-start(bf16[32,7296]{1,0:T(8,128)(2,1)} %collective-permute-done.2.refs_1_), channel_id=1, source_target_pairs={{0,4},{2,6},{4,0},{6,2},{8,12},{10,14},{12,8},{14,10},{16,20},{18,... | collective-permute-start | bytes 1400840 | tf_op jit(solution)/shard_map/ppermute | solution.py:41
  19.4 6.1 %collective-permute-done.4.refs_2_ = bf16[32,7296]{1,0:T(8,128)(2,1)} collective-permute-done((bf16[32,7296]{1,0:T(8,128)(2,1)}, bf16[32,7296]{1,0:T(8,128)(2,1)}, u32[]{:S(2)}, u32[]{:S(2)}) %collective-permute-start.4) | collective-permute-done | bytes 466976 | tf_op jit(solution)/shard_map/ppermute | solution.py:41
  25.6 1.9 %copy-done = bf16[7168,256]{1,0:T(8,128)(2,1)} copy-done((bf16[7168,256]{1,0:T(8,128)(2,1)}, bf16[7168,256]{1,0:T(8,128)(2,1)S(1)}, u32[]{:S(2)}) %copy-start) | copy-done | bytes 3670040
  27.5 1.9 %collective-permute-start.7 = (bf16[32,7296]{1,0:T(8,128)(2,1)}, bf16[32,7296]{1,0:T(8,128)(2,1)S(1)}, u32[]{:S(2)}, u32[]{:S(2)}) collective-permute-start(bf16[32,7296]{1,0:T(8,128)(2,1)} %collective-permute-done.4.refs_2_), channel_id=1, source_target_pairs={{0,2},{2,0},{4,6},{6,4},{8,10},{10,8},{12,14},{14,12},{16,18},{18,... | collective-permute-start | bytes 1400840 | tf_op jit(solution)/shard_map/ppermute | solution.py:41
  31.1 2.5 %collective-permute-start.10 = (bf16[32,7296]{1,0:T(8,128)(2,1)}, bf16[32,7296]{1,0:T(8,128)(2,1)S(1)}, u32[]{:S(2)}, u32[]{:S(2)}) collective-permute-start(bf16[32,7296]{1,0:T(8,128)(2,1)} %collective-permute-done.8.refs_3_), channel_id=1, source_target_pairs={{0,2},{2,0},{4,6},{6,4},{8,10},{10,8},{12,14},{14,12},{16,18},{18,... | collective-permute-start | bytes 1400840 | tf_op jit(solution)/shard_map/ppermute | solution.py:41
  33.6 2.4 %collective-permute-done.7.refs_1_ = bf16[32,7296]{1,0:T(8,128)(2,1)S(1)} collective-permute-done((bf16[32,7296]{1,0:T(8,128)(2,1)}, bf16[32,7296]{1,0:T(8,128)(2,1)S(1)}, u32[]{:S(2)}, u32[]{:S(2)}) %collective-permute-start.7) | collective-permute-done | bytes 466976 | tf_op jit(solution)/shard_map/ppermute | solution.py:41
  37.7 2.0 %copy-done.1 = bf16[7168,256]{1,0:T(8,128)(2,1)S(1)} copy-done((bf16[7168,256]{1,0:T(8,128)(2,1)S(1)}, bf16[7168,256]{1,0:T(8,128)(2,1)}, u32[]{:S(2)}) %copy-start.1) | copy-done | bytes 3670040
  40.8 7.1 %early.1 = (bf16[128,512]{1,0:T(8,128)(2,1)S(1)}, f32[128,256]{1,0:T(8,128)S(1)}, bf16[7168,256]{1,0:T(8,128)(2,1)S(1)}, bf16[7168,256]{1,0:T(8,128)(2,1)S(1)}, bf16[256,7168]{1,0:T(8,128)(2,1)S(1)}) custom-call(s32[2]{0:T(128)S(1)} %pad_add_fusion.ids_ref, bf16[32,7296]{1,0:T(8,128)(2,1)S(1)} %copy-done.4, bf16[32,7296]{1,0:T(8,128)(2,1)} %collective-permute-done.2.refs_1_, ...), custom_call_target="tpu_custom_call" | custom-call | flops 1879048192 | bytes 16515072 | tf_op jit(solution)/shard_map/early/pallas_call | solution.py:148
  48.2 8.9 %experts.1 = (bf16[32,7168]{1,0:T(8,128)(2,1)S(1)}, bf16[32,7168]{1,0:T(8,128)(2,1)S(1)}, bf16[32,7168]{1,0:T(8,128)(2,1)S(1)}, bf16[32,7168]{1,0:T(8,128)(2,1)S...) custom-call(s32[2]{0:T(128)S(1)} %pad_add_fusion.ids_ref, ...), custom_call_target="tpu_custom_call" | custom-call | flops 3758096384 | bytes 29360128 | tf_op jit(solution)/shard_map/experts/pallas_call | solution.py:204
  57.6 2.4 %collective-permute-start.13 = (bf16[32,7168]{1,0:T(8,128)(2,1)S(1)}, bf16[32,7168]{1,0:T(8,128)(2,1)S(1)}, u32[]{:S(2)}, u32[]{:S(2)}) collective-permute-start(bf16[32,7168]{1,0:T(8,128)(2,1)S(1)} %get-tuple-element.48), channel_id=1, source_target_pairs={{0,2},{2,0},{4,6},{6,4},{8,10},{10,8},{12,14},{14,12},{16,18},{18,... | collective-permute-start | bytes 1376264 | tf_op jit(solution)/shard_map/ppermute | solution.py:41
  60.0 9.7 %collective-permute-done.15 = bf16[32,7168]{1,0:T(8,128)(2,1)S(1)} collective-permute-done((bf16[32,7168]{1,0:T(8,128)(2,1)S(1)}, bf16[32,7168]{1,0:T(8,128)(2,1)S(1)}, u32[]{:S(2)}, u32[]{:S(2)}) %collective-permute-start.15) | collective-permute-done | bytes 458784 | tf_op jit(solution)/shard_map/ppermute | solution.py:41
  69.8 1.4 %collective-permute-start.17 = (bf16[32,7168]{1,0:T(8,128)(2,1)S(1)}, bf16[32,7168]{1,0:T(8,128)(2,1)S(1)}, u32[]{:S(2)}, u32[]{:S(2)}) collective-permute-start(bf16[32,7168]{1,0:T(8,128)(2,1)S(1)} %add_convert_fusion.2), channel_id=1, source_target_pairs={{0,2},{2,0},{4,6},{6,4},{8,10},{10,8},{12,14},{14,12},{16,18},{18,... | collective-permute-start | bytes 1376264 | tf_op jit(solution)/shard_map/ppermute | solution.py:41
  72.2 5.3 %collective-permute-done.17 = bf16[32,7168]{1,0:T(8,128)(2,1)S(1)} collective-permute-done((bf16[32,7168]{1,0:T(8,128)(2,1)S(1)}, bf16[32,7168]{1,0:T(8,128)(2,1)S(1)}, u32[]{:S(2)}, u32[]{:S(2)}) %collective-permute-start.17) | collective-permute-done | bytes 458784 | tf_op jit(solution)/shard_map/ppermute | solution.py:41
  77.7 2.6 %collective-permute-start.18 = (bf16[32,7168]{1,0:T(8,128)(2,1)S(1)}, bf16[32,7168]{1,0:T(8,128)(2,1)S(1)}, u32[]{:S(2)}, u32[]{:S(2)}) collective-permute-start(bf16[32,7168]{1,0:T(8,128)(2,1)S(1)} %add_convert_fusion.1), channel_id=1, source_target_pairs={{0,8},{2,10},{4,12},{6,14},{8,0},{10,2},{12,4},{14,6},{16,24},{18,... | collective-permute-start | bytes 1376264 | tf_op jit(solution)/shard_map/ppermute | solution.py:41
  80.3 6.5 %collective-permute-done.14 = bf16[32,7168]{1,0:T(8,128)(2,1)S(1)} collective-permute-done((bf16[32,7168]{1,0:T(8,128)(2,1)S(1)}, bf16[32,7168]{1,0:T(8,128)(2,1)S(1)}, u32[]{:S(2)}, u32[]{:S(2)}) %collective-permute-start.14) | collective-permute-done | bytes 458784 | tf_op jit(solution)/shard_map/ppermute | solution.py:41
  86.7 1.9 %collective-permute-start.20 = (bf16[32,7168]{1,0:T(8,128)(2,1)S(1)}, bf16[32,7168]{1,0:T(8,128)(2,1)S(1)}, u32[]{:S(2)}, u32[]{:S(2)}) collective-permute-start(bf16[32,7168]{1,0:T(8,128)(2,1)S(1)} %get-tuple-element.56), channel_id=1, source_target_pairs={{0,2},{2,0},{4,6},{6,4},{8,10},{10,8},{12,14},{14,12},{16,18},{18,... | collective-permute-start | bytes 1376264 | tf_op jit(solution)/shard_map/ppermute | solution.py:41
  88.7 2.0 %collective-permute-done.18 = bf16[32,7168]{1,0:T(8,128)(2,1)S(1)} collective-permute-done((bf16[32,7168]{1,0:T(8,128)(2,1)S(1)}, bf16[32,7168]{1,0:T(8,128)(2,1)S(1)}, u32[]{:S(2)}, u32[]{:S(2)}) %collective-permute-start.18) | collective-permute-done | bytes 458784 | tf_op jit(solution)/shard_map/ppermute | solution.py:41
  91.1 3.7 %collective-permute-done.20 = bf16[32,7168]{1,0:T(8,128)(2,1)S(1)} collective-permute-done((bf16[32,7168]{1,0:T(8,128)(2,1)S(1)}, bf16[32,7168]{1,0:T(8,128)(2,1)S(1)}, u32[]{:S(2)}, u32[]{:S(2)}) %collective-permute-start.20) | collective-permute-done | bytes 458784 | tf_op jit(solution)/shard_map/ppermute | solution.py:41
  94.8 3.5 %collective-permute-done.19 = bf16[32,7168]{1,0:T(8,128)(2,1)S(1)} collective-permute-done((bf16[32,7168]{1,0:T(8,128)(2,1)S(1)}, bf16[32,7168]{1,0:T(8,128)(2,1)S(1)}, u32[]{:S(2)}, u32[]{:S(2)}) %collective-permute-start.19) | collective-permute-done | bytes 458784 | tf_op jit(solution)/shard_map/ppermute | solution.py:41
  98.5 16.3 %collective-permute-start.21 = (bf16[16,7168]{1,0:T(8,128)(2,1)S(1)}, bf16[16,7168]{1,0:T(8,128)(2,1)S(1)}, u32[]{:S(2)}, u32[]{:S(2)}) collective-permute-start(bf16[16,7168]{1,0:T(8,128)(2,1)S(1)} %slice.15), channel_id=1, source_target_pairs={{0,1},{1,0},{2,3},{3,2},{4,5},{5,4},{6,7},{7,6},{8,9},{9,8},{10,11... | collective-permute-start | bytes 688136 | tf_op jit(solution)/shard_map/ppermute | solution.py:49
  (47 shorter events, 13.1 us)
Async XLA Ops:
  0.0 2.0 %collective-permute-start = (bf16[16,7168]{1,0:T(8,128)(2,1)}, bf16[16,7168]{1,0:T(8,128)(2,1)S(1)}, u32[]{:S(2)}, u32[]{:S(2)}) collective-permute-start(bf16[16,7168]{1,0:T(8,128)(2,1)} %refs_1_.1), channel_id=1, source_target_pairs={{0,1},{1,0},{2,3},{3,2},{4,5},{5,4},{6,7},{7,6},{8,9},{9,8},{10,11... | collective-permute-start | bytes 688136 | tf_op jit(solution)/shard_map/ppermute | solution.py:49
  0.7 1.4 %collective-permute-start.1 = (s32[4,16]{1,0:T(4,128)}, s32[4,16]{1,0:T(4,128)S(1)}, u32[]{:S(2)}, u32[]{:S(2)}) collective-permute-start(s32[4,16]{1,0:T(4,128)} %bitcast.16), channel_id=1, source_target_pairs={{0,1},{1,0},{2,3},{3,2},{4,5},{5,4},{6,7},{7,6},{8,9},{9,8},{10,11... | collective-permute-start | bytes 776 | tf_op jit(solution)/shard_map/ppermute | solution.py:49
  2.1 23.5 %collective-permute-start.6 = (bf16[7168,256]{1,0:T(8,128)(2,1)}, bf16[7168,256]{1,0:T(8,128)(2,1)S(1)}, u32[]{:S(2)}, u32[]{:S(2)}) collective-permute-start(bf16[7168,256]{1,0:T(8,128)(2,1)} %bitcast.8), channel_id=1, source_target_pairs={{0,1},{1,0},{2,3},{3,2},{4,5},{5,4},{6,7},{7,6},{8,9},{9,8},{10,11... | collective-permute-start | bytes 11010056 | tf_op jit(solution)/shard_map/ppermute | solution.py:49
  2.4 28.7 %collective-permute-start.9 = (bf16[7168,256]{1,0:T(8,128)(2,1)}, bf16[7168,256]{1,0:T(8,128)(2,1)}, u32[]{:S(2)}, u32[]{:S(2)}) collective-permute-start(bf16[7168,256]{1,0:T(8,128)(2,1)} %bitcast.10), channel_id=1, source_target_pairs={{0,1},{1,0},{2,3},{3,2},{4,5},{5,4},{6,7},{7,6},{8,9},{9,8},{10,11... | collective-permute-start | bytes 11010056 | tf_op jit(solution)/shard_map/ppermute | solution.py:49
  2.6 45.2 %collective-permute-start.12 = (bf16[256,7168]{1,0:T(8,128)(2,1)}, bf16[256,7168]{1,0:T(8,128)(2,1)}, u32[]{:S(2)}, u32[]{:S(2)}) collective-permute-start(bf16[256,7168]{1,0:T(8,128)(2,1)} %bitcast.12), channel_id=1, source_target_pairs={{0,1},{1,0},{2,3},{3,2},{4,5},{5,4},{6,7},{7,6},{8,9},{9,8},{10,11... | collective-permute-start | bytes 11010056 | tf_op jit(solution)/shard_map/ppermute | solution.py:49
  5.2 8.1 %collective-permute-start.3 = (bf16[32,7296]{1,0:T(8,128)(2,1)}, bf16[32,7296]{1,0:T(8,128)(2,1)S(1)}, u32[]{:S(2)}, u32[]{:S(2)}) collective-permute-start(bf16[32,7296]{1,0:T(8,128)(2,1)} %prepare.1), channel_id=1, source_target_pairs={{0,2},{2,0},{4,6},{6,4},{8,10},{10,8},{12,14},{14,12},{16,18},{18,... | collective-permute-start | bytes 1400840 | tf_op jit(solution)/shard_map/ppermute | solution.py:41
  5.5 12.1 %collective-permute-start.2 = (bf16[32,7296]{1,0:T(8,128)(2,1)}, bf16[32,7296]{1,0:T(8,128)(2,1)}, u32[]{:S(2)}, u32[]{:S(2)}) collective-permute-start(bf16[32,7296]{1,0:T(8,128)(2,1)} %prepare.1), channel_id=1, source_target_pairs={{0,16},{2,18},{4,20},{6,22},{8,24},{10,26},{12,28},{14,30},{16,0},... | collective-permute-start | bytes 1400840 | tf_op jit(solution)/shard_map/ppermute | solution.py:41
  17.5 8.0 %collective-permute-start.4 = (bf16[32,7296]{1,0:T(8,128)(2,1)}, bf16[32,7296]{1,0:T(8,128)(2,1)}, u32[]{:S(2)}, u32[]{:S(2)}) collective-permute-start(bf16[32,7296]{1,0:T(8,128)(2,1)} %collective-permute-done.2.refs_1_), channel_id=1, source_target_pairs={{0,8},{2,10},{4,12},{6,14},{8,0},{10,2},{12,4},{14,6},{16,24},{18,... | collective-permute-start | bytes 1400840 | tf_op jit(solution)/shard_map/ppermute | solution.py:41
  17.5 13.6 %collective-permute-start.8 = (bf16[32,7296]{1,0:T(8,128)(2,1)}, bf16[32,7296]{1,0:T(8,128)(2,1)}, u32[]{:S(2)}, u32[]{:S(2)}) collective-permute-start(bf16[32,7296]{1,0:T(8,128)(2,1)} %collective-permute-done.2.refs_1_), channel_id=1, source_target_pairs={{0,4},{2,6},{4,0},{6,2},{8,12},{10,14},{12,8},{14,10},{16,20},{18,... | collective-permute-start | bytes 1400840 | tf_op jit(solution)/shard_map/ppermute | solution.py:41
  27.5 8.4 %collective-permute-start.7 = (bf16[32,7296]{1,0:T(8,128)(2,1)}, bf16[32,7296]{1,0:T(8,128)(2,1)S(1)}, u32[]{:S(2)}, u32[]{:S(2)}) collective-permute-start(bf16[32,7296]{1,0:T(8,128)(2,1)} %collective-permute-done.4.refs_2_), channel_id=1, source_target_pairs={{0,2},{2,0},{4,6},{6,4},{8,10},{10,8},{12,14},{14,12},{16,18},{18,... | collective-permute-start | bytes 1400840 | tf_op jit(solution)/shard_map/ppermute | solution.py:41
  29.4 7.2 %collective-permute-start.5 = (bf16[32,7296]{1,0:T(8,128)(2,1)}, bf16[32,7296]{1,0:T(8,128)(2,1)S(1)}, u32[]{:S(2)}, u32[]{:S(2)}) collective-permute-start(bf16[32,7296]{1,0:T(8,128)(2,1)} %collective-permute-done.2.refs_1_), channel_id=1, source_target_pairs={{0,2},{2,0},{4,6},{6,4},{8,10},{10,8},{12,14},{14,12},{16,18},{18,... | collective-permute-start | bytes 1400840 | tf_op jit(solution)/shard_map/ppermute | solution.py:41
  31.1 16.7 %collective-permute-start.10 = (bf16[32,7296]{1,0:T(8,128)(2,1)}, bf16[32,7296]{1,0:T(8,128)(2,1)S(1)}, u32[]{:S(2)}, u32[]{:S(2)}) collective-permute-start(bf16[32,7296]{1,0:T(8,128)(2,1)} %collective-permute-done.8.refs_3_), channel_id=1, source_target_pairs={{0,2},{2,0},{4,6},{6,4},{8,10},{10,8},{12,14},{14,12},{16,18},{18,... | collective-permute-start | bytes 1400840 | tf_op jit(solution)/shard_map/ppermute | solution.py:41
  35.9 12.3 %collective-permute-start.11 = (bf16[32,7296]{1,0:T(8,128)(2,1)S(1)}, bf16[32,7296]{1,0:T(8,128)(2,1)S(1)}, u32[]{:S(2)}, u32[]{:S(2)}) collective-permute-start(bf16[32,7296]{1,0:T(8,128)(2,1)S(1)} %collective-permute-done.7.refs_1_), channel_id=1, source_target_pairs={{0,4},{2,6},{4,0},{6,2},{8,12},{10,14},{12,8},{14,10},{16,20},{18,... | collective-permute-start | bytes 1400840 | tf_op jit(solution)/shard_map/ppermute | solution.py:41
  37.7 2.0 %copy-start.1 = (bf16[7168,256]{1,0:T(8,128)(2,1)S(1)}, bf16[7168,256]{1,0:T(8,128)(2,1)}, u32[]{:S(2)}) copy-start(bf16[7168,256]{1,0:T(8,128)(2,1)} %copy-done) | copy-start | bytes 11010052
  40.7 7.5 %copy-start.2 = (bf16[7168,256]{1,0:T(8,128)(2,1)S(1)}, bf16[7168,256]{1,0:T(8,128)(2,1)}, u32[]{:S(2)}) copy-start(bf16[7168,256]{1,0:T(8,128)(2,1)} %copy-done) | copy-start | bytes 11010052
  57.1 12.6 %collective-permute-start.15 = (bf16[32,7168]{1,0:T(8,128)(2,1)S(1)}, bf16[32,7168]{1,0:T(8,128)(2,1)S(1)}, u32[]{:S(2)}, u32[]{:S(2)}) collective-permute-start(bf16[32,7168]{1,0:T(8,128)(2,1)S(1)} %get-tuple-element.49), channel_id=1, source_target_pairs={{0,4},{2,6},{4,0},{6,2},{8,12},{10,14},{12,8},{14,10},{16,20},{18,... | collective-permute-start | bytes 1376264 | tf_op jit(solution)/shard_map/ppermute | solution.py:41
  57.6 13.6 %collective-permute-start.13 = (bf16[32,7168]{1,0:T(8,128)(2,1)S(1)}, bf16[32,7168]{1,0:T(8,128)(2,1)S(1)}, u32[]{:S(2)}, u32[]{:S(2)}) collective-permute-start(bf16[32,7168]{1,0:T(8,128)(2,1)S(1)} %get-tuple-element.48), channel_id=1, source_target_pairs={{0,2},{2,0},{4,6},{6,4},{8,10},{10,8},{12,14},{14,12},{16,18},{18,... | collective-permute-start | bytes 1376264 | tf_op jit(solution)/shard_map/ppermute | solution.py:41
  69.8 7.7 %collective-permute-start.17 = (bf16[32,7168]{1,0:T(8,128)(2,1)S(1)}, bf16[32,7168]{1,0:T(8,128)(2,1)S(1)}, u32[]{:S(2)}, u32[]{:S(2)}) collective-permute-start(bf16[32,7168]{1,0:T(8,128)(2,1)S(1)} %add_convert_fusion.2), channel_id=1, source_target_pairs={{0,2},{2,0},{4,6},{6,4},{8,10},{10,8},{12,14},{14,12},{16,18},{18,... | collective-permute-start | bytes 1376264 | tf_op jit(solution)/shard_map/ppermute | solution.py:41
  71.3 15.4 %collective-permute-start.14 = (bf16[32,7168]{1,0:T(8,128)(2,1)S(1)}, bf16[32,7168]{1,0:T(8,128)(2,1)S(1)}, u32[]{:S(2)}, u32[]{:S(2)}) collective-permute-start(bf16[32,7168]{1,0:T(8,128)(2,1)S(1)} %add_convert_fusion.3), channel_id=1, source_target_pairs={{0,4},{2,6},{4,0},{6,2},{8,12},{10,14},{12,8},{14,10},{16,20},{18,... | collective-permute-start | bytes 1376264 | tf_op jit(solution)/shard_map/ppermute | solution.py:41
  71.5 17.1 %collective-permute-start.16 = (bf16[32,7168]{1,0:T(8,128)(2,1)S(1)}, bf16[32,7168]{1,0:T(8,128)(2,1)S(1)}, u32[]{:S(2)}, u32[]{:S(2)}) collective-permute-start(bf16[32,7168]{1,0:T(8,128)(2,1)S(1)} %get-tuple-element.50), channel_id=1, source_target_pairs={{0,2},{2,0},{4,6},{6,4},{8,10},{10,8},{12,14},{14,12},{16,18},{18,... | collective-permute-start | bytes 1376264 | tf_op jit(solution)/shard_map/ppermute | solution.py:41
  77.7 13.0 %collective-permute-start.18 = (bf16[32,7168]{1,0:T(8,128)(2,1)S(1)}, bf16[32,7168]{1,0:T(8,128)(2,1)S(1)}, u32[]{:S(2)}, u32[]{:S(2)}) collective-permute-start(bf16[32,7168]{1,0:T(8,128)(2,1)S(1)} %add_convert_fusion.1), channel_id=1, source_target_pairs={{0,8},{2,10},{4,12},{6,14},{8,0},{10,2},{12,4},{14,6},{16,24},{18,... | collective-permute-start | bytes 1376264 | tf_op jit(solution)/shard_map/ppermute | solution.py:41
  86.7 8.1 %collective-permute-start.20 = (bf16[32,7168]{1,0:T(8,128)(2,1)S(1)}, bf16[32,7168]{1,0:T(8,128)(2,1)S(1)}, u32[]{:S(2)}, u32[]{:S(2)}) collective-permute-start(bf16[32,7168]{1,0:T(8,128)(2,1)S(1)} %get-tuple-element.56), channel_id=1, source_target_pairs={{0,2},{2,0},{4,6},{6,4},{8,10},{10,8},{12,14},{14,12},{16,18},{18,... | collective-permute-start | bytes 1376264 | tf_op jit(solution)/shard_map/ppermute | solution.py:41
  90.9 7.4 %collective-permute-start.19 = (bf16[32,7168]{1,0:T(8,128)(2,1)S(1)}, bf16[32,7168]{1,0:T(8,128)(2,1)S(1)}, u32[]{:S(2)}, u32[]{:S(2)}) collective-permute-start(bf16[32,7168]{1,0:T(8,128)(2,1)S(1)} %add_convert_fusion), channel_id=1, source_target_pairs={{0,16},{2,18},{4,20},{6,22},{8,24},{10,26},{12,28},{14,30},{16,0},... | collective-permute-start | bytes 1376264 | tf_op jit(solution)/shard_map/ppermute | solution.py:41
  98.5 17.4 %collective-permute-start.21 = (bf16[16,7168]{1,0:T(8,128)(2,1)S(1)}, bf16[16,7168]{1,0:T(8,128)(2,1)S(1)}, u32[]{:S(2)}, u32[]{:S(2)}) collective-permute-start(bf16[16,7168]{1,0:T(8,128)(2,1)S(1)} %slice.15), channel_id=1, source_target_pairs={{0,1},{1,0},{2,3},{3,2},{4,5},{5,4},{6,7},{7,6},{8,9},{9,8},{10,11... | collective-permute-start | bytes 688136 | tf_op jit(solution)/shard_map/ppermute | solution.py:49
  (5 other events, 5.6 us)

commit v12 on v8

--- a/solution.py
+++ b/solution.py
@@ -36,7 +36,7 @@
 
 
 def across(value, bits, ep_count):
-    pairs = [(i * 2 + c, (i ^ bit) * 2 + c) for c, bit in enumerate(bits) if bit for i in range(ep_count)]
+    pairs = [(i * 2 + c, (i ^ bit) * 2 + c) for c, bit in enumerate(bits) for i in range(ep_count)]
     return lax.ppermute(value, ("ep", "grp"), pairs)
 
 
@@ -274,11 +274,14 @@
         chosen.append(between_cores(routes.T))
     own = prepare(gain, hiddens, chosen)
     weights = [(w[0, 0], between_cores(after(w[0, 0], hiddens[1:] + chosen[1:]))) for w in (w_gate, w_up, w_down)]
+    router_t = jnp.pad(router_w.T, ((0, -expert_count % 16), (0, 0)))
     held = [own]
     for slot, (parent, *bits) in enumerate(plan, 1):
         ended = held[1 : slot + 1 - most_open[slot - 1]]
         if slot in weights_end:
             ended.append(weights[weights_end[slot]][1])
+        if paired and slot == 3:
+            ended.append(router_t)
         held.append(across(after(held[parent], ended), bits, ep_count))
     first = 0
     if paired:
@@ -287,7 +290,6 @@
         held[spare] = jnp.where(core == 1, own, held[spare])
 
     ids = jnp.stack([core * local_experts + place, (1 - core) * local_experts + place]).astype(jnp.int32)
-    router_t = jnp.pad(router_w.T, ((0, -expert_count % 16), (0, 0)))
     done = early(ids, held[1 : 1 + EARLY], router_t, *weights[:2]) if paired else ()
     outs = experts(ids, held[1 + EARLY :] if paired else held, done, router_t, *weights)
 
@@ -301,6 +303,8 @@
     returned = []
     for slot, (parent, *bits) in return_plan:
         value = summed(slot).astype(jnp.bfloat16)
+        if paired and slot == spare:
+            value = jnp.where(core == 1, jnp.zeros_like(value), value)
         value = after(value, returned[: max(0, len(returned) + 1 - OPEN_RETURN)])
         returned.append(across(value, bits, ep_count))
         terms[parent].append(returned[-1])

time: 110 us -> 111 us (level)
  transfers between devices with their start and end apart: 22 -> 22, of which waited for: 15 -> 15; matrix products, arithmetic and copies ran while one was open for 1% -> 2% of each run, Pallas kernels for 9% -> 9%
where the time goes in v12:
time: 111 us; the launch traced here: 110 us
  waiting for transfers between devices  53.7 us (48%)
  starting transfers between devices  28.8 us (26%)
  Pallas kernels  22.7 us (20%)
  local copies, waits for them, and re-layouts  2.98 us (3%)
  other arithmetic  1.67 us (2%)
    ppermute x16, waiting for transfers between devices, across(): return lax.ppermute(value, ('ep', 'grp'), pairs)  50.9 us
    ppermute x16, starting transfers between devices, across(): return lax.ppermute(value, ('ep', 'grp'), pairs)  27.3 us
    pallas_call x1, Pallas kernels, experts(): pl.pallas_call(functools.partial(experts_kernel, blocks, done_rows, rows,...  13 us
    pallas_call x1, Pallas kernels, early(): pl.pallas_call(functools.partial(early_kernel, blocks, k_steps, k_tile),...  7.48 us
    ppermute x6, waiting for transfers between devices, between_cores(): return lax.ppermute(value, 'grp', [(0, 1), (1, 0)])  2.8 us
  transfers between devices with their start and end apart: 22, of which 15 were waited for; matrix products, arithmetic and copies ran while one was open for 2% of the time, Pallas kernels for 9%

profile of v12, /device:TPU:0, one launch (start us, length us, event | category | flops | bytes accessed | tf_op | source)
XLA Modules:
  0.0 110.0 jit_solution(9204821338787923614)
XLA Ops:
  2.7 2.2 %prepare.1 = bf16[32,7296]{1,0:T(8,128)(2,1)} custom-call(f32[1,7168]{1,0:T(1,128)} %bitcast.17, bf16[16,7168]{1,0:T(8,128)(2,1)} %refs_1_.1, bf16[16,7168]{1,0:T(8,128)(2,1)} %copy-done.1, s32[4,16]{1,0:T(4,128)} %bitcast.19, s32[4,16]{1,0:T(4,128)} %copy-done.2), custom_call_target="tpu_custom_call" | custom-call | flops 1376256 | bytes 917504 | tf_op jit(solution)/shard_map/prepare/pallas_call | solution.py:86
  4.9 2.7 %collective-permute-start.3 = (bf16[32,7296]{1,0:T(8,128)(2,1)}, bf16[32,7296]{1,0:T(8,128)(2,1)S(1)}, u32[]{:S(2)}, u32[]{:S(2)}) collective-permute-start(bf16[32,7296]{1,0:T(8,128)(2,1)} %prepare.1), channel_id=1, source_target_pairs={{0,2},{2,0},{4,6},{6,4},{8,10},{10,8},{12,14},{14,12},{16,18},{18,... | collective-permute-start | bytes 1400840 | tf_op jit(solution)/shard_map/ppermute | solution.py:40
  7.7 2.6 %collective-permute-start.2 = (bf16[32,7296]{1,0:T(8,128)(2,1)}, bf16[32,7296]{1,0:T(8,128)(2,1)S(1)}, u32[]{:S(2)}, u32[]{:S(2)}) collective-permute-start(bf16[32,7296]{1,0:T(8,128)(2,1)} %prepare.1), channel_id=1, source_target_pairs={{0,16},{2,18},{4,20},{6,22},{8,24},{10,26},{12,28},{14,30},{16,0},... | collective-permute-start | bytes 1400840 | tf_op jit(solution)/shard_map/ppermute | solution.py:40
  11.2 3.2 %collective-permute-done.3.refs_0_ = bf16[32,7296]{1,0:T(8,128)(2,1)S(1)} collective-permute-done((bf16[32,7296]{1,0:T(8,128)(2,1)}, bf16[32,7296]{1,0:T(8,128)(2,1)S(1)}, u32[]{:S(2)}, u32[]{:S(2)}) %collective-permute-start.3) | collective-permute-done | bytes 466976 | tf_op jit(solution)/shard_map/ppermute | solution.py:40
  14.4 7.0 %collective-permute-done.2.refs_1_ = bf16[32,7296]{1,0:T(8,128)(2,1)S(1)} collective-permute-done((bf16[32,7296]{1,0:T(8,128)(2,1)}, bf16[32,7296]{1,0:T(8,128)(2,1)S(1)}, u32[]{:S(2)}, u32[]{:S(2)}) %collective-permute-start.2) | collective-permute-done | bytes 466976 | tf_op jit(solution)/shard_map/ppermute | solution.py:40
  21.5 1.8 %collective-permute-start.4 = (bf16[32,7296]{1,0:T(8,128)(2,1)S(1)}, bf16[32,7296]{1,0:T(8,128)(2,1)S(1)}, u32[]{:S(2)}, u32[]{:S(2)}) collective-permute-start(bf16[32,7296]{1,0:T(8,128)(2,1)S(1)} %collective-permute-done.2.refs_1_), channel_id=1, source_target_pairs={{0,8},{2,10},{4,12},{6,14},{8,0},{10,2},{12,4},{14,6},{16,24},{18,... | collective-permute-start | bytes 1400840 | tf_op jit(solution)/shard_map/ppermute | solution.py:40
  24.7 5.3 %collective-permute-done.4.refs_2_ = bf16[32,7296]{1,0:T(8,128)(2,1)S(1)} collective-permute-done((bf16[32,7296]{1,0:T(8,128)(2,1)S(1)}, bf16[32,7296]{1,0:T(8,128)(2,1)S(1)}, u32[]{:S(2)}, u32[]{:S(2)}) %collective-permute-start.4) | collective-permute-done | bytes 466976 | tf_op jit(solution)/shard_map/ppermute | solution.py:40
  30.8 3.1 %collective-permute-start.12 = (bf16[32,7296]{1,0:T(8,128)(2,1)S(1)}, bf16[32,7296]{1,0:T(8,128)(2,1)S(1)}, u32[]{:S(2)}, u32[]{:S(2)}) collective-permute-start(bf16[32,7296]{1,0:T(8,128)(2,1)S(1)} %collective-permute-done.2.refs_1_), channel_id=1, source_target_pairs={{0,2},{2,0},{4,6},{6,4},{8,10},{10,8},{12,14},{14,12},{16,18},{18,... | collective-permute-start | bytes 1400840 | tf_op jit(solution)/shard_map/ppermute | solution.py:40
  34.1 2.8 %collective-permute-done.7.refs_3_ = bf16[32,7296]{1,0:T(8,128)(2,1)S(1)} collective-permute-done((bf16[32,7296]{1,0:T(8,128)(2,1)S(1)}, bf16[32,7296]{1,0:T(8,128)(2,1)S(1)}, u32[]{:S(2)}, u32[]{:S(2)}) %collective-permute-start.7) | collective-permute-done | bytes 466976 | tf_op jit(solution)/shard_map/ppermute | solution.py:40
  36.9 1.7 %collective-permute-done.6.refs_0_ = bf16[32,7296]{1,0:T(8,128)(2,1)S(1)} collective-permute-done((bf16[32,7296]{1,0:T(8,128)(2,1)S(1)}, bf16[32,7296]{1,0:T(8,128)(2,1)S(1)}, u32[]{:S(2)}, u32[]{:S(2)}) %collective-permute-start.6) | collective-permute-done | bytes 466976 | tf_op jit(solution)/shard_map/ppermute | solution.py:40
  38.6 2.5 %collective-permute-start.10 = (bf16[32,7296]{1,0:T(8,128)(2,1)S(1)}, bf16[32,7296]{1,0:T(8,128)(2,1)S(1)}, u32[]{:S(2)}, u32[]{:S(2)}) collective-permute-start(bf16[32,7296]{1,0:T(8,128)(2,1)S(1)} %collective-permute-done.6.refs_0_), channel_id=1, source_target_pairs={{0,4},{2,6},{4,0},{6,2},{8,12},{10,14},{12,8},{14,10},{16,20},{18,... | collective-permute-start | bytes 1400840 | tf_op jit(solution)/shard_map/ppermute | solution.py:40
  41.1 2.5 %collective-permute-done.12 = bf16[32,7296]{1,0:T(8,128)(2,1)S(1)} collective-permute-done((bf16[32,7296]{1,0:T(8,128)(2,1)S(1)}, bf16[32,7296]{1,0:T(8,128)(2,1)S(1)}, u32[]{:S(2)}, u32[]{:S(2)}) %collective-permute-start.12) | collective-permute-done | bytes 466976 | tf_op jit(solution)/shard_map/ppermute | solution.py:40
  43.7 2.0 %copy-done = bf16[1,1,7168,256]{3,2,1,0:T(8,128)(2,1)S(1)} copy-done((bf16[1,1,7168,256]{3,2,1,0:T(8,128)(2,1)S(1)}, bf16[1,1,7168,256]{3,2,1,0:T(8,128)(2,1)}, u32[]{:S(2)}) %copy-start) | copy-done | bytes 3670040
  45.7 7.5 %early.1 = (bf16[160,512]{1,0:T(8,128)(2,1)S(1)}, f32[160,256]{1,0:T(8,128)S(1)}) custom-call(s32[2]{0:T(128)S(1)} %pad_add_fusion.ids_ref, bf16[32,7296]{1,0:T(8,128)(2,1)S(1)} %collective-permute-done.3.refs_0_, bf16[32,7296]{1,0:T(8,128)(2,1)S(1)} %collective-permute-done.2.refs_1_, bf16[32,7296]{1,0:T(8,128)(2,1)S(1)} %collective-permute-done.4.refs_2_, ...), custom_call_target="tpu_custom_call" | custom-call | flops 2348810240 | bytes 16973824 | tf_op jit(solution)/shard_map/early/pallas_call | solution.py:152
  53.2 13.0 %experts.1 = (bf16[32,7168]{1,0:T(8,128)(2,1)S(1)}, bf16[32,7168]{1,0:T(8,128)(2,1)S(1)}, bf16[32,7168]{1,0:T(8,128)(2,1)S(1)}, bf16[32,7168]{1,0:T(8,128)(2,1)S...) custom-call(s32[2]{0:T(128)S(1)} %pad_add_fusion.ids_ref, ...), custom_call_target="tpu_custom_call" | custom-call | flops 3288334336 | bytes 29360128 | tf_op jit(solution)/shard_map/experts/pallas_call | solution.py:239
  66.3 2.5 %collective-permute-start.15 = (bf16[32,7168]{1,0:T(8,128)(2,1)S(1)}, bf16[32,7168]{1,0:T(8,128)(2,1)S(1)}, u32[]{:S(2)}, u32[]{:S(2)}) collective-permute-start(bf16[32,7168]{1,0:T(8,128)(2,1)S(1)} %get-tuple-element.43), channel_id=1, source_target_pairs={{0,4},{2,6},{4,0},{6,2},{8,12},{10,14},{12,8},{14,10},{16,20},{18,... | collective-permute-start | bytes 1376264 | tf_op jit(solution)/shard_map/ppermute | solution.py:40
  68.9 6.3 %collective-permute-done.15 = bf16[32,7168]{1,0:T(8,128)(2,1)S(1)} collective-permute-done((bf16[32,7168]{1,0:T(8,128)(2,1)S(1)}, bf16[32,7168]{1,0:T(8,128)(2,1)S(1)}, u32[]{:S(2)}, u32[]{:S(2)}) %collective-permute-start.15) | collective-permute-done | bytes 458784 | tf_op jit(solution)/shard_map/ppermute | solution.py:40
  75.8 1.6 %collective-permute-done.13 = bf16[32,7168]{1,0:T(8,128)(2,1)S(1)} collective-permute-done((bf16[32,7168]{1,0:T(8,128)(2,1)S(1)}, bf16[32,7168]{1,0:T(8,128)(2,1)S(1)}, u32[]{:S(2)}, u32[]{:S(2)}) %collective-permute-start.13) | collective-permute-done | bytes 458784 | tf_op jit(solution)/shard_map/ppermute | solution.py:40
  77.7 3.9 %collective-permute-start.16 = (bf16[32,7168]{1,0:T(8,128)(2,1)S(1)}, bf16[32,7168]{1,0:T(8,128)(2,1)S(1)}, u32[]{:S(2)}, u32[]{:S(2)}) collective-permute-start(bf16[32,7168]{1,0:T(8,128)(2,1)S(1)} %broadcast_select_fusion.1), channel_id=1, source_target_pairs={{0,2},{2,0},{4,6},{6,4},{8,10},{10,8},{12,14},{14,12},{16,18},{18,... | collective-permute-start | bytes 1376264 | tf_op jit(solution)/shard_map/ppermute | solution.py:40
  81.6 2.3 %collective-permute-done.17 = bf16[32,7168]{1,0:T(8,128)(2,1)S(1)} collective-permute-done((bf16[32,7168]{1,0:T(8,128)(2,1)S(1)}, bf16[32,7168]{1,0:T(8,128)(2,1)S(1)}, u32[]{:S(2)}, u32[]{:S(2)}) %collective-permute-start.17) | collective-permute-done | bytes 458784 | tf_op jit(solution)/shard_map/ppermute | solution.py:40
  85.4 5.6 %collective-permute-done.14 = bf16[32,7168]{1,0:T(8,128)(2,1)S(1)} collective-permute-done((bf16[32,7168]{1,0:T(8,128)(2,1)S(1)}, bf16[32,7168]{1,0:T(8,128)(2,1)S(1)}, u32[]{:S(2)}, u32[]{:S(2)}) %collective-permute-start.14) | collective-permute-done | bytes 458784 | tf_op jit(solution)/shard_map/ppermute | solution.py:40
  92.8 3.8 %collective-permute-start.19 = (bf16[32,7168]{1,0:T(8,128)(2,1)S(1)}, bf16[32,7168]{1,0:T(8,128)(2,1)S(1)}, u32[]{:S(2)}, u32[]{:S(2)}) collective-permute-start(bf16[32,7168]{1,0:T(8,128)(2,1)S(1)} %add_convert_fusion), channel_id=1, source_target_pairs={{0,16},{2,18},{4,20},{6,22},{8,24},{10,26},{12,28},{14,30},{16,0},... | collective-permute-start | bytes 1376264 | tf_op jit(solution)/shard_map/ppermute | solution.py:40
  96.6 2.9 %collective-permute-done.20 = bf16[32,7168]{1,0:T(8,128)(2,1)S(1)} collective-permute-done((bf16[32,7168]{1,0:T(8,128)(2,1)S(1)}, bf16[32,7168]{1,0:T(8,128)(2,1)S(1)}, u32[]{:S(2)}, u32[]{:S(2)}) %collective-permute-start.20) | collective-permute-done | bytes 458784 | tf_op jit(solution)/shard_map/ppermute | solution.py:40
  99.5 8.0 %collective-permute-done.19 = bf16[32,7168]{1,0:T(8,128)(2,1)S(1)} collective-permute-done((bf16[32,7168]{1,0:T(8,128)(2,1)S(1)}, bf16[32,7168]{1,0:T(8,128)(2,1)S(1)}, u32[]{:S(2)}, u32[]{:S(2)}) %collective-permute-start.19) | collective-permute-done | bytes 458784 | tf_op jit(solution)/shard_map/ppermute | solution.py:40
  (40 shorter events, 12.8 us)
Async XLA Ops:
  0.0 1.8 %collective-permute-start = (bf16[16,7168]{1,0:T(8,128)(2,1)}, bf16[16,7168]{1,0:T(8,128)(2,1)S(1)}, u32[]{:S(2)}, u32[]{:S(2)}) collective-permute-start(bf16[16,7168]{1,0:T(8,128)(2,1)} %refs_1_.1), channel_id=1, source_target_pairs={{0,1},{1,0},{2,3},{3,2},{4,5},{5,4},{6,7},{7,6},{8,9},{9,8},{10,11... | collective-permute-start | bytes 688136 | tf_op jit(solution)/shard_map/ppermute | solution.py:48
  0.5 1.4 %collective-permute-start.1 = (s32[4,16]{1,0:T(4,128)}, s32[4,16]{1,0:T(4,128)S(1)}, u32[]{:S(2)}, u32[]{:S(2)}) collective-permute-start(s32[4,16]{1,0:T(4,128)} %bitcast.18), channel_id=1, source_target_pairs={{0,1},{1,0},{2,3},{3,2},{4,5},{5,4},{6,7},{7,6},{8,9},{9,8},{10,11... | collective-permute-start | bytes 776 | tf_op jit(solution)/shard_map/ppermute | solution.py:48
  1.8 0.9 copy-start.2
  1.8 28.2 %collective-permute-start.5 = (bf16[7168,256]{1,0:T(8,128)(2,1)}, bf16[7168,256]{1,0:T(8,128)(2,1)}, u32[]{:S(2)}, u32[]{:S(2)}) collective-permute-start(bf16[7168,256]{1,0:T(8,128)(2,1)} %bitcast.8), channel_id=1, source_target_pairs={{0,1},{1,0},{2,3},{3,2},{4,5},{5,4},{6,7},{7,6},{8,9},{9,8},{10,11... | collective-permute-start | bytes 11010056 | tf_op jit(solution)/shard_map/ppermute | solution.py:48
  2.2 34.6 %collective-permute-start.8 = (bf16[7168,256]{1,0:T(8,128)(2,1)}, bf16[7168,256]{1,0:T(8,128)(2,1)}, u32[]{:S(2)}, u32[]{:S(2)}) collective-permute-start(bf16[7168,256]{1,0:T(8,128)(2,1)} %bitcast.11), channel_id=1, source_target_pairs={{0,1},{1,0},{2,3},{3,2},{4,5},{5,4},{6,7},{7,6},{8,9},{9,8},{10,11... | collective-permute-start | bytes 11010056 | tf_op jit(solution)/shard_map/ppermute | solution.py:48
  2.4 50.8 %collective-permute-start.11 = (bf16[256,7168]{1,0:T(8,128)(2,1)}, bf16[256,7168]{1,0:T(8,128)(2,1)}, u32[]{:S(2)}, u32[]{:S(2)}) collective-permute-start(bf16[256,7168]{1,0:T(8,128)(2,1)} %bitcast.14), channel_id=1, source_target_pairs={{0,1},{1,0},{2,3},{3,2},{4,5},{5,4},{6,7},{7,6},{8,9},{9,8},{10,11... | collective-permute-start | bytes 11010056 | tf_op jit(solution)/shard_map/ppermute | solution.py:48
  4.9 9.5 %collective-permute-start.3 = (bf16[32,7296]{1,0:T(8,128)(2,1)}, bf16[32,7296]{1,0:T(8,128)(2,1)S(1)}, u32[]{:S(2)}, u32[]{:S(2)}) collective-permute-start(bf16[32,7296]{1,0:T(8,128)(2,1)} %prepare.1), channel_id=1, source_target_pairs={{0,2},{2,0},{4,6},{6,4},{8,10},{10,8},{12,14},{14,12},{16,18},{18,... | collective-permute-start | bytes 1400840 | tf_op jit(solution)/shard_map/ppermute | solution.py:40
  7.7 13.8 %collective-permute-start.2 = (bf16[32,7296]{1,0:T(8,128)(2,1)}, bf16[32,7296]{1,0:T(8,128)(2,1)S(1)}, u32[]{:S(2)}, u32[]{:S(2)}) collective-permute-start(bf16[32,7296]{1,0:T(8,128)(2,1)} %prepare.1), channel_id=1, source_target_pairs={{0,16},{2,18},{4,20},{6,22},{8,24},{10,26},{12,28},{14,30},{16,0},... | collective-permute-start | bytes 1400840 | tf_op jit(solution)/shard_map/ppermute | solution.py:40
  21.5 8.6 %collective-permute-start.4 = (bf16[32,7296]{1,0:T(8,128)(2,1)S(1)}, bf16[32,7296]{1,0:T(8,128)(2,1)S(1)}, u32[]{:S(2)}, u32[]{:S(2)}) collective-permute-start(bf16[32,7296]{1,0:T(8,128)(2,1)S(1)} %collective-permute-done.2.refs_1_), channel_id=1, source_target_pairs={{0,8},{2,10},{4,12},{6,14},{8,0},{10,2},{12,4},{14,6},{16,24},{18,... | collective-permute-start | bytes 1400840 | tf_op jit(solution)/shard_map/ppermute | solution.py:40
  23.2 13.6 %collective-permute-start.7 = (bf16[32,7296]{1,0:T(8,128)(2,1)S(1)}, bf16[32,7296]{1,0:T(8,128)(2,1)S(1)}, u32[]{:S(2)}, u32[]{:S(2)}) collective-permute-start(bf16[32,7296]{1,0:T(8,128)(2,1)S(1)} %collective-permute-done.2.refs_1_), channel_id=1, source_target_pairs={{0,4},{2,6},{4,0},{6,2},{8,12},{10,14},{12,8},{14,10},{16,20},{18,... | collective-permute-start | bytes 1400840 | tf_op jit(solution)/shard_map/ppermute | solution.py:40
  30.0 8.6 %collective-permute-start.6 = (bf16[32,7296]{1,0:T(8,128)(2,1)S(1)}, bf16[32,7296]{1,0:T(8,128)(2,1)S(1)}, u32[]{:S(2)}, u32[]{:S(2)}) collective-permute-start(bf16[32,7296]{1,0:T(8,128)(2,1)S(1)} %collective-permute-done.4.refs_2_), channel_id=1, source_target_pairs={{0,2},{2,0},{4,6},{6,4},{8,10},{10,8},{12,14},{14,12},{16,18},{18,... | collective-permute-start | bytes 1400840 | tf_op jit(solution)/shard_map/ppermute | solution.py:40
  30.8 12.8 %collective-permute-start.12 = (bf16[32,7296]{1,0:T(8,128)(2,1)S(1)}, bf16[32,7296]{1,0:T(8,128)(2,1)S(1)}, u32[]{:S(2)}, u32[]{:S(2)}) collective-permute-start(bf16[32,7296]{1,0:T(8,128)(2,1)S(1)} %collective-permute-done.2.refs_1_), channel_id=1, source_target_pairs={{0,2},{2,0},{4,6},{6,4},{8,10},{10,8},{12,14},{14,12},{16,18},{18,... | collective-permute-start | bytes 1400840 | tf_op jit(solution)/shard_map/ppermute | solution.py:40
  36.9 16.4 %collective-permute-start.9 = (bf16[32,7296]{1,0:T(8,128)(2,1)S(1)}, bf16[32,7296]{1,0:T(8,128)(2,1)S(1)}, u32[]{:S(2)}, u32[]{:S(2)}) collective-permute-start(bf16[32,7296]{1,0:T(8,128)(2,1)S(1)} %collective-permute-done.7.refs_3_), channel_id=1, source_target_pairs={{0,2},{2,0},{4,6},{6,4},{8,10},{10,8},{12,14},{14,12},{16,18},{18,... | collective-permute-start | bytes 1400840 | tf_op jit(solution)/shard_map/ppermute | solution.py:40
  38.6 14.6 %collective-permute-start.10 = (bf16[32,7296]{1,0:T(8,128)(2,1)S(1)}, bf16[32,7296]{1,0:T(8,128)(2,1)S(1)}, u32[]{:S(2)}, u32[]{:S(2)}) collective-permute-start(bf16[32,7296]{1,0:T(8,128)(2,1)S(1)} %collective-permute-done.6.refs_0_), channel_id=1, source_target_pairs={{0,4},{2,6},{4,0},{6,2},{8,12},{10,14},{12,8},{14,10},{16,20},{18,... | collective-permute-start | bytes 1400840 | tf_op jit(solution)/shard_map/ppermute | solution.py:40
  43.7 2.0 %copy-start = (bf16[1,1,7168,256]{3,2,1,0:T(8,128)(2,1)S(1)}, bf16[1,1,7168,256]{3,2,1,0:T(8,128)(2,1)}, u32[]{:S(2)}) copy-start(bf16[1,1,7168,256]{3,2,1,0:T(8,128)(2,1)} %param.11) | copy-start | bytes 11010052
  66.3 9.0 %collective-permute-start.15 = (bf16[32,7168]{1,0:T(8,128)(2,1)S(1)}, bf16[32,7168]{1,0:T(8,128)(2,1)S(1)}, u32[]{:S(2)}, u32[]{:S(2)}) collective-permute-start(bf16[32,7168]{1,0:T(8,128)(2,1)S(1)} %get-tuple-element.43), channel_id=1, source_target_pairs={{0,4},{2,6},{4,0},{6,2},{8,12},{10,14},{12,8},{14,10},{16,20},{18,... | collective-permute-start | bytes 1376264 | tf_op jit(solution)/shard_map/ppermute | solution.py:40
  68.9 8.5 %collective-permute-start.13 = (bf16[32,7168]{1,0:T(8,128)(2,1)S(1)}, bf16[32,7168]{1,0:T(8,128)(2,1)S(1)}, u32[]{:S(2)}, u32[]{:S(2)}) collective-permute-start(bf16[32,7168]{1,0:T(8,128)(2,1)S(1)} %get-tuple-element.42), channel_id=1, source_target_pairs={{0,2},{2,0},{4,6},{6,4},{8,10},{10,8},{12,14},{14,12},{16,18},{18,... | collective-permute-start | bytes 1376264 | tf_op jit(solution)/shard_map/ppermute | solution.py:40
  75.4 8.5 %collective-permute-start.17 = (bf16[32,7168]{1,0:T(8,128)(2,1)S(1)}, bf16[32,7168]{1,0:T(8,128)(2,1)S(1)}, u32[]{:S(2)}, u32[]{:S(2)}) collective-permute-start(bf16[32,7168]{1,0:T(8,128)(2,1)S(1)} %add_convert_fusion.2), channel_id=1, source_target_pairs={{0,2},{2,0},{4,6},{6,4},{8,10},{10,8},{12,14},{14,12},{16,18},{18,... | collective-permute-start | bytes 1376264 | tf_op jit(solution)/shard_map/ppermute | solution.py:40
  77.5 13.5 %collective-permute-start.14 = (bf16[32,7168]{1,0:T(8,128)(2,1)S(1)}, bf16[32,7168]{1,0:T(8,128)(2,1)S(1)}, u32[]{:S(2)}, u32[]{:S(2)}) collective-permute-start(bf16[32,7168]{1,0:T(8,128)(2,1)S(1)} %add_convert_fusion.3), channel_id=1, source_target_pairs={{0,4},{2,6},{4,0},{6,2},{8,12},{10,14},{12,8},{14,10},{16,20},{18,... | collective-permute-start | bytes 1376264 | tf_op jit(solution)/shard_map/ppermute | solution.py:40
  77.7 13.4 %collective-permute-start.16 = (bf16[32,7168]{1,0:T(8,128)(2,1)S(1)}, bf16[32,7168]{1,0:T(8,128)(2,1)S(1)}, u32[]{:S(2)}, u32[]{:S(2)}) collective-permute-start(bf16[32,7168]{1,0:T(8,128)(2,1)S(1)} %broadcast_select_fusion.1), channel_id=1, source_target_pairs={{0,2},{2,0},{4,6},{6,4},{8,10},{10,8},{12,14},{14,12},{16,18},{18,... | collective-permute-start | bytes 1376264 | tf_op jit(solution)/shard_map/ppermute | solution.py:40
  84.1 8.5 %collective-permute-start.18 = (bf16[32,7168]{1,0:T(8,128)(2,1)S(1)}, bf16[32,7168]{1,0:T(8,128)(2,1)S(1)}, u32[]{:S(2)}, u32[]{:S(2)}) collective-permute-start(bf16[32,7168]{1,0:T(8,128)(2,1)S(1)} %add_convert_fusion.1), channel_id=1, source_target_pairs={{0,8},{2,10},{4,12},{6,14},{8,0},{10,2},{12,4},{14,6},{16,24},{18,... | collective-permute-start | bytes 1376264 | tf_op jit(solution)/shard_map/ppermute | solution.py:40
  91.0 8.5 %collective-permute-start.20 = (bf16[32,7168]{1,0:T(8,128)(2,1)S(1)}, bf16[32,7168]{1,0:T(8,128)(2,1)S(1)}, u32[]{:S(2)}, u32[]{:S(2)}) collective-permute-start(bf16[32,7168]{1,0:T(8,128)(2,1)S(1)} %get-tuple-element.50), channel_id=1, source_target_pairs={{0,2},{2,0},{4,6},{6,4},{8,10},{10,8},{12,14},{14,12},{16,18},{18,... | collective-permute-start | bytes 1376264 | tf_op jit(solution)/shard_map/ppermute | solution.py:40
  92.8 14.7 %collective-permute-start.19 = (bf16[32,7168]{1,0:T(8,128)(2,1)S(1)}, bf16[32,7168]{1,0:T(8,128)(2,1)S(1)}, u32[]{:S(2)}, u32[]{:S(2)}) collective-permute-start(bf16[32,7168]{1,0:T(8,128)(2,1)S(1)} %add_convert_fusion), channel_id=1, source_target_pairs={{0,16},{2,18},{4,20},{6,22},{8,24},{10,26},{12,28},{14,30},{16,0},... | collective-permute-start | bytes 1376264 | tf_op jit(solution)/shard_map/ppermute | solution.py:40
  107.7 1.6 %collective-permute-start.21 = (bf16[16,7168]{1,0:T(8,128)(2,1)S(1)}, bf16[16,7168]{1,0:T(8,128)(2,1)S(1)}, u32[]{:S(2)}, u32[]{:S(2)}) collective-permute-start(bf16[16,7168]{1,0:T(8,128)(2,1)S(1)} %slice.15), channel_id=1, source_target_pairs={{0,1},{1,0},{2,3},{3,2},{4,5},{5,4},{6,7},{7,6},{8,9},{9,8},{10,11... | collective-permute-start | bytes 688136 | tf_op jit(solution)/shard_map/ppermute | solution.py:48
  (1 other events, 0.9 us)
